TPU v7x, 32 devices: a whole 2x2x4 slice. The times are simulated.
32 devices in a mesh: wide: 16 (over z, y, x), narrow: 2 (over core).
Axes of the slice: x: 2, y: 2, z: 4, core: 2. Of those that a mesh axis runs over, the one named last changes fastest.
Arguments:
- stream: bfloat16 [32768, 768], P(('wide', 'narrow')), may hold values from -6 to 6
- seq_lengths: int32 [16, 2], P('wide'), may hold values from 0 to 2048, as said below
- cotangent: float32 [32768, 768], P(('wide', 'narrow')), may hold values from -6 to 6
- w_qkv: bfloat16 [2, 768, 3, 768], P(None, None, None, 'narrow'), may hold values from -0.21875 to 0.21875
- w_out: bfloat16 [2, 768, 768], P(None, 'narrow'), may hold values from -6 to 6
- w_in: bfloat16 [2, 768, 3072], P(None, None, 'narrow'), may hold values from -0.21875 to 0.21875
- w_back: bfloat16 [2, 3072, 768], P(None, 'narrow'), may hold values from -0.109375 to 0.109375
- norm_params: float32 [2, 4, 768], replicated, may hold values from -2.5 to 2.5, as said below
- qkv_master: float32 [2, 768, 3, 768], P(None, 'wide', None, 'narrow'), may hold values from -0.21875 to 0.21875
- qkv_first: float32 [2, 768, 3, 768], P(None, 'wide', None, 'narrow'), may hold values from -0.00390625 to 0.00390625
- qkv_second: float32 [2, 768, 3, 768], P(None, 'wide', None, 'narrow'), may hold values from 7.06119e-08 to 2.824476e-07
- out_master: float32 [2, 768, 768], P(None, ('narrow', 'wide')), may hold values from -0.21875 to 0.21875
- out_first: float32 [2, 768, 768], P(None, ('narrow', 'wide')), may hold values from -0.00036621094 to 0.00036621094
- out_second: float32 [2, 768, 768], P(None, ('narrow', 'wide')), may hold values from 6.2061234e-10 to 2.4824494e-09
- in_master: float32 [2, 768, 3072], P(None, 'wide', 'narrow'), may hold values from -0.21875 to 0.21875
- in_first: float32 [2, 768, 3072], P(None, 'wide', 'narrow'), may hold values from -0.00390625 to 0.00390625
- in_second: float32 [2, 768, 3072], P(None, 'wide', 'narrow'), may hold values from 7.06119e-08 to 2.824476e-07
- back_master: float32 [2, 3072, 768], P(None, ('narrow', 'wide')), may hold values from -0.109375 to 0.109375
- back_first: float32 [2, 3072, 768], P(None, ('narrow', 'wide')), may hold values from -0.00390625 to 0.00390625
- back_second: float32 [2, 3072, 768], P(None, ('narrow', 'wide')), may hold values from 7.06119e-08 to 2.824476e-07
- norm_master: float32 [2, 4, 768], P(None, None, ('wide', 'narrow')), may hold values from -2.5 to 2.5, as said below
- norm_first: float32 [2, 4, 768], P(None, None, ('wide', 'narrow')), may hold values from -0.00390625 to 0.00390625
- norm_second: float32 [2, 4, 768], P(None, None, ('wide', 'narrow')), may hold values from 7.06119e-08 to 2.824476e-07
Outputs:
- output: float32 [32768, 768], P(('wide', 'narrow'))
- stream_grad: float32 [32768, 768], P(('wide', 'narrow'))
- qkv_master_new: float32 [2, 768, 3, 768], P(None, 'wide', None, 'narrow')
- qkv_first_new: float32 [2, 768, 3, 768], P(None, 'wide', None, 'narrow')
- qkv_second_new: float32 [2, 768, 3, 768], P(None, 'wide', None, 'narrow')
- out_master_new: float32 [2, 768, 768], P(None, ('narrow', 'wide'))
- out_first_new: float32 [2, 768, 768], P(None, ('narrow', 'wide'))
- out_second_new: float32 [2, 768, 768], P(None, ('narrow', 'wide'))
- in_master_new: float32 [2, 768, 3072], P(None, 'wide', 'narrow')
- in_first_new: float32 [2, 768, 3072], P(None, 'wide', 'narrow')
- in_second_new: float32 [2, 768, 3072], P(None, 'wide', 'narrow')
- back_master_new: float32 [2, 3072, 768], P(None, ('narrow', 'wide'))
- back_first_new: float32 [2, 3072, 768], P(None, ('narrow', 'wide'))
- back_second_new: float32 [2, 3072, 768], P(None, ('narrow', 'wide'))
- norm_master_new: float32 [2, 4, 768], P(None, None, ('wide', 'narrow'))
- norm_first_new: float32 [2, 4, 768], P(None, None, ('wide', 'narrow'))
- norm_second_new: float32 [2, 4, 768], P(None, None, ('wide', 'narrow'))
- clip_norm: float32 [1], replicated
Inputs may be any that keep to these rules, and one draw needn't show every extreme that they name: `seq_lengths`: row b holds the lengths of bucket b's sequences, laid end to end from the bucket's first slot; the rest of the bucket is padding. Either both entries are 1024, or the first lies from 1024 to 2048 and the second is 0. Some bucket holds one sequence of 2048, some bucket two of 1024. `norm_params`: rows 0 and 2 of each layer are positive gains, rows 1 and 3 shifts. `norm_master`: rows 0 and 2 of each layer are positive gains, rows 1 and 3 shifts.
All inputs are finite; a program needn't handle non-finite values.
Results may differ from a plain program's by a relative error of at most 0.023.
Values may be sent and summed in bfloat16 or wider, within the bound.
No kernel may reach another device: no remote copies, remote signals or barrier semaphores. Data moves between devices by JAX's collectives and lax.ppermute only.
A program may use at most 320 MiB of HBM per device.

v0:
```python
import functools
import math

import jax
import jax.numpy as jnp
from jax import lax
from jax.sharding import PartitionSpec as P

HEAD = 64
LAYERS = 2
BLOCK = 512


HIGH = lax.Precision.HIGHEST
EPS_NORM = 1e-05
CLIP = 1.0
BETA_ONE = 0.5
BETA_TWO = 0.5
ADAM_EPS = 1e-08
LR_MATRIX = 0.1
LR_NORMS = 0.5
DECAY_MATRIX = 0.1
STEP_NUMBER = 4.0


def row_layout(lengths, row_count):
    row_index = jnp.arange(row_count, dtype=jnp.int32)
    first_len = lengths[0]
    second_len = lengths[1]
    in_first = row_index < first_len
    in_second = (row_index >= first_len) & (row_index < first_len + second_len)
    segment = jnp.where(in_first, 0, jnp.where(in_second, 1, -1)).astype(jnp.int32)
    position = jnp.where(
        in_first, row_index, jnp.where(in_second, row_index - first_len, row_index)
    )
    seq_span = jnp.where(in_first, first_len, jnp.where(in_second, second_len, 1))
    phase_angle = 0.5 * math.pi * position.astype(jnp.float32) / seq_span.astype(jnp.float32)
    return (segment, jnp.cos(phase_angle), jnp.sin(phase_angle))


def attend(packed, segment, cosine, sine, block_rows, head_count):
    row_count = packed.shape[0]
    width = packed.shape[2]
    head_size = width // head_count
    block_count = row_count // block_rows

    def split_blocks(values):
        return values.reshape((block_count, block_rows) + values.shape[1:])

    queries = packed[:, 0].reshape(row_count, head_count, head_size)
    keys = packed[:, 1].reshape(row_count, head_count, head_size)
    value_rows = packed[:, 2].reshape(row_count, head_count, head_size)
    block_inputs = (
        split_blocks(queries),
        split_blocks(keys),
        split_blocks(value_rows),
        split_blocks(segment),
        split_blocks(cosine),
        split_blocks(sine),
    )
    local_index = jnp.arange(block_rows, dtype=jnp.int32)

    @jax.checkpoint
    def block_step(carry_in, pieces):
        kv_state, key_total, before = carry_in
        query_part, key_part, value_part, seg_part, cos_part, sin_part = pieces
        query_feat = jax.nn.relu(query_part)
        key_feat = jax.nn.relu(key_part)
        query_cat = jnp.concatenate(
            [query_feat * cos_part[:, None, None], query_feat * sin_part[:, None, None]], axis=2
        )
        key_cat = jnp.concatenate(
            [key_feat * cos_part[:, None, None], key_feat * sin_part[:, None, None]], axis=2
        )
        live_mask = seg_part >= 0
        same_seq = (
            (seg_part[:, None] == seg_part[None, :])
            & (local_index[None, :] <= local_index[:, None])
            & live_mask[:, None]
        )
        scores = jnp.einsum("ihf,jhf->hij", query_cat, key_cat, precision=HIGH)
        scores = jnp.where(same_seq[None], scores, 0.0)
        numerator = jnp.einsum("hij,jhd->ihd", scores, value_part, precision=HIGH)
        denominator = jnp.transpose(jnp.sum(scores, axis=2))
        carried = ((seg_part == before) & live_mask).astype(query_feat.dtype)
        numerator = numerator + carried[:, None, None] * jnp.einsum(
            "ihf,hfd->ihd", query_cat, kv_state, precision=HIGH
        )
        denominator = denominator + carried[:, None] * jnp.einsum(
            "ihf,hf->ih", query_cat, key_total, precision=HIGH
        )
        block_out = numerator / jnp.maximum(denominator, 1.0)[:, :, None]
        last_seg = seg_part[block_rows - 1]
        keep_state = (last_seg == before).astype(query_feat.dtype)
        take_rows = ((seg_part == last_seg) & live_mask).astype(query_feat.dtype)
        kept_keys = key_cat * take_rows[:, None, None]
        kv_state = keep_state * kv_state + jnp.einsum(
            "jhf,jhd->hfd", kept_keys, value_part, precision=HIGH
        )
        key_total = keep_state * key_total + jnp.sum(kept_keys, axis=0)
        return ((kv_state, key_total, last_seg), block_out.reshape(block_rows, width))

    start_carry = (
        jnp.zeros((head_count, 2 * head_size, head_size), jnp.float32),
        jnp.zeros((head_count, 2 * head_size), jnp.float32),
        jnp.asarray(-1, dtype=jnp.int32),
    )
    carry_end, outputs_all = lax.scan(block_step, start_carry, block_inputs)
    return outputs_all.reshape(row_count, width)


def normalize(residual_in, gain_row, shift_row):
    row_mean = jnp.mean(residual_in, axis=-1, keepdims=True)
    centered = residual_in - row_mean
    variance = jnp.mean(centered * centered, axis=-1, keepdims=True)
    return centered * lax.rsqrt(variance + EPS_NORM) * gain_row + shift_row


def adamw(
    master, moment_one, moment_two, gradient, factor, fix_one, fix_two, step_rate, decay_rate
):
    clipped = gradient * factor
    moment_one = BETA_ONE * moment_one + (1.0 - BETA_ONE) * clipped
    moment_two = BETA_TWO * moment_two + (1.0 - BETA_TWO) * clipped * clipped
    update = moment_one / fix_one / (jnp.sqrt(moment_two / fix_two) + ADAM_EPS)
    master = master - step_rate * (update + decay_rate * master)
    return (master, moment_one, moment_two)


def gather_rows(values):
    return lax.all_gather(values, "narrow", axis=0, tiled=True)


def reduce_rows(part_sum):
    return lax.psum_scatter(
        part_sum.astype(jnp.bfloat16), "narrow", scatter_dimension=0, tiled=True
    ).astype(jnp.float32)


def gather_grads(values):
    return lax.all_gather(values, "narrow", axis=0, tiled=True)


def reduce_grads(part_sum):
    return lax.psum_scatter(
        part_sum.astype(jnp.bfloat16), "narrow", scatter_dimension=0, tiled=True
    ).astype(jnp.float32)


def shards(
    stream,
    seq_lengths,
    cotangent,
    w_qkv,
    w_out,
    w_in,
    w_back,
    norm_params,
    qkv_master,
    qkv_first,
    qkv_second,
    out_master,
    out_first,
    out_second,
    in_master,
    in_first,
    in_second,
    back_master,
    back_first,
    back_second,
    norm_master,
    norm_first,
    norm_second,
):
    half_rows = stream.shape[0]
    bucket_rows = half_rows * lax.axis_size("narrow")
    heads_here = w_qkv.shape[3] // HEAD
    segment, cosine, sine = row_layout(seq_lengths[0], bucket_rows)
    row_offset = lax.axis_index("narrow") * half_rows
    own_segment = lax.dynamic_slice_in_dim(segment, row_offset, half_rows)
    live_rows = (own_segment >= 0).astype(jnp.float32)
    attention = functools.partial(
        attend, segment=segment, cosine=cosine, sine=sine, block_rows=BLOCK, head_count=heads_here
    )
    current = stream.astype(jnp.float32)
    kept_layers = []
    for layer_index in range(LAYERS):
        attn_in = gather_rows(current.astype(jnp.bfloat16))
        projected = jnp.einsum(
            "td,dce->tce", attn_in, w_qkv[layer_index], preferred_element_type=jnp.float32
        )
        mixed, attention_back = jax.vjp(attention, projected)
        mixed_low = mixed.astype(jnp.bfloat16)
        branch = reduce_rows(
            jnp.dot(mixed_low, w_out[layer_index], preferred_element_type=jnp.float32)
        )
        first_norm, first_back = jax.vjp(
            normalize, current + branch, norm_params[layer_index, 0], norm_params[layer_index, 1]
        )
        ffn_in = gather_rows(first_norm.astype(jnp.bfloat16))
        hidden_pre = jnp.dot(ffn_in, w_in[layer_index], preferred_element_type=jnp.float32)
        activated, gelu_back = jax.vjp(jax.nn.gelu, hidden_pre)
        hidden_low = activated.astype(jnp.bfloat16)
        ffn_out = reduce_rows(
            jnp.dot(hidden_low, w_back[layer_index], preferred_element_type=jnp.float32)
        )
        current, second_back = jax.vjp(
            normalize,
            first_norm + ffn_out,
            norm_params[layer_index, 2],
            norm_params[layer_index, 3],
        )
        kept_layers.append(
            (
                attn_in,
                attention_back,
                mixed_low,
                first_back,
                ffn_in,
                gelu_back,
                hidden_low,
                second_back,
            )
        )
    upstream = cotangent * live_rows[:, None]
    layer_sets = []
    norm_rows = []
    for layer_index in reversed(range(LAYERS)):
        (
            attn_in,
            attention_back,
            mixed_low,
            first_back,
            ffn_in,
            gelu_back,
            hidden_low,
            second_back,
        ) = kept_layers[layer_index]
        grad_second, grad_gain_two, grad_shift_two = second_back(upstream)
        grad_ffn = gather_grads(grad_second.astype(jnp.bfloat16))
        back_grad = jnp.einsum(
            "tf,td->fd", hidden_low, grad_ffn, preferred_element_type=jnp.float32
        )
        grad_act = jnp.einsum(
            "td,fd->tf", grad_ffn, w_back[layer_index], preferred_element_type=jnp.float32
        )
        (grad_hidden,) = gelu_back(grad_act)
        grad_hidden_low = grad_hidden.astype(jnp.bfloat16)
        in_grad = jnp.einsum(
            "td,tf->df", ffn_in, grad_hidden_low, preferred_element_type=jnp.float32
        )
        grad_first_norm = grad_second + reduce_grads(
            jnp.einsum(
                "tf,df->td", grad_hidden_low, w_in[layer_index], preferred_element_type=jnp.float32
            )
        )
        grad_first, grad_gain_one, grad_shift_one = first_back(grad_first_norm)
        grad_branch = gather_grads(grad_first.astype(jnp.bfloat16))
        out_grad = jnp.einsum(
            "te,td->ed", mixed_low, grad_branch, preferred_element_type=jnp.float32
        )
        grad_mixed = jnp.einsum(
            "td,ed->te", grad_branch, w_out[layer_index], preferred_element_type=jnp.float32
        )
        (grad_projected,) = attention_back(grad_mixed)
        grad_projected_low = grad_projected.astype(jnp.bfloat16)
        qkv_grad = jnp.einsum(
            "td,tce->dce", attn_in, grad_projected_low, preferred_element_type=jnp.float32
        )
        upstream = grad_first + reduce_grads(
            jnp.einsum(
                "tce,dce->td",
                grad_projected_low,
                w_qkv[layer_index],
                preferred_element_type=jnp.float32,
            )
        )
        norm_rows.insert(
            0, jnp.stack([grad_gain_one, grad_shift_one, grad_gain_two, grad_shift_two])
        )
        layer_sets.insert(0, (qkv_grad, out_grad, in_grad, back_grad))
    stacked = tuple(
        (jnp.stack([layer_set[kind_index] for layer_set in layer_sets]) for kind_index in range(4))
    )
    stacked = (
        lax.psum_scatter(stacked[0], "wide", scatter_dimension=1, tiled=True),
        lax.psum_scatter(stacked[1], "wide", scatter_dimension=1, tiled=True),
        lax.psum_scatter(stacked[2], "wide", scatter_dimension=1, tiled=True),
        lax.psum_scatter(stacked[3], "wide", scatter_dimension=1, tiled=True),
    )
    norm_reduced = lax.psum_scatter(
        jnp.stack(norm_rows), ("wide", "narrow"), scatter_dimension=2, tiled=True
    )
    local_squares = jnp.zeros((), jnp.float32)
    for grad_piece in stacked + (norm_reduced,):
        local_squares = local_squares + jnp.sum(grad_piece * grad_piece)
    squares = lax.psum(local_squares, ("wide", "narrow"))
    clip_norm = jnp.sqrt(squares)
    factor = jnp.minimum(1.0, CLIP / clip_norm)
    fix_one = 1.0 - BETA_ONE**STEP_NUMBER
    fix_two = 1.0 - BETA_TWO**STEP_NUMBER
    qkv_new = adamw(
        qkv_master,
        qkv_first,
        qkv_second,
        stacked[0],
        factor,
        fix_one,
        fix_two,
        LR_MATRIX,
        DECAY_MATRIX,
    )
    out_new = adamw(
        out_master,
        out_first,
        out_second,
        stacked[1],
        factor,
        fix_one,
        fix_two,
        LR_MATRIX,
        DECAY_MATRIX,
    )
    in_new = adamw(
        in_master,
        in_first,
        in_second,
        stacked[2],
        factor,
        fix_one,
        fix_two,
        LR_MATRIX,
        DECAY_MATRIX,
    )
    back_new = adamw(
        back_master,
        back_first,
        back_second,
        stacked[3],
        factor,
        fix_one,
        fix_two,
        LR_MATRIX,
        DECAY_MATRIX,
    )
    norm_new = adamw(
        norm_master, norm_first, norm_second, norm_reduced, factor, fix_one, fix_two, LR_NORMS, 0.0
    )
    return (
        current,
        upstream,
        qkv_new[0],
        qkv_new[1],
        qkv_new[2],
        out_new[0],
        out_new[1],
        out_new[2],
        in_new[0],
        in_new[1],
        in_new[2],
        back_new[0],
        back_new[1],
        back_new[2],
        norm_new[0],
        norm_new[1],
        norm_new[2],
        clip_norm.reshape(1),
    )


def solution(mesh):
    in_specs = (
        P(("wide", "narrow"), None),
        P("wide", None),
        P(("wide", "narrow"), None),
        P(None, None, None, "narrow"),
        P(None, "narrow", None),
        P(None, None, "narrow"),
        P(None, "narrow", None),
        P(),
        P(None, "wide", None, "narrow"),
        P(None, "wide", None, "narrow"),
        P(None, "wide", None, "narrow"),
        P(None, ("narrow", "wide"), None),
        P(None, ("narrow", "wide"), None),
        P(None, ("narrow", "wide"), None),
        P(None, "wide", "narrow"),
        P(None, "wide", "narrow"),
        P(None, "wide", "narrow"),
        P(None, ("narrow", "wide"), None),
        P(None, ("narrow", "wide"), None),
        P(None, ("narrow", "wide"), None),
        P(None, None, ("wide", "narrow")),
        P(None, None, ("wide", "narrow")),
        P(None, None, ("wide", "narrow")),
    )
    out_specs = (
        P(("wide", "narrow"), None),
        P(("wide", "narrow"), None),
        P(None, "wide", None, "narrow"),
        P(None, "wide", None, "narrow"),
        P(None, "wide", None, "narrow"),
        P(None, ("narrow", "wide"), None),
        P(None, ("narrow", "wide"), None),
        P(None, ("narrow", "wide"), None),
        P(None, "wide", "narrow"),
        P(None, "wide", "narrow"),
        P(None, "wide", "narrow"),
        P(None, ("narrow", "wide"), None),
        P(None, ("narrow", "wide"), None),
        P(None, ("narrow", "wide"), None),
        P(None, None, ("wide", "narrow")),
        P(None, None, ("wide", "narrow")),
        P(None, None, ("wide", "narrow")),
        P(),
    )
    return jax.shard_map(shards, mesh=mesh, in_specs=in_specs, out_specs=out_specs, check_vma=False)
```

profile of v0, /device:TPU:0, one launch (start us, length us, event | category | flops | bytes accessed | tf_op | source)
XLA Modules:
  0.0 2459.9 jit_solution(689388746760601351)
XLA Ops:
  12.6 11.8 all-gather.9.cloned.1.call-done
  76.5 117.7 %while.94 = (s32[]{:T(128)}, f32[6,128,64]{1,2,0:T(8,128)S(1)}, f32[6,128]{1,0:T(8,128)S(1)}, s32[]{:T(128)}, bf16[4,512,384]{2,1,0:T(8,128)(2,1)}, /*index=5*/f...) while((s32[]{:T(128)}, f32[6,128,64]{1,2,0:T(8,128)S(1)}, ...), condition=%wide.region_3.4_spmd.clone, body=%wide.region_0.3_spmd.clone.sunk | while | flops 4244107008 | bytes 35331352 | solution.py:108
  202.3 10.9 reduce-scatter.13.cloned.1.call-done
  218.1 13.4 all-gather.11.cloned.1.call-done
  243.8 10.4 convolution_convert_fusion.5
  254.7 11.8 reduce-scatter.15.cloned.1.call-done
  272.4 13.4 all-gather.13.cloned.1.call-done
  341.1 110.0 %while.95 = (s32[]{:T(128)}, f32[6,128,64]{1,2,0:T(8,128)S(1)}, f32[6,128]{1,0:T(8,128)S(1)}, s32[]{:T(128)}, bf16[4,512,384]{2,1,0:T(8,128)(2,1)}, /*index=5*/f...) while((s32[]{:T(128)}, f32[6,128,64]{1,2,0:T(8,128)S(1)}, ...), condition=%wide.region_13.14_spmd.clone, body=%wide.region_10.13_spmd.clone.sunk | while | flops 4244107008 | bytes 47914292 | solution.py:108
  456.2 12.2 reduce-scatter.17.cloned.1.call-done
  474.2 13.4 all-gather.15.cloned.1.call-done
  499.9 10.4 convolution_convert_fusion.4
  511.3 11.2 reduce-scatter.19.cloned.1.call-done
  534.8 13.4 all-gather.17.cloned.1.call-done
  548.2 15.7 fusion.223
  574.7 12.2 reduce-scatter.21.cloned.1.call-done
  596.4 13.3 all-gather.19.cloned.1.call-done
  621.4 502.3 %while.96 = (s32[]{:T(128)}, f32[6,128,64]{1,2,0:T(8,128)S(1)}, f32[6,128]{1,0:T(8,128)S(1)}, f32[4,512,6,64]{1,0,3,2:T(4,128)}, f32[4,512,6,64]{1,0,3,2:T(4,128...) while((s32[]{:T(128)}, f32[6,128,64]{1,2,0:T(8,128)S(1)}, ...), condition=%wide.region_28.29_spmd.clone, body=%wide.region_25.28_spmd.clone.sunk | while | flops 12414674944 | bytes 150156048 | solution.py:108
  666.5 16.1 dynamic_update_slice.143
  695.5 10.7 fusion.504
  713.1 16.1 dynamic_update_slice.142
  729.2 16.0 dynamic_update_slice.141
  790.4 16.1 dynamic_update_slice.143
  819.3 10.7 fusion.504
  837.0 16.1 dynamic_update_slice.142
  853.0 16.0 dynamic_update_slice.141
  914.2 16.1 dynamic_update_slice.143
  943.2 10.7 fusion.504
  960.8 16.1 dynamic_update_slice.142
  976.9 16.0 dynamic_update_slice.141
  1038.1 16.1 dynamic_update_slice.143
  1067.0 10.7 fusion.504
  1084.7 16.1 dynamic_update_slice.142
  1100.8 16.0 dynamic_update_slice.141
  1137.7 10.3 bitcast_convert_fusion.1
  1148.1 12.2 reduce-scatter.23.cloned.1.call-done
  1169.9 13.4 all-gather.21.cloned.1.call-done
  1183.3 15.8 fusion.216
  1210.0 12.2 reduce-scatter.25.cloned.1.call-done
  1260.6 506.8 %while.97 = (s32[]{:T(128)}, f32[6,128,64]{1,2,0:T(8,128)S(1)}, f32[6,128]{1,0:T(8,128)S(1)}, f32[4,512,6,64]{1,0,3,2:T(4,128)}, f32[4,512,6,64]{1,0,3,2:T(4,128...) while((s32[]{:T(128)}, f32[6,128,64]{1,2,0:T(8,128)S(1)}, ...), condition=%wide.region_38.39_spmd.clone, body=%wide.region_35.38_spmd.clone.sunk | while | flops 12414674944 | bytes 150156048 | solution.py:108
  1306.6 16.1 dynamic_update_slice.146
  1335.6 10.7 fusion.535
  1353.2 16.1 dynamic_update_slice.145
  1369.3 16.1 dynamic_update_slice.144
  1431.4 16.1 dynamic_update_slice.146
  1460.3 10.7 fusion.535
  1477.9 16.1 dynamic_update_slice.145
  1494.0 16.0 dynamic_update_slice.144
  1556.1 16.1 dynamic_update_slice.146
  1585.0 10.7 fusion.535
  1602.6 16.1 dynamic_update_slice.145
  1618.7 16.0 dynamic_update_slice.144
  1680.8 16.1 dynamic_update_slice.146
  1709.7 10.7 fusion.535
  1727.3 16.1 dynamic_update_slice.145
  1743.4 16.0 dynamic_update_slice.144
  1792.8 13.6 copy.283
  1828.5 9.9 convolution_bitcast_fusion
  1838.5 9.9 convolution_bitcast_fusion.1
  1854.6 9.5 bitcast_convert_fusion
  1866.1 41.9 %all-reduce.7 = f32[2,4,768]{2,1,0:T(4,128)S(1)} all-reduce(f32[2,4,768]{2,1,0:T(4,128)S(1)} %pad_maximum_fusion.28), channel_id=14, replica_groups=mesh['wide'=16,'narrow'=2] {'wide','narrow'}, use_global_device_ids=true, to_apply=%region_56.57.clone | all-reduce | flops 6144 | bytes 49152
  1910.2 124.8 %all-reduce.10.cloned.1.call-done = f32[2,768,3,384]{3,0,2,1:T(2,128)} async-done(((f32[2,768,3,384]{3,0,2,1:T(2,128)}), f32[2,768,3,384]{3,0,2,1:T(2,128)}) %all-reduce.10.cloned.1.call-update) | async-done | bytes 7077904
  2039.0 171.6 %reduce-scatter.31.cloned.1.call-done = f32[2,48,1536]{2,1,0:T(8,128)} async-done(((f32[2,768,1536]{2,1,0:T(8,128)}), f32[2,48,1536]{2,1,0:T(8,128)}) %reduce-scatter.31.cloned.1.call-update) | async-done | bytes 589840 | tf_op jit(solution)/shard_map/reduce_scatter | solution.py:288
  2213.1 174.0 %reduce-scatter.33.cloned.1.call-done = f32[2,96,768]{2,1,0:T(8,128)} async-done(((f32[2,1536,768]{2,1,0:T(8,128)}), f32[2,96,768]{2,1,0:T(8,128)}) %reduce-scatter.33.cloned.1.call-update) | async-done | bytes 589840 | tf_op jit(solution)/shard_map/reduce_scatter | solution.py:289
  2402.8 40.5 %psum.7 = f32[]{:T(128)} all-reduce(f32[]{:T(128)S(6)} %add.445), channel_id=1, replica_groups=mesh['wide'=16,'narrow'=2] {'wide','narrow'}, use_global_device_ids=true, to_apply=%region_58.59 | all-reduce | flops 1 | bytes 8 | tf_op jit(solution)/shard_map/psum | solution.py:297
  (1068 shorter events, 1081.0 us)
Async XLA Ops:
  7.2 17.2 all-gather.9.cloned.1.call-start
  7.9 205.3 %reduce-scatter.13.cloned.1.call-start = ((), (), s32[]{:S(2)}) async-start(), calls=%async_computation.12 | async-start | bytes 4718592 | tf_op jit(solution)/shard_map/reduce_scatter | solution.py:135
  201.0 30.5 %all-gather.11.cloned.1.call-start = ((), (), s32[]{:S(2)}) async-start(), calls=%async_computation.13 | async-start | bytes 4718592 | tf_op jit(solution)/shard_map/all_gather | solution.py:131
  202.3 64.1 %copy-start.81 = (f32[768]{0:T(1024)}, f32[768]{0:T(1024)S(1)}, u32[]{:S(2)}) copy-start(f32[768]{0:T(1024)S(1)} %get-tuple-element.1522) | copy-start | bytes 9220
  202.3 266.0 %copy-start.83 = (f32[768]{0:T(1024)}, f32[768]{0:T(1024)S(1)}, u32[]{:S(2)}) copy-start(f32[768]{0:T(1024)S(1)} %get-tuple-element.1520) | copy-start | bytes 9220
  215.2 51.2 %copy-start.74 = (f32[1024]{0:T(1024)}, f32[1024]{0:T(1024)S(1)}, u32[]{:S(2)}) copy-start(f32[1024]{0:T(1024)S(1)} %broadcast_multiply_fusion.5) | copy-start | bytes 12292
  216.0 50.4 %copy-start.85 = (f32[1024]{0:T(1024)}, f32[1024]{0:T(1024)S(1)}, u32[]{:S(2)}) copy-start(f32[1024]{0:T(1024)S(1)} %fusion.297) | copy-start | bytes 12292
  218.1 48.4 %reduce-scatter.15.cloned.1.call-start = ((), (), s32[]{:S(2)}) async-start(), calls=%async_computation.14 | async-start | bytes 4718592 | tf_op jit(solution)/shard_map/reduce_scatter | solution.py:135
  254.2 31.5 %all-gather.13.cloned.1.call-start = ((), (), s32[]{:S(2)}) async-start(), calls=%async_computation.15 | async-start | bytes 4718592 | tf_op jit(solution)/shard_map/all_gather | solution.py:131
  270.0 198.3 %copy-start.22 = (f32[1024,768]{1,0:T(8,128)}, f32[1024,768]{1,0:T(8,128)S(1)}, u32[]{:S(2)}) copy-start(f32[1024,768]{1,0:T(8,128)S(1)} %get-tuple-element.1682) | copy-start | bytes 9437188
  270.0 198.3 %copy-start.76 = (f32[1024]{0:T(1024)}, f32[1024]{0:T(1024)S(1)}, u32[]{:S(2)}) copy-start(f32[1024]{0:T(1024)S(1)} %broadcast_multiply_fusion.4) | copy-start | bytes 12292
  270.6 197.8 %copy-start.87 = (f32[1024]{0:T(1024)}, f32[1024]{0:T(1024)S(1)}, u32[]{:S(2)}) copy-start(f32[1024]{0:T(1024)S(1)} %fusion.298) | copy-start | bytes 12292
  272.3 196.0 %reduce-scatter.17.cloned.1.call-start = ((), (), s32[]{:S(2)}) async-start(), calls=%async_computation.16 | async-start | bytes 4718592 | tf_op jit(solution)/shard_map/reduce_scatter | solution.py:135
  456.1 31.4 %all-gather.15.cloned.1.call-start = ((), (), s32[]{:S(2)}) async-start(), calls=%async_computation.17 | async-start | bytes 4718592 | tf_op jit(solution)/shard_map/all_gather | solution.py:131
  474.1 48.4 %reduce-scatter.19.cloned.1.call-start = ((), (), s32[]{:S(2)}) async-start(), calls=%async_computation.18 | async-start | bytes 4718592 | tf_op jit(solution)/shard_map/reduce_scatter | solution.py:135
  510.3 38.0 %all-gather.17.cloned.1.call-start = ((), (), s32[]{:S(2)}) async-start(), calls=%async_computation.19 | async-start | bytes 4718592 | tf_op jit(solution)/shard_map/all_gather | solution.py:141
  534.8 52.1 %reduce-scatter.21.cloned.1.call-start = ((), (), s32[]{:S(2)}) async-start(), calls=%async_computation.20 | async-start | bytes 4718592 | tf_op jit(solution)/shard_map/reduce_scatter | solution.py:145
  574.7 35.1 %all-gather.19.cloned.1.call-start = ((), (), s32[]{:S(2)}) async-start(), calls=%async_computation.21 | async-start | bytes 4718592 | tf_op jit(solution)/shard_map/all_gather | solution.py:141
  596.3 563.9 %reduce-scatter.23.cloned.1.call-start = ((), (), s32[]{:S(2)}) async-start(), calls=%async_computation.22 | async-start | bytes 4718592 | tf_op jit(solution)/shard_map/reduce_scatter | solution.py:145
  639.0 20.5 copy-start
  713.1 32.1 %copy-start.57 = (f32[6,128,64]{1,2,0:T(8,128)S(1)}, f32[6,128,64]{1,2,0:T(8,128)}, u32[]{:S(2)}) copy-start(f32[6,128,64]{1,2,0:T(8,128)} %convolution_add_fusion.4) | copy-start | bytes 589828 | tf_op jit(solution)/shard_map/transpose(jvp())/while
  762.9 20.5 copy-start
  836.9 32.1 %copy-start.57 = (f32[6,128,64]{1,2,0:T(8,128)S(1)}, f32[6,128,64]{1,2,0:T(8,128)}, u32[]{:S(2)}) copy-start(f32[6,128,64]{1,2,0:T(8,128)} %convolution_add_fusion.4) | copy-start | bytes 589828 | tf_op jit(solution)/shard_map/transpose(jvp())/while
  886.7 20.5 copy-start
  960.8 32.1 %copy-start.57 = (f32[6,128,64]{1,2,0:T(8,128)S(1)}, f32[6,128,64]{1,2,0:T(8,128)}, u32[]{:S(2)}) copy-start(f32[6,128,64]{1,2,0:T(8,128)} %convolution_add_fusion.4) | copy-start | bytes 589828 | tf_op jit(solution)/shard_map/transpose(jvp())/while
  1010.6 20.5 copy-start
  1084.7 32.1 %copy-start.57 = (f32[6,128,64]{1,2,0:T(8,128)S(1)}, f32[6,128,64]{1,2,0:T(8,128)}, u32[]{:S(2)}) copy-start(f32[6,128,64]{1,2,0:T(8,128)} %convolution_add_fusion.4) | copy-start | bytes 589828 | tf_op jit(solution)/shard_map/transpose(jvp())/while
  1137.7 22.5 copy-start.77
  1137.7 22.5 copy-start.84
  1137.7 22.5 copy-start.88
  1137.7 22.5 copy-start.91
  1148.0 35.3 %all-gather.21.cloned.1.call-start = ((), (), s32[]{:S(2)}) async-start(), calls=%async_computation.23 | async-start | bytes 4718592 | tf_op jit(solution)/shard_map/all_gather | solution.py:141
  1169.8 52.3 %reduce-scatter.25.cloned.1.call-start = ((), (), s32[]{:S(2)}) async-start(), calls=%async_computation.24 | async-start | bytes 4718592 | tf_op jit(solution)/shard_map/reduce_scatter | solution.py:145
  1201.7 20.4 copy-start.75
  1201.7 20.4 copy-start.82
  1201.7 20.4 copy-start.86
  1209.9 35.6 %all-gather.23.cloned.1.call-start = ((), (), s32[]{:S(2)}) async-start(), calls=%async_computation.25 | async-start | bytes 4718592 | tf_op jit(solution)/shard_map/all_gather | solution.py:141
  1232.1 676.5 %reduce-scatter.29.cloned.1.call-start = ((), (), s32[]{:S(2)}) async-start(), calls=%async_computation.27 | async-start | bytes 2506752 | tf_op jit(solution)/shard_map/reduce_scatter | solution.py:287
  1253.9 781.1 %all-reduce.10.cloned.1.call-start = ((), (), s32[]{:S(2)}) async-start(), calls=%async_computation.30 | async-start | bytes 14155776
  1279.0 20.5 copy-start.2
  1352.4 16.9 copy-start.27
  1353.2 32.2 %copy-start.56 = (f32[6,128,64]{1,2,0:T(8,128)S(1)}, f32[6,128,64]{1,2,0:T(8,128)}, u32[]{:S(2)}) copy-start(f32[6,128,64]{1,2,0:T(8,128)} %convolution_add_fusion.5) | copy-start | bytes 589828 | tf_op jit(solution)/shard_map/transpose(jvp())/while
  1403.8 20.5 copy-start.2
  1477.9 32.1 %copy-start.56 = (f32[6,128,64]{1,2,0:T(8,128)S(1)}, f32[6,128,64]{1,2,0:T(8,128)}, u32[]{:S(2)}) copy-start(f32[6,128,64]{1,2,0:T(8,128)} %convolution_add_fusion.5) | copy-start | bytes 589828 | tf_op jit(solution)/shard_map/transpose(jvp())/while
  1528.5 20.5 copy-start.2
  1602.6 32.1 %copy-start.56 = (f32[6,128,64]{1,2,0:T(8,128)S(1)}, f32[6,128,64]{1,2,0:T(8,128)}, u32[]{:S(2)}) copy-start(f32[6,128,64]{1,2,0:T(8,128)} %convolution_add_fusion.5) | copy-start | bytes 589828 | tf_op jit(solution)/shard_map/transpose(jvp())/while
  1653.2 20.5 copy-start.2
  1727.3 32.1 %copy-start.56 = (f32[6,128,64]{1,2,0:T(8,128)S(1)}, f32[6,128,64]{1,2,0:T(8,128)}, u32[]{:S(2)}) copy-start(f32[6,128,64]{1,2,0:T(8,128)} %convolution_add_fusion.5) | copy-start | bytes 589828 | tf_op jit(solution)/shard_map/transpose(jvp())/while
  1806.4 404.3 %reduce-scatter.31.cloned.1.call-start = ((), (), s32[]{:S(2)}) async-start(), calls=%async_computation.28 | async-start | bytes 10027008 | tf_op jit(solution)/shard_map/reduce_scatter | solution.py:288
  1826.6 560.5 %reduce-scatter.33.cloned.1.call-start = ((), (), s32[]{:S(2)}) async-start(), calls=%async_computation.29 | async-start | bytes 10027008 | tf_op jit(solution)/shard_map/reduce_scatter | solution.py:289
  1852.7 546.6 %reduce-scatter.27.cloned.1.call-start = ((), (), s32[]{:S(2)}) async-start(), calls=%async_computation.26 | async-start | bytes 4718592 | tf_op jit(solution)/shard_map/reduce_scatter | solution.py:145
  1864.1 535.2 %copy-start.49 = (f32[1024,768]{1,0:T(8,128)S(1)}, f32[1024,768]{1,0:T(8,128)}, u32[]{:S(2)}) copy-start(f32[1024,768]{1,0:T(8,128)} %copy-done.48) | copy-start | bytes 9437188
  1864.1 535.1 %copy-start.94 = (f32[1024]{0:T(1024)S(1)}, f32[1024]{0:T(1024)}, u32[]{:S(2)}) copy-start(f32[1024]{0:T(1024)} %copy-done.93) | copy-start | bytes 12292
  2390.3 53.8 %copy-start.109 = (f32[2,4,24]{2,1,0:T(4,128)S(1)}, f32[2,4,24]{2,1,0:T(4,128)}, u32[]{:S(2)}) copy-start(f32[2,4,24]{2,1,0:T(4,128)} %param.51) | copy-start | bytes 2308
  2390.3 53.7 %copy-start.110 = (f32[2,4,24]{2,1,0:T(4,128)S(1)}, f32[2,4,24]{2,1,0:T(4,128)}, u32[]{:S(2)}) copy-start(f32[2,4,24]{2,1,0:T(4,128)} %param.52) | copy-start | bytes 2308
  2390.3 53.7 %copy-start.111 = (f32[2,4,24]{2,1,0:T(4,128)S(1)}, f32[2,4,24]{2,1,0:T(4,128)}, u32[]{:S(2)}) copy-start(f32[2,4,24]{2,1,0:T(4,128)} %param.53) | copy-start | bytes 2308
  2402.7 44.7 %copy-start.73 = (f32[2,24,768]{2,1,0:T(8,128)S(1)}, f32[2,24,768]{2,1,0:T(8,128)}, u32[]{:S(2)}) copy-start(f32[2,24,768]{2,1,0:T(8,128)} %reduce-scatter.29.cloned.1.call-done) | copy-start | bytes 442372
  2402.7 44.7 %copy-start.78 = (f32[2,24,768]{2,1,0:T(8,128)S(1)}, f32[2,24,768]{2,1,0:T(8,128)}, u32[]{:S(2)}) copy-start(f32[2,24,768]{2,1,0:T(8,128)} %param.42) | copy-start | bytes 442372
  2402.7 44.7 %copy-start.79 = (f32[2,24,768]{2,1,0:T(8,128)S(1)}, f32[2,24,768]{2,1,0:T(8,128)}, u32[]{:S(2)}) copy-start(f32[2,24,768]{2,1,0:T(8,128)} %param.43) | copy-start | bytes 442372
  2402.7 44.7 %copy-start.80 = (f32[2,24,768]{2,1,0:T(8,128)S(1)}, f32[2,24,768]{2,1,0:T(8,128)}, u32[]{:S(2)}) copy-start(f32[2,24,768]{2,1,0:T(8,128)} %param.44) | copy-start | bytes 442372
  2402.7 45.6 %copy-start.64 = (f32[2,96,768]{2,1,0:T(8,128)S(1)}, f32[2,96,768]{2,1,0:T(8,128)}, u32[]{:S(2)}) copy-start(f32[2,96,768]{2,1,0:T(8,128)} %reduce-scatter.33.cloned.1.call-done) | copy-start | bytes 1769476
  2402.7 45.6 %copy-start.67 = (f32[2,96,768]{2,1,0:T(8,128)S(1)}, f32[2,96,768]{2,1,0:T(8,128)}, u32[]{:S(2)}) copy-start(f32[2,96,768]{2,1,0:T(8,128)} %param.48) | copy-start | bytes 1769476
  2402.8 45.6 %copy-start.68 = (f32[2,96,768]{2,1,0:T(8,128)S(1)}, f32[2,96,768]{2,1,0:T(8,128)}, u32[]{:S(2)}) copy-start(f32[2,96,768]{2,1,0:T(8,128)} %param.49) | copy-start | bytes 1769476
  2402.8 45.6 %copy-start.69 = (f32[2,96,768]{2,1,0:T(8,128)S(1)}, f32[2,96,768]{2,1,0:T(8,128)}, u32[]{:S(2)}) copy-start(f32[2,96,768]{2,1,0:T(8,128)} %param.50) | copy-start | bytes 1769476
  (185 other events, 1184.7 us)
Sparse Core Ops, SparseCore 0:
  9.6 14.8 all-gather.8
  201.1 12.0 reduce-scatter.12
  218.2 13.2 all-gather.10
  254.3 12.0 reduce-scatter.14
  272.4 13.2 all-gather.12
  456.2 12.0 reduce-scatter.16
  474.2 13.2 all-gather.14
  510.4 12.0 reduce-scatter.18
  534.9 13.2 all-gather.16
  574.8 12.0 reduce-scatter.20
  596.4 13.2 all-gather.18
  1148.1 12.0 reduce-scatter.22
  1170.0 13.2 all-gather.20
  1210.0 12.0 reduce-scatter.24
  1232.2 13.2 all-gather.22
  1254.0 129.5 reduce-scatter.28
  1806.5 228.4 all-reduce.9
  2040.5 170.0 reduce-scatter.30
  2217.3 169.8 reduce-scatter.32
  2389.2 9.9 reduce-scatter.26
where the time goes:
time: 2480 us; the launch traced here: 2460 us
  matrix products  774 us (31%)
  local copies, waits for them, and re-layouts  720 us (29%)
  waiting for transfers between devices  655 us (26%)
  other arithmetic  153 us (6%)
  blocking collectives  82.4 us (3%)
  loops' own time  51 us (2%)
    dynamic_update_slice x72, local copies, waits for them, and re-layouts, attend(): carry_end, outputs_all = lax.scan(block_step, start_carry, block_inputs)  451 us
    dot_general x32, matrix products, block_step(): scores = jnp.einsum('ihf,jhf->hij', query_cat, key_cat, precision=HIGH)  233 us
    dot_general x32, matrix products, block_step(): numerator = jnp.einsum('hij,jhd->ihd', scores, value_part, precision=HIGH)  179 us
    reduce_scatter x1, waiting for transfers between devices, shards(): lax.psum_scatter(stacked[3], 'wide', scatter_dimension=1, tiled=True)  174 us
    reduce_scatter x1, waiting for transfers between devices, shards(): lax.psum_scatter(stacked[2], 'wide', scatter_dimension=1, tiled=True)  172 us
    unnamed x21, waiting for transfers between devices  126 us
    dot_general x32, matrix products, block_step(): jnp.einsum('ihf,hfd->ihd', query_cat, kv_state, precision=HIGH)  71.8 us
    squeeze x40, local copies, waits for them, and re-layouts, attend(): carry_end, outputs_all = lax.scan(block_step, start_carry, block_inputs)  70.6 us
  transfers between devices with their start and end apart: 20, of which 19 were waited for; matrix products, arithmetic and copies ran while one was open for 25% of the time, Pallas kernels for 0%

commit v1 on v0

v1 whole, which is shorter than its diff:
```python
import functools
import math

import jax
import jax.numpy as jnp
from jax import lax
from jax.experimental import pallas as pl
from jax.experimental.pallas import tpu as pltpu
from jax.sharding import PartitionSpec as P

HEAD = 64
LAYERS = 2
CHUNK = 256
FF_BLOCK = 512
VMEM = 56 * 1024 * 1024

EPS_NORM = 1e-05
CLIP = 1.0
BETA_ONE = 0.5
BETA_TWO = 0.5
ADAM_EPS = 1e-08
LR_MATRIX = 0.1
LR_NORMS = 0.5
DECAY_MATRIX = 0.1
STEP_NUMBER = 4.0

F32 = jnp.float32
BF16 = jnp.bfloat16


def params(axes=1):
    return pltpu.CompilerParams(
        vmem_limit_bytes=VMEM, dimension_semantics=("arbitrary",) * axes
    )


def cost(flops, nbytes):
    return pl.CostEstimate(flops=int(flops), bytes_accessed=int(nbytes), transcendentals=0)


def dot(a, b):
    return jnp.dot(a, b, preferred_element_type=F32)


def dot_nt(a, b):
    return lax.dot_general(a, b, (((1,), (1,)), ((), ())), preferred_element_type=F32)


def dot_tn(a, b):
    return lax.dot_general(a, b, (((0,), (0,)), ((), ())), preferred_element_type=F32)


def low_lanes(rows):
    return lax.broadcasted_iota(jnp.int32, (rows, 128), 1) < HEAD


def shape(dims, dtype):
    return jax.ShapeDtypeStruct(dims, dtype)


def whole(array_shape):
    return pl.BlockSpec(array_shape, lambda *_: (0,) * len(array_shape))


def row_spec(rows, cols, index=lambda i: i):
    return pl.BlockSpec((rows, cols), lambda i: (index(i), 0))


def layer_spec(array, layer):
    rest = array.shape[1:]
    return pl.BlockSpec((None,) + rest, lambda *_: (layer,) + (0,) * len(rest))


def vext_of(v_pair):
    return jnp.concatenate([v_pair, jnp.ones_like(v_pair)], axis=1)


def project_kernel(x_ref, w_ref, cos_ref, sin_ref, qc_ref, kc_ref, v_ref, kv_ref):
    rows = x_ref.shape[0]
    pairs = v_ref.shape[1] // 128

    @pl.when(pl.program_id(0) == 0)
    def _():
        kv_ref[...] = jnp.zeros_like(kv_ref)

    x = x_ref[...]
    low = low_lanes(rows)
    cos, sin = cos_ref[...], sin_ref[...]

    def features(values, out_ref):
        cats = []
        for pair in range(pairs):
            tile = jnp.maximum(values[:, pair * 128 : pair * 128 + 128], 0.0)
            along = tile * cos
            across = pltpu.roll(tile, HEAD, 1) * sin
            for cat in (jnp.where(low, along, across), jnp.where(low, across, along)):
                cats.append(cat.astype(BF16))
        for head, cat in enumerate(cats):
            out_ref[:, head * 128 : head * 128 + 128] = cat
        return cats

    features(dot(x, w_ref[0]), qc_ref)
    k_cats = features(dot(x, w_ref[1]), kc_ref)
    v = dot(x, w_ref[2]).astype(BF16)
    v_ref[...] = v
    for pair in range(pairs):
        vext = vext_of(v[:, pair * 128 : pair * 128 + 128])
        for head in (2 * pair, 2 * pair + 1):
            kv_ref[head] += dot_tn(k_cats[head], vext)


def project(x, w, layer, cos, sin):
    rows, width = x.shape
    half = w.shape[3]
    heads = half // HEAD
    return pl.pallas_call(
        project_kernel,
        grid=(rows // CHUNK,),
        in_specs=[
            row_spec(CHUNK, width),
            layer_spec(w, layer),
            row_spec(CHUNK, 128),
            row_spec(CHUNK, 128),
        ],
        out_specs=[
            row_spec(CHUNK, heads * 128),
            row_spec(CHUNK, heads * 128),
            row_spec(CHUNK, half),
            whole((heads, 128, 256)),
        ],
        out_shape=[
            shape((rows, heads * 128), BF16),
            shape((rows, heads * 128), BF16),
            shape((rows, half), BF16),
            shape((heads, 128, 256), F32),
        ],
        compiler_params=params(),
        cost_estimate=cost(2 * rows * width * 3 * half, 8e6),
        name="project",
    )(x, w, cos, sin)


def norm_rows(r, gain, shift):
    mean = jnp.mean(r, axis=1, keepdims=True)
    centered = r - mean
    var = jnp.mean(centered * centered, axis=1, keepdims=True)
    rstd = lax.rsqrt(var + EPS_NORM)
    x_hat = centered * rstd
    return x_hat * gain + shift, x_hat, rstd


def attend_kernel(
    flag_ref, qo_ref, qp_ref, ko_ref, kp_ref, vo_ref, vp_ref, kvo_ref, kvp_ref, wo_ref, wp_ref,
    resid_ref, norm_ref,
    mo_ref, mp_ref, rden_ref, first_ref, low_ref, xhat_ref, rstd_ref, state_out_ref,
    state,
):
    rows = qo_ref.shape[0]
    half = vo_ref.shape[1]
    pairs = half // 128
    heads = 2 * pairs

    @pl.when(pl.program_id(0) == 0)
    def _():
        carry = flag_ref[0, 0]
        state[:heads] = kvo_ref[...] * carry
        state[heads:] = kvp_ref[...] * carry

    low = low_lanes(rows)
    row = lax.broadcasted_iota(jnp.int32, (rows, rows), 0)
    col = lax.broadcasted_iota(jnp.int32, (rows, rows), 1)
    causal = col <= row
    branch = None
    for side, (q_ref, k_ref, v_ref, m_ref, w_ref) in enumerate(
        ((qo_ref, ko_ref, vo_ref, mo_ref, wo_ref), (qp_ref, kp_ref, vp_ref, mp_ref, wp_ref))
    ):
        for pair in range(pairs):
            vext = vext_of(v_ref[:, pair * 128 : pair * 128 + 128])
            sums = []
            for head in (2 * pair, 2 * pair + 1):
                at = side * heads + head
                q = q_ref[:, head * 128 : head * 128 + 128]
                k = k_ref[:, head * 128 : head * 128 + 128]
                kv = state[at]
                kv_low = kv.astype(BF16)
                state_out_ref[0, at] = kv_low
                scores = jnp.where(causal, dot_nt(q, k), 0.0).astype(BF16)
                sums.append(
                    dot(
                        jnp.concatenate([scores, q], axis=1),
                        jnp.concatenate([vext, kv_low], axis=0),
                    )
                )
                state[at] = kv + dot_tn(k, vext)
            num = jnp.where(low, sums[0][:, :128], sums[1][:, :128])
            den = jnp.where(low, sums[0][:, 128:], sums[1][:, 128:])
            rden = 1.0 / jnp.maximum(den, 1.0)
            base = side * half + pair * 128
            rden_ref[:, base : base + 128] = rden
            m_ref[:, pair * 128 : pair * 128 + 128] = (num * rden).astype(BF16)
        part = dot(m_ref[...], w_ref[...])
        branch = part if branch is None else branch + part
    r = resid_ref[...].astype(F32) + branch
    y, x_hat, rstd = norm_rows(r, norm_ref[0:1], norm_ref[1:2])
    first_ref[...] = y
    low_ref[...] = y.astype(BF16)
    xhat_ref[...] = x_hat.astype(BF16)
    rstd_ref[...] = rstd


def attend(flag, own, peer, kv_own, kv_peer, w_own, w_peer, layer, resid, norms):
    rows, width = resid.shape
    half = own[2].shape[1]
    heads = half // HEAD
    steps = rows // CHUNK
    cat, narrow = row_spec(CHUNK, heads * 128), row_spec(CHUNK, half)
    full = row_spec(CHUNK, width)
    return pl.pallas_call(
        attend_kernel,
        grid=(steps,),
        in_specs=[
            pl.BlockSpec(memory_space=pltpu.SMEM),
            cat, cat, cat, cat, narrow, narrow,
            whole(kv_own.shape), whole(kv_peer.shape),
            layer_spec(w_own, layer), layer_spec(w_peer, layer),
            full, layer_spec(norms, layer),
        ],
        out_specs=[
            narrow, narrow, full, full, full, full, row_spec(CHUNK, 1),
            pl.BlockSpec((1, 2 * heads, 128, 256), lambda i: (i, 0, 0, 0)),
        ],
        out_shape=[
            shape((rows, half), BF16),
            shape((rows, half), BF16),
            shape((rows, width), F32),
            shape((rows, width), F32),
            shape((rows, width), BF16),
            shape((rows, width), BF16),
            shape((rows, 1), F32),
            shape((steps, 2 * heads, 128, 256), BF16),
        ],
        scratch_shapes=[pltpu.VMEM((2 * heads, 128, 256), F32)],
        compiler_params=params(),
        cost_estimate=cost(rows * width * (2 * width + 8 * CHUNK), 25e6),
        name="attend",
    )(
        flag, own[0], peer[0], own[1], peer[1], own[2], peer[2], kv_own, kv_peer,
        w_own, w_peer, resid, norms,
    )


def gelu_both(u):
    root = math.sqrt(2.0 / math.pi)
    square = u * u
    t = jnp.tanh(u * (root + (root * 0.044715) * square))
    gate = 0.5 + 0.5 * t
    slope = gate + (u * (0.5 - 0.5 * (t * t))) * (root + (3.0 * root * 0.044715) * square)
    return u * gate, slope


def feed_kernel(
    x_ref, first_ref, wio_ref, wip_ref, wbo_ref, wbp_ref, norm_ref,
    ho_ref, hp_ref, slope_ref, out_ref, low_ref, xhat_ref, rstd_ref,
    acc,
):
    step, steps = pl.program_id(0), pl.num_programs(0)
    rows = x_ref.shape[0]

    def side(w_in, w_back, h_ref, fresh):
        def part(i, _):
            at = pl.ds(pl.multiple_of(i * CHUNK, CHUNK), CHUNK)
            act, slope = gelu_both(dot(x_ref[at, :], w_in[...]))
            act = act.astype(BF16)
            h_ref[at, :] = act
            slope_ref[at, :] = slope.astype(BF16)
            acc[at, :] += dot(act, w_back[...])
            return 0

        lax.fori_loop(0, rows // CHUNK, part, 0, unroll=True)

    @pl.when(step == 0)
    def _():
        acc[...] = first_ref[...]

    @pl.when(step < steps // 2)
    def _():
        side(wio_ref, wbo_ref, ho_ref, step == 0)

    @pl.when(step >= steps // 2)
    def _():
        side(wip_ref, wbp_ref, hp_ref, False)

    @pl.when(step == steps - 1)
    def _():
        def part(i, _):
            at = pl.ds(pl.multiple_of(i * CHUNK, CHUNK), CHUNK)
            y, x_hat, rstd = norm_rows(acc[at, :], norm_ref[2:3], norm_ref[3:4])
            out_ref[at, :] = y
            low_ref[at, :] = y.astype(BF16)
            xhat_ref[at, :] = x_hat.astype(BF16)
            rstd_ref[at, :] = rstd
            return 0

        lax.fori_loop(0, rows // CHUNK, part, 0)


def ff_specs(layer, width, blocks):
    own = lambda j: jnp.minimum(j, blocks - 1)
    peer = lambda j: jnp.maximum(j - blocks, 0)
    w_in = [
        pl.BlockSpec((None, width, FF_BLOCK), lambda j, f=f: (layer, 0, f(j))) for f in (own, peer)
    ]
    w_back = [
        pl.BlockSpec((None, FF_BLOCK, width), lambda j, f=f: (layer, f(j), 0)) for f in (own, peer)
    ]
    return own, peer, w_in, w_back


def feed(x, first, wi_own, wi_peer, wb_own, wb_peer, layer, norms):
    rows, width = x.shape
    half = wi_own.shape[2]
    blocks = half // FF_BLOCK
    own, peer, w_in, w_back = ff_specs(layer, width, blocks)
    return pl.pallas_call(
        feed_kernel,
        grid=(2 * blocks,),
        in_specs=[
            whole((rows, width)), whole((rows, width)), *w_in, *w_back, layer_spec(norms, layer)
        ],
        out_specs=[
            pl.BlockSpec((rows, FF_BLOCK), lambda j: (0, own(j))),
            pl.BlockSpec((rows, FF_BLOCK), lambda j: (0, peer(j))),
            pl.BlockSpec((rows, FF_BLOCK), lambda j: (0, j)),
            whole((rows, width)), whole((rows, width)), whole((rows, width)), whole((rows, 1)),
        ],
        out_shape=[
            shape((rows, half), BF16),
            shape((rows, half), BF16),
            shape((rows, 2 * half), BF16),
            shape((rows, width), F32),
            shape((rows, width), BF16),
            shape((rows, width), BF16),
            shape((rows, 1), F32),
        ],
        scratch_shapes=[pltpu.VMEM((rows, width), F32)],
        compiler_params=params(),
        cost_estimate=cost(8 * rows * width * half, 40e6),
        name="feed",
    )(x, first, wi_own, wi_peer, wb_own, wb_peer, norms)


def norm_back(y, x_hat, rstd, gain):
    scaled = y * gain
    mean = jnp.mean(scaled, axis=1, keepdims=True)
    along = jnp.mean(scaled * x_hat, axis=1, keepdims=True)
    gain_grad = jnp.sum(y * x_hat, axis=0, keepdims=True)
    shift_grad = jnp.sum(y, axis=0, keepdims=True)
    return (scaled - mean - x_hat * along) * rstd, gain_grad, shift_grad


def feed_back_kernel(
    up_ref, live_ref, xh2_ref, rs2_ref, xh1_ref, rs1_ref, slope_ref,
    wio_ref, wip_ref, wbo_ref, wbp_ref, norm_ref,
    gf_ref, gho_ref, ghp_ref, first_ref, gb_ref, ng_ref,
    acc,
):
    step, steps = pl.program_id(0), pl.num_programs(0)
    rows = up_ref.shape[0]

    @pl.when(step == 0)
    def _():
        ng_ref[...] = jnp.zeros_like(ng_ref)

        def part(i, _):
            at = pl.ds(pl.multiple_of(i * CHUNK, CHUNK), CHUNK)
            y = up_ref[at, :] * live_ref[at, :]
            grad, gain_grad, shift_grad = norm_back(
                y, xh2_ref[at, :].astype(F32), rs2_ref[at, :], norm_ref[2:3]
            )
            acc[at, :] = grad
            gf_ref[at, :] = grad.astype(BF16)
            ng_ref[2:3] += gain_grad
            ng_ref[3:4] += shift_grad
            return 0

        lax.fori_loop(0, rows // CHUNK, part, 0)

    def side(w_in, w_back, gh_ref):
        def part(i, _):
            at = pl.ds(pl.multiple_of(i * CHUNK, CHUNK), CHUNK)
            act = dot_nt(gf_ref[at, :], w_back[...])
            gh = (act * slope_ref[at, :].astype(F32)).astype(BF16)
            gh_ref[at, :] = gh
            acc[at, :] += dot_nt(gh, w_in[...])
            return 0

        lax.fori_loop(0, rows // CHUNK, part, 0, unroll=True)

    @pl.when(step < steps // 2)
    def _():
        side(wio_ref, wbo_ref, gho_ref)

    @pl.when(step >= steps // 2)
    def _():
        side(wip_ref, wbp_ref, ghp_ref)

    @pl.when(step == steps - 1)
    def _():
        def part(i, _):
            at = pl.ds(pl.multiple_of(i * CHUNK, CHUNK), CHUNK)
            grad, gain_grad, shift_grad = norm_back(
                acc[at, :], xh1_ref[at, :].astype(F32), rs1_ref[at, :], norm_ref[0:1]
            )
            first_ref[at, :] = grad
            gb_ref[at, :] = grad.astype(BF16)
            ng_ref[0:1] += gain_grad
            ng_ref[1:2] += shift_grad
            return 0

        lax.fori_loop(0, rows // CHUNK, part, 0)


def feed_back(
    up, live, xh2, rs2, xh1, rs1, slope, wi_own, wi_peer, wb_own, wb_peer, layer, norms
):
    rows, width = up.shape
    half = wi_own.shape[2]
    blocks = half // FF_BLOCK
    own, peer, w_in, w_back = ff_specs(layer, width, blocks)
    full, thin = whole((rows, width)), whole((rows, 1))
    return pl.pallas_call(
        feed_back_kernel,
        grid=(2 * blocks,),
        in_specs=[
            full, thin, full, thin, full, thin,
            pl.BlockSpec((rows, FF_BLOCK), lambda j: (0, j)),
            *w_in, *w_back, layer_spec(norms, layer),
        ],
        out_specs=[
            full,
            pl.BlockSpec((rows, FF_BLOCK), lambda j: (0, own(j))),
            pl.BlockSpec((rows, FF_BLOCK), lambda j: (0, peer(j))),
            full, full, whole((4, width)),
        ],
        out_shape=[
            shape((rows, width), BF16),
            shape((rows, half), BF16),
            shape((rows, half), BF16),
            shape((rows, width), F32),
            shape((rows, width), BF16),
            shape((4, width), F32),
        ],
        scratch_shapes=[pltpu.VMEM((rows, width), F32)],
        compiler_params=params(),
        cost_estimate=cost(8 * rows * width * half, 45e6),
        name="feed_back",
    )(up, live, xh2, rs2, xh1, rs1, slope, wi_own, wi_peer, wb_own, wb_peer, norms)


def mix_back_kernel(
    gb_ref, wo_ref, wp_ref, rden_ref, mo_ref, mp_ref, qo_ref, qp_ref, gext_ref, dkv_ref
):
    rows = gb_ref.shape[0]
    half = mo_ref.shape[1]
    pairs = half // 128
    heads = 2 * pairs

    @pl.when(pl.program_id(0) == 0)
    def _():
        dkv_ref[...] = jnp.zeros_like(dkv_ref)

    low = low_lanes(rows)
    r = lax.broadcasted_iota(jnp.int32, (256, 256), 0) % 128
    c = lax.broadcasted_iota(jnp.int32, (256, 256), 1)
    spread = jnp.where((r < HEAD) == (c < 128), -1.0 / 128.0, 0.0).astype(BF16)
    gb = gb_ref[...]
    for side, (w_ref, m_ref, q_ref) in enumerate(
        ((wo_ref, mo_ref, qo_ref), (wp_ref, mp_ref, qp_ref))
    ):
        gm = dot_nt(gb, w_ref[...])
        for pair in range(pairs):
            base = side * half + pair * 128
            rden = rden_ref[:, base : base + 128]
            g = gm[:, pair * 128 : pair * 128 + 128] * rden
            m = m_ref[:, pair * 128 : pair * 128 + 128].astype(F32)
            prod = jnp.where(rden < 1.0, g * m, 0.0)
            high = prod.astype(BF16)
            rest = (prod - high.astype(F32)).astype(BF16)
            minus_c = dot(jnp.concatenate([high, rest], axis=1), spread).astype(BF16)
            for odd in (0, 1):
                head = 2 * pair + odd
                at = side * heads + head
                mine = jnp.where(low, 0.0, g) if odd else jnp.where(low, g, 0.0)
                gext = jnp.concatenate(
                    [mine.astype(BF16), minus_c[:, odd * 128 : odd * 128 + 128]], axis=1
                )
                gext_ref[:, at * 256 : at * 256 + 256] = gext
                dkv_ref[at] += dot_tn(q_ref[:, head * 128 : head * 128 + 128], gext)


def mix_back(gb, w_own, w_peer, layer, rden, m_own, m_peer, q_own, q_peer):
    rows, width = gb.shape
    half = m_own.shape[1]
    heads = half // HEAD
    full, narrow, cat = (row_spec(CHUNK, n) for n in (width, half, heads * 128))
    return pl.pallas_call(
        mix_back_kernel,
        grid=(rows // CHUNK,),
        in_specs=[
            full, layer_spec(w_own, layer), layer_spec(w_peer, layer),
            full, narrow, narrow, cat, cat,
        ],
        out_specs=[row_spec(CHUNK, heads * 512), whole((2 * heads, 128, 256))],
        out_shape=[
            shape((rows, heads * 512), BF16),
            shape((2 * heads, 128, 256), F32),
        ],
        compiler_params=params(),
        cost_estimate=cost(3 * rows * width * width, 25e6),
        name="mix_back",
    )(gb, w_own, w_peer, rden, m_own, m_peer, q_own, q_peer)


def attend_back_kernel(
    flag_ref, qo_ref, qp_ref, ko_ref, kp_ref, vo_ref, vp_ref, gext_ref, state_ref, dkv_ref,
    cos_ref, sin_ref,
    go_ref, gp_ref,
    dstate,
):
    rows = qo_ref.shape[0]
    half = vo_ref.shape[1]
    pairs = half // 128
    heads = 2 * pairs

    @pl.when(pl.program_id(0) == 0)
    def _():
        dstate[...] = dkv_ref[...] * flag_ref[0, 0]

    low = low_lanes(rows)
    row = lax.broadcasted_iota(jnp.int32, (rows, rows), 0)
    col = lax.broadcasted_iota(jnp.int32, (rows, rows), 1)
    causal, anti = col <= row, row <= col
    cos, sin = cos_ref[...], sin_ref[...]
    trig_even = jnp.where(low, cos, sin)
    trig_odd = jnp.where(low, sin, cos)
    for side, (q_ref, k_ref, v_ref, out_ref) in enumerate(
        ((qo_ref, ko_ref, vo_ref, go_ref), (qp_ref, kp_ref, vp_ref, gp_ref))
    ):
        for pair in range(pairs):
            vext = vext_of(v_ref[:, pair * 128 : pair * 128 + 128])
            dq, dk, dv = [], [], None
            for odd in (0, 1):
                head = 2 * pair + odd
                at = side * heads + head
                trig = trig_odd if odd else trig_even
                q = q_ref[:, head * 128 : head * 128 + 128]
                k = k_ref[:, head * 128 : head * 128 + 128]
                gext = gext_ref[:, at * 256 : at * 256 + 256]
                back = dstate[at]
                back_low = back.astype(BF16)
                score_t = jnp.where(anti, dot_nt(k, q), 0.0).astype(BF16)
                ds = jnp.where(causal, dot_nt(gext, vext), 0.0).astype(BF16)
                ds_t = jnp.where(anti, dot_nt(vext, gext), 0.0).astype(BF16)
                q_grad = (dot(ds, k) + dot_nt(gext, state_ref[0, at])) * trig
                k_grad = (dot(ds_t, q) + dot_nt(vext, back_low)) * trig
                v_grad = dot(
                    jnp.concatenate([score_t, k], axis=1),
                    jnp.concatenate([gext[:, :128], back_low[:, :128]], axis=0),
                )
                dstate[at] = back + dot_tn(q, gext)
                q_grad = q_grad + pltpu.roll(q_grad, HEAD, 1)
                k_grad = k_grad + pltpu.roll(k_grad, HEAD, 1)
                dq.append(jnp.where(q > 0, q_grad, 0.0))
                dk.append(jnp.where(k > 0, k_grad, 0.0))
                dv = v_grad if dv is None else dv + v_grad
            for kind, value in enumerate(
                (jnp.where(low, dq[0], dq[1]), jnp.where(low, dk[0], dk[1]), dv)
            ):
                base = kind * half + pair * 128
                out_ref[:, base : base + 128] = value.astype(BF16)


def attend_back(flag, own, peer, gext, states, dkv, cos, sin):
    rows = cos.shape[0]
    half = own[2].shape[1]
    heads = half // HEAD
    steps = rows // CHUNK
    back = lambda i: steps - 1 - i
    cat, narrow, trig = (row_spec(CHUNK, n, back) for n in (heads * 128, half, 128))
    return pl.pallas_call(
        attend_back_kernel,
        grid=(steps,),
        in_specs=[
            pl.BlockSpec(memory_space=pltpu.SMEM),
            cat, cat, cat, cat, narrow, narrow,
            row_spec(CHUNK, heads * 512, back),
            pl.BlockSpec((1, 2 * heads, 128, 256), lambda i: (back(i), 0, 0, 0)),
            whole(dkv.shape), trig, trig,
        ],
        out_specs=[row_spec(CHUNK, 3 * half, back)] * 2,
        out_shape=[shape((rows, 3 * half), BF16)] * 2,
        scratch_shapes=[pltpu.VMEM((2 * heads, 128, 256), F32)],
        compiler_params=params(),
        cost_estimate=cost(40 * rows * half * CHUNK, 25e6),
        name="attend_back",
    )(
        flag, own[0], peer[0], own[1], peer[1], own[2], peer[2], gext, states, dkv, cos, sin
    )


def input_back_kernel(go_ref, gp_ref, wo_ref, wp_ref, first_ref, out_ref):
    half = wo_ref.shape[2]
    total = first_ref[...]
    for g_ref, w_ref in ((go_ref, wo_ref), (gp_ref, wp_ref)):
        for kind in range(3):
            total = total + dot_nt(g_ref[:, kind * half : kind * half + half], w_ref[kind])
    out_ref[...] = total


def input_back(g_own, g_peer, w_own, w_peer, layer, first):
    rows, width = first.shape
    third = row_spec(CHUNK, g_own.shape[1])
    full = row_spec(CHUNK, width)
    return pl.pallas_call(
        input_back_kernel,
        grid=(rows // CHUNK,),
        in_specs=[third, third, layer_spec(w_own, layer), layer_spec(w_peer, layer), full],
        out_specs=full,
        out_shape=shape((rows, width), F32),
        compiler_params=params(),
        cost_estimate=cost(4 * rows * width * g_own.shape[1], 15e6),
        name="input_back",
    )(g_own, g_peer, w_own, w_peer, first)


def weight_kernel(a_ref, b_ref, c_ref, d_ref, out_ref):
    out_ref[...] = (dot_tn(a_ref[...], b_ref[...]) + dot_tn(c_ref[...], d_ref[...])).astype(
        out_ref.dtype
    )


def weight_grad(a, b, c, d, block_m, block_n, name):
    rows, m = a.shape
    n = b.shape[1]
    left = pl.BlockSpec((rows, block_m), lambda i, j: (0, i))
    right = pl.BlockSpec((rows, block_n), lambda i, j: (0, j))
    return pl.pallas_call(
        weight_kernel,
        grid=(m // block_m, n // block_n),
        in_specs=[left, right, left, right],
        out_specs=pl.BlockSpec((block_m, block_n), lambda i, j: (i, j)),
        out_shape=shape((m, n), BF16),
        compiler_params=params(2),
        cost_estimate=cost(4 * rows * m * n, 4 * rows * (m + n) + 2 * m * n),
        name=name,
    )(a, b, c, d)


def swap(values):
    return lax.ppermute(values, "narrow", [(0, 1), (1, 0)])


def halve(values, bit, count):
    me = (lax.axis_index("wide") // bit) % 2
    keep = lax.dynamic_index_in_dim(values, me, 0, keepdims=False)
    send = lax.dynamic_index_in_dim(values, 1 - me, 0, keepdims=False)
    got = lax.ppermute(send, "wide", [(i, i ^ bit) for i in range(count)])
    return (keep.astype(F32) + got.astype(F32)).astype(BF16)


def scatter_sum(values, count, bits):
    if bits is None:
        return lax.psum_scatter(values, "wide", scatter_dimension=0, tiled=False)
    order = len(bits)
    rest = values.shape[1:]
    values = values.reshape((2,) * order + rest)
    axes = list(range(order - 1, -1, -1))
    place = {1 << k: order - 1 - k for k in range(order)}
    left = [1 << k for k in range(order - 1, -1, -1)]
    for bit in bits:
        at = left.index(bit)
        values = jnp.moveaxis(values, at, 0)
        left.remove(bit)
        values = halve(values, bit, count)
    return values


def adamw(master, first, second, gradient, factor, step_rate, decay_rate):
    fix_one = 1.0 - BETA_ONE**STEP_NUMBER
    fix_two = 1.0 - BETA_TWO**STEP_NUMBER
    clipped = gradient * factor
    first = BETA_ONE * first + (1.0 - BETA_ONE) * clipped
    second = BETA_TWO * second + (1.0 - BETA_TWO) * clipped * clipped
    update = first / fix_one / (jnp.sqrt(second / fix_two) + ADAM_EPS)
    master = master - step_rate * (update + decay_rate * master)
    return (master, first, second)


def row_tables(lengths, rows):
    index = lax.axis_index("narrow") * rows + jnp.arange(rows, dtype=jnp.int32)
    first_len, second_len = lengths[0], lengths[1]
    in_first = index < first_len
    in_second = (index >= first_len) & (index < first_len + second_len)
    live = (in_first | in_second).astype(F32)
    position = jnp.where(in_second, index - first_len, index)
    span = jnp.where(in_first, first_len, jnp.where(in_second, second_len, 1))
    angle = 0.5 * math.pi * position.astype(F32) / span.astype(F32)
    cos = (jnp.cos(angle) * live)[:, None]
    sin = (jnp.sin(angle) * live)[:, None]
    goes_on = (first_len > rows).astype(F32).reshape(1, 1)
    return (
        jnp.broadcast_to(cos, (rows, 128)),
        jnp.broadcast_to(sin, (rows, 128)),
        live[:, None],
        goes_on,
    )


def shards(
    stream, seq_lengths, cotangent, w_qkv, w_out, w_in, w_back, norm_params,
    qkv_master, qkv_first, qkv_second, out_master, out_first, out_second,
    in_master, in_first, in_second, back_master, back_first, back_second,
    norm_master, norm_first, norm_second,
):
    rows, width = stream.shape
    half = w_qkv.shape[3]
    wide = lax.axis_size("wide")
    narrow = lax.axis_size("narrow")
    bits = [1, 2, 4, 8] if wide == 16 else None
    cos, sin, live, flag = row_tables(seq_lengths[0], rows)

    qkv = jnp.transpose(w_qkv, (0, 2, 1, 3))
    qkv_peer = swap(qkv)
    out_peer, in_peer, back_peer = swap(w_out), swap(w_in), swap(w_back)

    low = stream
    current = stream
    kept = []
    for layer in range(LAYERS):
        *own, kv_own = project(low, qkv, layer, cos, sin)
        *peer, kv_peer = project(low, qkv_peer, layer, cos, sin)
        kv_in_peer = lax.ppermute(kv_own, "narrow", [(0, 1)])
        kv_in_own = lax.ppermute(kv_peer, "narrow", [(0, 1)])
        attn_in_peer = swap(low)
        m_own, m_peer, rden, first, ffn_in, xh1, rs1, states = attend(
            flag, own, peer, kv_in_own, kv_in_peer, w_out, out_peer, layer, current, norm_params
        )
        h_own, h_peer, slope, out, out_low, xh2, rs2 = feed(
            ffn_in, first, w_in, in_peer, w_back, back_peer, layer, norm_params
        )
        kept.append(
            (low, attn_in_peer, own, peer, m_own, swap(m_peer), m_peer, rden, ffn_in, swap(ffn_in), xh1, rs1,
             states, h_own, swap(h_peer), slope, xh2, rs2)
        )
        current, low = out, out_low

    up = cotangent
    chunks = []
    norm_grads = []
    for layer in reversed(range(LAYERS)):
        (low, low_peer, own, peer, m_own, m_got, m_peer, rden, ffn_in, ffn_peer, xh1, rs1,
         states, h_own, h_got, slope, xh2, rs2) = kept[layer]
        alive = live if layer == LAYERS - 1 else jnp.ones_like(live)
        gf, gh_own, gh_peer, grad_first, gb, ng = feed_back(
            up, alive, xh2, rs2, xh1, rs1, slope, w_in, in_peer, w_back, back_peer, layer, norm_params
        )
        gf_got, gh_got, gb_got = swap(gf), swap(gh_peer), swap(gb)
        gext, dkv = mix_back(gb, w_out, out_peer, layer, rden, m_own, m_peer, own[0], peer[0])
        heads = half // HEAD
        dkv_in = lax.ppermute(
            jnp.concatenate([dkv[heads:], dkv[:heads]], axis=0), "narrow", [(1, 0)]
        )
        back_grad = weight_grad(h_own, gf, h_got, gf_got, 512, width, "back_grad")
        in_grad = weight_grad(ffn_in, gh_own, ffn_peer, gh_got, width, 512, "in_grad")
        g_own, g_peer = attend_back(flag, own, peer, gext, states, dkv_in, cos, sin)
        g_got = swap(g_peer)
        up = input_back(g_own, g_peer, qkv, qkv_peer, layer, grad_first)
        out_grad = weight_grad(m_own, gb, m_got, gb_got, half, width, "out_grad")
        qkv_grad = weight_grad(low, g_own, low_peer, g_got, width, half, "qkv_grad")
        qkv_grad = qkv_grad.reshape(wide, width // wide, 3, half)
        back_grad, in_grad, out_grad = (
            g.reshape((wide, g.shape[0] // wide) + g.shape[1:]) for g in (back_grad, in_grad, out_grad)
        )
        chunks.insert(0, [scatter_sum(g, wide, bits).astype(F32) for g in (qkv_grad, out_grad, in_grad, back_grad)])
        norm_grads.insert(0, ng)

    stacked = [jnp.stack([chunks[l][kind] for l in range(LAYERS)]) for kind in range(4)]
    stacked[0] = stacked[0]
    norm_reduced = lax.psum_scatter(
        jnp.stack(norm_grads), ("wide", "narrow"), scatter_dimension=2, tiled=True
    )
    squares = sum(jnp.sum(g * g) for g in stacked + [norm_reduced])
    clip_norm = jnp.sqrt(lax.psum(squares, ("wide", "narrow")))
    factor = jnp.minimum(1.0, CLIP / clip_norm)
    matrix = lambda m, f, s, g: adamw(m, f, s, g, factor, LR_MATRIX, DECAY_MATRIX)
    qkv_new = matrix(qkv_master, qkv_first, qkv_second, stacked[0])
    out_new = matrix(out_master, out_first, out_second, stacked[1])
    in_new = matrix(in_master, in_first, in_second, stacked[2])
    back_new = matrix(back_master, back_first, back_second, stacked[3])
    norm_new = adamw(norm_master, norm_first, norm_second, norm_reduced, factor, LR_NORMS, 0.0)
    return (current, up, *qkv_new, *out_new, *in_new, *back_new, *norm_new, clip_norm.reshape(1))


def solution(mesh):
    rows = P(("wide", "narrow"), None)
    qkv = P(None, "wide", None, "narrow")
    deep = P(None, ("narrow", "wide"), None)
    in_part = P(None, "wide", "narrow")
    norm = P(None, None, ("wide", "narrow"))
    states = (qkv,) * 3 + (deep,) * 3 + (in_part,) * 3 + (deep,) * 3 + (norm,) * 3
    in_specs = (
        rows, P("wide", None), rows,
        P(None, None, None, "narrow"), P(None, "narrow", None), P(None, None, "narrow"),
        P(None, "narrow", None), P(),
    ) + states
    out_specs = (rows, rows) + states + (P(),)
    return jax.shard_map(shards, mesh=mesh, in_specs=in_specs, out_specs=out_specs, check_vma=False)
```

time: 2480 us -> 655 us (0.26)
  matrix products: 774 us -> 0 us
  local copies, waits for them, and re-layouts: 720 us -> 38.6 us
  waiting for transfers between devices: 655 us -> 130 us
  Pallas kernels: 0 us -> 308 us
  other arithmetic: 153 us -> 27.7 us
  starting transfers between devices: 1.62 us -> 59.1 us
  loops' own time: 51 us -> 0 us
    dot_general x168 -> x0, matrix products: 774 us -> none  [the longest x32 233 us: block_step(): scores = jnp.einsum('ihf,jhf->hij', query_cat, key_cat, precision=HIGH)]
    dynamic_update_slice x72 -> x0, local copies, waits for them, and re-layouts: 451 us -> none  [attend(): carry_end, outputs_all = lax.scan(block_step, start_carry, block_inputs)]
    reduce_scatter x11 -> x0, waiting for transfers between devices: 437 us -> none  [the longest x1 174 us: shards(): lax.psum_scatter(stacked[3], 'wide', scatter_dimension=1, tiled=True)]
    pallas_call x0 -> x24, Pallas kernels: none -> 308 us  [the longest x8 62.7 us: weight_grad(): pl.pallas_call(weight_kernel, grid=(m // block_m, n // block_n), in_specs...]
    ppermute x0 -> x58, waiting for transfers between devices: none -> 130 us  [the longest x32 128 us: halve(): got = lax.ppermute(send, 'wide', [(i, i ^ bit) for i in range(count)])]
    unnamed x21 -> x0, waiting for transfers between devices: 126 us -> none
    squeeze x46 -> x24, local copies, waits for them, and re-layouts: 102 us -> 4.62 us  [halve(): send = lax.dynamic_index_in_dim(values, 1 - me, 0, keepdims=False)]
    all_gather x8 -> x0, waiting for transfers between devices: 92.3 us -> none  [the longest x4 51.9 us: gather_rows(): return lax.all_gather(values, 'narrow', axis=0, tiled=True)]
  transfers between devices with their start and end apart: 20 -> 58, of which waited for: 19 -> 19; matrix products, arithmetic and copies ran while one was open for 25% -> 8% of each run, Pallas kernels for 0% -> 30%
where the time goes in v1:
time: 655 us; the launch traced here: 650 us
  Pallas kernels  308 us (47%)
  waiting for transfers between devices  130 us (20%)
  blocking collectives  78 us (12%)
  starting transfers between devices  59.1 us (9%)
  local copies, waits for them, and re-layouts  38.6 us (6%)
  other arithmetic  27.7 us (4%)
  between operations  9.07 us (1%)
    ppermute x32, waiting for transfers between devices, halve(): got = lax.ppermute(send, 'wide', [(i, i ^ bit) for i in range(count)])  128 us
    pallas_call x8, Pallas kernels, weight_grad(): pl.pallas_call(weight_kernel, grid=(m // block_m, n // block_n), in_specs...  62.7 us
    pallas_call x2, Pallas kernels, feed_back(): pl.pallas_call(feed_back_kernel, grid=(2 * blocks,), in_specs=[full, thin...  52.2 us
    pallas_call x2, Pallas kernels, feed(): pl.pallas_call(feed_kernel, grid=(2 * blocks,), in_specs=[whole((rows, wi...  49.3 us
    pallas_call x2, Pallas kernels, attend_back(): pl.pallas_call(attend_back_kernel, grid=(steps,), in_specs=[pl.BlockSpec(...  43 us
    ppermute x32, starting transfers between devices, halve(): got = lax.ppermute(send, 'wide', [(i, i ^ bit) for i in range(count)])  41.4 us
    unnamed x1, blocking collectives  39.4 us
    psum x1, blocking collectives, shards(): clip_norm = jnp.sqrt(lax.psum(squares, ('wide', 'narrow')))  38.6 us
  transfers between devices with their start and end apart: 58, of which 19 were waited for; matrix products, arithmetic and copies ran while one was open for 8% of the time, Pallas kernels for 30%

profile of v1, /device:TPU:0, one launch (start us, length us, event | category | flops | bytes accessed | tf_op | source)
XLA Modules:
  0.0 650.2 jit_solution(7957737490325218188)
XLA Ops:
  7.7 7.1 %project.4 = (bf16[1024,768]{1,0:T(8,128)(2,1)}, bf16[1024,768]{1,0:T(8,128)(2,1)}, bf16[1024,384]{1,0:T(8,128)(2,1)}, f32[6,128,256]{2,1,0:T(8,128)}) custom-call(bf16[1024,768]{1,0:T(8,128)(2,1)} %a_ref.1, bf16[2,3,768,384]{3,2,1,0:T(8,128)(2,1)} %bitcast.216, f32[1024,128]{1,0:T(8,128)} %broadcast_in_dim.28.cos_ref, f32[1024,128]{1,0:T(8,128)} %broadcast_in_dim.29.sin_ref), custom_call_target="tpu_custom_call" | custom-call | flops 1811939328 | bytes 8000000 | tf_op jit(solution)/shard_map/project/pallas_call | solution.py:116
  14.9 2.4 collective-permute-start.2
  17.3 7.2 %project.5 = (bf16[1024,768]{1,0:T(8,128)(2,1)}, bf16[1024,768]{1,0:T(8,128)(2,1)}, bf16[1024,384]{1,0:T(8,128)(2,1)}, f32[6,128,256]{2,1,0:T(8,128)}) custom-call(bf16[1024,768]{1,0:T(8,128)(2,1)} %a_ref.1, bf16[2,3,768,384]{3,2,1,0:T(8,128)(2,1)} %collective-permute-done.w_ref.wp_ref, f32[1024,128]{1,0:T(8,128)} %broadcast_in_dim.28.cos_ref, ...), custom_call_target="tpu_custom_call" | custom-call | flops 1811939328 | bytes 8000000 | tf_op jit(solution)/shard_map/project/pallas_call | solution.py:116
  28.8 16.1 %attend.2 = (bf16[1024,384]{1,0:T(8,128)(2,1)}, bf16[1024,384]{1,0:T(8,128)(2,1)}, f32[1024,768]{1,0:T(8,128)}, f32[1024,768]{1,0:T(8,128)}, bf16[1024,768]{1,0:...) custom-call(f32[1,1]{1,0:T(1,128)} %bitcast.3.flag_ref, ...), custom_call_target="tpu_custom_call" | custom-call | flops 2818572288 | bytes 25000000 | tf_op jit(solution)/shard_map/attend/pallas_call | solution.py:218
  44.9 24.6 %feed.2 = (bf16[1024,1536]{1,0:T(8,128)(2,1)}, bf16[1024,1536]{1,0:T(8,128)(2,1)}, bf16[1024,3072]{1,0:T(8,128)(2,1)}, f32[1024,768]{1,0:T(8,128)}, bf16[1024,76...) custom-call(bf16[1024,768]{1,0:T(8,128)(2,1)} %get-tuple-element.91.x_ref.a_ref, ...), custom_call_target="tpu_custom_call" | custom-call | flops 9663676416 | bytes 40000000 | tf_op jit(solution)/shard_map/feed/pallas_call | solution.py:324
  69.5 7.2 %project.6 = (bf16[1024,768]{1,0:T(8,128)(2,1)}, bf16[1024,768]{1,0:T(8,128)(2,1)}, bf16[1024,384]{1,0:T(8,128)(2,1)}, f32[6,128,256]{2,1,0:T(8,128)}) custom-call(bf16[1024,768]{1,0:T(8,128)(2,1)} %get-tuple-element.93.x_ref.a_ref, bf16[2,3,768,384]{3,2,1,0:T(8,128)(2,1)} %bitcast.217, f32[1024,128]{1,0:T(8,128)} %broadcast_in_dim.28.cos_ref, ...), custom_call_target="tpu_custom_call" | custom-call | flops 1811939328 | bytes 8000000 | tf_op jit(solution)/shard_map/project/pallas_call | solution.py:116
  76.7 7.2 %project.7 = (bf16[1024,768]{1,0:T(8,128)(2,1)}, bf16[1024,768]{1,0:T(8,128)(2,1)}, bf16[1024,384]{1,0:T(8,128)(2,1)}, f32[6,128,256]{2,1,0:T(8,128)}) custom-call(bf16[1024,768]{1,0:T(8,128)(2,1)} %get-tuple-element.93.x_ref.a_ref, bf16[2,3,768,384]{3,2,1,0:T(8,128)(2,1)} %collective-permute-done.w_ref.wp_ref, f32[1024,128]{1,0:T(8,128)} %broadcast_in_dim.28.cos_ref, ...), custom_call_target="tpu_custom_call" | custom-call | flops 1811939328 | bytes 8000000 | tf_op jit(solution)/shard_map/project/pallas_call | solution.py:116
  83.9 2.3 collective-permute-start.6
  87.8 1.6 fusion.26.live_ref
  90.6 16.2 %attend.3 = (bf16[1024,384]{1,0:T(8,128)(2,1)}, bf16[1024,384]{1,0:T(8,128)(2,1)}, f32[1024,768]{1,0:T(8,128)}, f32[1024,768]{1,0:T(8,128)}, bf16[1024,768]{1,0:...) custom-call(f32[1,1]{1,0:T(1,128)} %bitcast.3.flag_ref, ...), custom_call_target="tpu_custom_call" | custom-call | flops 2818572288 | bytes 25000000 | tf_op jit(solution)/shard_map/attend/pallas_call | solution.py:218
  106.9 24.6 %feed.3 = (bf16[1024,1536]{1,0:T(8,128)(2,1)}, bf16[1024,1536]{1,0:T(8,128)(2,1)}, bf16[1024,3072]{1,0:T(8,128)(2,1)}, f32[1024,768]{1,0:T(8,128)}, bf16[1024,76...) custom-call(bf16[1024,768]{1,0:T(8,128)(2,1)} %get-tuple-element.103.x_ref.a_ref, ...), custom_call_target="tpu_custom_call" | custom-call | flops 9663676416 | bytes 40000000 | tf_op jit(solution)/shard_map/feed/pallas_call | solution.py:324
  131.5 26.3 %feed_back.2 = (bf16[1024,768]{1,0:T(8,128)(2,1)}, bf16[1024,1536]{1,0:T(8,128)(2,1)}, bf16[1024,1536]{1,0:T(8,128)(2,1)}, f32[1024,768]{1,0:T(8,128)}, bf16[1024,768]{1,0:T(8,128)(2,1)}, /*index=5*/f32[4,768]{1,0:T(4,128)}) custom-call(f32[1024,768]{1,0:T(8,128)} %up_ref.1, f32[1024,1]{1,0:T(8,128)} %fusion.26.live_ref, ...), custom_call_target="tpu_custom_call" | custom-call | flops 9663676416 | bytes 45000000 | tf_op jit(solution)/shard_map/feed_back/pallas_call | solution.py:431
  158.4 10.1 %mix_back.2 = (bf16[1024,3072]{1,0:T(8,128)(2,1)}, f32[12,128,256]{2,1,0:T(8,128)}) custom-call(bf16[1024,768]{1,0:T(8,128)(2,1)} %get-tuple-element.111.gb_ref.b_ref, bf16[2,384,768]{2,1,0:T(8,128)(2,1)} %wo_ref.7, bf16[2,384,768]{2,1,0:T(8,128)(2,1)} %copy-done, f32[1024,768]{1,0:T(8,128)} %get-tuple-element.112.rden_ref, ...), custom_call_target="tpu_custom_call" | custom-call | flops 1811939328 | bytes 25000000 | tf_op jit(solution)/shard_map/mix_back/pallas_call | solution.py:506
  171.5 4.6 out_grad.3
  177.9 2.6 collective-permute-start.30
  181.9 6.3 collective-permute-done.30
  189.5 2.2 collective-permute-start.31
  191.7 21.5 %attend_back.2 = (bf16[1024,1152]{1,0:T(8,128)(2,1)}, bf16[1024,1152]{1,0:T(8,128)(2,1)}) custom-call(f32[1,1]{1,0:T(1,128)} %bitcast.3.flag_ref, bf16[1024,768]{1,0:T(8,128)(2,1)} %get-tuple-element.94.qo_ref, bf16[1024,768]{1,0:T(8,128)(2,1)} %get-tuple-element.95.qp_ref, bf16[1024,768]{1,0:T(8,128)(2,1)} %get-tuple-element.96.ko_ref, ...), custom_call_target="tpu_custom_call" | custom-call | flops 4026531840 | bytes 25000000 | tf_op jit(solution)/shard_map/attend_back/pallas_call | solution.py:590
  213.3 1.6 collective-permute-start.32
  215.0 9.8 %input_back.2.up_ref = f32[1024,768]{1,0:T(8,128)} custom-call(bf16[1024,1152]{1,0:T(8,128)(2,1)} %get-tuple-element.118.go_ref.b_ref, bf16[1024,1152]{1,0:T(8,128)(2,1)} %get-tuple-element.119.gp_ref, bf16[2,3,768,384]{3,2,1,0:T(8,128)(2,1)} %bitcast.218, bf16[2,3,768,384]{3,2,1,0:T(8,128)(2,1)} %collective-permute-done.w_ref.wp_ref, ...), custom_call_target="tpu_custom_call" | custom-call | flops 3623878656 | bytes 15000000 | tf_op jit(solution)/shard_map/input_back/pallas_call | solution.py:624
  225.6 25.9 %feed_back.3 = (bf16[1024,768]{1,0:T(8,128)(2,1)}, bf16[1024,1536]{1,0:T(8,128)(2,1)}, bf16[1024,1536]{1,0:T(8,128)(2,1)}, f32[1024,768]{1,0:T(8,128)}, bf16[1024,768]{1,0:T(8,128)(2,1)}, /*index=5*/f32[4,768]{1,0:T(4,128)}) custom-call(f32[1024,768]{1,0:T(8,128)} %input_back.2.up_ref, f32[1024,1]{1,0:T(8,128)} %broadcast_in_dim.30.live_ref, ...), custom_call_target="tpu_custom_call" | custom-call | flops 9663676416 | bytes 45000000 | tf_op jit(solution)/shard_map/feed_back/pallas_call | solution.py:431
  251.5 10.2 %mix_back.3 = (bf16[1024,3072]{1,0:T(8,128)(2,1)}, f32[12,128,256]{2,1,0:T(8,128)}) custom-call(bf16[1024,768]{1,0:T(8,128)(2,1)} %get-tuple-element.126.gb_ref.b_ref, bf16[2,384,768]{2,1,0:T(8,128)(2,1)} %wo_ref.7, bf16[2,384,768]{2,1,0:T(8,128)(2,1)} %copy-done, f32[1024,768]{1,0:T(8,128)} %get-tuple-element.127.rden_ref, ...), custom_call_target="tpu_custom_call" | custom-call | flops 1811939328 | bytes 25000000 | tf_op jit(solution)/shard_map/mix_back/pallas_call | solution.py:506
  262.7 2.7 collective-permute-start.33
  265.4 39.4 %all-reduce = f32[2,4,768]{2,1,0:T(4,128)S(1)} all-reduce(f32[2,4,768]{2,1,0:T(4,128)S(1)} %pad_maximum_fusion.6), channel_id=2, replica_groups=mesh['wide'=16,'narrow'=2] {'wide','narrow'}, use_global_device_ids=true, to_apply=%region_4.5.clone | all-reduce | flops 6144 | bytes 49152
  308.8 8.9 %in_grad.3 = bf16[768,1536]{1,0:T(8,128)(2,1)} custom-call(bf16[1024,768]{1,0:T(8,128)(2,1)} %get-tuple-element.103.x_ref.a_ref, bf16[1024,1536]{1,0:T(8,128)(2,1)} %get-tuple-element.138.b_ref, bf16[1024,768]{1,0:T(8,128)(2,1)} %copy-done.45, bf16[1024,1536]{1,0:T(8,128)(2,1)} %collective-permute-done.41.d_ref), custom_call_target="tpu_custom_call" | custom-call | flops 4831838208 | bytes 11796480 | tf_op jit(solution)/shard_map/in_grad/pallas_call | solution.py:647
  317.7 1.9 constant_dynamic-slice_fusion.5
  320.7 4.7 out_grad.2
  328.4 9.0 %back_grad.2 = bf16[1536,768]{1,0:T(8,128)(2,1)} custom-call(bf16[1024,1536]{1,0:T(8,128)(2,1)} %get-tuple-element.140.a_ref, bf16[1024,768]{1,0:T(8,128)(2,1)} %get-tuple-element.141.b_ref, bf16[1024,1536]{1,0:T(8,128)(2,1)} %collective-permute-done.46.c_ref, bf16[1024,768]{1,0:T(8,128)(2,1)} %collective-permute-done.47.d_ref), custom_call_target="tpu_custom_call" | custom-call | flops 4831838208 | bytes 11796480 | tf_op jit(solution)/shard_map/back_grad/pallas_call | solution.py:647
  337.4 2.3 collective-permute-start.35
  339.7 2.3 collective-permute-start.24
  342.0 9.1 %back_grad.3 = bf16[1536,768]{1,0:T(8,128)(2,1)} custom-call(bf16[1024,1536]{1,0:T(8,128)(2,1)} %get-tuple-element.143.a_ref, bf16[1024,768]{1,0:T(8,128)(2,1)} %get-tuple-element.144.b_ref, bf16[1024,1536]{1,0:T(8,128)(2,1)} %collective-permute-done.52.c_ref, bf16[1024,768]{1,0:T(8,128)(2,1)} %collective-permute-done.53.d_ref), custom_call_target="tpu_custom_call" | custom-call | flops 4831838208 | bytes 11796480 | tf_op jit(solution)/shard_map/back_grad/pallas_call | solution.py:647
  353.3 3.4 collective-permute-done.25
  357.2 1.6 collective-permute-start.26
  358.8 21.5 %attend_back.3 = (bf16[1024,1152]{1,0:T(8,128)(2,1)}, bf16[1024,1152]{1,0:T(8,128)(2,1)}) custom-call(f32[1,1]{1,0:T(1,128)} %bitcast.3.flag_ref, bf16[1024,768]{1,0:T(8,128)(2,1)} %get-tuple-element.83.qo_ref, bf16[1024,768]{1,0:T(8,128)(2,1)} %get-tuple-element.84.qp_ref, bf16[1024,768]{1,0:T(8,128)(2,1)} %get-tuple-element.85.ko_ref, ...), custom_call_target="tpu_custom_call" | custom-call | flops 4026531840 | bytes 25000000 | tf_op jit(solution)/shard_map/attend_back/pallas_call | solution.py:590
  386.2 1.7 collective-permute-start.48
  388.2 8.7 %qkv_grad.3 = bf16[768,1152]{1,0:T(8,128)(2,1)} custom-call(bf16[1024,768]{1,0:T(8,128)(2,1)} %get-tuple-element.93.x_ref.a_ref, bf16[1024,1152]{1,0:T(8,128)(2,1)} %get-tuple-element.118.go_ref.b_ref, bf16[1024,768]{1,0:T(8,128)(2,1)} %collective-permute-done.16.c_ref, bf16[1024,1152]{1,0:T(8,128)(2,1)} %collective-permute-done.17.d_ref), custom_call_target="tpu_custom_call" | custom-call | flops 3623878656 | bytes 9633792 | tf_op jit(solution)/shard_map/qkv_grad/pallas_call | solution.py:647
  397.0 3.5 reshape_reshape.25
  403.0 1.7 fusion.2
  405.6 9.7 %collective-permute-done.48 = bf16[2,2,2,96,768]{4,3,0,1,2:T(8,128)(2,1)} collective-permute-done((bf16[2,2,2,96,768]{4,3,0,1,2:T(8,128)(2,1)}, bf16[2,2,2,96,768]{4,3,0,1,2:T(8,128)(2,1)}, u32[]{:S(2)}, u32[]{:S(2)}) %collective-permute-start.48) | collective-permute-done | bytes 1179680 | tf_op jit(solution)/shard_map/ppermute | solution.py:667
  415.3 1.7 fusion.1
  417.0 23.2 %collective-permute-done.54 = bf16[2,2,2,96,768]{4,3,0,1,2:T(8,128)(2,1)} collective-permute-done((bf16[2,2,2,96,768]{4,3,0,1,2:T(8,128)(2,1)}, bf16[2,2,2,96,768]{4,3,0,1,2:T(8,128)(2,1)}, u32[]{:S(2)}, u32[]{:S(2)}) %collective-permute-start.54) | collective-permute-done | bytes 1179680 | tf_op jit(solution)/shard_map/ppermute | solution.py:667
  440.2 1.7 collective-permute-start.18
  441.9 1.6 fusion
  448.4 8.9 %in_grad.2 = bf16[768,1536]{1,0:T(8,128)(2,1)} custom-call(bf16[1024,768]{1,0:T(8,128)(2,1)} %get-tuple-element.91.x_ref.a_ref, bf16[1024,1536]{1,0:T(8,128)(2,1)} %get-tuple-element.136.b_ref, bf16[1024,768]{1,0:T(8,128)(2,1)} %copy-done.46, bf16[1024,1536]{1,0:T(8,128)(2,1)} %collective-permute-done.35.d_ref), custom_call_target="tpu_custom_call" | custom-call | flops 4831838208 | bytes 11796480 | tf_op jit(solution)/shard_map/in_grad/pallas_call | solution.py:647
  457.3 1.9 constant_dynamic-slice_fusion.7
  459.3 2.4 collective-permute-done.18
  461.7 1.7 collective-permute-start.43
  465.9 9.7 %collective-permute-done.55 = bf16[2,2,96,768]{3,2,0,1:T(8,128)(2,1)} collective-permute-done((bf16[2,2,96,768]{3,2,0,1:T(8,128)(2,1)}, bf16[2,2,96,768]{3,2,0,1:T(8,128)(2,1)}, u32[]{:S(2)}, u32[]{:S(2)}) %collective-permute-start.55) | collective-permute-done | bytes 589856 | tf_op jit(solution)/shard_map/ppermute | solution.py:667
  477.7 10.4 %collective-permute-done.43 = bf16[2,2,48,1536]{3,2,0,1:T(8,128)(2,1)S(1)} collective-permute-done((bf16[2,2,48,1536]{3,2,0,1:T(8,128)(2,1)S(1)}, bf16[2,2,48,1536]{3,2,0,1:T(8,128)(2,1)S(1)}, u32[]{:S(2)}, u32[]{:S(2)}) %collective-permute-start.43) | collective-permute-done | bytes 589856 | tf_op jit(solution)/shard_map/ppermute | solution.py:667
  488.7 7.3 %collective-permute-done.50 = bf16[2,96,768]{2,1,0:T(8,128)(2,1)S(1)} collective-permute-done((bf16[2,96,768]{2,1,0:T(8,128)(2,1)S(1)}, bf16[2,96,768]{2,1,0:T(8,128)(2,1)S(1)}, u32[]{:S(2)}, u32[]{:S(2)}) %collective-permute-start.50) | collective-permute-done | bytes 294944 | tf_op jit(solution)/shard_map/ppermute | solution.py:667
  496.6 8.6 %collective-permute-done.44 = bf16[2,48,1536]{2,1,0:T(8,128)(2,1)S(1)} collective-permute-done((bf16[2,48,1536]{2,1,0:T(8,128)(2,1)S(1)}, bf16[2,48,1536]{2,1,0:T(8,128)(2,1)S(1)}, u32[]{:S(2)}, u32[]{:S(2)}) %collective-permute-start.44) | collective-permute-done | bytes 294944 | tf_op jit(solution)/shard_map/ppermute | solution.py:667
  505.7 8.8 %collective-permute-done.56 = bf16[2,96,768]{2,1,0:T(8,128)(2,1)S(1)} collective-permute-done((bf16[2,96,768]{2,1,0:T(8,128)(2,1)S(1)}, bf16[2,96,768]{2,1,0:T(8,128)(2,1)S(1)}, u32[]{:S(2)}, u32[]{:S(2)}) %collective-permute-start.56) | collective-permute-done | bytes 294944 | tf_op jit(solution)/shard_map/ppermute | solution.py:667
  517.8 10.1 %collective-permute-done.45 = bf16[48,1536]{1,0:T(8,128)(2,1)S(1)} collective-permute-done((bf16[48,1536]{1,0:T(8,128)(2,1)S(1)}, bf16[48,1536]{1,0:T(8,128)(2,1)S(1)}, u32[]{:S(2)}, u32[]{:S(2)}) %collective-permute-start.45) | collective-permute-done | bytes 147488 | tf_op jit(solution)/shard_map/ppermute | solution.py:667
  528.6 1.6 collective-permute-start.20
  530.2 5.4 collective-permute-done.57
  540.4 8.7 %qkv_grad.2 = bf16[768,1152]{1,0:T(8,128)(2,1)} custom-call(bf16[1024,768]{1,0:T(8,128)(2,1)} %a_ref.1, bf16[1024,1152]{1,0:T(8,128)(2,1)} %get-tuple-element.133.go_ref.b_ref, bf16[1024,768]{1,0:T(8,128)(2,1)} %collective-permute-done.10.c_ref, bf16[1024,1152]{1,0:T(8,128)(2,1)} %collective-permute-done.11.d_ref), custom_call_target="tpu_custom_call" | custom-call | flops 3623878656 | bytes 9633792 | tf_op jit(solution)/shard_map/qkv_grad/pallas_call | solution.py:647
  549.1 3.3 reshape_reshape.24
  558.4 8.1 %collective-permute-done.12 = bf16[2,2,2,48,3,384]{5,3,4,2,1,0:T(8,128)(2,1)S(1)} collective-permute-done((bf16[2,2,2,48,3,384]{5,3,4,2,1,0:T(8,128)(2,1)S(1)}, bf16[2,2,2,48,3,384]{5,3,4,2,1,0:T(8,128)(2,1)S(1)}, u32[]{:S(2)}, u32[]{:S(2)}) %collective-permute-start.12) | collective-permute-done | bytes 884768 | tf_op jit(solution)/shard_map/ppermute | solution.py:667
  568.0 7.1 %collective-permute-done.13 = bf16[2,2,48,3,384]{4,2,3,1,0:T(8,128)(2,1)S(1)} collective-permute-done((bf16[2,2,48,3,384]{4,2,3,1,0:T(8,128)(2,1)S(1)}, bf16[2,2,48,3,384]{4,2,3,1,0:T(8,128)(2,1)S(1)}, u32[]{:S(2)}, u32[]{:S(2)}) %collective-permute-start.13) | collective-permute-done | bytes 442400 | tf_op jit(solution)/shard_map/ppermute | solution.py:667
  578.2 3.1 collective-permute-done.14
  581.4 2.8 collective-permute-start.15
  585.0 3.3 collective-permute-done.15
  592.4 9.9 %input_back.3 = f32[1024,768]{1,0:T(8,128)} custom-call(bf16[1024,1152]{1,0:T(8,128)(2,1)} %get-tuple-element.133.go_ref.b_ref, bf16[1024,1152]{1,0:T(8,128)(2,1)} %get-tuple-element.134.gp_ref, bf16[2,3,768,384]{3,2,1,0:T(8,128)(2,1)} %bitcast.219, bf16[2,3,768,384]{3,2,1,0:T(8,128)(2,1)} %collective-permute-done.w_ref.wp_ref, ...), custom_call_target="tpu_custom_call" | custom-call | flops 3623878656 | bytes 15000000 | tf_op jit(solution)/shard_map/input_back/pallas_call | solution.py:624
  602.3 38.6 %psum.7 = f32[]{:T(128)} all-reduce(f32[]{:T(128)S(6)} %add.410), channel_id=1, replica_groups=mesh['wide'=16,'narrow'=2] {'wide','narrow'}, use_global_device_ids=true, to_apply=%region_6.7 | all-reduce | flops 1 | bytes 8 | tf_op jit(solution)/shard_map/psum | solution.py:793
  (269 shorter events, 81.4 us)
Async XLA Ops:
  0.7 16.6 %collective-permute-start = (bf16[2,3,768,384]{3,2,1,0:T(8,128)(2,1)}, bf16[2,3,768,384]{3,2,1,0:T(8,128)(2,1)}, u32[]{:S(2)}, u32[]{:S(2)}) collective-permute-start(bf16[2,3,768,384]{3,2,1,0:T(8,128)(2,1)} %bitcast.215), channel_id=1, source_target_pairs={{0,1},{1,0},{2,3},{3,2},{4,5},{5,4},{6,7},{7,6},{8,9},{9,8},{10,11... | collective-permute-start | bytes 10616840 | tf_op jit(solution)/shard_map/ppermute | solution.py:660
  1.2 43.7 %collective-permute-start.4 = (bf16[2,768,1536]{2,1,0:T(8,128)(2,1)}, bf16[2,768,1536]{2,1,0:T(8,128)(2,1)}, u32[]{:S(2)}, u32[]{:S(2)}) collective-permute-start(bf16[2,768,1536]{2,1,0:T(8,128)(2,1)} %wio_ref.7), channel_id=1, source_target_pairs={{0,1},{1,0},{2,3},{3,2},{4,5},{5,4},{6,7},{7,6},{8,9},{9,8},{10,11... | collective-permute-start | bytes 14155784 | tf_op jit(solution)/shard_map/ppermute | solution.py:660
  1.3 43.6 %collective-permute-start.5 = (bf16[2,1536,768]{2,1,0:T(8,128)(2,1)}, bf16[2,1536,768]{2,1,0:T(8,128)(2,1)}, u32[]{:S(2)}, u32[]{:S(2)}) collective-permute-start(bf16[2,1536,768]{2,1,0:T(8,128)(2,1)} %wbo_ref.7), channel_id=1, source_target_pairs={{0,1},{1,0},{2,3},{3,2},{4,5},{5,4},{6,7},{7,6},{8,9},{9,8},{10,11... | collective-permute-start | bytes 14155784 | tf_op jit(solution)/shard_map/ppermute | solution.py:660
  1.7 24.9 %collective-permute-start.3 = (bf16[2,384,768]{2,1,0:T(8,128)(2,1)}, bf16[2,384,768]{2,1,0:T(8,128)(2,1)S(1)}, u32[]{:S(2)}, u32[]{:S(2)}) collective-permute-start(bf16[2,384,768]{2,1,0:T(8,128)(2,1)} %wo_ref.7), channel_id=1, source_target_pairs={{0,1},{1,0},{2,3},{3,2},{4,5},{5,4},{6,7},{7,6},{8,9},{9,8},{10,11... | collective-permute-start | bytes 3538952 | tf_op jit(solution)/shard_map/ppermute | solution.py:660
  14.9 11.7 %collective-permute-start.2 = (f32[6,128,256]{2,1,0:T(8,128)}, f32[6,128,256]{2,1,0:T(8,128)S(1)}, u32[]{:S(2)}, u32[]{:S(2)}) collective-permute-start(f32[6,128,256]{2,1,0:T(8,128)} %get-tuple-element.90), channel_id=1, source_target_pairs={{0,1},{2,3},{4,5},{6,7},{8,9},{10,11},{12,13},{14,15},{16,17},{18,... | collective-permute-start | bytes 2359304 | tf_op jit(solution)/shard_map/ppermute | solution.py:742
  24.4 3.4 collective-permute-start.1
  83.9 5.5 collective-permute-start.6
  86.3 3.2 collective-permute-start.7
  157.8 13.6 %collective-permute-start.29 = (bf16[1024,768]{1,0:T(8,128)(2,1)}, bf16[1024,768]{1,0:T(8,128)(2,1)}, u32[]{:S(2)}, u32[]{:S(2)}) collective-permute-start(bf16[1024,768]{1,0:T(8,128)(2,1)} %get-tuple-element.111.gb_ref.b_ref), channel_id=1, source_target_pairs={{0,1},{1,0},{2,3},{3,2},{4,5},{5,4},{6,7},{7,6},{8,9},{9,8},{10,11... | collective-permute-start | bytes 4718600 | tf_op jit(solution)/shard_map/ppermute | solution.py:660
  158.0 13.4 %collective-permute-start.28 = (bf16[1024,384]{1,0:T(8,128)(2,1)}, bf16[1024,384]{1,0:T(8,128)(2,1)}, u32[]{:S(2)}, u32[]{:S(2)}) collective-permute-start(bf16[1024,384]{1,0:T(8,128)(2,1)} %get-tuple-element.114.mp_ref), channel_id=1, source_target_pairs={{0,1},{1,0},{2,3},{3,2},{4,5},{5,4},{6,7},{7,6},{8,9},{9,8},{10,11... | collective-permute-start | bytes 2359304 | tf_op jit(solution)/shard_map/ppermute | solution.py:660
  170.1 19.4 %collective-permute-start.8 = (f32[12,128,256]{2,1,0:T(8,128)S(1)}, f32[12,128,256]{2,1,0:T(8,128)S(1)}, u32[]{:S(2)}, u32[]{:S(2)}) collective-permute-start(f32[12,128,256]{2,1,0:T(8,128)S(1)} %pad_maximum_fusion), channel_id=1, source_target_pairs={{1,0},{3,2},{5,4},{7,6},{9,8},{11,10},{13,12},{15,14},{17,16},{19,... | collective-permute-start | bytes 4718600 | tf_op jit(solution)/shard_map/ppermute | solution.py:770
  177.9 10.3 %collective-permute-start.30 = (bf16[2,2,2,24,768]{4,3,0,1,2:T(8,128)(2,1)}, bf16[2,2,2,24,768]{4,3,0,1,2:T(8,128)(2,1)}, u32[]{:S(2)}, u32[]{:S(2)}) collective-permute-start(bf16[2,2,2,24,768]{4,3,0,1,2:T(8,128)(2,1)} %bitcast.213), channel_id=1, source_target_pairs={{0,2},{2,0},{4,6},{6,4},{8,10},{10,8},{12,14},{14,12},{16,18},{18,... | collective-permute-start | bytes 884744 | tf_op jit(solution)/shard_map/ppermute | solution.py:667
  180.4 81.4 %collective-permute-start.22 = (bf16[1024,384]{1,0:T(8,128)(2,1)}, bf16[1024,384]{1,0:T(8,128)(2,1)S(1)}, u32[]{:S(2)}, u32[]{:S(2)}) collective-permute-start(bf16[1024,384]{1,0:T(8,128)(2,1)} %get-tuple-element.129.mp_ref), channel_id=1, source_target_pairs={{0,1},{1,0},{2,3},{3,2},{4,5},{5,4},{6,7},{7,6},{8,9},{9,8},{10,11... | collective-permute-start | bytes 2359304 | tf_op jit(solution)/shard_map/ppermute | solution.py:660
  181.4 145.2 %collective-permute-start.46 = (bf16[1024,1536]{1,0:T(8,128)(2,1)}, bf16[1024,1536]{1,0:T(8,128)(2,1)}, u32[]{:S(2)}, u32[]{:S(2)}) collective-permute-start(bf16[1024,1536]{1,0:T(8,128)(2,1)} %get-tuple-element.142), channel_id=1, source_target_pairs={{0,1},{1,0},{2,3},{3,2},{4,5},{5,4},{6,7},{7,6},{8,9},{9,8},{10,11... | collective-permute-start | bytes 9437192 | tf_op jit(solution)/shard_map/ppermute | solution.py:660
  181.4 81.4 %collective-permute-start.40 = (bf16[1024,768]{1,0:T(8,128)(2,1)}, bf16[1024,768]{1,0:T(8,128)(2,1)S(1)}, u32[]{:S(2)}, u32[]{:S(2)}) collective-permute-start(bf16[1024,768]{1,0:T(8,128)(2,1)} %get-tuple-element.103.x_ref.a_ref), channel_id=1, source_target_pairs={{0,1},{1,0},{2,3},{3,2},{4,5},{5,4},{6,7},{7,6},{8,9},{9,8},{10,11... | collective-permute-start | bytes 4718600 | tf_op jit(solution)/shard_map/ppermute | solution.py:660
  188.1 120.1 %collective-permute-start.41 = (bf16[1024,1536]{1,0:T(8,128)(2,1)}, bf16[1024,1536]{1,0:T(8,128)(2,1)}, u32[]{:S(2)}, u32[]{:S(2)}) collective-permute-start(bf16[1024,1536]{1,0:T(8,128)(2,1)} %get-tuple-element.139), channel_id=1, source_target_pairs={{0,1},{1,0},{2,3},{3,2},{4,5},{5,4},{6,7},{7,6},{8,9},{9,8},{10,11... | collective-permute-start | bytes 9437192 | tf_op jit(solution)/shard_map/ppermute | solution.py:660
  189.5 23.7 %collective-permute-start.31 = (bf16[2,2,24,768]{3,2,0,1:T(8,128)(2,1)S(1)}, bf16[2,2,24,768]{3,2,0,1:T(8,128)(2,1)S(1)}, u32[]{:S(2)}, u32[]{:S(2)}) collective-permute-start(bf16[2,2,24,768]{3,2,0,1:T(8,128)(2,1)S(1)} %dynamic-slice_bitcast_fusion.14), channel_id=1, source_target_pairs={{0,4},{2,6},{4,0},{6,2},{8,12},{10,14},{12,8},{14,10},{16,20},{18,... | collective-permute-start | bytes 442376 | tf_op jit(solution)/shard_map/ppermute | solution.py:667
  213.3 11.4 %collective-permute-start.32 = (bf16[2,24,768]{2,1,0:T(8,128)(2,1)S(1)}, bf16[2,24,768]{2,1,0:T(8,128)(2,1)S(1)}, u32[]{:S(2)}, u32[]{:S(2)}) collective-permute-start(bf16[2,24,768]{2,1,0:T(8,128)(2,1)S(1)} %dynamic-slice_bitcast_fusion.18), channel_id=1, source_target_pairs={{0,8},{2,10},{4,12},{6,14},{8,0},{10,2},{12,4},{14,6},{16,24},{18,... | collective-permute-start | bytes 221192 | tf_op jit(solution)/shard_map/ppermute | solution.py:667
  224.7 114.9 %collective-permute-start.52 = (bf16[1024,1536]{1,0:T(8,128)(2,1)}, bf16[1024,1536]{1,0:T(8,128)(2,1)}, u32[]{:S(2)}, u32[]{:S(2)}) collective-permute-start(bf16[1024,1536]{1,0:T(8,128)(2,1)} %get-tuple-element.145), channel_id=1, source_target_pairs={{0,1},{1,0},{2,3},{3,2},{4,5},{5,4},{6,7},{7,6},{8,9},{9,8},{10,11... | collective-permute-start | bytes 9437192 | tf_op jit(solution)/shard_map/ppermute | solution.py:660
  261.8 58.9 %collective-permute-start.23 = (bf16[1024,768]{1,0:T(8,128)(2,1)S(1)}, bf16[1024,768]{1,0:T(8,128)(2,1)}, u32[]{:S(2)}, u32[]{:S(2)}) collective-permute-start(bf16[1024,768]{1,0:T(8,128)(2,1)S(1)} %copy-done.1), channel_id=1, source_target_pairs={{0,1},{1,0},{2,3},{3,2},{4,5},{5,4},{6,7},{7,6},{8,9},{9,8},{10,11... | collective-permute-start | bytes 4718600 | tf_op jit(solution)/shard_map/ppermute | solution.py:660
  262.7 42.8 %collective-permute-start.33 = (bf16[24,768]{1,0:T(8,128)(2,1)S(1)}, bf16[24,768]{1,0:T(8,128)(2,1)S(1)}, u32[]{:S(2)}, u32[]{:S(2)}) collective-permute-start(bf16[24,768]{1,0:T(8,128)(2,1)S(1)} %dynamic-slice_bitcast_fusion.20), channel_id=1, source_target_pairs={{0,16},{2,18},{4,20},{6,22},{8,24},{10,26},{12,28},{14,30},{16,0},... | collective-permute-start | bytes 110600 | tf_op jit(solution)/shard_map/ppermute | solution.py:667
  305.5 21.7 %collective-permute-start.47 = (bf16[1024,768]{1,0:T(8,128)(2,1)}, bf16[1024,768]{1,0:T(8,128)(2,1)}, u32[]{:S(2)}, u32[]{:S(2)}) collective-permute-start(bf16[1024,768]{1,0:T(8,128)(2,1)} %get-tuple-element.141.b_ref), channel_id=1, source_target_pairs={{0,1},{1,0},{2,3},{3,2},{4,5},{5,4},{6,7},{7,6},{8,9},{9,8},{10,11... | collective-permute-start | bytes 4718600 | tf_op jit(solution)/shard_map/ppermute | solution.py:660
  308.2 29.2 %collective-permute-start.53 = (bf16[1024,768]{1,0:T(8,128)(2,1)}, bf16[1024,768]{1,0:T(8,128)(2,1)}, u32[]{:S(2)}, u32[]{:S(2)}) collective-permute-start(bf16[1024,768]{1,0:T(8,128)(2,1)} %get-tuple-element.144.b_ref), channel_id=1, source_target_pairs={{0,1},{1,0},{2,3},{3,2},{4,5},{5,4},{6,7},{7,6},{8,9},{9,8},{10,11... | collective-permute-start | bytes 4718600 | tf_op jit(solution)/shard_map/ppermute | solution.py:660
  308.8 76.8 %copy-start.31 = (bf16[1,24,768]{2,1,0:T(8,128)(2,1)}, bf16[1,24,768]{2,1,0:T(8,128)(2,1)S(1)}, u32[]{:S(2)}) copy-start(bf16[1,24,768]{2,1,0:T(8,128)(2,1)S(1)} %fusion.53) | copy-start | bytes 110596
  320.7 65.5 %collective-permute-start.16 = (bf16[1024,768]{1,0:T(8,128)(2,1)}, bf16[1024,768]{1,0:T(8,128)(2,1)}, u32[]{:S(2)}, u32[]{:S(2)}) collective-permute-start(bf16[1024,768]{1,0:T(8,128)(2,1)} %get-tuple-element.93.x_ref.a_ref), channel_id=1, source_target_pairs={{0,1},{1,0},{2,3},{3,2},{4,5},{5,4},{6,7},{7,6},{8,9},{9,8},{10,11... | collective-permute-start | bytes 4718600 | tf_op jit(solution)/shard_map/ppermute | solution.py:660
  326.6 61.3 %collective-permute-start.17 = (bf16[1024,1152]{1,0:T(8,128)(2,1)S(1)}, bf16[1024,1152]{1,0:T(8,128)(2,1)}, u32[]{:S(2)}, u32[]{:S(2)}) collective-permute-start(bf16[1024,1152]{1,0:T(8,128)(2,1)S(1)} %copy-done.5), channel_id=1, source_target_pairs={{0,1},{1,0},{2,3},{3,2},{4,5},{5,4},{6,7},{7,6},{8,9},{9,8},{10,11... | collective-permute-start | bytes 7077896 | tf_op jit(solution)/shard_map/ppermute | solution.py:660
  327.2 30.0 %collective-permute-start.9 = (f32[12,128,256]{2,1,0:T(8,128)}, f32[12,128,256]{2,1,0:T(8,128)}, u32[]{:S(2)}, u32[]{:S(2)}) collective-permute-start(f32[12,128,256]{2,1,0:T(8,128)} %pad_maximum_fusion.1), channel_id=1, source_target_pairs={{1,0},{3,2},{5,4},{7,6},{9,8},{11,10},{13,12},{15,14},{17,16},{19,... | collective-permute-start | bytes 4718600 | tf_op jit(solution)/shard_map/ppermute | solution.py:770
  337.4 109.8 %collective-permute-start.35 = (bf16[1024,1536]{1,0:T(8,128)(2,1)}, bf16[1024,1536]{1,0:T(8,128)(2,1)}, u32[]{:S(2)}, u32[]{:S(2)}) collective-permute-start(bf16[1024,1536]{1,0:T(8,128)(2,1)} %get-tuple-element.137), channel_id=1, source_target_pairs={{0,1},{1,0},{2,3},{3,2},{4,5},{5,4},{6,7},{7,6},{8,9},{9,8},{10,11... | collective-permute-start | bytes 9437192 | tf_op jit(solution)/shard_map/ppermute | solution.py:660
  339.7 11.3 %collective-permute-start.24 = (bf16[2,2,2,24,768]{4,3,0,1,2:T(8,128)(2,1)S(1)}, bf16[2,2,2,24,768]{4,3,0,1,2:T(8,128)(2,1)S(1)}, u32[]{:S(2)}, u32[]{:S(2)}) collective-permute-start(bf16[2,2,2,24,768]{4,3,0,1,2:T(8,128)(2,1)S(1)} %bitcast.228), channel_id=1, source_target_pairs={{0,2},{2,0},{4,6},{6,4},{8,10},{10,8},{12,14},{14,12},{16,18},{18,... | collective-permute-start | bytes 884744 | tf_op jit(solution)/shard_map/ppermute | solution.py:667
  351.1 5.6 collective-permute-start.25
  356.7 45.6 %collective-permute-start.42 = (bf16[2,2,2,48,1536]{4,3,0,1,2:T(8,128)(2,1)}, bf16[2,2,2,48,1536]{4,3,0,1,2:T(8,128)(2,1)}, u32[]{:S(2)}, u32[]{:S(2)}) collective-permute-start(bf16[2,2,2,48,1536]{4,3,0,1,2:T(8,128)(2,1)} %bitcast.209), channel_id=1, source_target_pairs={{0,2},{2,0},{4,6},{6,4},{8,10},{10,8},{12,14},{14,12},{16,18},{18,... | collective-permute-start | bytes 3538952 | tf_op jit(solution)/shard_map/ppermute | solution.py:667
  357.2 23.1 %collective-permute-start.26 = (bf16[2,24,768]{2,1,0:T(8,128)(2,1)S(1)}, bf16[2,24,768]{2,1,0:T(8,128)(2,1)S(1)}, u32[]{:S(2)}, u32[]{:S(2)}) collective-permute-start(bf16[2,24,768]{2,1,0:T(8,128)(2,1)S(1)} %dynamic-slice_bitcast_fusion.19), channel_id=1, source_target_pairs={{0,8},{2,10},{4,12},{6,14},{8,0},{10,2},{12,4},{14,6},{16,24},{18,... | collective-permute-start | bytes 221192 | tf_op jit(solution)/shard_map/ppermute | solution.py:667
  380.3 5.2 collective-permute-start.27
  385.5 154.8 %collective-permute-start.10 = (bf16[1024,768]{1,0:T(8,128)(2,1)}, bf16[1024,768]{1,0:T(8,128)(2,1)}, u32[]{:S(2)}, u32[]{:S(2)}) collective-permute-start(bf16[1024,768]{1,0:T(8,128)(2,1)} %a_ref.1), channel_id=1, source_target_pairs={{0,1},{1,0},{2,3},{3,2},{4,5},{5,4},{6,7},{7,6},{8,9},{9,8},{10,11... | collective-permute-start | bytes 4718600 | tf_op jit(solution)/shard_map/ppermute | solution.py:660
  386.2 29.1 %collective-permute-start.48 = (bf16[2,2,2,96,768]{4,3,0,1,2:T(8,128)(2,1)}, bf16[2,2,2,96,768]{4,3,0,1,2:T(8,128)(2,1)}, u32[]{:S(2)}, u32[]{:S(2)}) collective-permute-start(bf16[2,2,2,96,768]{4,3,0,1,2:T(8,128)(2,1)} %bitcast.208), channel_id=1, source_target_pairs={{0,2},{2,0},{4,6},{6,4},{8,10},{10,8},{12,14},{14,12},{16,18},{18,... | collective-permute-start | bytes 3538952 | tf_op jit(solution)/shard_map/ppermute | solution.py:667
  387.9 52.3 %collective-permute-start.54 = (bf16[2,2,2,96,768]{4,3,0,1,2:T(8,128)(2,1)}, bf16[2,2,2,96,768]{4,3,0,1,2:T(8,128)(2,1)}, u32[]{:S(2)}, u32[]{:S(2)}) collective-permute-start(bf16[2,2,2,96,768]{4,3,0,1,2:T(8,128)(2,1)} %bitcast.207), channel_id=1, source_target_pairs={{0,2},{2,0},{4,6},{6,4},{8,10},{10,8},{12,14},{14,12},{16,18},{18,... | collective-permute-start | bytes 3538952 | tf_op jit(solution)/shard_map/ppermute | solution.py:667
  403.0 42.2 %collective-permute-start.34 = (bf16[1024,768]{1,0:T(8,128)(2,1)S(1)}, bf16[1024,768]{1,0:T(8,128)(2,1)S(1)}, u32[]{:S(2)}, u32[]{:S(2)}) collective-permute-start(bf16[1024,768]{1,0:T(8,128)(2,1)S(1)} %copy-done.44), channel_id=1, source_target_pairs={{0,1},{1,0},{2,3},{3,2},{4,5},{5,4},{6,7},{7,6},{8,9},{9,8},{10,11... | collective-permute-start | bytes 4718600 | tf_op jit(solution)/shard_map/ppermute | solution.py:660
  415.3 125.1 %collective-permute-start.11 = (bf16[1024,1152]{1,0:T(8,128)(2,1)S(1)}, bf16[1024,1152]{1,0:T(8,128)(2,1)}, u32[]{:S(2)}, u32[]{:S(2)}) collective-permute-start(bf16[1024,1152]{1,0:T(8,128)(2,1)S(1)} %copy-done.4), channel_id=1, source_target_pairs={{0,1},{1,0},{2,3},{3,2},{4,5},{5,4},{6,7},{7,6},{8,9},{9,8},{10,11... | collective-permute-start | bytes 7077896 | tf_op jit(solution)/shard_map/ppermute | solution.py:660
  440.2 21.5 %collective-permute-start.18 = (bf16[2,2,2,48,3,384]{5,3,4,2,1,0:T(8,128)(2,1)}, bf16[2,2,2,48,3,384]{5,3,4,2,1,0:T(8,128)(2,1)S(1)}, u32[]{:S(2)}, u32[]{:S(2)}) collective-permute-start(bf16[2,2,2,48,3,384]{5,3,4,2,1,0:T(8,128)(2,1)} %bitcast.211), channel_id=1, source_target_pairs={{0,2},{2,0},{4,6},{6,4},{8,10},{10,8},{12,14},{14,12},{16,18},{18,... | collective-permute-start | bytes 2654216 | tf_op jit(solution)/shard_map/ppermute | solution.py:667
  446.3 17.3 %collective-permute-start.49 = (bf16[2,2,96,768]{3,2,0,1:T(8,128)(2,1)}, bf16[2,2,96,768]{3,2,0,1:T(8,128)(2,1)}, u32[]{:S(2)}, u32[]{:S(2)}) collective-permute-start(bf16[2,2,96,768]{3,2,0,1:T(8,128)(2,1)} %dynamic-slice_bitcast_fusion.1), channel_id=1, source_target_pairs={{0,4},{2,6},{4,0},{6,2},{8,12},{10,14},{12,8},{14,10},{16,20},{18,... | collective-permute-start | bytes 1769480 | tf_op jit(solution)/shard_map/ppermute | solution.py:667
  447.3 28.3 %collective-permute-start.55 = (bf16[2,2,96,768]{3,2,0,1:T(8,128)(2,1)}, bf16[2,2,96,768]{3,2,0,1:T(8,128)(2,1)}, u32[]{:S(2)}, u32[]{:S(2)}) collective-permute-start(bf16[2,2,96,768]{3,2,0,1:T(8,128)(2,1)} %dynamic-slice_bitcast_fusion), channel_id=1, source_target_pairs={{0,4},{2,6},{4,0},{6,2},{8,12},{10,14},{12,8},{14,10},{16,20},{18,... | collective-permute-start | bytes 1769480 | tf_op jit(solution)/shard_map/ppermute | solution.py:667
  461.7 26.4 %collective-permute-start.43 = (bf16[2,2,48,1536]{3,2,0,1:T(8,128)(2,1)S(1)}, bf16[2,2,48,1536]{3,2,0,1:T(8,128)(2,1)S(1)}, u32[]{:S(2)}, u32[]{:S(2)}) collective-permute-start(bf16[2,2,48,1536]{3,2,0,1:T(8,128)(2,1)S(1)} %copy-done.21), channel_id=1, source_target_pairs={{0,4},{2,6},{4,0},{6,2},{8,12},{10,14},{12,8},{14,10},{16,20},{18,... | collective-permute-start | bytes 1769480 | tf_op jit(solution)/shard_map/ppermute | solution.py:667
  463.7 74.5 %collective-permute-start.36 = (bf16[2,2,2,48,1536]{4,3,0,1,2:T(8,128)(2,1)S(1)}, bf16[2,2,2,48,1536]{4,3,0,1,2:T(8,128)(2,1)S(1)}, u32[]{:S(2)}, u32[]{:S(2)}) collective-permute-start(bf16[2,2,2,48,1536]{4,3,0,1,2:T(8,128)(2,1)S(1)} %bitcast.226), channel_id=1, source_target_pairs={{0,2},{2,0},{4,6},{6,4},{8,10},{10,8},{12,14},{14,12},{16,18},{18,... | collective-permute-start | bytes 3538952 | tf_op jit(solution)/shard_map/ppermute | solution.py:667
  475.6 40.6 %collective-permute-start.19 = (bf16[2,2,48,3,384]{4,2,3,1,0:T(8,128)(2,1)S(1)}, bf16[2,2,48,3,384]{4,2,3,1,0:T(8,128)(2,1)S(1)}, u32[]{:S(2)}, u32[]{:S(2)}) collective-permute-start(bf16[2,2,48,3,384]{4,2,3,1,0:T(8,128)(2,1)S(1)} %copy_bitcast_fusion.12), channel_id=1, source_target_pairs={{0,4},{2,6},{4,0},{6,2},{8,12},{10,14},{12,8},{14,10},{16,20},{18,... | collective-permute-start | bytes 1327112 | tf_op jit(solution)/shard_map/ppermute | solution.py:667
  488.1 8.0 %collective-permute-start.50 = (bf16[2,96,768]{2,1,0:T(8,128)(2,1)S(1)}, bf16[2,96,768]{2,1,0:T(8,128)(2,1)S(1)}, u32[]{:S(2)}, u32[]{:S(2)}) collective-permute-start(bf16[2,96,768]{2,1,0:T(8,128)(2,1)S(1)} %dynamic-slice_bitcast_fusion.5), channel_id=1, source_target_pairs={{0,8},{2,10},{4,12},{6,14},{8,0},{10,2},{12,4},{14,6},{16,24},{18,... | collective-permute-start | bytes 884744 | tf_op jit(solution)/shard_map/ppermute | solution.py:667
  496.1 9.2 %collective-permute-start.44 = (bf16[2,48,1536]{2,1,0:T(8,128)(2,1)S(1)}, bf16[2,48,1536]{2,1,0:T(8,128)(2,1)S(1)}, u32[]{:S(2)}, u32[]{:S(2)}) collective-permute-start(bf16[2,48,1536]{2,1,0:T(8,128)(2,1)S(1)} %dynamic-slice_bitcast_fusion.6), channel_id=1, source_target_pairs={{0,8},{2,10},{4,12},{6,14},{8,0},{10,2},{12,4},{14,6},{16,24},{18,... | collective-permute-start | bytes 884744 | tf_op jit(solution)/shard_map/ppermute | solution.py:667
  505.2 9.2 %collective-permute-start.56 = (bf16[2,96,768]{2,1,0:T(8,128)(2,1)S(1)}, bf16[2,96,768]{2,1,0:T(8,128)(2,1)S(1)}, u32[]{:S(2)}, u32[]{:S(2)}) collective-permute-start(bf16[2,96,768]{2,1,0:T(8,128)(2,1)S(1)} %dynamic-slice_bitcast_fusion.4), channel_id=1, source_target_pairs={{0,8},{2,10},{4,12},{6,14},{8,0},{10,2},{12,4},{14,6},{16,24},{18,... | collective-permute-start | bytes 884744 | tf_op jit(solution)/shard_map/ppermute | solution.py:667
  514.5 14.1 %collective-permute-start.51 = (bf16[96,768]{1,0:T(8,128)(2,1)S(1)}, bf16[96,768]{1,0:T(8,128)(2,1)S(1)}, u32[]{:S(2)}, u32[]{:S(2)}) collective-permute-start(bf16[96,768]{1,0:T(8,128)(2,1)S(1)} %dynamic-slice_bitcast_fusion.11), channel_id=1, source_target_pairs={{0,16},{2,18},{4,20},{6,22},{8,24},{10,26},{12,28},{14,30},{16,0},... | collective-permute-start | bytes 442376 | tf_op jit(solution)/shard_map/ppermute | solution.py:667
  516.1 11.7 %collective-permute-start.45 = (bf16[48,1536]{1,0:T(8,128)(2,1)S(1)}, bf16[48,1536]{1,0:T(8,128)(2,1)S(1)}, u32[]{:S(2)}, u32[]{:S(2)}) collective-permute-start(bf16[48,1536]{1,0:T(8,128)(2,1)S(1)} %dynamic-slice_bitcast_fusion.12), channel_id=1, source_target_pairs={{0,16},{2,18},{4,20},{6,22},{8,24},{10,26},{12,28},{14,30},{16,0},... | collective-permute-start | bytes 442376 | tf_op jit(solution)/shard_map/ppermute | solution.py:667
  527.9 7.8 %collective-permute-start.57 = (bf16[96,768]{1,0:T(8,128)(2,1)S(1)}, bf16[96,768]{1,0:T(8,128)(2,1)S(1)}, u32[]{:S(2)}, u32[]{:S(2)}) collective-permute-start(bf16[96,768]{1,0:T(8,128)(2,1)S(1)} %dynamic-slice_bitcast_fusion.10), channel_id=1, source_target_pairs={{0,16},{2,18},{4,20},{6,22},{8,24},{10,26},{12,28},{14,30},{16,0},... | collective-permute-start | bytes 442376 | tf_op jit(solution)/shard_map/ppermute | solution.py:667
  528.6 8.7 %collective-permute-start.20 = (bf16[2,48,3,384]{3,1,2,0:T(8,128)(2,1)S(1)}, bf16[2,48,3,384]{3,1,2,0:T(8,128)(2,1)S(1)}, u32[]{:S(2)}, u32[]{:S(2)}) collective-permute-start(bf16[2,48,3,384]{3,1,2,0:T(8,128)(2,1)S(1)} %dynamic-slice_bitcast_fusion.8), channel_id=1, source_target_pairs={{0,8},{2,10},{4,12},{6,14},{8,0},{10,2},{12,4},{14,6},{16,24},{18,... | collective-permute-start | bytes 663560 | tf_op jit(solution)/shard_map/ppermute | solution.py:667
  538.0 16.6 %collective-permute-start.21 = (bf16[48,3,384]{2,0,1:T(8,128)(2,1)}, bf16[48,3,384]{2,0,1:T(8,128)(2,1)}, u32[]{:S(2)}, u32[]{:S(2)}) collective-permute-start(bf16[48,3,384]{2,0,1:T(8,128)(2,1)} %dynamic-slice_bitcast_fusion.16), channel_id=1, source_target_pairs={{0,16},{2,18},{4,20},{6,22},{8,24},{10,26},{12,28},{14,30},{16,0},... | collective-permute-start | bytes 331784 | tf_op jit(solution)/shard_map/ppermute | solution.py:667
  539.4 16.1 %collective-permute-start.37 = (bf16[2,2,48,1536]{3,2,0,1:T(8,128)(2,1)}, bf16[2,2,48,1536]{3,2,0,1:T(8,128)(2,1)}, u32[]{:S(2)}, u32[]{:S(2)}) collective-permute-start(bf16[2,2,48,1536]{3,2,0,1:T(8,128)(2,1)} %dynamic-slice_bitcast_fusion.3), channel_id=1, source_target_pairs={{0,4},{2,6},{4,0},{6,2},{8,12},{10,14},{12,8},{14,10},{16,20},{18,... | collective-permute-start | bytes 1769480 | tf_op jit(solution)/shard_map/ppermute | solution.py:667
  553.4 13.1 %collective-permute-start.12 = (bf16[2,2,2,48,3,384]{5,3,4,2,1,0:T(8,128)(2,1)S(1)}, bf16[2,2,2,48,3,384]{5,3,4,2,1,0:T(8,128)(2,1)S(1)}, u32[]{:S(2)}, u32[]{:S(2)}) collective-permute-start(bf16[2,2,2,48,3,384]{5,3,4,2,1,0:T(8,128)(2,1)S(1)} %bitcast.227), channel_id=1, source_target_pairs={{0,2},{2,0},{4,6},{6,4},{8,10},{10,8},{12,14},{14,12},{16,18},{18,... | collective-permute-start | bytes 2654216 | tf_op jit(solution)/shard_map/ppermute | solution.py:667
  556.8 11.1 %collective-permute-start.38 = (bf16[2,48,1536]{2,1,0:T(8,128)(2,1)S(1)}, bf16[2,48,1536]{2,1,0:T(8,128)(2,1)S(1)}, u32[]{:S(2)}, u32[]{:S(2)}) collective-permute-start(bf16[2,48,1536]{2,1,0:T(8,128)(2,1)S(1)} %dynamic-slice_bitcast_fusion.7), channel_id=1, source_target_pairs={{0,8},{2,10},{4,12},{6,14},{8,0},{10,2},{12,4},{14,6},{16,24},{18,... | collective-permute-start | bytes 884744 | tf_op jit(solution)/shard_map/ppermute | solution.py:667
  566.8 8.4 %collective-permute-start.13 = (bf16[2,2,48,3,384]{4,2,3,1,0:T(8,128)(2,1)S(1)}, bf16[2,2,48,3,384]{4,2,3,1,0:T(8,128)(2,1)S(1)}, u32[]{:S(2)}, u32[]{:S(2)}) collective-permute-start(bf16[2,2,48,3,384]{4,2,3,1,0:T(8,128)(2,1)S(1)} %copy_bitcast_fusion.13), channel_id=1, source_target_pairs={{0,4},{2,6},{4,0},{6,2},{8,12},{10,14},{12,8},{14,10},{16,20},{18,... | collective-permute-start | bytes 1327112 | tf_op jit(solution)/shard_map/ppermute | solution.py:667
  575.3 6.0 collective-permute-start.14
  576.9 7.3 %collective-permute-start.39 = (bf16[48,1536]{1,0:T(8,128)(2,1)S(1)}, bf16[48,1536]{1,0:T(8,128)(2,1)S(1)}, u32[]{:S(2)}, u32[]{:S(2)}) collective-permute-start(bf16[48,1536]{1,0:T(8,128)(2,1)S(1)} %dynamic-slice_bitcast_fusion.13), channel_id=1, source_target_pairs={{0,16},{2,18},{4,20},{6,22},{8,24},{10,26},{12,28},{14,30},{16,0},... | collective-permute-start | bytes 442376 | tf_op jit(solution)/shard_map/ppermute | solution.py:667
  581.4 6.9 %collective-permute-start.15 = (bf16[48,3,384]{2,0,1:T(8,128)(2,1)S(1)}, bf16[48,3,384]{2,0,1:T(8,128)(2,1)S(1)}, u32[]{:S(2)}, u32[]{:S(2)}) collective-permute-start(bf16[48,3,384]{2,0,1:T(8,128)(2,1)S(1)} %dynamic-slice_bitcast_fusion.17), channel_id=1, source_target_pairs={{0,16},{2,18},{4,20},{6,22},{8,24},{10,26},{12,28},{14,30},{16,0},... | collective-permute-start | bytes 331784 | tf_op jit(solution)/shard_map/ppermute | solution.py:667
  592.3 50.7 %copy-start.11 = (bf16[1,96,768]{2,1,0:T(8,128)(2,1)S(1)}, bf16[1,96,768]{2,1,0:T(8,128)(2,1)}, u32[]{:S(2)}) copy-start(bf16[1,96,768]{2,1,0:T(8,128)(2,1)} %copy-done.10) | copy-start | bytes 442372
  592.3 50.7 %copy-start.13 = (bf16[1,96,768]{2,1,0:T(8,128)(2,1)S(1)}, bf16[1,96,768]{2,1,0:T(8,128)(2,1)}, u32[]{:S(2)}) copy-start(bf16[1,96,768]{2,1,0:T(8,128)(2,1)} %copy-done.12) | copy-start | bytes 442372
  592.4 50.7 %copy-start.22 = (f32[2,96,768]{2,1,0:T(8,128)S(1)}, f32[2,96,768]{2,1,0:T(8,128)}, u32[]{:S(2)}) copy-start(f32[2,96,768]{2,1,0:T(8,128)} %param.40) | copy-start | bytes 1769476
  592.4 50.7 %copy-start.23 = (f32[2,96,768]{2,1,0:T(8,128)S(1)}, f32[2,96,768]{2,1,0:T(8,128)}, u32[]{:S(2)}) copy-start(f32[2,96,768]{2,1,0:T(8,128)} %param.41) | copy-start | bytes 1769476
  592.4 50.7 %copy-start.24 = (f32[2,96,768]{2,1,0:T(8,128)S(1)}, f32[2,96,768]{2,1,0:T(8,128)}, u32[]{:S(2)}) copy-start(f32[2,96,768]{2,1,0:T(8,128)} %param.42) | copy-start | bytes 1769476
  (42 other events, 352.9 us)

commit v2 on v1

v2 whole, which is shorter than its diff:
```python
import functools
import math

import jax
import jax.numpy as jnp
from jax import lax
from jax.experimental import pallas as pl
from jax.experimental.pallas import tpu as pltpu
from jax.sharding import Mesh
from jax.sharding import PartitionSpec as P

HEAD = 64
LAYERS = 2
CHUNK = 256
FF_BLOCK = 768
VMEM = 64 * 1024 * 1024 - 128 * 1024
FOLD_WEIGHT = 1e12

EPS_NORM = 1e-05
CLIP = 1.0
BETA_ONE = 0.5
BETA_TWO = 0.5
ADAM_EPS = 1e-08
LR_MATRIX = 0.1
LR_NORMS = 0.5
DECAY_MATRIX = 0.1
STEP_NUMBER = 4.0

F32 = jnp.float32
BF16 = jnp.bfloat16


def run(
    kernel, args, in_specs, out_specs, out_shape, grid, name,
    scratch=(), after=(), aliases=None, weight=0,
):
    count, extra = len(args), len(after)

    def body(*refs):
        kernel(*refs[:count], *refs[count + extra :])

    return pl.pallas_call(
        body,
        grid=grid,
        in_specs=list(in_specs) + [pl.BlockSpec(memory_space=pl.ANY)] * extra,
        out_specs=out_specs,
        out_shape=out_shape,
        scratch_shapes=list(scratch),
        input_output_aliases=aliases or {},
        compiler_params=pltpu.CompilerParams(
            vmem_limit_bytes=VMEM, dimension_semantics=("arbitrary",) * len(grid)
        ),
        cost_estimate=pl.CostEstimate(
            flops=int(weight), bytes_accessed=int(weight), transcendentals=0
        ),
        name=name,
    )(*args, *after)


def dot(a, b):
    return jnp.dot(a, b, preferred_element_type=F32)


def dot_nt(a, b):
    return lax.dot_general(a, b, (((1,), (1,)), ((), ())), preferred_element_type=F32)


def dot_tn(a, b):
    return lax.dot_general(a, b, (((0,), (0,)), ((), ())), preferred_element_type=F32)


def low_lanes(rows):
    return lax.broadcasted_iota(jnp.int32, (rows, 128), 1) < HEAD


def shape(dims, dtype):
    return jax.ShapeDtypeStruct(dims, dtype)


IN_SMEM = pl.BlockSpec(memory_space=pltpu.SMEM)


def whole(array_shape):
    return pl.BlockSpec(array_shape, lambda *_: (0,) * len(array_shape))


def row_spec(rows, cols, index=lambda i: i):
    return pl.BlockSpec((rows, cols), lambda i: (index(i), 0))


def layer_spec(array, layer):
    rest = array.shape[1:]
    return pl.BlockSpec((None,) + rest, lambda *_: (layer,) + (0,) * len(rest))


def vext_of(v_pair):
    return jnp.concatenate([v_pair, jnp.ones_like(v_pair)], axis=1)


def project_kernel(x_ref, *refs):
    sides = (len(refs) - 3) // 4
    weights, (cos_ref, sin_ref) = refs[:sides], refs[sides : sides + 2]
    outs, kv_ref = refs[sides + 2 : -1], refs[-1]
    rows = x_ref.shape[0]
    x = x_ref[...]
    low = low_lanes(rows)
    cos, sin = cos_ref[...], sin_ref[...]
    first = pl.program_id(0) == 0

    def features(values, out_ref):
        for pair in range(values.shape[1] // 128):
            tile = jnp.maximum(values[:, pair * 128 : pair * 128 + 128], 0.0)
            along = tile * cos
            across = pltpu.roll(tile, HEAD, 1) * sin
            base = pair * 256
            out_ref[:, base : base + 128] = jnp.where(low, along, across).astype(BF16)
            out_ref[:, base + 128 : base + 256] = jnp.where(low, across, along).astype(BF16)

    for side in range(sides):
        w_ref = weights[side]
        q_ref, k_ref, v_ref = outs[3 * side : 3 * side + 3]
        other = sides - 1 - side
        v = dot(x, w_ref[2]).astype(BF16)
        v_ref[...] = v
        features(dot(x, w_ref[1]), k_ref)
        features(dot(x, w_ref[0]), q_ref)
        for pair in range(v.shape[1] // 128):
            both = dot_tn(
                k_ref[:, pair * 256 : pair * 256 + 256],
                vext_of(v[:, pair * 128 : pair * 128 + 128]),
            )
            for odd in (0, 1):
                part = both[odd * 128 : odd * 128 + 128]
                head = 2 * pair + odd
                kv_ref[other, head] = jnp.where(first, part, kv_ref[other, head] + part)


def project(x, weights, layer, cos, sin, after=()):
    rows, width = x.shape
    half = weights[0].shape[3]
    heads = half // HEAD
    block = rows // 2
    cat = row_spec(block, heads * 128)
    return run(
        project_kernel,
        (x, *weights, cos, sin),
        [row_spec(block, width)]
        + [layer_spec(w, layer) for w in weights]
        + [row_spec(block, 128)] * 2,
        [cat, cat, row_spec(block, half)] * len(weights)
        + [whole((len(weights), heads, 128, 256))],
        [
            shape((rows, heads * 128), BF16),
            shape((rows, heads * 128), BF16),
            shape((rows, half), BF16),
        ]
        * len(weights)
        + [shape((len(weights), heads, 128, 256), F32)],
        (rows // block,),
        "project",
        (),
        after,
    )


def norm_rows(r, gain, shift):
    mean = jnp.mean(r, axis=1, keepdims=True)
    centered = r - mean
    var = jnp.mean(centered * centered, axis=1, keepdims=True)
    rstd = lax.rsqrt(var + EPS_NORM)
    x_hat = centered * rstd
    return x_hat * gain + shift, x_hat, rstd


def attend_kernel(
    flag_ref, qo_ref, qp_ref, ko_ref, kp_ref, vo_ref, vp_ref, kvo_ref, kvp_ref, wo_ref, wp_ref,
    resid_ref, norm_ref,
    mo_ref, mp_ref, rden_ref, first_ref, low_ref, xhat_ref, rstd_ref, state_out_ref,
    state,
):
    rows = qo_ref.shape[0]
    half = vo_ref.shape[1]
    pairs = half // 128
    heads = 2 * pairs

    @pl.when(pl.program_id(0) == 0)
    def _():
        carry = flag_ref[0, 0]
        state[:heads] = kvo_ref[...] * carry
        state[heads:] = kvp_ref[...] * carry

    low = low_lanes(rows)
    row = lax.broadcasted_iota(jnp.int32, (rows, rows), 0)
    col = lax.broadcasted_iota(jnp.int32, (rows, rows), 1)
    causal = col <= row
    branch = None
    for side, (q_ref, k_ref, v_ref, m_ref, w_ref) in enumerate(
        ((qo_ref, ko_ref, vo_ref, mo_ref, wo_ref), (qp_ref, kp_ref, vp_ref, mp_ref, wp_ref))
    ):
        for pair in range(pairs):
            vext = vext_of(v_ref[:, pair * 128 : pair * 128 + 128])
            sums = []
            for head in (2 * pair, 2 * pair + 1):
                at = side * heads + head
                q = q_ref[:, head * 128 : head * 128 + 128]
                k = k_ref[:, head * 128 : head * 128 + 128]
                kv = state[at]
                kv_low = kv.astype(BF16)
                state_out_ref[0, at] = kv_low
                scores = jnp.where(causal, dot_nt(q, k), 0.0).astype(BF16)
                sums.append(
                    dot(
                        jnp.concatenate([scores, q], axis=1),
                        jnp.concatenate([vext, kv_low], axis=0),
                    )
                )
                state[at] = kv + dot_tn(k, vext)
            num = jnp.where(low, sums[0][:, :128], sums[1][:, :128])
            den = jnp.where(low, sums[0][:, 128:], sums[1][:, 128:])
            rden = 1.0 / jnp.maximum(den, 1.0)
            base = side * half + pair * 128
            rden_ref[:, base : base + 128] = rden
            m_ref[:, pair * 128 : pair * 128 + 128] = (num * rden).astype(BF16)
        part = dot(m_ref[...], w_ref[...])
        branch = part if branch is None else branch + part
    r = resid_ref[...].astype(F32) + branch
    y, x_hat, rstd = norm_rows(r, norm_ref[0:1], norm_ref[1:2])
    first_ref[...] = y
    low_ref[...] = y.astype(BF16)
    xhat_ref[...] = x_hat.astype(BF16)
    rstd_ref[...] = jnp.broadcast_to(rstd, rstd_ref.shape)


def attend(flag, own, peer, kv, kv_at, w_own, w_peer, layer, resid, norms, after=()):
    rows, width = resid.shape
    half = own[2].shape[1]
    heads = half // HEAD
    steps = rows // CHUNK
    cat, narrow = row_spec(CHUNK, heads * 128), row_spec(CHUNK, half)
    full = row_spec(CHUNK, width)
    return run(
        attend_kernel,
        (flag, own[0], peer[0], own[1], peer[1], own[2], peer[2], *kv,
         w_own, w_peer, resid, norms),
        [
            IN_SMEM,
            cat, cat, cat, cat, narrow, narrow,
            *(pl.BlockSpec((None,) + a.shape[1:], lambda *_, n=n: (n, 0, 0, 0)) for a, n in zip(kv, kv_at)),
            layer_spec(w_own, layer), layer_spec(w_peer, layer),
            full, layer_spec(norms, layer),
        ],
        [
            narrow, narrow, full, full, full, full, row_spec(CHUNK, 128),
            pl.BlockSpec((1, 2 * heads, 128, 256), lambda i: (i, 0, 0, 0)),
        ],
        [
            shape((rows, half), BF16),
            shape((rows, half), BF16),
            shape((rows, width), F32),
            shape((rows, width), F32),
            shape((rows, width), BF16),
            shape((rows, width), BF16),
            shape((rows, 128), F32),
            shape((steps, 2 * heads, 128, 256), BF16),
        ],
        (steps,),
        "attend",
        [pltpu.VMEM((2 * heads, 128, 256), F32)],
        after,
    )


def gelu_both(u):
    root = math.sqrt(2.0 / math.pi)
    a = root + (root * 0.044715) * (u * u)
    gate = 0.5 + 0.5 * jnp.tanh(u * a)
    act = u * gate
    return act, gate + (act - act * gate) * (6.0 * a - 4.0 * root)


def feed_kernel(
    x_ref, first_ref, wio_ref, wip_ref, wbo_ref, wbp_ref, norm_ref,
    ho_ref, hp_ref, slope_ref, out_ref, low_ref, xhat_ref, rstd_ref,
    acc,
):
    step, steps = pl.program_id(0), pl.num_programs(0)
    rows = x_ref.shape[0]

    def side(w_in, w_back, h_ref, base):
        for i in range(rows // CHUNK):
            at = slice(i * CHUNK, i * CHUNK + CHUNK)
            act, slope = gelu_both(dot(x_ref[at, :], w_in[...]))
            act = act.astype(BF16)
            h_ref[at, :] = act
            slope_ref[at, :] = slope.astype(BF16)
            acc[at, :] = base[at, :] + dot(act, w_back[...])

    @pl.when(step == 0)
    def _():
        side(wio_ref, wbo_ref, ho_ref, first_ref)

    @pl.when((step > 0) & (step < steps // 2))
    def _():
        side(wio_ref, wbo_ref, ho_ref, acc)

    @pl.when(step >= steps // 2)
    def _():
        side(wip_ref, wbp_ref, hp_ref, acc)

    @pl.when(step == steps - 1)
    def _():
        def part(i, _):
            at = pl.ds(pl.multiple_of(i * CHUNK, CHUNK), CHUNK)
            y, x_hat, rstd = norm_rows(acc[at, :], norm_ref[2:3], norm_ref[3:4])
            out_ref[at, :] = y
            low_ref[at, :] = y.astype(BF16)
            xhat_ref[at, :] = x_hat.astype(BF16)
            rstd_ref[at, :] = jnp.broadcast_to(rstd, (CHUNK, 128))
            return 0

        lax.fori_loop(0, rows // CHUNK, part, 0)


def ff_specs(layer, width, blocks):
    own = lambda j: jnp.minimum(j, blocks - 1)
    peer = lambda j: jnp.maximum(j - blocks, 0)
    w_in = [
        pl.BlockSpec((None, width, FF_BLOCK), lambda j, f=f: (layer, 0, f(j))) for f in (own, peer)
    ]
    w_back = [
        pl.BlockSpec((None, FF_BLOCK, width), lambda j, f=f: (layer, f(j), 0)) for f in (own, peer)
    ]
    return own, peer, w_in, w_back


def feed(x, first, wi_own, wi_peer, wb_own, wb_peer, layer, norms, last, after=()):
    rows, width = x.shape
    half = wi_own.shape[2]
    blocks = half // FF_BLOCK
    own, peer, w_in, w_back = ff_specs(layer, width, blocks)
    full = whole((rows, width))
    return run(
        feed_kernel,
        (x, first, wi_own, wi_peer, wb_own, wb_peer, norms),
        [full, full, *w_in, *w_back, layer_spec(norms, layer)],
        [
            pl.BlockSpec((rows, FF_BLOCK), lambda j: (0, own(j))),
            pl.BlockSpec((rows, FF_BLOCK), lambda j: (0, peer(j))),
            pl.BlockSpec((rows, FF_BLOCK), lambda j: (0, j)),
            full, full, full, whole((rows, 128)),
        ],
        [
            shape((rows, half), BF16),
            shape((rows, half), BF16),
            shape((rows, 2 * half), BF16),
            shape((rows, width), F32),
            shape((rows, width), BF16),
            shape((rows, width), BF16),
            shape((rows, 128), F32),
        ],
        (2 * blocks,),
        "feed",
        [pltpu.VMEM((rows, width), F32)],
        after,
    )


def norm_back(y, x_hat, rstd, gain):
    scaled = y * gain
    mean = jnp.mean(scaled, axis=1, keepdims=True)
    along = jnp.mean(scaled * x_hat, axis=1, keepdims=True)
    gain_grad = jnp.sum(y * x_hat, axis=0, keepdims=True)
    shift_grad = jnp.sum(y, axis=0, keepdims=True)
    return (scaled - mean - x_hat * along) * rstd, gain_grad, shift_grad


def feed_back_kernel(
    up_ref, live_ref, xh2_ref, rs2_ref, xh1_ref, rs1_ref, slope_ref,
    wio_ref, wip_ref, wbo_ref, wbp_ref, norm_ref,
    gfb_ref, gho_ref, ghp_ref, first_ref, ng_ref,
    acc,
):
    step, steps = pl.program_id(0), pl.num_programs(0)
    rows, width = up_ref.shape
    tiles = width // 128

    def chunk(i):
        return pl.ds(pl.multiple_of(i * CHUNK, CHUNK), CHUNK)

    def wide(ref, at):
        return jnp.concatenate([ref[at, :]] * tiles, axis=1)

    @pl.when(step == 0)
    def _():
        ng_ref[...] = jnp.zeros_like(ng_ref)

        def part(i, _):
            at = chunk(i)
            y = up_ref[at, :]
            if live_ref is not None:
                y = y * wide(live_ref, at)
            grad, gain_grad, shift_grad = norm_back(
                y, xh2_ref[at, :].astype(F32), wide(rs2_ref, at), norm_ref[2:3]
            )
            acc[at, :] = grad
            gfb_ref[0, at, :] = grad.astype(BF16)
            ng_ref[2:3] += gain_grad
            ng_ref[3:4] += shift_grad
            return 0

        lax.fori_loop(0, rows // CHUNK, part, 0)

    def side(w_in, w_back, gh_ref):
        for i in range(rows // CHUNK):
            at = slice(i * CHUNK, i * CHUNK + CHUNK)
            act = dot_nt(gfb_ref[0, at, :], w_back[...])
            gh = (act * slope_ref[at, :].astype(F32)).astype(BF16)
            gh_ref[at, :] = gh
            acc[at, :] += dot_nt(gh, w_in[...])

    @pl.when(step < steps // 2)
    def _():
        side(wio_ref, wbo_ref, gho_ref)

    @pl.when(step >= steps // 2)
    def _():
        side(wip_ref, wbp_ref, ghp_ref)

    @pl.when(step == steps - 1)
    def _():
        def part(i, _):
            at = chunk(i)
            grad, gain_grad, shift_grad = norm_back(
                acc[at, :], xh1_ref[at, :].astype(F32), wide(rs1_ref, at), norm_ref[0:1]
            )
            first_ref[at, :] = grad
            gfb_ref[1, at, :] = grad.astype(BF16)
            ng_ref[0:1] += gain_grad
            ng_ref[1:2] += shift_grad
            return 0

        lax.fori_loop(0, rows // CHUNK, part, 0)


def feed_back(
    up, live, xh2, rs2, xh1, rs1, slope, wi_own, wi_peer, wb_own, wb_peer, layer, norms, after=()
):
    rows, width = up.shape
    half = wi_own.shape[2]
    blocks = half // FF_BLOCK
    own, peer, w_in, w_back = ff_specs(layer, width, blocks)
    full, thin = whole((rows, width)), whole((rows, 128))
    if live is None:

        def kernel(up_ref, *refs):
            feed_back_kernel(up_ref, None, *refs)

        args, specs = (up,), [full]
    else:
        kernel, args, specs = feed_back_kernel, (up, live), [full, thin]
    return run(
        kernel,
        args + (xh2, rs2, xh1, rs1, slope, wi_own, wi_peer, wb_own, wb_peer, norms),
        specs
        + [
            full, thin, full, thin,
            pl.BlockSpec((rows, FF_BLOCK), lambda j: (0, j)),
            *w_in, *w_back, layer_spec(norms, layer),
        ],
        [
            whole((2, rows, width)),
            pl.BlockSpec((rows, FF_BLOCK), lambda j: (0, own(j))),
            pl.BlockSpec((rows, FF_BLOCK), lambda j: (0, peer(j))),
            full, whole((4, width)),
        ],
        [
            shape((2, rows, width), BF16),
            shape((rows, half), BF16),
            shape((rows, half), BF16),
            shape((rows, width), F32),
            shape((4, width), F32),
        ],
        (2 * blocks,),
        "feed_back",
        [pltpu.VMEM((rows, width), F32)],
        after,
    )


def mix_back_kernel(
    gfb_ref, wo_ref, wp_ref, rden_ref, mo_ref, mp_ref, qo_ref, qp_ref, gx_ref, dkv_ref
):
    rows = gfb_ref.shape[0]
    half = mo_ref.shape[1]
    pairs = half // 128
    first = pl.program_id(0) == 0
    wide_low = jnp.concatenate([low_lanes(rows)] * 2, axis=1)
    r = lax.broadcasted_iota(jnp.int32, (256, 128), 0) % 128
    c = lax.broadcasted_iota(jnp.int32, (256, 128), 1)
    spread_c = jnp.where((r < HEAD) == (c < HEAD), -1.0 / HEAD, 0.0).astype(BF16)
    gb = gfb_ref[...]
    for side, (w_ref, m_ref, q_ref) in enumerate(
        ((wo_ref, mo_ref, qo_ref), (wp_ref, mp_ref, qp_ref))
    ):
        gm = dot_nt(gb, w_ref[...])
        for pair in range(pairs):
            base = side * half + pair * 128
            rden = rden_ref[:, base : base + 128]
            g = gm[:, pair * 128 : pair * 128 + 128] * rden
            m = m_ref[:, pair * 128 : pair * 128 + 128].astype(F32)
            prod = jnp.where(rden < 1.0, g * m, 0.0)
            high = prod.astype(BF16)
            rest = (prod - high.astype(F32)).astype(BF16)
            minus_c = dot(jnp.concatenate([high, rest], axis=1), spread_c).astype(BF16)
            gx = jnp.concatenate([g.astype(BF16), minus_c], axis=1)
            gx_ref[:, 2 * base : 2 * base + 256] = gx
            for odd in (0, 1):
                at = side * 2 * pairs + 2 * pair + odd
                part = dot_tn(
                    q_ref[:, (2 * pair + odd) * 128 : (2 * pair + odd) * 128 + 128],
                    own_lanes(gx, wide_low, odd),
                )
                dkv_ref[at] = jnp.where(first, part, dkv_ref[at] + part)


def own_lanes(gx, wide_low, odd):
    zero = jnp.zeros_like(gx)
    return jnp.where(wide_low, zero, gx) if odd else jnp.where(wide_low, gx, zero)


def mix_back(gfb, w_own, w_peer, layer, rden, m_own, m_peer, q_own, q_peer, after=()):
    _, rows, width = gfb.shape
    half = m_own.shape[1]
    heads = half // HEAD
    full, narrow, cat = (row_spec(CHUNK, n) for n in (width, half, heads * 128))
    return run(
        mix_back_kernel,
        (gfb, w_own, w_peer, rden, m_own, m_peer, q_own, q_peer),
        [
            pl.BlockSpec((None, CHUNK, width), lambda i: (1, i, 0)),
            layer_spec(w_own, layer), layer_spec(w_peer, layer),
            full, narrow, narrow, cat, cat,
        ],
        [row_spec(CHUNK, 2 * width), whole((2 * heads, 128, 256))],
        [
            shape((rows, 2 * width), BF16),
            shape((2 * heads, 128, 256), F32),
        ],
        (rows // CHUNK,),
        "mix_back",
        (),
        after,
    )


def attend_back_kernel(
    flag_ref, qo_ref, qp_ref, ko_ref, kp_ref, vo_ref, vp_ref, gx_ref, state_ref, dkv_ref,
    cos_ref, sin_ref,
    go_ref, gp_ref,
    dstate,
):
    rows = qo_ref.shape[0]
    half = vo_ref.shape[1]
    pairs = half // 128
    heads = 2 * pairs

    @pl.when(pl.program_id(0) == 0)
    def _():
        carry = flag_ref[0, 0]
        dstate[:heads] = dkv_ref[heads:] * carry
        dstate[heads:] = dkv_ref[:heads] * carry

    low = low_lanes(rows)
    wide_low = jnp.concatenate([low, low], axis=1)
    row = lax.broadcasted_iota(jnp.int32, (rows, rows), 0)
    col = lax.broadcasted_iota(jnp.int32, (rows, rows), 1)
    causal, anti = col <= row, row <= col
    cos, sin = cos_ref[...], sin_ref[...]
    trig_even = jnp.where(low, cos, sin)
    trig_odd = jnp.where(low, sin, cos)
    for side, (q_ref, k_ref, v_ref, out_ref) in enumerate(
        ((qo_ref, ko_ref, vo_ref, go_ref), (qp_ref, kp_ref, vp_ref, gp_ref))
    ):
        for pair in range(pairs):
            vext = vext_of(v_ref[:, pair * 128 : pair * 128 + 128])
            wide = 2 * (side * half + pair * 128)
            gx = gx_ref[:, wide : wide + 256]
            dq, dk, left, right = [], [], [], []
            for odd in (0, 1):
                head = 2 * pair + odd
                at = side * heads + head
                trig = trig_odd if odd else trig_even
                q = q_ref[:, head * 128 : head * 128 + 128]
                k = k_ref[:, head * 128 : head * 128 + 128]
                gext = own_lanes(gx, wide_low, odd)
                back = dstate[at]
                back_low = back.astype(BF16)
                score_t = jnp.where(anti, dot_nt(k, q), 0.0).astype(BF16)
                ds = jnp.where(causal, dot_nt(gext, vext), 0.0).astype(BF16)
                q_grad = (dot(ds, k) + dot_nt(gext, state_ref[0, at])) * trig
                k_grad = (dot_tn(ds, q) + dot_nt(vext, back_low)) * trig
                left += [score_t, k]
                right += [gext[:, :128], back_low[:, :128]]
                dstate[at] = back + dot_tn(q, gext)
                q_grad = q_grad + pltpu.roll(q_grad, HEAD, 1)
                k_grad = k_grad + pltpu.roll(k_grad, HEAD, 1)
                dq.append(jnp.where(q > 0, q_grad, 0.0))
                dk.append(jnp.where(k > 0, k_grad, 0.0))
            dv = dot(jnp.concatenate(left, axis=1), jnp.concatenate(right, axis=0))
            for kind, value in enumerate(
                (jnp.where(low, dq[0], dq[1]), jnp.where(low, dk[0], dk[1]), dv)
            ):
                base = kind * half + pair * 128
                out_ref[:, base : base + 128] = value.astype(BF16)


def attend_back(flag, own, peer, gx, states, dkv, cos, sin, after=()):
    rows = cos.shape[0]
    half = own[2].shape[1]
    heads = half // HEAD
    steps = rows // CHUNK
    back = lambda i: steps - 1 - i
    cat, narrow, trig = (row_spec(CHUNK, n, back) for n in (heads * 128, half, 128))
    return run(
        attend_back_kernel,
        (flag, own[0], peer[0], own[1], peer[1], own[2], peer[2], gx, states, dkv, cos, sin),
        [
            IN_SMEM,
            cat, cat, cat, cat, narrow, narrow,
            row_spec(CHUNK, heads * 256, back),
            pl.BlockSpec((1, 2 * heads, 128, 256), lambda i: (back(i), 0, 0, 0)),
            whole(dkv.shape), trig, trig,
        ],
        [row_spec(CHUNK, 3 * half, back)] * 2,
        [shape((rows, 3 * half), BF16)] * 2,
        (steps,),
        "attend_back",
        [pltpu.VMEM((2 * heads, 128, 256), F32)],
        after,
    )


def input_back_kernel(go_ref, gp_ref, wo_ref, wp_ref, first_ref, out_ref):
    half = wo_ref.shape[2]
    total = first_ref[...]
    for g_ref, w_ref in ((go_ref, wo_ref), (gp_ref, wp_ref)):
        for kind in range(3):
            total = total + dot_nt(g_ref[:, kind * half : kind * half + half], w_ref[kind])
    out_ref[...] = total


def input_back(g_own, g_peer, w_own, w_peer, layer, first, after=()):
    rows, width = first.shape
    block = rows // 2
    third, full = row_spec(block, g_own.shape[1]), row_spec(block, width)
    return run(
        input_back_kernel,
        (g_own, g_peer, w_own, w_peer, first),
        [third, third, layer_spec(w_own, layer), layer_spec(w_peer, layer), full],
        full,
        shape((rows, width), F32),
        (rows // block,),
        "input_back",
        (),
        after,
    )


def weight_kernel(a_ref, b_ref, c_ref, d_ref, out_ref):
    out_ref[...] = (dot_tn(a_ref[...], b_ref[...]) + dot_tn(c_ref[...], d_ref[...])).astype(
        out_ref.dtype
    )


def weight_grad(a, b, c, d, block_m, block_n, name):
    rows, m = a.shape
    n = b.shape[1]
    left = pl.BlockSpec((rows, block_m), lambda i, j: (0, i))
    right = pl.BlockSpec((rows, block_n), lambda i, j: (0, j))
    return run(
        weight_kernel,
        (a, b, c, d),
        [left, right, left, right],
        pl.BlockSpec((block_m, block_n), lambda i, j: (i, j)),
        shape((m, n), BF16),
        (m // block_m, n // block_n),
        name,
    )


FF_ROWS = 224
Q_ROWS = 144


def blocks_of(index_ref, scr, rows, z_local, x_first, other, kept):
    x, y = index_ref[0, 0], index_ref[0, 1]
    if x_first:
        spot = other * 2 + (x if kept else 1 - x)
    else:
        spot = (y if kept else 1 - y) * 2 + other
    start = pl.multiple_of((z_local * 4 + spot) * rows, 8)
    return scr[pl.ds(start, rows), :]


def back_pack_kernel(index_ref, a_ref, b_ref, c_ref, d_ref, ka, sa, kb, sb, scr):
    rows = scr.shape[0] // 4
    scr[...] = dot_tn(a_ref[...], b_ref[...]) + dot_tn(c_ref[...], d_ref[...])
    z = pl.program_id(0)
    for x_first, (keep, send) in ((True, (ka, sa)), (False, (kb, sb))):

        @pl.when((z < 2) == x_first)
        def _():
            for other in range(2):
                for kept, out in ((True, keep), (False, send)):
                    out[0, other] = blocks_of(
                        index_ref, scr, rows, 0, x_first, other, kept
                    ).astype(BF16)


def half_spec(array, at):
    return pl.BlockSpec((None,) + array.shape[1:], lambda *_: (at, 0, 0))


def back_pack(index, a, b, c, d, after=()):
    rows, m = a.shape
    n = b.shape[2]
    block = m // 4
    left = pl.BlockSpec((rows, block), lambda z: (0, z))
    buffer = shape((2, 2, FF_ROWS, n), BF16)
    low = pl.BlockSpec((1, 2, block // 4, n), lambda z: (jnp.minimum(z, 1), 0, 0, 0))
    high = pl.BlockSpec((1, 2, block // 4, n), lambda z: (jnp.maximum(z - 2, 0), 0, 0, 0))
    return run(
        back_pack_kernel,
        (index, a, b, c, d),
        [IN_SMEM, left, half_spec(b, 0), left, half_spec(d, 0)],
        [low, low, high, high],
        [buffer] * 4,
        (4,),
        "back_grad",
        [pltpu.VMEM((block, n), F32)],
        after,
    )


def spread(index_ref, scr, rows, outs, tail=None):
    ka, sa, kb, sb = outs
    for x_first, keep, send in ((True, ka, sa), (False, kb, sb)):
        for z in range(2):
            z_local = z if x_first else z + 2
            for other in range(2):
                for kept, out in ((True, keep), (False, send)):
                    value = blocks_of(index_ref, scr, rows, z_local, x_first, other, kept)
                    if tail is not None:
                        x, y = index_ref[0, 0], index_ref[0, 1]
                        if x_first:
                            w = z_local * 4 + other * 2 + (x if kept else 1 - x)
                        else:
                            w = z_local * 4 + (y if kept else 1 - y) * 2 + other
                        value = jnp.concatenate([value, tail(w)], axis=0)
                    out[z, other] = value.astype(BF16)


def in_pack_kernel(index_ref, a_ref, b_ref, c_ref, d_ref, _ka, _sa, _kb, _sb, ka, sa, kb, sb, scr):
    scr[...] = dot_tn(a_ref[...], b_ref[...]) + dot_tn(c_ref[...], d_ref[...])
    spread(index_ref, scr, scr.shape[0] // 16, (ka, sa, kb, sb))


def column_pack(index, a, b, c, d, buffers, block_n, block_rows, first_block, name, after=()):
    rows, m = a.shape
    n = b.shape[1]
    right = pl.BlockSpec((rows, block_n), lambda j: (0, j))
    out = pl.BlockSpec((2, 2, m // 16, block_n), lambda j: (0, 0, first_block + j, 0))
    specs = [IN_SMEM, whole(a.shape), right, whole(c.shape), right]
    scratch = [pltpu.VMEM((m, block_n), F32)]
    if buffers is None:

        def fresh(index_ref, a_ref, b_ref, c_ref, d_ref, *outs):
            in_pack_kernel(index_ref, a_ref, b_ref, c_ref, d_ref, *([None] * 4), *outs)

        return run(
            fresh, (index, a, b, c, d), specs, [out] * 4,
            [shape((2, 2, block_rows, block_n), BF16)] * 4, (n // block_n,), name, scratch, after,
        )
    return run(
        in_pack_kernel,
        (index, a, b, c, d, *buffers),
        specs + [pl.BlockSpec(memory_space=pl.ANY)] * 4,
        [out] * 4,
        [shape(buffer.shape, BF16) for buffer in buffers],
        (n // block_n,),
        name,
        scratch,
        after,
        {5 + i: i for i in range(4)},
    )


def out_pack_kernel(
    index_ref, a_ref, b_ref, c_ref, d_ref, norm_ref, _ka, _sa, _kb, _sb, ka, sa, kb, sb, scr
):
    scr[...] = dot_tn(a_ref[...], b_ref[...]) + dot_tn(c_ref[...], d_ref[...])
    blank = jnp.zeros((8, scr.shape[1] - 128), F32)
    spread(
        index_ref, scr, scr.shape[0] // 16, (ka, sa, kb, sb),
        lambda w: jnp.concatenate([norm_ref[w], blank], axis=1),
    )


def out_pack(index, a, b, c, d, norms, buffers, after=()):
    m, n = a.shape[1], b.shape[2]
    block = m // 16 + 8
    out = pl.BlockSpec((2, 2, block, n), lambda j: (0, 0, (FF_ROWS - block) // block, 0))
    return run(
        out_pack_kernel,
        (index, a, b, c, d, norms, *buffers),
        [IN_SMEM, whole(a.shape), half_spec(b, 1), whole(c.shape), half_spec(d, 1)]
        + [whole(norms.shape)]
        + [pl.BlockSpec(memory_space=pl.ANY)] * 4,
        [out] * 4,
        [shape(buffer.shape, BF16) for buffer in buffers],
        (1,),
        "out_grad",
        [pltpu.VMEM((m, n), F32)],
        after,
        {6 + i: i for i in range(4)},
    )


def swap(values, axis="narrow"):
    return lax.ppermute(values, axis, [(0, 1), (1, 0)])


def sum_of(a_ref, b_ref, *at):
    return (a_ref[at].astype(F32) + b_ref[at].astype(F32)).astype(BF16)


def fold_split_kernel(index_ref, ka, ga, kb, gb, ka_out, sa_out, kb_out, sb_out):
    x, y = index_ref[0, 0], index_ref[0, 1]
    ka_out[0] = sum_of(ka, ga, 0, y)
    sa_out[0] = sum_of(ka, ga, 0, 1 - y)
    kb_out[0] = sum_of(kb, gb, 0, x)
    sb_out[0] = sum_of(kb, gb, 0, 1 - x)


def fold_split(index, ka, ga, kb, gb, after=()):
    _, _, r, c = ka.shape
    return run(
        fold_split_kernel,
        (index, ka, ga, kb, gb),
        [IN_SMEM]
        + [pl.BlockSpec((1, 2, r, c), lambda z: (z, 0, 0, 0))] * 4,
        [pl.BlockSpec((1, r, c), lambda z: (z, 0, 0))] * 4,
        [shape((2, r, c), BF16)] * 4,
        (2,),
        "fold_split",
        (),
        after,
        weight=FOLD_WEIGHT,
    )


def fold_join_kernel(ka, ga, kb, gb, out):
    out[0, 0] = sum_of(ka, ga, 0)
    out[1, 0] = sum_of(kb, gb, 0)


def fold_join(ka, ga, kb, gb, after=()):
    _, r, c = ka.shape
    return run(
        fold_join_kernel,
        (ka, ga, kb, gb),
        [pl.BlockSpec((1, r, c), lambda z: (z, 0, 0))] * 4,
        pl.BlockSpec((2, 1, r, c), lambda z: (0, z, 0, 0)),
        shape((2, 2, r, c), BF16),
        (2,),
        "fold_join",
        (),
        after,
        weight=FOLD_WEIGHT,
    )


def fold_near_kernel(index_ref, ka, ga, kb, gb, keep, send):
    z = index_ref[0, 2]
    for half, (k, g) in enumerate(((ka, ga), (kb, gb))):
        keep[half] = sum_of(k, g, z)
        send[half] = sum_of(k, g, 1 - z)


def fold_near(index, ka, ga, kb, gb, after=()):
    return run(
        fold_near_kernel,
        (index, ka, ga, kb, gb),
        [IN_SMEM] + [whole(ka.shape)] * 4,
        [whole(ka.shape)] * 2,
        [shape(ka.shape, BF16)] * 2,
        (1,),
        "fold_near",
        (),
        after,
        weight=FOLD_WEIGHT,
    )


def fold_far_kernel(index_ref, k, g, keep, send):
    z = index_ref[0, 3]
    keep[...] = sum_of(k, g, z)
    send[...] = sum_of(k, g, 1 - z)


def fold_far(index, keep, got):
    return run(
        fold_far_kernel,
        (index, keep, got),
        [IN_SMEM] + [whole(keep.shape)] * 2,
        [whole(keep.shape[1:])] * 2,
        [shape(keep.shape[1:], BF16)] * 2,
        (1,),
        "fold_far",
    )


def shuffle(values, axis, bit):
    return lax.ppermute(values, axis, [(i, i ^ bit) for i in range(lax.axis_size(axis))])


def adamw(master, first, second, gradient, factor, step_rate, decay_rate):
    fix_one = 1.0 - BETA_ONE**STEP_NUMBER
    fix_two = 1.0 - BETA_TWO**STEP_NUMBER
    clipped = gradient * factor
    first = BETA_ONE * first + (1.0 - BETA_ONE) * clipped
    second = BETA_TWO * second + (1.0 - BETA_TWO) * clipped * clipped
    update = first / fix_one / (jnp.sqrt(second / fix_two) + ADAM_EPS)
    master = master - step_rate * (update + decay_rate * master)
    return (master, first, second)


def row_tables(lengths, rows):
    index = lax.axis_index("narrow") * rows + jnp.arange(rows, dtype=jnp.int32)
    first_len, second_len = lengths[0], lengths[1]
    in_first = index < first_len
    in_second = (index >= first_len) & (index < first_len + second_len)
    live = (in_first | in_second).astype(F32)
    position = jnp.where(in_second, index - first_len, index)
    span = jnp.where(in_first, first_len, jnp.where(in_second, second_len, 1))
    angle = 0.5 * math.pi * position.astype(F32) / span.astype(F32)
    cos = (jnp.cos(angle) * live)[:, None]
    sin = (jnp.sin(angle) * live)[:, None]
    goes_on = (first_len > rows).astype(F32).reshape(1, 1)
    second = lax.axis_index("narrow").astype(F32)
    return (
        jnp.broadcast_to(cos, (rows, 128)),
        jnp.broadcast_to(sin, (rows, 128)),
        jnp.broadcast_to(live[:, None], (rows, 128)),
        goes_on * second,
        goes_on * (1.0 - second),
    )


def shards(
    stream, seq_lengths, cotangent, w_qkv, w_out, w_in, w_back, norm_params,
    qkv_master, qkv_first, qkv_second, out_master, out_first, out_second,
    in_master, in_first, in_second, back_master, back_first, back_second,
    norm_master, norm_first, norm_second,
    wide_axes,
):
    rows, width = stream.shape
    half = w_qkv.shape[3]
    heads = half // HEAD
    every = wide_axes + ("narrow",)
    wide = math.prod(lax.axis_size(axis) for axis in wide_axes)
    by_axes = len(wide_axes) == 3
    cos, sin, live, takes, gives = row_tables(seq_lengths[0], rows)
    if by_axes:
        z, y, x = (lax.axis_index(axis) for axis in wide_axes)
        index = jnp.stack([x, y, z % 2, z // 2]).astype(jnp.int32).reshape(1, 4)

    qkv = jnp.transpose(w_qkv, (0, 2, 1, 3))
    qkv_peer = swap(qkv)
    out_peer, in_peer, back_peer = swap(w_out), swap(w_in), swap(w_back)

    low = stream
    current = stream
    kept = []
    got = [None] * LAYERS
    for layer in range(LAYERS):
        before = () if layer == 0 else got[layer - 1][1:3]
        if layer == 0:
            *own, kv_own = project(low, (qkv,), layer, cos, sin)
            *peer, kv_peer = project(low, (qkv_peer,), layer, cos, sin)
            kv, kv_at = (swap(kv_peer), swap(kv_own)), (0, 0)
        else:
            *parts, kv = project(low, (qkv, qkv_peer), layer, cos, sin, before)
            own, peer = parts[:3], parts[3:]
            kv, kv_at = (swap(kv),) * 2, (0, 1)
        low_got = swap(low)
        before = () if layer == 0 else (got[layer - 1][0], got[layer - 1][3])
        m_own, m_peer, rden, first, ffn_in, xh1, rs1, states = attend(
            takes, own, peer, kv, kv_at, w_out, out_peer, layer, current, norm_params, before
        )
        last = layer == LAYERS - 1
        h_own, h_peer, slope, out, out_low, xh2, rs2 = feed(
            ffn_in, first, w_in, in_peer, w_back, back_peer, layer, norm_params, last,
            (low_got,) if last else (),
        )
        got[layer] = (low_got, swap(m_peer), swap(ffn_in), swap(h_peer))
        kept.append(
            (low, own, peer, m_own, m_peer, rden, ffn_in, xh1, rs1, states, h_own, slope, xh2, rs2)
        )
        current, low = out, out_low

    up = cotangent
    norm_grads = [None] * LAYERS
    shares = [None] * LAYERS
    scatter_z = lambda joined: lax.psum_scatter(joined.reshape((4,) + joined.shape[2:]), "z")
    after = got[LAYERS - 1][1:3]
    for layer in reversed(range(LAYERS)):
        (low, own, peer, m_own, m_peer, rden, ffn_in, xh1, rs1, states, h_own, slope, xh2, rs2) = (
            kept[layer]
        )
        low_got, m_got, ffn_got, h_got = got[layer]
        last = layer == 0
        gfb, gh_own, gh_peer, grad_first, norm_grads[layer] = feed_back(
            up, None if last else live, xh2, rs2, xh1, rs1, slope, w_in, in_peer, w_back, back_peer,
            layer, norm_params, after,
        )
        gfb_got, gh_got = swap(gfb), swap(gh_peer)
        after = ()
        if last and by_axes:
            share_ff = fold_join(*ff_second, (gfb,))
            share_ff = scatter_z(share_ff)
            ka, sa, kb, sb = fold_split(index, *q_first, (gfb,))
            q_second = (ka, swap(sa, "y"), kb, swap(sb, "x"))
            after = (ka,)
        gx, dkv = mix_back(
            gfb, w_out, out_peer, layer, rden, m_own, m_peer, own[0], peer[0], after
        )
        dkv_got = swap(dkv)
        norm_sum = jnp.stack(norm_grads) if last else None
        if not by_axes:
            back_grad = weight_grad(h_own, gfb[0], h_got, gfb_got[0], 512, width, "back_grad")
            in_grad = weight_grad(ffn_in, gh_own, ffn_got, gh_got, width, 512, "in_grad")
            out_grad = weight_grad(m_own, gfb[1], m_got, gfb_got[1], half, width, "out_grad")
            g_own, g_peer = attend_back(gives, own, peer, gx, states, dkv_got, cos, sin)
            up = input_back(g_own, g_peer, qkv, qkv_peer, layer, grad_first)
            qkv_grad = weight_grad(low, g_own, low_got, swap(g_peer), width, half, "qkv_grad")
            shares[layer] = [
                lax.psum_scatter(g, wide_axes, scatter_dimension=0, tiled=True).astype(F32)
                for g in (qkv_grad, out_grad, in_grad, back_grad)
            ]
            shares[layer][0] = shares[layer][0].reshape(-1, 3, half)
            after = ()
            continue
        if last:
            pair = norm_sum.reshape(8, width)
            pair = pair + swap(pair)
            pair = jnp.transpose(pair.reshape(8, wide, width // wide), (1, 0, 2))
            pair = jnp.pad(pair, ((0, 0), (0, 0), (0, 128 - width // wide)))
        else:
            pair = jnp.zeros((wide, 8, 128), F32)
        buffers = back_pack(index, h_own, gfb, h_got, gfb_got, (gx,))
        buffers = column_pack(
            index, ffn_in, gh_own, ffn_got, gh_got, buffers, width, FF_ROWS, 2, "in_grad"
        )
        after = ()
        if last:
            joined = fold_join(*q_second, (buffers[0],))
            share_q = scatter_z(joined)
            after = (joined,)
        ka, sa, kb, sb = out_pack(index, m_own, gfb, m_got, gfb_got, pair, buffers, after)
        ff_first = (ka, swap(sa, "x"), kb, swap(sb, "y"))
        g_own, g_peer = attend_back(gives, own, peer, gx, states, dkv_got, cos, sin, (ka,))
        g_got = swap(g_peer)
        up = input_back(g_own, g_peer, qkv, qkv_peer, layer, grad_first)
        ka, sa, kb, sb = fold_split(index, *ff_first, (up,))
        ff_second = (ka, swap(sa, "y"), kb, swap(sb, "x"))
        q_ka, q_sa, q_kb, q_sb = column_pack(
            index, low, g_own, low_got, g_got, None, half, Q_ROWS, 0, "qkv_grad", (ka,)
        )
        q_first = (q_ka, swap(q_sa, "x"), q_kb, swap(q_sb, "y"))
        after = (q_ka,)
        if not last:
            continue
        joined = fold_join(*ff_second, (q_ka,))
        share_ff0 = scatter_z(joined)
        ka, sa, kb, sb = fold_split(index, *q_first, (joined,))
        keep, send = fold_near(index, ka, swap(sa, "y"), kb, swap(sb, "x"))
        keep, send = fold_far(index, keep, shuffle(send, "z", 1))
        share_q0 = keep.astype(F32) + shuffle(send, "z", 2).astype(F32)
        for at, ff, q in ((0, share_ff0, share_q0), (1, share_ff, share_q)):
            ff, q = ff.astype(F32), q.astype(F32)
            rows_in = width // wide
            shares[at] = [
                jnp.transpose(q.reshape(3, rows_in, half), (1, 0, 2)),
                ff[192:216],
                jnp.concatenate([ff[96:144], ff[144:192]], axis=1),
                ff[:96],
            ]

    stacked = [jnp.stack([shares[l][kind] for l in range(LAYERS)]) for kind in range(4)]
    if by_axes:
        part = width // wide // 2
        norm_reduced = lax.dynamic_slice_in_dim(
            share_ff0[216:224].astype(F32), lax.axis_index("narrow") * part, part, 1
        ).reshape(LAYERS, 4, part)
    else:
        norm_reduced = lax.psum_scatter(norm_sum, every, scatter_dimension=2, tiled=True)
    squares = sum(jnp.sum(g * g) for g in stacked + [norm_reduced])
    count = wide * lax.axis_size("narrow")
    squares = lax.all_to_all(
        jnp.broadcast_to(squares, (count, 128)), every, 0, 0, tiled=True
    ).sum(0)[:1]
    clip_norm = jnp.sqrt(squares)
    factor = jnp.minimum(1.0, CLIP / clip_norm[0])
    matrix = lambda m, f, s, g: adamw(m, f, s, g, factor, LR_MATRIX, DECAY_MATRIX)
    qkv_new = matrix(qkv_master, qkv_first, qkv_second, stacked[0])
    out_new = matrix(out_master, out_first, out_second, stacked[1])
    in_new = matrix(in_master, in_first, in_second, stacked[2])
    back_new = matrix(back_master, back_first, back_second, stacked[3])
    norm_new = adamw(norm_master, norm_first, norm_second, norm_reduced, factor, LR_NORMS, 0.0)
    return (current, up, *qkv_new, *out_new, *in_new, *back_new, *norm_new, clip_norm)


def solution(mesh):
    wide_axes = ("wide",)
    if mesh.shape["wide"] == 16:
        wide_axes = ("z", "y", "x")
        mesh = Mesh(mesh.devices.reshape(4, 2, 2, 2), wide_axes + ("narrow",))
    rows = P(wide_axes + ("narrow",), None)
    qkv = P(None, wide_axes, None, "narrow")
    deep = P(None, ("narrow",) + wide_axes, None)
    in_part = P(None, wide_axes, "narrow")
    norm = P(None, None, wide_axes + ("narrow",))
    states = (qkv,) * 3 + (deep,) * 3 + (in_part,) * 3 + (deep,) * 3 + (norm,) * 3
    in_specs = (
        rows, P(wide_axes, None), rows,
        P(None, None, None, "narrow"), P(None, "narrow", None), P(None, None, "narrow"),
        P(None, "narrow", None), P(),
    ) + states
    out_specs = (rows, rows) + states + (P(),)
    return jax.shard_map(
        functools.partial(shards, wide_axes=wide_axes),
        mesh=mesh, in_specs=in_specs, out_specs=out_specs, check_vma=False,
    )
```

time: 655 us -> 483 us (0.74)
  waiting for transfers between devices: 130 us -> 56.2 us
  blocking collectives: 78 us -> 10.4 us
  starting transfers between devices: 59.1 us -> 28.5 us
  local copies, waits for them, and re-layouts: 38.6 us -> 11.1 us
  Pallas kernels: 308 us -> 330 us
  between operations: 9.07 us -> 20.9 us
  other arithmetic: 27.7 us -> 19.5 us
    ppermute x58 -> x42, waiting for transfers between devices: 130 us -> 55.4 us  [the longest x40 33.4 us: swap(): return lax.ppermute(values, axis, [(0, 1), (1, 0)])]
    unnamed x1 -> x0, blocking collectives: 39.4 us -> none
    psum x1 -> x0, blocking collectives: 38.6 us -> none  [shards(): clip_norm = jnp.sqrt(lax.psum(squares, ('wide', 'narrow')))]
    ppermute x58 -> x42, starting transfers between devices: 59.1 us -> 28.3 us  [the longest x40 24.9 us: swap(): return lax.ppermute(values, axis, [(0, 1), (1, 0)])]
    pallas_call x24 -> x32, Pallas kernels: 308 us -> 330 us  [run(): pl.pallas_call(body, grid=grid, in_specs=list(in_specs) + [pl.BlockSpec(m...]
    another operation x18 -> x0, local copies, waits for them, and re-layouts: 22.1 us -> none
    all_to_all x0 -> x1, blocking collectives: none -> 10.4 us  [shards(): lax.all_to_all(jnp.broadcast_to(squares, (count, 128)), every, 0, 0, tile...]
    convert_element_type x24 -> x2, other arithmetic: 11.4 us -> 2.99 us  [shards(): ff, q = (ff.astype(F32), q.astype(F32))]
  transfers between devices with their start and end apart: 58 -> 45, of which waited for: 19 -> 13; matrix products, arithmetic and copies ran while one was open for 8% -> 4% of each run, Pallas kernels for 30% -> 67%
where the time goes in v2:
time: 483 us; the launch traced here: 477 us
  Pallas kernels  330 us (68%)
  waiting for transfers between devices  56.2 us (12%)
  starting transfers between devices  28.5 us (6%)
  between operations  20.9 us (4%)
  other arithmetic  19.5 us (4%)
  local copies, waits for them, and re-layouts  11.1 us (2%)
  blocking collectives  10.4 us (2%)
    pallas_call x32, Pallas kernels, run(): pl.pallas_call(body, grid=grid, in_specs=list(in_specs) + [pl.BlockSpec(m...  330 us
    ppermute x40, waiting for transfers between devices, swap(): return lax.ppermute(values, axis, [(0, 1), (1, 0)])  33.4 us
    ppermute x40, starting transfers between devices, swap(): return lax.ppermute(values, axis, [(0, 1), (1, 0)])  24.9 us
    ppermute x2, waiting for transfers between devices, shuffle(): lax.ppermute(values, axis, [(i, i ^ bit) for i in range(lax.axis_size(axi...  22 us
    all_to_all x1, blocking collectives, shards(): lax.all_to_all(jnp.broadcast_to(squares, (count, 128)), every, 0, 0, tile...  10.4 us
  transfers between devices with their start and end apart: 45, of which 13 were waited for; matrix products, arithmetic and copies ran while one was open for 4% of the time, Pallas kernels for 67%

profile of v2, /device:TPU:0, one launch (start us, length us, event | category | flops | bytes accessed | tf_op | source)
XLA Modules:
  0.0 476.9 jit_solution(11870354382211770801)
XLA Ops:
  8.3 1.3 fusion.20
  11.0 1.3 sine_select_fusion
  14.3 6.6 %project.3 = (bf16[1024,768]{1,0:T(8,128)(2,1)}, bf16[1024,768]{1,0:T(8,128)(2,1)}, bf16[1024,384]{1,0:T(8,128)(2,1)}, f32[1,6,128,256]{3,2,1,0:T(8,128)}) custom-call(bf16[1024,768]{1,0:T(8,128)(2,1)} %refs_1_.5, bf16[2,3,768,384]{3,2,1,0:T(8,128)(2,1)} %bitcast.47, f32[1024,128]{1,0:T(8,128)} %broadcast_in_dim.36.refs_2_.refs_3_.refs_10_, ...), custom_call_target="tpu_custom_call" | custom-call | tf_op jit(solution)/shard_map/project/pallas_call | solution.py:42
  21.3 6.2 %collective-permute-done.refs_1_.refs_2_.refs_3_ = bf16[2,3,768,384]{3,2,1,0:T(8,128)(2,1)} collective-permute-done((bf16[2,3,768,384]{3,2,1,0:T(8,128)(2,1)}, bf16[2,3,768,384]{3,2,1,0:T(8,128)(2,1)}, u32[]{:S(2)}, u32[]{:S(2)}) %collective-permute-start) | collective-permute-done | bytes 3538976 | tf_op jit(solution)/shard_map/ppermute | solution.py:830
  27.4 6.6 %project.4 = (bf16[1024,768]{1,0:T(8,128)(2,1)}, bf16[1024,768]{1,0:T(8,128)(2,1)}, bf16[1024,384]{1,0:T(8,128)(2,1)}, f32[1,6,128,256]{3,2,1,0:T(8,128)}) custom-call(bf16[1024,768]{1,0:T(8,128)(2,1)} %refs_1_.5, bf16[2,3,768,384]{3,2,1,0:T(8,128)(2,1)} %collective-permute-done.refs_1_.refs_2_.refs_3_, ...), custom_call_target="tpu_custom_call" | custom-call | tf_op jit(solution)/shard_map/project/pallas_call | solution.py:42
  35.1 1.6 collective-permute-done.1.refs_7_
  36.6 16.1 %attend.2 = (bf16[1024,384]{1,0:T(8,128)(2,1)}, bf16[1024,384]{1,0:T(8,128)(2,1)}, f32[1024,768]{1,0:T(8,128)}, f32[1024,768]{1,0:T(8,128)}, bf16[1024,768]{1,0:...) custom-call(f32[1,1]{1,0:T(1,128)} %bitcast.1.refs_0_, ...), custom_call_target="tpu_custom_call" | custom-call | tf_op jit(solution)/shard_map/attend/pallas_call | solution.py:42
  53.2 22.9 %feed.2 = (bf16[1024,1536]{1,0:T(8,128)(2,1)}, bf16[1024,1536]{1,0:T(8,128)(2,1)}, bf16[1024,3072]{1,0:T(8,128)(2,1)}, f32[1024,768]{1,0:T(8,128)}, bf16[1024,76...) custom-call(bf16[1024,768]{1,0:T(8,128)(2,1)} %get-tuple-element.140.refs_0_.refs_1_, ...), custom_call_target="tpu_custom_call" | custom-call | tf_op jit(solution)/shard_map/feed/pallas_call | solution.py:42
  76.8 6.5 %collective-permute-done.6.refs_5_.refs_3_ = bf16[1024,384]{1,0:T(8,128)(2,1)} collective-permute-done((bf16[1024,384]{1,0:T(8,128)(2,1)}, bf16[1024,384]{1,0:T(8,128)(2,1)}, u32[]{:S(2)}, u32[]{:S(2)}) %collective-permute-start.6) | collective-permute-done | bytes 786464 | tf_op jit(solution)/shard_map/ppermute | solution.py:830
  83.3 11.1 %project.5 = (bf16[1024,768]{1,0:T(8,128)(2,1)}, bf16[1024,768]{1,0:T(8,128)(2,1)}, bf16[1024,384]{1,0:T(8,128)(2,1)}, bf16[1024,768]{1,0:T(8,128)(2,1)}, bf16[1...) custom-call(bf16[1024,768]{1,0:T(8,128)(2,1)} %get-tuple-element.142.refs_0_.refs_1_, ...), custom_call_target="tpu_custom_call" | custom-call | tf_op jit(solution)/shard_map/project/pallas_call | solution.py:42
  95.0 3.2 collective-permute-done.8.refs_7_.refs_8_
  98.2 15.9 %attend.3 = (bf16[1024,384]{1,0:T(8,128)(2,1)}, bf16[1024,384]{1,0:T(8,128)(2,1)}, f32[1024,768]{1,0:T(8,128)}, f32[1024,768]{1,0:T(8,128)}, bf16[1024,768]{1,0:...) custom-call(f32[1,1]{1,0:T(1,128)} %bitcast.1.refs_0_, ...), custom_call_target="tpu_custom_call" | custom-call | tf_op jit(solution)/shard_map/attend/pallas_call | solution.py:42
  115.3 23.2 %feed.3 = (bf16[1024,1536]{1,0:T(8,128)(2,1)}, bf16[1024,1536]{1,0:T(8,128)(2,1)}, bf16[1024,3072]{1,0:T(8,128)(2,1)}, f32[1024,768]{1,0:T(8,128)}, bf16[1024,76...) custom-call(bf16[1024,768]{1,0:T(8,128)(2,1)} %get-tuple-element.153.refs_0_.refs_1_, ...), custom_call_target="tpu_custom_call" | custom-call | tf_op jit(solution)/shard_map/feed/pallas_call | solution.py:42
  139.8 24.8 %feed_back.2 = (bf16[2,1024,768]{2,1,0:T(8,128)(2,1)}, bf16[1024,1536]{1,0:T(8,128)(2,1)}, bf16[1024,1536]{1,0:T(8,128)(2,1)}, f32[1024,768]{1,0:T(8,128)}, f32[4,768]{1,0:T(4,128)}) custom-call(f32[1024,768]{1,0:T(8,128)} %refs_0_.5, f32[1024,128]{1,0:T(8,128)} %broadcast_in_dim.38.refs_1_, bf16[1024,768]{1,0:T(8,128)(2,1)} %get-tuple-element.156.refs_2_, ...), custom_call_target="tpu_custom_call" | custom-call | tf_op jit(solution)/shard_map/feed_back/pallas_call | solution.py:42
  165.1 9.5 %mix_back.2 = (bf16[1024,1536]{1,0:T(8,128)(2,1)}, f32[12,128,256]{2,1,0:T(8,128)}) custom-call(bf16[2,1024,768]{2,1,0:T(8,128)(2,1)} %get-tuple-element.162.refs_0_.refs_2_, bf16[2,384,768]{2,1,0:T(8,128)(2,1)} %refs_1_.4, bf16[2,384,768]{2,1,0:T(8,128)(2,1)} %collective-permute-done.3.refs_10_.refs_2_, f32[1024,768]{1,0:T(8,128)} %get-tuple-element.163.refs_3_, ...), custom_call_target="tpu_custom_call" | custom-call | tf_op jit(solution)/shard_map/mix_back/pallas_call | solution.py:42
  175.6 9.6 %back_grad.2 = (bf16[2,2,224,768]{3,2,1,0:T(8,128)(2,1)}, bf16[2,2,224,768]{3,2,1,0:T(8,128)(2,1)}, bf16[2,2,224,768]{3,2,1,0:T(8,128)(2,1)}, bf16[2,2,224,768]{3,2,1,0:T(8,128)(2,1)}) custom-call(s32[1,4]{1,0:T(1,128)} %add_bitcast_fusion.refs_0_, bf16[1024,1536]{1,0:T(8,128)(2,1)} %get-tuple-element.170.refs_1_, ...), custom_call_target="tpu_custom_call" | custom-call | tf_op jit(solution)/shard_map/back_grad/pallas_call | solution.py:42
  185.3 9.6 %in_grad.2 = (bf16[2,2,224,768]{3,2,1,0:T(8,128)(2,1)}, bf16[2,2,224,768]{3,2,1,0:T(8,128)(2,1)}, bf16[2,2,224,768]{3,2,1,0:T(8,128)(2,1)}, bf16[2,2,224,768]{3,2,1,0:T(8,128)(2,1)}) custom-call(s32[1,4]{1,0:T(1,128)} %add_bitcast_fusion.refs_0_, ...), custom_call_target="tpu_custom_call", output_to_operand_aliasing={{0}: (5, {}), {1}: (6, {}), {2}: (7, {}), {3}: (8, {})} | custom-call | tf_op jit(solution)/shard_map/in_grad/pallas_call | solution.py:42
  195.5 4.7 out_grad.2
  200.1 2.6 collective-permute-start.19
  202.8 1.5 collective-permute-start.20
  204.3 25.2 %attend_back.2 = (bf16[1024,1152]{1,0:T(8,128)(2,1)}, bf16[1024,1152]{1,0:T(8,128)(2,1)}) custom-call(f32[1,1]{1,0:T(1,128)} %bitcast.4.refs_0_, bf16[1024,768]{1,0:T(8,128)(2,1)} %get-tuple-element.144.refs_1_.refs_6_, bf16[1024,768]{1,0:T(8,128)(2,1)} %get-tuple-element.145.refs_2_.refs_7_, bf16[1024,768]{1,0:T(8,128)(2,1)} %get-tuple-element.146.refs_3_, ...), custom_call_target="tpu_custom_call" | custom-call | tf_op jit(solution)/shard_map/attend_back/pallas_call | solution.py:42
  229.6 9.9 %input_back.2.refs_5_.refs_0_ = f32[1024,768]{1,0:T(8,128)} custom-call(bf16[1024,1152]{1,0:T(8,128)(2,1)} %get-tuple-element.181.refs_0_.refs_2_, bf16[1024,1152]{1,0:T(8,128)(2,1)} %get-tuple-element.182.refs_1_, bf16[2,3,768,384]{3,2,1,0:T(8,128)(2,1)} %bitcast.49, bf16[2,3,768,384]{3,2,1,0:T(8,128)(2,1)} %collective-permute-done.refs_1_.refs_2_.refs_3_, ...), custom_call_target="tpu_custom_call" | custom-call | tf_op jit(solution)/shard_map/input_back/pallas_call | solution.py:42
  239.5 3.9 fold_split.4
  243.4 9.0 %qkv_grad.2 = (bf16[2,2,144,384]{3,2,1,0:T(8,128)(2,1)}, bf16[2,2,144,384]{3,2,1,0:T(8,128)(2,1)}, bf16[2,2,144,384]{3,2,1,0:T(8,128)(2,1)}, bf16[2,2,144,384]{3,2,1,0:T(8,128)(2,1)}) custom-call(s32[1,4]{1,0:T(1,128)} %add_bitcast_fusion.refs_0_, bf16[1024,768]{1,0:T(8,128)(2,1)} %get-tuple-element.142.refs_0_.refs_1_, ...), custom_call_target="tpu_custom_call" | custom-call | tf_op jit(solution)/shard_map/qkv_grad/pallas_call | solution.py:42
  253.1 24.4 %feed_back.3 = (bf16[2,1024,768]{2,1,0:T(8,128)(2,1)}, bf16[1024,1536]{1,0:T(8,128)(2,1)}, bf16[1024,1536]{1,0:T(8,128)(2,1)}, f32[1024,768]{1,0:T(8,128)}, f32[4,768]{1,0:T(4,128)}) custom-call(f32[1024,768]{1,0:T(8,128)} %input_back.2.refs_5_.refs_0_, bf16[1024,768]{1,0:T(8,128)(2,1)} %get-tuple-element.184.refs_1_, ...), custom_call_target="tpu_custom_call" | custom-call | tf_op jit(solution)/shard_map/feed_back/pallas_call | solution.py:42
  278.0 2.4 fold_split.5
  280.4 2.0 collective-permute-start.27
  282.4 1.5 collective-permute-start.28
  284.0 3.7 collective-permute-done.25
  287.7 2.0 collective-permute-start.40
  290.4 9.4 %mix_back.3 = (bf16[1024,1536]{1,0:T(8,128)(2,1)}, f32[12,128,256]{2,1,0:T(8,128)}) custom-call(bf16[2,1024,768]{2,1,0:T(8,128)(2,1)} %get-tuple-element.194.refs_5_.refs_0_.refs_2_.refs_4_, bf16[2,384,768]{2,1,0:T(8,128)(2,1)} %refs_1_.4, bf16[2,384,768]{2,1,0:T(8,128)(2,1)} %collective-permute-done.3.refs_10_.refs_2_, ...), custom_call_target="tpu_custom_call" | custom-call | tf_op jit(solution)/shard_map/mix_back/pallas_call | solution.py:42
  299.9 9.6 %back_grad.3 = (bf16[2,2,224,768]{3,2,1,0:T(8,128)(2,1)}, bf16[2,2,224,768]{3,2,1,0:T(8,128)(2,1)}, bf16[2,2,224,768]{3,2,1,0:T(8,128)(2,1)}, bf16[2,2,224,768]{3,2,1,0:T(8,128)(2,1)}) custom-call(s32[1,4]{1,0:T(1,128)} %add_bitcast_fusion.refs_0_, bf16[1024,1536]{1,0:T(8,128)(2,1)} %get-tuple-element.208.refs_1_, ...), custom_call_target="tpu_custom_call" | custom-call | tf_op jit(solution)/shard_map/back_grad/pallas_call | solution.py:42
  309.6 9.5 %in_grad.3 = (bf16[2,2,224,768]{3,2,1,0:T(8,128)(2,1)}, bf16[2,2,224,768]{3,2,1,0:T(8,128)(2,1)}, bf16[2,2,224,768]{3,2,1,0:T(8,128)(2,1)}, bf16[2,2,224,768]{3,2,1,0:T(8,128)(2,1)}) custom-call(s32[1,4]{1,0:T(1,128)} %add_bitcast_fusion.refs_0_, ...), custom_call_target="tpu_custom_call", output_to_operand_aliasing={{0}: (5, {}), {1}: (6, {}), {2}: (7, {}), {3}: (8, {})} | custom-call | tf_op jit(solution)/shard_map/in_grad/pallas_call | solution.py:42
  319.1 2.1 fold_join.3.refs_10_
  321.3 4.7 out_grad.3
  326.0 2.0 collective-permute-start.30
  328.0 2.7 fold_join.5
  330.8 25.0 %attend_back.3 = (bf16[1024,1152]{1,0:T(8,128)(2,1)}, bf16[1024,1152]{1,0:T(8,128)(2,1)}) custom-call(f32[1,1]{1,0:T(1,128)} %bitcast.4.refs_0_, bf16[1024,768]{1,0:T(8,128)(2,1)} %get-tuple-element.132.refs_1_.refs_6_, bf16[1024,768]{1,0:T(8,128)(2,1)} %get-tuple-element.133.refs_2_.refs_7_, bf16[1024,768]{1,0:T(8,128)(2,1)} %get-tuple-element.134.refs_3_, ...), custom_call_target="tpu_custom_call" | custom-call | tf_op jit(solution)/shard_map/attend_back/pallas_call | solution.py:42
  356.0 10.0 %input_back.3.refs_5_ = f32[1024,768]{1,0:T(8,128)} custom-call(bf16[1024,1152]{1,0:T(8,128)(2,1)} %get-tuple-element.221.refs_0_.refs_2_, bf16[1024,1152]{1,0:T(8,128)(2,1)} %get-tuple-element.222.refs_1_, bf16[2,3,768,384]{3,2,1,0:T(8,128)(2,1)} %bitcast.50, bf16[2,3,768,384]{3,2,1,0:T(8,128)(2,1)} %collective-permute-done.refs_1_.refs_2_.refs_3_, ...), custom_call_target="tpu_custom_call" | custom-call | tf_op jit(solution)/shard_map/input_back/pallas_call | solution.py:42
  366.0 3.9 fold_split.6
  369.9 1.9 collective-permute-start.34
  372.0 1.4 slice.72
  373.4 1.9 convert_element_type.64
  375.3 1.6 slice.78
  377.0 9.2 %qkv_grad.3 = (bf16[2,2,144,384]{3,2,1,0:T(8,128)(2,1)}, bf16[2,2,144,384]{3,2,1,0:T(8,128)(2,1)}, bf16[2,2,144,384]{3,2,1,0:T(8,128)(2,1)}, bf16[2,2,144,384]{3,2,1,0:T(8,128)(2,1)}) custom-call(s32[1,4]{1,0:T(1,128)} %add_bitcast_fusion.refs_0_, bf16[1024,768]{1,0:T(8,128)(2,1)} %refs_1_.5, bf16[1024,1152]{1,0:T(8,128)(2,1)} %get-tuple-element.221.refs_0_.refs_2_, ...), custom_call_target="tpu_custom_call" | custom-call | tf_op jit(solution)/shard_map/qkv_grad/pallas_call | solution.py:42
  386.2 1.9 collective-permute-start.32
  388.3 1.8 collective-permute-done.35.refs_3_
  390.1 2.7 fold_join.4.refs_5_
  392.8 6.4 %collective-permute-done.32.refs_2_ = bf16[2,2,144,384]{3,2,1,0:T(8,128)(2,1)} collective-permute-done((bf16[2,2,144,384]{3,2,1,0:T(8,128)(2,1)}, bf16[2,2,144,384]{3,2,1,0:T(8,128)(2,1)}, u32[]{:S(2)}, u32[]{:S(2)}) %collective-permute-start.32) | collective-permute-done | bytes 442400 | tf_op jit(solution)/shard_map/ppermute | solution.py:830
  400.1 2.4 fold_split.7
  402.9 1.6 collective-permute-start.37
  404.5 1.7 slice_bitcast_fusion.1
  406.3 2.7 collective-permute-done.36.refs_2_
  409.3 2.1 fold_near.1
  411.4 1.6 collective-permute-start.38
  413.0 1.7 maximum_bitcast_fusion.1
  414.7 12.3 %collective-permute-done.38.refs_2_ = bf16[2,144,384]{2,1,0:T(8,128)(2,1)} collective-permute-done((bf16[2,144,384]{2,1,0:T(8,128)(2,1)}, bf16[2,144,384]{2,1,0:T(8,128)(2,1)}, u32[]{:S(2)}, u32[]{:S(2)}) %collective-permute-start.38) | collective-permute-done | bytes 221216 | tf_op jit(solution)/shard_map/ppermute | solution.py:924
  427.0 1.8 fold_far.1
  428.8 1.9 collective-permute-start.39
  431.6 9.7 %collective-permute-done.39 = bf16[144,384]{1,0:T(8,128)(2,1)S(1)} collective-permute-done((bf16[144,384]{1,0:T(8,128)(2,1)}, bf16[144,384]{1,0:T(8,128)(2,1)S(1)}, u32[]{:S(2)}, u32[]{:S(2)}) %collective-permute-start.39) | collective-permute-done | bytes 110624 | tf_op jit(solution)/shard_map/ppermute | solution.py:924
  451.1 10.4 %all_to_all.6 = f32[32,1,128]{2,1,0:T(1,128)S(1)} all-to-all(f32[32,1,128]{2,1,0:T(1,128)S(1)} %broadcast_in_dim.40), channel_id=1, replica_groups=mesh['z'=4,'y'=2,'x'=2,'narrow'=2] {'z','y','x','narrow'}, dimensions={0} | all-to-all | bytes 32768 | tf_op jit(solution)/shard_map/all_to_all | solution.py:1110
  463.0 1.7 multiply_subtract_fusion.3
  464.8 1.6 multiply_subtract_fusion.1
  466.8 1.5 multiply_subtract_fusion
  (142 shorter events, 24.9 us)
Async XLA Ops:
  7.2 364.8 %reduce-scatter.8.cloned.1.call-start = ((), (), s32[]{:S(2)}) async-start(), calls=%async_computation.6 | async-start | bytes 1720320 | tf_op jit(solution)/shard_map/reduce_scatter | solution.py:1015
  7.2 45.9 %collective-permute-start.4 = (bf16[2,768,1536]{2,1,0:T(8,128)(2,1)}, bf16[2,768,1536]{2,1,0:T(8,128)(2,1)}, u32[]{:S(2)}, u32[]{:S(2)}) collective-permute-start(bf16[2,768,1536]{2,1,0:T(8,128)(2,1)} %refs_6_.5), channel_id=1, source_target_pairs={{0,1},{1,0},{2,3},{3,2},{4,5},{5,4},{6,7},{7,6},{8,9},{9,8},{10,11... | collective-permute-start | bytes 14155784 | tf_op jit(solution)/shard_map/ppermute | solution.py:830
  7.8 45.4 %collective-permute-start.5 = (bf16[2,1536,768]{2,1,0:T(8,128)(2,1)}, bf16[2,1536,768]{2,1,0:T(8,128)(2,1)}, u32[]{:S(2)}, u32[]{:S(2)}) collective-permute-start(bf16[2,1536,768]{2,1,0:T(8,128)(2,1)} %refs_8_.1), channel_id=1, source_target_pairs={{0,1},{1,0},{2,3},{3,2},{4,5},{5,4},{6,7},{7,6},{8,9},{9,8},{10,11... | collective-permute-start | bytes 14155784 | tf_op jit(solution)/shard_map/ppermute | solution.py:830
  7.8 19.6 %collective-permute-start = (bf16[2,3,768,384]{3,2,1,0:T(8,128)(2,1)}, bf16[2,3,768,384]{3,2,1,0:T(8,128)(2,1)}, u32[]{:S(2)}, u32[]{:S(2)}) collective-permute-start(bf16[2,3,768,384]{3,2,1,0:T(8,128)(2,1)} %bitcast.46), channel_id=1, source_target_pairs={{0,1},{1,0},{2,3},{3,2},{4,5},{5,4},{6,7},{7,6},{8,9},{9,8},{10,11... | collective-permute-start | bytes 10616840 | tf_op jit(solution)/shard_map/ppermute | solution.py:830
  8.3 26.8 %collective-permute-start.3 = (bf16[2,384,768]{2,1,0:T(8,128)(2,1)}, bf16[2,384,768]{2,1,0:T(8,128)(2,1)}, u32[]{:S(2)}, u32[]{:S(2)}) collective-permute-start(bf16[2,384,768]{2,1,0:T(8,128)(2,1)} %refs_1_.4), channel_id=1, source_target_pairs={{0,1},{1,0},{2,3},{3,2},{4,5},{5,4},{6,7},{7,6},{8,9},{9,8},{10,11... | collective-permute-start | bytes 3538952 | tf_op jit(solution)/shard_map/ppermute | solution.py:830
  20.9 14.2 %collective-permute-start.2 = (f32[1,6,128,256]{3,2,1,0:T(8,128)}, f32[1,6,128,256]{3,2,1,0:T(8,128)}, u32[]{:S(2)}, u32[]{:S(2)}) collective-permute-start(f32[1,6,128,256]{3,2,1,0:T(8,128)} %get-tuple-element.139), channel_id=1, source_target_pairs={{0,1},{1,0},{2,3},{3,2},{4,5},{5,4},{6,7},{7,6},{8,9},{9,8},{10,11... | collective-permute-start | bytes 2359304 | tf_op jit(solution)/shard_map/ppermute | solution.py:830
  34.0 2.6 collective-permute-start.1
  52.7 30.6 %collective-permute-start.7 = (bf16[1024,768]{1,0:T(8,128)(2,1)}, bf16[1024,768]{1,0:T(8,128)(2,1)}, u32[]{:S(2)}, u32[]{:S(2)}) collective-permute-start(bf16[1024,768]{1,0:T(8,128)(2,1)} %get-tuple-element.140.refs_0_.refs_1_), channel_id=1, source_target_pairs={{0,1},{1,0},{2,3},{3,2},{4,5},{5,4},{6,7},{7,6},{8,9},{9,8},{10,11... | collective-permute-start | bytes 4718600 | tf_op jit(solution)/shard_map/ppermute | solution.py:830
  76.1 22.1 %collective-permute-start.10 = (bf16[1024,1536]{1,0:T(8,128)(2,1)}, bf16[1024,1536]{1,0:T(8,128)(2,1)}, u32[]{:S(2)}, u32[]{:S(2)}) collective-permute-start(bf16[1024,1536]{1,0:T(8,128)(2,1)} %get-tuple-element.152), channel_id=1, source_target_pairs={{0,1},{1,0},{2,3},{3,2},{4,5},{5,4},{6,7},{7,6},{8,9},{9,8},{10,11... | collective-permute-start | bytes 9437192 | tf_op jit(solution)/shard_map/ppermute | solution.py:830
  76.3 7.0 %collective-permute-start.6 = (bf16[1024,384]{1,0:T(8,128)(2,1)}, bf16[1024,384]{1,0:T(8,128)(2,1)}, u32[]{:S(2)}, u32[]{:S(2)}) collective-permute-start(bf16[1024,384]{1,0:T(8,128)(2,1)} %get-tuple-element.143.refs_5_), channel_id=1, source_target_pairs={{0,1},{1,0},{2,3},{3,2},{4,5},{5,4},{6,7},{7,6},{8,9},{9,8},{10,11... | collective-permute-start | bytes 2359304 | tf_op jit(solution)/shard_map/ppermute | solution.py:830
  76.7 18.3 %collective-permute-start.9 = (bf16[1024,768]{1,0:T(8,128)(2,1)}, bf16[1024,768]{1,0:T(8,128)(2,1)}, u32[]{:S(2)}, u32[]{:S(2)}) collective-permute-start(bf16[1024,768]{1,0:T(8,128)(2,1)} %refs_1_.5), channel_id=1, source_target_pairs={{0,1},{1,0},{2,3},{3,2},{4,5},{5,4},{6,7},{7,6},{8,9},{9,8},{10,11... | collective-permute-start | bytes 4718600 | tf_op jit(solution)/shard_map/ppermute | solution.py:830
  94.4 3.8 collective-permute-start.8
  94.6 20.8 %collective-permute-start.11 = (bf16[1024,768]{1,0:T(8,128)(2,1)}, bf16[1024,768]{1,0:T(8,128)(2,1)}, u32[]{:S(2)}, u32[]{:S(2)}) collective-permute-start(bf16[1024,768]{1,0:T(8,128)(2,1)} %get-tuple-element.142.refs_0_.refs_1_), channel_id=1, source_target_pairs={{0,1},{1,0},{2,3},{3,2},{4,5},{5,4},{6,7},{7,6},{8,9},{9,8},{10,11... | collective-permute-start | bytes 4718600 | tf_op jit(solution)/shard_map/ppermute | solution.py:830
  114.1 24.6 %collective-permute-start.13 = (bf16[1024,768]{1,0:T(8,128)(2,1)}, bf16[1024,768]{1,0:T(8,128)(2,1)}, u32[]{:S(2)}, u32[]{:S(2)}) collective-permute-start(bf16[1024,768]{1,0:T(8,128)(2,1)} %get-tuple-element.153.refs_0_.refs_1_), channel_id=1, source_target_pairs={{0,1},{1,0},{2,3},{3,2},{4,5},{5,4},{6,7},{7,6},{8,9},{9,8},{10,11... | collective-permute-start | bytes 4718600 | tf_op jit(solution)/shard_map/ppermute | solution.py:830
  114.3 24.4 %collective-permute-start.12 = (bf16[1024,384]{1,0:T(8,128)(2,1)}, bf16[1024,384]{1,0:T(8,128)(2,1)}, u32[]{:S(2)}, u32[]{:S(2)}) collective-permute-start(bf16[1024,384]{1,0:T(8,128)(2,1)} %get-tuple-element.161.refs_5_), channel_id=1, source_target_pairs={{0,1},{1,0},{2,3},{3,2},{4,5},{5,4},{6,7},{7,6},{8,9},{9,8},{10,11... | collective-permute-start | bytes 2359304 | tf_op jit(solution)/shard_map/ppermute | solution.py:830
  138.5 37.1 %collective-permute-start.17 = (bf16[1024,1536]{1,0:T(8,128)(2,1)}, bf16[1024,1536]{1,0:T(8,128)(2,1)}, u32[]{:S(2)}, u32[]{:S(2)}) collective-permute-start(bf16[1024,1536]{1,0:T(8,128)(2,1)} %get-tuple-element.171), channel_id=1, source_target_pairs={{0,1},{1,0},{2,3},{3,2},{4,5},{5,4},{6,7},{7,6},{8,9},{9,8},{10,11... | collective-permute-start | bytes 9437192 | tf_op jit(solution)/shard_map/ppermute | solution.py:830
  164.6 11.1 %collective-permute-start.15 = (bf16[2,1024,768]{2,1,0:T(8,128)(2,1)}, bf16[2,1024,768]{2,1,0:T(8,128)(2,1)}, u32[]{:S(2)}, u32[]{:S(2)}) collective-permute-start(bf16[2,1024,768]{2,1,0:T(8,128)(2,1)} %get-tuple-element.162.refs_0_.refs_2_), channel_id=1, source_target_pairs={{0,1},{1,0},{2,3},{3,2},{4,5},{5,4},{6,7},{7,6},{8,9},{9,8},{10,11... | collective-permute-start | bytes 9437192 | tf_op jit(solution)/shard_map/ppermute | solution.py:830
  165.0 20.3 %collective-permute-start.16 = (bf16[1024,1536]{1,0:T(8,128)(2,1)}, bf16[1024,1536]{1,0:T(8,128)(2,1)}, u32[]{:S(2)}, u32[]{:S(2)}) collective-permute-start(bf16[1024,1536]{1,0:T(8,128)(2,1)} %get-tuple-element.169), channel_id=1, source_target_pairs={{0,1},{1,0},{2,3},{3,2},{4,5},{5,4},{6,7},{7,6},{8,9},{9,8},{10,11... | collective-permute-start | bytes 9437192 | tf_op jit(solution)/shard_map/ppermute | solution.py:830
  174.6 29.7 %collective-permute-start.14 = (f32[12,128,256]{2,1,0:T(8,128)}, f32[12,128,256]{2,1,0:T(8,128)}, u32[]{:S(2)}, u32[]{:S(2)}) collective-permute-start(f32[12,128,256]{2,1,0:T(8,128)} %get-tuple-element.167), channel_id=1, source_target_pairs={{0,1},{1,0},{2,3},{3,2},{4,5},{5,4},{6,7},{7,6},{8,9},{9,8},{10,11... | collective-permute-start | bytes 4718600 | tf_op jit(solution)/shard_map/ppermute | solution.py:830
  200.1 39.3 %collective-permute-start.19 = (bf16[2,2,224,768]{3,2,1,0:T(8,128)(2,1)}, bf16[2,2,224,768]{3,2,1,0:T(8,128)(2,1)}, u32[]{:S(2)}, u32[]{:S(2)}) collective-permute-start(bf16[2,2,224,768]{3,2,1,0:T(8,128)(2,1)} %get-tuple-element.189), channel_id=1, source_target_pairs={{0,2},{2,0},{1,3},{3,1},{4,6},{6,4},{5,7},{7,5},{8,10},{10,8},{9,1... | collective-permute-start | bytes 4128776 | tf_op jit(solution)/shard_map/ppermute | solution.py:830
  202.8 36.7 %collective-permute-start.20 = (bf16[2,2,224,768]{3,2,1,0:T(8,128)(2,1)}, bf16[2,2,224,768]{3,2,1,0:T(8,128)(2,1)}, u32[]{:S(2)}, u32[]{:S(2)}) collective-permute-start(bf16[2,2,224,768]{3,2,1,0:T(8,128)(2,1)} %get-tuple-element.191), channel_id=1, source_target_pairs={{0,4},{4,0},{1,5},{5,1},{2,6},{6,2},{3,7},{7,3},{8,12},{12,8},{9,1... | collective-permute-start | bytes 4128776 | tf_op jit(solution)/shard_map/ppermute | solution.py:830
  229.5 13.9 %collective-permute-start.18 = (bf16[1024,1152]{1,0:T(8,128)(2,1)}, bf16[1024,1152]{1,0:T(8,128)(2,1)}, u32[]{:S(2)}, u32[]{:S(2)}) collective-permute-start(bf16[1024,1152]{1,0:T(8,128)(2,1)} %get-tuple-element.182.refs_1_), channel_id=1, source_target_pairs={{0,1},{1,0},{2,3},{3,2},{4,5},{5,4},{6,7},{7,6},{8,9},{9,8},{10,11... | collective-permute-start | bytes 7077896 | tf_op jit(solution)/shard_map/ppermute | solution.py:830
  252.4 25.6 %collective-permute-start.21 = (bf16[2,2,144,384]{3,2,1,0:T(8,128)(2,1)}, bf16[2,2,144,384]{3,2,1,0:T(8,128)(2,1)}, u32[]{:S(2)}, u32[]{:S(2)}) collective-permute-start(bf16[2,2,144,384]{3,2,1,0:T(8,128)(2,1)} %get-tuple-element.197), channel_id=1, source_target_pairs={{0,2},{2,0},{1,3},{3,1},{4,6},{6,4},{5,7},{7,5},{8,10},{10,8},{9,1... | collective-permute-start | bytes 1327112 | tf_op jit(solution)/shard_map/ppermute | solution.py:830
  253.0 25.0 %collective-permute-start.22 = (bf16[2,2,144,384]{3,2,1,0:T(8,128)(2,1)}, bf16[2,2,144,384]{3,2,1,0:T(8,128)(2,1)}, u32[]{:S(2)}, u32[]{:S(2)}) collective-permute-start(bf16[2,2,144,384]{3,2,1,0:T(8,128)(2,1)} %get-tuple-element.199), channel_id=1, source_target_pairs={{0,4},{4,0},{1,5},{5,1},{2,6},{6,2},{3,7},{7,3},{8,12},{12,8},{9,1... | collective-permute-start | bytes 1327112 | tf_op jit(solution)/shard_map/ppermute | solution.py:830
  277.4 22.4 %collective-permute-start.24 = (bf16[2,1024,768]{2,1,0:T(8,128)(2,1)}, bf16[2,1024,768]{2,1,0:T(8,128)(2,1)}, u32[]{:S(2)}, u32[]{:S(2)}) collective-permute-start(bf16[2,1024,768]{2,1,0:T(8,128)(2,1)} %get-tuple-element.194.refs_5_.refs_0_.refs_2_.refs_4_), channel_id=1, source_target_pairs={{0,1},{1,0},{2,3},{3,2},{4,5},{5,4},{6,7},{7,6},{8,9},{9,8},{10,11... | collective-permute-start | bytes 9437192 | tf_op jit(solution)/shard_map/ppermute | solution.py:830
  277.7 31.8 %collective-permute-start.26 = (bf16[1024,1536]{1,0:T(8,128)(2,1)}, bf16[1024,1536]{1,0:T(8,128)(2,1)}, u32[]{:S(2)}, u32[]{:S(2)}) collective-permute-start(bf16[1024,1536]{1,0:T(8,128)(2,1)} %get-tuple-element.207), channel_id=1, source_target_pairs={{0,1},{1,0},{2,3},{3,2},{4,5},{5,4},{6,7},{7,6},{8,9},{9,8},{10,11... | collective-permute-start | bytes 9437192 | tf_op jit(solution)/shard_map/ppermute | solution.py:830
  278.0 5.9 %copy-start.15 = (f32[4,768]{1,0:T(4,128)S(1)}, f32[4,768]{1,0:T(4,128)}, u32[]{:S(2)}) copy-start(f32[4,768]{1,0:T(4,128)} %get-tuple-element.205) | copy-start | bytes 36868
  278.0 5.9 %copy-start.16 = (f32[4,768]{1,0:T(4,128)S(1)}, f32[4,768]{1,0:T(4,128)}, u32[]{:S(2)}) copy-start(f32[4,768]{1,0:T(4,128)} %get-tuple-element.204) | copy-start | bytes 36868
  280.4 38.7 %collective-permute-start.27 = (bf16[2,144,384]{2,1,0:T(8,128)(2,1)}, bf16[2,144,384]{2,1,0:T(8,128)(2,1)}, u32[]{:S(2)}, u32[]{:S(2)}) collective-permute-start(bf16[2,144,384]{2,1,0:T(8,128)(2,1)} %get-tuple-element.217), channel_id=1, source_target_pairs={{0,4},{4,0},{1,5},{5,1},{2,6},{6,2},{3,7},{7,3},{8,12},{12,8},{9,1... | collective-permute-start | bytes 663560 | tf_op jit(solution)/shard_map/ppermute | solution.py:830
  282.4 36.7 %collective-permute-start.28 = (bf16[2,144,384]{2,1,0:T(8,128)(2,1)}, bf16[2,144,384]{2,1,0:T(8,128)(2,1)}, u32[]{:S(2)}, u32[]{:S(2)}) collective-permute-start(bf16[2,144,384]{2,1,0:T(8,128)(2,1)} %get-tuple-element.219), channel_id=1, source_target_pairs={{0,2},{2,0},{1,3},{3,1},{4,6},{6,4},{5,7},{7,5},{8,10},{10,8},{9,1... | collective-permute-start | bytes 663560 | tf_op jit(solution)/shard_map/ppermute | solution.py:830
  283.9 3.8 collective-permute-start.25
  287.7 40.3 %collective-permute-start.40 = (bf16[2,224,768]{2,1,0:T(8,128)(2,1)}, bf16[2,224,768]{2,1,0:T(8,128)(2,1)}, u32[]{:S(2)}, u32[]{:S(2)}) collective-permute-start(bf16[2,224,768]{2,1,0:T(8,128)(2,1)} %get-tuple-element.243), channel_id=1, source_target_pairs={{0,4},{4,0},{1,5},{5,1},{2,6},{6,2},{3,7},{7,3},{8,12},{12,8},{9,1... | collective-permute-start | bytes 2064392 | tf_op jit(solution)/shard_map/ppermute | solution.py:830
  299.8 28.2 %collective-permute-start.41 = (bf16[2,224,768]{2,1,0:T(8,128)(2,1)}, bf16[2,224,768]{2,1,0:T(8,128)(2,1)}, u32[]{:S(2)}, u32[]{:S(2)}) collective-permute-start(bf16[2,224,768]{2,1,0:T(8,128)(2,1)} %get-tuple-element.245), channel_id=1, source_target_pairs={{0,2},{2,0},{1,3},{3,1},{4,6},{6,4},{5,7},{7,5},{8,10},{10,8},{9,1... | collective-permute-start | bytes 2064392 | tf_op jit(solution)/shard_map/ppermute | solution.py:830
  309.5 21.3 %collective-permute-start.23 = (f32[12,128,256]{2,1,0:T(8,128)}, f32[12,128,256]{2,1,0:T(8,128)}, u32[]{:S(2)}, u32[]{:S(2)}) collective-permute-start(f32[12,128,256]{2,1,0:T(8,128)} %get-tuple-element.203), channel_id=1, source_target_pairs={{0,1},{1,0},{2,3},{3,2},{4,5},{5,4},{6,7},{7,6},{8,9},{9,8},{10,11... | collective-permute-start | bytes 4718600 | tf_op jit(solution)/shard_map/ppermute | solution.py:830
  326.0 40.0 %collective-permute-start.30 = (bf16[2,2,224,768]{3,2,1,0:T(8,128)(2,1)}, bf16[2,2,224,768]{3,2,1,0:T(8,128)(2,1)}, u32[]{:S(2)}, u32[]{:S(2)}) collective-permute-start(bf16[2,2,224,768]{3,2,1,0:T(8,128)(2,1)} %get-tuple-element.224), channel_id=1, source_target_pairs={{0,2},{2,0},{1,3},{3,1},{4,6},{6,4},{5,7},{7,5},{8,10},{10,8},{9,1... | collective-permute-start | bytes 4128776 | tf_op jit(solution)/shard_map/ppermute | solution.py:830
  328.0 38.0 %collective-permute-start.31 = (bf16[2,2,224,768]{3,2,1,0:T(8,128)(2,1)}, bf16[2,2,224,768]{3,2,1,0:T(8,128)(2,1)}, u32[]{:S(2)}, u32[]{:S(2)}) collective-permute-start(bf16[2,2,224,768]{3,2,1,0:T(8,128)(2,1)} %get-tuple-element.226), channel_id=1, source_target_pairs={{0,4},{4,0},{1,5},{5,1},{2,6},{6,2},{3,7},{7,3},{8,12},{12,8},{9,1... | collective-permute-start | bytes 4128776 | tf_op jit(solution)/shard_map/ppermute | solution.py:830
  330.8 99.9 %reduce-scatter.4.cloned.1.call-start = ((), (), s32[]{:S(2)}) async-start(), calls=%async_computation.4 | async-start | bytes 552960 | tf_op jit(solution)/shard_map/reduce_scatter | solution.py:1015
  355.8 21.2 %collective-permute-start.29 = (bf16[1024,1152]{1,0:T(8,128)(2,1)}, bf16[1024,1152]{1,0:T(8,128)(2,1)}, u32[]{:S(2)}, u32[]{:S(2)}) collective-permute-start(bf16[1024,1152]{1,0:T(8,128)(2,1)} %get-tuple-element.222.refs_1_), channel_id=1, source_target_pairs={{0,1},{1,0},{2,3},{3,2},{4,5},{5,4},{6,7},{7,6},{8,9},{9,8},{10,11... | collective-permute-start | bytes 7077896 | tf_op jit(solution)/shard_map/ppermute | solution.py:830
  369.9 18.3 %collective-permute-start.34 = (bf16[2,224,768]{2,1,0:T(8,128)(2,1)}, bf16[2,224,768]{2,1,0:T(8,128)(2,1)}, u32[]{:S(2)}, u32[]{:S(2)}) collective-permute-start(bf16[2,224,768]{2,1,0:T(8,128)(2,1)} %get-tuple-element.232), channel_id=1, source_target_pairs={{0,4},{4,0},{1,5},{5,1},{2,6},{6,2},{3,7},{7,3},{8,12},{12,8},{9,1... | collective-permute-start | bytes 2064392 | tf_op jit(solution)/shard_map/ppermute | solution.py:830
  371.8 18.2 %collective-permute-start.35 = (bf16[2,224,768]{2,1,0:T(8,128)(2,1)}, bf16[2,224,768]{2,1,0:T(8,128)(2,1)}, u32[]{:S(2)}, u32[]{:S(2)}) collective-permute-start(bf16[2,224,768]{2,1,0:T(8,128)(2,1)} %get-tuple-element.234), channel_id=1, source_target_pairs={{0,2},{2,0},{1,3},{3,1},{4,6},{6,4},{5,7},{7,5},{8,10},{10,8},{9,1... | collective-permute-start | bytes 2064392 | tf_op jit(solution)/shard_map/ppermute | solution.py:830
  377.0 66.7 %reduce-scatter.6.cloned.1.call-start = ((), (), s32[]{:S(2)}) async-start(), calls=%async_computation.5 | async-start | bytes 1720320 | tf_op jit(solution)/shard_map/reduce_scatter | solution.py:1015
  386.2 12.9 %collective-permute-start.32 = (bf16[2,2,144,384]{3,2,1,0:T(8,128)(2,1)}, bf16[2,2,144,384]{3,2,1,0:T(8,128)(2,1)}, u32[]{:S(2)}, u32[]{:S(2)}) collective-permute-start(bf16[2,2,144,384]{3,2,1,0:T(8,128)(2,1)} %get-tuple-element.229), channel_id=1, source_target_pairs={{0,2},{2,0},{1,3},{3,1},{4,6},{6,4},{5,7},{7,5},{8,10},{10,8},{9,1... | collective-permute-start | bytes 1327112 | tf_op jit(solution)/shard_map/ppermute | solution.py:830
  388.1 12.0 %collective-permute-start.33 = (bf16[2,2,144,384]{3,2,1,0:T(8,128)(2,1)}, bf16[2,2,144,384]{3,2,1,0:T(8,128)(2,1)}, u32[]{:S(2)}, u32[]{:S(2)}) collective-permute-start(bf16[2,2,144,384]{3,2,1,0:T(8,128)(2,1)} %get-tuple-element.231), channel_id=1, source_target_pairs={{0,4},{4,0},{1,5},{5,1},{2,6},{6,2},{3,7},{7,3},{8,12},{12,8},{9,1... | collective-permute-start | bytes 1327112 | tf_op jit(solution)/shard_map/ppermute | solution.py:830
  402.5 6.4 %collective-permute-start.36 = (bf16[2,144,384]{2,1,0:T(8,128)(2,1)}, bf16[2,144,384]{2,1,0:T(8,128)(2,1)}, u32[]{:S(2)}, u32[]{:S(2)}) collective-permute-start(bf16[2,144,384]{2,1,0:T(8,128)(2,1)} %get-tuple-element.236), channel_id=1, source_target_pairs={{0,4},{4,0},{1,5},{5,1},{2,6},{6,2},{3,7},{7,3},{8,12},{12,8},{9,1... | collective-permute-start | bytes 663560 | tf_op jit(solution)/shard_map/ppermute | solution.py:830
  402.9 6.4 %collective-permute-start.37 = (bf16[2,144,384]{2,1,0:T(8,128)(2,1)}, bf16[2,144,384]{2,1,0:T(8,128)(2,1)}, u32[]{:S(2)}, u32[]{:S(2)}) collective-permute-start(bf16[2,144,384]{2,1,0:T(8,128)(2,1)} %get-tuple-element.238), channel_id=1, source_target_pairs={{0,2},{2,0},{1,3},{3,1},{4,6},{6,4},{5,7},{7,5},{8,10},{10,8},{9,1... | collective-permute-start | bytes 663560 | tf_op jit(solution)/shard_map/ppermute | solution.py:830
  411.4 15.6 %collective-permute-start.38 = (bf16[2,144,384]{2,1,0:T(8,128)(2,1)}, bf16[2,144,384]{2,1,0:T(8,128)(2,1)}, u32[]{:S(2)}, u32[]{:S(2)}) collective-permute-start(bf16[2,144,384]{2,1,0:T(8,128)(2,1)} %get-tuple-element.240), channel_id=1, source_target_pairs={{0,8},{8,0},{16,24},{24,16},{1,9},{9,1},{17,25},{25,17},{2,10},{10... | collective-permute-start | bytes 663560 | tf_op jit(solution)/shard_map/ppermute | solution.py:924
  428.8 16.1 %copy-start.3 = (f32[1,24,768]{2,1,0:T(8,128)S(1)}, f32[1,24,768]{2,1,0:T(8,128)}, u32[]{:S(2)}) copy-start(f32[1,24,768]{2,1,0:T(8,128)} %slice.72) | copy-start | bytes 221188
  428.8 12.6 %collective-permute-start.39 = (bf16[144,384]{1,0:T(8,128)(2,1)}, bf16[144,384]{1,0:T(8,128)(2,1)S(1)}, u32[]{:S(2)}, u32[]{:S(2)}) collective-permute-start(bf16[144,384]{1,0:T(8,128)(2,1)} %get-tuple-element.242), channel_id=1, source_target_pairs={{0,16},{8,24},{16,0},{24,8},{1,17},{9,25},{17,1},{25,9},{2,18},{10... | collective-permute-start | bytes 331784 | tf_op jit(solution)/shard_map/ppermute | solution.py:924
  442.3 4.6 copy-start.1
  444.8 3.5 copy-start
  444.8 16.9 %copy-start.10 = (f32[2,48,3,384]{3,1,2,0:T(8,128)S(1)}, f32[2,48,3,384]{3,1,2,0:T(8,128)}, u32[]{:S(2)}) copy-start(f32[2,48,3,384]{3,1,2,0:T(8,128)} %param.31) | copy-start | bytes 1327108
  444.8 16.9 %copy-start.11 = (f32[2,48,3,384]{3,1,2,0:T(8,128)S(1)}, f32[2,48,3,384]{3,1,2,0:T(8,128)}, u32[]{:S(2)}) copy-start(f32[2,48,3,384]{3,1,2,0:T(8,128)} %param.32) | copy-start | bytes 1327108
  444.8 16.9 %copy-start.12 = (f32[2,48,3,384]{3,1,2,0:T(8,128)S(1)}, f32[2,48,3,384]{3,1,2,0:T(8,128)}, u32[]{:S(2)}) copy-start(f32[2,48,3,384]{3,1,2,0:T(8,128)} %param.33) | copy-start | bytes 1327108
  461.5 1.6 copy-start.13
  461.5 1.6 copy-start.14
  461.7 3.1 copy-start.4
  461.7 3.1 copy-start.5
  461.7 3.1 copy-start.6
  464.8 1.6 copy-start.7
  464.8 1.6 copy-start.8
  464.8 2.0 copy-start.9
  466.8 1.5 copy-start.17
  466.8 1.5 copy-start.18
  466.8 1.5 copy-start.19
  (1 other events, 1.2 us)
Sparse Core Ops, SparseCore 0:
  330.9 33.0 reduce-scatter.7
  377.1 21.7 reduce-scatter.3
  406.4 37.2 reduce-scatter.5

commit v3 on v2

v3 whole, which is shorter than its diff:
```python
import functools
import math

import jax
import jax.numpy as jnp
from jax import lax
from jax.experimental import pallas as pl
from jax.experimental.pallas import tpu as pltpu
from jax.sharding import Mesh
from jax.sharding import PartitionSpec as P

HEAD = 64
LAYERS = 2
CHUNK = 256
FF_BLOCK = 768
VMEM = 64 * 1024 * 1024 - 128 * 1024
FOLD_WEIGHT = 1e12

EPS_NORM = 1e-05
CLIP = 1.0
BETA_ONE = 0.5
BETA_TWO = 0.5
ADAM_EPS = 1e-08
LR_MATRIX = 0.1
LR_NORMS = 0.5
DECAY_MATRIX = 0.1
STEP_NUMBER = 4.0

F32 = jnp.float32
BF16 = jnp.bfloat16


def run(
    kernel, args, in_specs, out_specs, out_shape, grid, name,
    scratch=(), after=(), aliases=None, weight=0, vmem=None,
):
    count, extra = len(args), len(after)

    def body(*refs):
        kernel(*refs[:count], *refs[count + extra :])

    return pl.pallas_call(
        body,
        grid=grid,
        in_specs=list(in_specs) + [pl.BlockSpec(memory_space=pl.ANY)] * extra,
        out_specs=out_specs,
        out_shape=out_shape,
        scratch_shapes=list(scratch),
        input_output_aliases=aliases or {},
        compiler_params=pltpu.CompilerParams(
            vmem_limit_bytes=vmem or VMEM, dimension_semantics=("arbitrary",) * len(grid)
        ),
        cost_estimate=pl.CostEstimate(
            flops=int(weight), bytes_accessed=int(weight), transcendentals=0
        ),
        name=name,
    )(*args, *after)


def dot(a, b):
    return jnp.dot(a, b, preferred_element_type=F32)


def dot_nt(a, b):
    return lax.dot_general(a, b, (((1,), (1,)), ((), ())), preferred_element_type=F32)


def dot_tn(a, b):
    return lax.dot_general(a, b, (((0,), (0,)), ((), ())), preferred_element_type=F32)


def low_lanes(rows):
    return lax.broadcasted_iota(jnp.int32, (rows, 128), 1) < HEAD


def shape(dims, dtype):
    return jax.ShapeDtypeStruct(dims, dtype)


IN_SMEM = pl.BlockSpec(memory_space=pltpu.SMEM)


def whole(array_shape):
    return pl.BlockSpec(array_shape, lambda *_: (0,) * len(array_shape))


def row_spec(rows, cols, index=lambda i: i):
    return pl.BlockSpec((rows, cols), lambda i: (index(i), 0))


def layer_spec(array, layer):
    rest = array.shape[1:]
    return pl.BlockSpec((None,) + rest, lambda *_: (layer,) + (0,) * len(rest))


def wide_low_lanes(rows):
    return jnp.concatenate([low_lanes(rows)] * 2, axis=1)


def own_lanes(pair, wide_low, odd):
    zero = jnp.zeros_like(pair)
    return jnp.where(wide_low, zero, pair) if odd else jnp.where(wide_low, pair, zero)


def pair_state(features, right):
    both = dot_tn(features, right)
    return jnp.where(wide_low_lanes(128), both[:128], both[128:])


def vext_of(v_pair):
    return jnp.concatenate([v_pair, jnp.ones_like(v_pair)], axis=1)


def tables_kernel(here_ref, cos_ref, sin_ref, live_ref):
    rows = cos_ref.shape[0]
    core, first_len, second_len = (here_ref[0, n] for n in (4, 5, 6))
    index = core * rows + lax.broadcasted_iota(jnp.int32, (rows, 128), 0)
    in_first = index < first_len
    in_second = jnp.logical_and(index >= first_len, index < first_len + second_len)
    live = jnp.where(jnp.logical_or(in_first, in_second), 1.0, 0.0)
    position = jnp.where(in_second, index - first_len, index).astype(F32)
    span = jnp.where(in_first, first_len, jnp.where(in_second, second_len, 1)).astype(F32)
    angle = jnp.where(live > 0.0, 0.5 * math.pi * position / span, 0.0)
    square = angle * angle
    cos = sin = jnp.zeros_like(angle)
    for n in range(7, -1, -1):
        cos = cos * square + (-1.0) ** n / math.factorial(2 * n)
        sin = sin * square + (-1.0) ** n / math.factorial(2 * n + 1)
    cos_ref[...] = cos * live
    sin_ref[...] = sin * angle * live
    live_ref[...] = live


def tables(here, rows):
    return run(
        tables_kernel, (here,), [IN_SMEM], [whole((rows, 128))] * 3,
        [shape((rows, 128), F32)] * 3, (1,), "tables",
    )


def project_kernel(x_ref, *refs):
    sides = (len(refs) - 3) // 4
    weights, (cos_ref, sin_ref) = refs[:sides], refs[sides : sides + 2]
    outs, kv_ref = refs[sides + 2 : -1], refs[-1]
    rows = x_ref.shape[0]
    x = x_ref[...]
    low = low_lanes(rows)
    cos, sin = cos_ref[...], sin_ref[...]
    first = pl.program_id(0) == 0

    def features(values, out_ref):
        for pair in range(values.shape[1] // 128):
            tile = jnp.maximum(values[:, pair * 128 : pair * 128 + 128], 0.0)
            along = tile * cos
            across = pltpu.roll(tile, HEAD, 1) * sin
            base = pair * 256
            out_ref[:, base : base + 128] = jnp.where(low, along, across).astype(BF16)
            out_ref[:, base + 128 : base + 256] = jnp.where(low, across, along).astype(BF16)

    for side in range(sides):
        w_ref = weights[side]
        q_ref, k_ref, v_ref = outs[3 * side : 3 * side + 3]
        other = sides - 1 - side
        v = dot(x, w_ref[2]).astype(BF16)
        v_ref[...] = v
        features(dot(x, w_ref[1]), k_ref)
        features(dot(x, w_ref[0]), q_ref)
        for pair in range(v.shape[1] // 128):
            part = pair_state(
                k_ref[:, pair * 256 : pair * 256 + 256],
                vext_of(v[:, pair * 128 : pair * 128 + 128]),
            )
            kv_ref[other, pair] = jnp.where(first, part, kv_ref[other, pair] + part)


def project(x, weights, layer, cos, sin, after=()):
    rows, width = x.shape
    half = weights[0].shape[3]
    heads = half // HEAD
    block = rows // 2
    cat = row_spec(block, heads * 128)
    return run(
        project_kernel,
        (x, *weights, cos, sin),
        [row_spec(block, width)]
        + [layer_spec(w, layer) for w in weights]
        + [row_spec(block, 128)] * 2,
        [cat, cat, row_spec(block, half)] * len(weights)
        + [whole((len(weights), heads // 2, 128, 256))],
        [
            shape((rows, heads * 128), BF16),
            shape((rows, heads * 128), BF16),
            shape((rows, half), BF16),
        ]
        * len(weights)
        + [shape((len(weights), heads // 2, 128, 256), F32)],
        (rows // block,),
        "project",
        (),
        after,
    )


def norm_rows(r, gain, shift):
    mean = jnp.mean(r, axis=1, keepdims=True)
    centered = r - mean
    var = jnp.mean(centered * centered, axis=1, keepdims=True)
    rstd = lax.rsqrt(var + EPS_NORM)
    x_hat = centered * rstd
    return x_hat * gain + shift, x_hat, rstd


def attend_kernel(
    here_ref, qo_ref, qp_ref, ko_ref, kp_ref, vo_ref, vp_ref, kvo_ref, kvp_ref, wo_ref, wp_ref,
    resid_ref, norm_ref,
    mo_ref, mp_ref, rden_ref, low_ref, xhat_ref, rstd_ref, state_out_ref,
    state,
):
    rows = qo_ref.shape[0]
    half = vo_ref.shape[1]
    pairs = half // 128

    @pl.when(pl.program_id(0) == 0)
    def _():
        carry = here_ref[0, 7].astype(F32) * here_ref[0, 4].astype(F32)
        state[:pairs] = kvo_ref[...] * carry
        state[pairs:] = kvp_ref[...] * carry

    low = low_lanes(rows)
    row = lax.broadcasted_iota(jnp.int32, (rows, rows), 0)
    col = lax.broadcasted_iota(jnp.int32, (rows, rows), 1)
    causal = col <= row
    branch = None
    for side, (q_ref, k_ref, v_ref, m_ref, w_ref) in enumerate(
        ((qo_ref, ko_ref, vo_ref, mo_ref, wo_ref), (qp_ref, kp_ref, vp_ref, mp_ref, wp_ref))
    ):
        for pair in range(pairs):
            at = side * pairs + pair
            vext = vext_of(v_ref[:, pair * 128 : pair * 128 + 128])
            k_pair = k_ref[:, pair * 256 : pair * 256 + 256]
            q = [q_ref[:, n * 128 : n * 128 + 128] for n in (2 * pair, 2 * pair + 1)]
            kv = state[at]
            kv_low = kv.astype(BF16)
            state_out_ref[0, at] = kv_low
            far = dot(jnp.concatenate(q, axis=0), kv_low)
            sums = []
            for odd in (0, 1):
                scores = dot_nt(q[odd], k_pair[:, odd * 128 : odd * 128 + 128])
                scores = jnp.where(causal, scores, 0.0).astype(BF16)
                sums.append(dot(scores, vext) + far[odd * rows : odd * rows + rows])
            state[at] = kv + pair_state(k_pair, vext)
            num = jnp.where(low, sums[0][:, :128], sums[1][:, :128])
            den = jnp.where(low, sums[0][:, 128:], sums[1][:, 128:])
            rden = 1.0 / jnp.maximum(den, 1.0)
            base = side * half + pair * 128
            rden_low = jnp.where(den > 1.0, jnp.minimum(rden, 1.0 - 2.0**-8), 1.0)
            rden_ref[:, base : base + 128] = rden_low.astype(BF16)
            m_ref[:, pair * 128 : pair * 128 + 128] = (num * rden).astype(BF16)
        part = dot(m_ref[...], w_ref[...])
        branch = part if branch is None else branch + part
    y, x_hat, rstd = norm_rows(resid_ref[...].astype(F32) + branch, norm_ref[0:1], norm_ref[1:2])
    low_ref[...] = y.astype(BF16)
    xhat_ref[...] = x_hat.astype(BF16)
    rstd_ref[...] = jnp.broadcast_to(rstd, rstd_ref.shape)


def attend(here, own, peer, kv, kv_at, w_own, w_peer, layer, resid, norms, after=()):
    rows, width = resid.shape
    half = own[2].shape[1]
    heads = half // HEAD
    steps = rows // CHUNK
    cat, narrow = row_spec(CHUNK, heads * 128), row_spec(CHUNK, half)
    full = row_spec(CHUNK, width)
    return run(
        attend_kernel,
        (here, own[0], peer[0], own[1], peer[1], own[2], peer[2], *kv,
         w_own, w_peer, resid, norms),
        [
            IN_SMEM,
            cat, cat, cat, cat, narrow, narrow,
            *(pl.BlockSpec((None,) + a.shape[1:], lambda *_, n=n: (n, 0, 0, 0)) for a, n in zip(kv, kv_at)),
            layer_spec(w_own, layer), layer_spec(w_peer, layer),
            full, layer_spec(norms, layer),
        ],
        [
            narrow, narrow, full, full, full, row_spec(CHUNK, 128),
            pl.BlockSpec((1, heads, 128, 256), lambda i: (i, 0, 0, 0)),
        ],
        [
            shape((rows, half), BF16),
            shape((rows, half), BF16),
            shape((rows, width), BF16),
            shape((rows, width), BF16),
            shape((rows, width), BF16),
            shape((rows, 128), F32),
            shape((steps, heads, 128, 256), BF16),
        ],
        (steps,),
        "attend",
        [pltpu.VMEM((heads, 128, 256), F32)],
        after,
    )


def gelu_both(u):
    root = math.sqrt(2.0 / math.pi)
    a = root + (root * 0.044715) * (u * u)
    gate = 0.5 + 0.5 * jnp.tanh(u * a)
    act = u * gate
    return act, gate + (act - act * gate) * (6.0 * a - 4.0 * root)


def feed_kernel(
    x_ref, wio_ref, wip_ref, wbo_ref, wbp_ref, norm_ref,
    ho_ref, hp_ref, slope_ref, out_ref, xhat_ref, rstd_ref,
    acc,
):
    step, steps = pl.program_id(0), pl.num_programs(0)
    rows = x_ref.shape[0]

    def side(w_in, w_back, h_ref, base):
        for i in range(rows // CHUNK):
            at = slice(i * CHUNK, i * CHUNK + CHUNK)
            act, slope = gelu_both(dot(x_ref[at, :], w_in[...]))
            act = act.astype(BF16)
            h_ref[at, :] = act
            slope_ref[at, :] = slope.astype(BF16)
            acc[at, :] = base[at, :].astype(F32) + dot(act, w_back[...])

    @pl.when(step == 0)
    def _():
        side(wio_ref, wbo_ref, ho_ref, x_ref)

    @pl.when((step > 0) & (step < steps // 2))
    def _():
        side(wio_ref, wbo_ref, ho_ref, acc)

    @pl.when(step >= steps // 2)
    def _():
        side(wip_ref, wbp_ref, hp_ref, acc)

    @pl.when(step == steps - 1)
    def _():
        def part(i, _):
            at = pl.ds(pl.multiple_of(i * CHUNK, CHUNK), CHUNK)
            y, x_hat, rstd = norm_rows(acc[at, :], norm_ref[2:3], norm_ref[3:4])
            out_ref[at, :] = y.astype(out_ref.dtype)
            xhat_ref[at, :] = x_hat.astype(BF16)
            rstd_ref[at, :] = jnp.broadcast_to(rstd, (CHUNK, 128))
            return 0

        lax.fori_loop(0, rows // CHUNK, part, 0)


def ff_specs(layer, width, blocks):
    own = lambda j: jnp.minimum(j, blocks - 1)
    peer = lambda j: jnp.maximum(j - blocks, 0)
    w_in = [
        pl.BlockSpec((None, width, FF_BLOCK), lambda j, f=f: (layer, 0, f(j))) for f in (own, peer)
    ]
    w_back = [
        pl.BlockSpec((None, FF_BLOCK, width), lambda j, f=f: (layer, f(j), 0)) for f in (own, peer)
    ]
    return own, peer, w_in, w_back


def feed(x, wi_own, wi_peer, wb_own, wb_peer, layer, norms, dtype, after=()):
    rows, width = x.shape
    half = wi_own.shape[2]
    blocks = half // FF_BLOCK
    own, peer, w_in, w_back = ff_specs(layer, width, blocks)
    full = whole((rows, width))
    return run(
        feed_kernel,
        (x, wi_own, wi_peer, wb_own, wb_peer, norms),
        [full, *w_in, *w_back, layer_spec(norms, layer)],
        [
            pl.BlockSpec((rows, FF_BLOCK), lambda j: (0, own(j))),
            pl.BlockSpec((rows, FF_BLOCK), lambda j: (0, peer(j))),
            pl.BlockSpec((rows, FF_BLOCK), lambda j: (0, j)),
            full, full, whole((rows, 128)),
        ],
        [
            shape((rows, half), BF16),
            shape((rows, half), BF16),
            shape((rows, 2 * half), BF16),
            shape((rows, width), dtype),
            shape((rows, width), BF16),
            shape((rows, 128), F32),
        ],
        (2 * blocks,),
        "feed",
        [pltpu.VMEM((rows, width), F32)],
        after,
    )


def norm_back(y, x_hat, rstd, gain):
    scaled = y * gain
    mean = jnp.mean(scaled, axis=1, keepdims=True)
    along = jnp.mean(scaled * x_hat, axis=1, keepdims=True)
    gain_grad = jnp.sum(y * x_hat, axis=0, keepdims=True)
    shift_grad = jnp.sum(y, axis=0, keepdims=True)
    return (scaled - mean - x_hat * along) * rstd, gain_grad, shift_grad


def feed_back_kernel(
    up_ref, live_ref, xh2_ref, rs2_ref, xh1_ref, rs1_ref, slope_ref,
    wio_ref, wip_ref, wbo_ref, wbp_ref, norm_ref,
    gfb_ref, gho_ref, ghp_ref, ng_ref,
    acc,
):
    step, steps = pl.program_id(0), pl.num_programs(0)
    rows, width = up_ref.shape
    tiles = width // 128

    def chunk(i):
        return pl.ds(pl.multiple_of(i * CHUNK, CHUNK), CHUNK)

    def wide(ref, at):
        return jnp.concatenate([ref[at, :]] * tiles, axis=1)

    @pl.when(step == 0)
    def _():
        ng_ref[...] = jnp.zeros_like(ng_ref)

        def part(i, _):
            at = chunk(i)
            y = up_ref[at, :].astype(F32)
            if live_ref is not None:
                y = y * wide(live_ref, at)
            grad, gain_grad, shift_grad = norm_back(
                y, xh2_ref[at, :].astype(F32), wide(rs2_ref, at), norm_ref[2:3]
            )
            acc[at, :] = grad
            gfb_ref[0, at, :] = grad.astype(BF16)
            ng_ref[2:3] += gain_grad
            ng_ref[3:4] += shift_grad
            return 0

        lax.fori_loop(0, rows // CHUNK, part, 0)

    def side(w_in, w_back, gh_ref):
        for i in range(rows // CHUNK):
            at = slice(i * CHUNK, i * CHUNK + CHUNK)
            act = dot_nt(gfb_ref[0, at, :], w_back[...])
            gh = (act * slope_ref[at, :].astype(F32)).astype(BF16)
            gh_ref[at, :] = gh
            acc[at, :] += dot_nt(gh, w_in[...])

    @pl.when(step < steps // 2)
    def _():
        side(wio_ref, wbo_ref, gho_ref)

    @pl.when(step >= steps // 2)
    def _():
        side(wip_ref, wbp_ref, ghp_ref)

    @pl.when(step == steps - 1)
    def _():
        def part(i, _):
            at = chunk(i)
            grad, gain_grad, shift_grad = norm_back(
                acc[at, :], xh1_ref[at, :].astype(F32), wide(rs1_ref, at), norm_ref[0:1]
            )
            gfb_ref[1, at, :] = grad.astype(BF16)
            ng_ref[0:1] += gain_grad
            ng_ref[1:2] += shift_grad
            return 0

        lax.fori_loop(0, rows // CHUNK, part, 0)


def feed_back(
    up, live, xh2, rs2, xh1, rs1, slope, wi_own, wi_peer, wb_own, wb_peer, layer, norms, after=()
):
    rows, width = up.shape
    half = wi_own.shape[2]
    blocks = half // FF_BLOCK
    own, peer, w_in, w_back = ff_specs(layer, width, blocks)
    full, thin = whole((rows, width)), whole((rows, 128))
    if live is None:

        def kernel(up_ref, *refs):
            feed_back_kernel(up_ref, None, *refs)

        args, specs = (up,), [full]
    else:
        kernel, args, specs = feed_back_kernel, (up, live), [full, thin]
    return run(
        kernel,
        args + (xh2, rs2, xh1, rs1, slope, wi_own, wi_peer, wb_own, wb_peer, norms),
        specs
        + [
            full, thin, full, thin,
            pl.BlockSpec((rows, FF_BLOCK), lambda j: (0, j)),
            *w_in, *w_back, layer_spec(norms, layer),
        ],
        [
            whole((2, rows, width)),
            pl.BlockSpec((rows, FF_BLOCK), lambda j: (0, own(j))),
            pl.BlockSpec((rows, FF_BLOCK), lambda j: (0, peer(j))),
            whole((4, width)),
        ],
        [
            shape((2, rows, width), BF16),
            shape((rows, half), BF16),
            shape((rows, half), BF16),
            shape((4, width), F32),
        ],
        (2 * blocks,),
        "feed_back",
        [pltpu.VMEM((rows, width), F32)],
        after,
    )


def mix_back_kernel(
    gfb_ref, wo_ref, wp_ref, rden_ref, mo_ref, mp_ref, qo_ref, qp_ref, gx_ref, dkv_ref, total
):
    rows = gfb_ref.shape[0]
    half = mo_ref.shape[1]
    pairs = half // 128
    first = pl.program_id(0) == 0
    r = lax.broadcasted_iota(jnp.int32, (256, 128), 0) % 128
    c = lax.broadcasted_iota(jnp.int32, (256, 128), 1)
    spread_c = jnp.where((r < HEAD) == (c < HEAD), -1.0 / HEAD, 0.0).astype(BF16)
    gb = gfb_ref[...]
    for side, (w_ref, m_ref, q_ref) in enumerate(
        ((wo_ref, mo_ref, qo_ref), (wp_ref, mp_ref, qp_ref))
    ):
        gm = dot_nt(gb, w_ref[...])
        for pair in range(pairs):
            base = side * half + pair * 128
            rden = rden_ref[:, base : base + 128].astype(F32)
            g = gm[:, pair * 128 : pair * 128 + 128] * rden
            m = m_ref[:, pair * 128 : pair * 128 + 128].astype(F32)
            prod = jnp.where(rden < 1.0, g * m, 0.0)
            high = prod.astype(BF16)
            rest = (prod - high.astype(F32)).astype(BF16)
            minus_c = dot(jnp.concatenate([high, rest], axis=1), spread_c).astype(BF16)
            gx = jnp.concatenate([g.astype(BF16), minus_c], axis=1)
            gx_ref[:, 2 * base : 2 * base + 256] = gx
            part = pair_state(q_ref[:, pair * 256 : pair * 256 + 256], gx)
            at = side * pairs + pair
            total[at] = jnp.where(first, part, total[at] + part)

    @pl.when(pl.program_id(0) == pl.num_programs(0) - 1)
    def _():
        dkv_ref[...] = total[...].astype(BF16)


def mix_back(gfb, w_own, w_peer, layer, rden, m_own, m_peer, q_own, q_peer, after=()):
    _, rows, width = gfb.shape
    half = m_own.shape[1]
    heads = half // HEAD
    full, narrow, cat = (row_spec(CHUNK, n) for n in (width, half, heads * 128))
    return run(
        mix_back_kernel,
        (gfb, w_own, w_peer, rden, m_own, m_peer, q_own, q_peer),
        [
            pl.BlockSpec((None, CHUNK, width), lambda i: (1, i, 0)),
            layer_spec(w_own, layer), layer_spec(w_peer, layer),
            full, narrow, narrow, cat, cat,
        ],
        [row_spec(CHUNK, 2 * width), whole((heads, 128, 256))],
        [
            shape((rows, 2 * width), BF16),
            shape((heads, 128, 256), BF16),
        ],
        (rows // CHUNK,),
        "mix_back",
        [pltpu.VMEM((heads, 128, 256), F32)],
        after,
    )


def attend_back_kernel(
    here_ref, qo_ref, qp_ref, ko_ref, kp_ref, vo_ref, vp_ref, gx_ref, state_ref, dkv_ref,
    cos_ref, sin_ref,
    go_ref, gp_ref,
    dstate,
):
    rows = qo_ref.shape[0]
    half = vo_ref.shape[1]
    pairs = half // 128

    @pl.when(pl.program_id(0) == 0)
    def _():
        carry = here_ref[0, 7].astype(F32) * (1 - here_ref[0, 4]).astype(F32)
        for at in range(2 * pairs):
            dstate[at] = dkv_ref[(at + pairs) % (2 * pairs)].astype(F32) * carry

    low = low_lanes(rows)
    wide_low, state_low = wide_low_lanes(rows), wide_low_lanes(128)
    row = lax.broadcasted_iota(jnp.int32, (rows, rows), 0)
    col = lax.broadcasted_iota(jnp.int32, (rows, rows), 1)
    causal, anti = col <= row, row <= col
    cos, sin = cos_ref[...], sin_ref[...]
    trig = jnp.where(low, cos, sin), jnp.where(low, sin, cos)
    for side, (q_ref, k_ref, v_ref, out_ref) in enumerate(
        ((qo_ref, ko_ref, vo_ref, go_ref), (qp_ref, kp_ref, vp_ref, gp_ref))
    ):
        for pair in range(pairs):
            at = side * pairs + pair
            vext = vext_of(v_ref[:, pair * 128 : pair * 128 + 128])
            gx = gx_ref[:, at * 256 : at * 256 + 256]
            gext = [own_lanes(gx, wide_low, odd) for odd in (0, 1)]
            both = jnp.concatenate(gext, axis=0)
            ds_both = dot_nt(both, vext)
            q_far = dot_nt(both, state_ref[0, at])
            dst_both = dot_nt(vext, both)
            left_over = dstate[at].astype(BF16)
            back = [own_lanes(left_over, state_low, odd) for odd in (0, 1)]
            k_far = dot_nt(vext, jnp.concatenate(back, axis=0))
            dstate[at] += pair_state(q_ref[:, pair * 256 : pair * 256 + 256], gx)
            dq, dk, left, right = [], [], [], []
            for odd in (0, 1):
                head = 2 * pair + odd
                here = slice(odd * rows, odd * rows + rows)
                q = q_ref[:, head * 128 : head * 128 + 128]
                k = k_ref[:, head * 128 : head * 128 + 128]
                score_t = jnp.where(anti, dot_nt(k, q), 0.0).astype(BF16)
                ds = jnp.where(causal, ds_both[here], 0.0).astype(BF16)
                ds_t = jnp.where(anti, dst_both[:, here], 0.0).astype(BF16)
                q_grad = (dot(ds, k) + q_far[here]) * trig[odd]
                k_grad = (dot(ds_t, q) + k_far[:, odd * 128 : odd * 128 + 128]) * trig[odd]
                left += [score_t, k]
                right += [gext[odd][:, :128], back[odd][:, :128]]
                q_grad = q_grad + pltpu.roll(q_grad, HEAD, 1)
                k_grad = k_grad + pltpu.roll(k_grad, HEAD, 1)
                dq.append(jnp.where(q > 0, q_grad, 0.0))
                dk.append(jnp.where(k > 0, k_grad, 0.0))
            dv = dot(jnp.concatenate(left, axis=1), jnp.concatenate(right, axis=0))
            for kind, value in enumerate(
                (jnp.where(low, dq[0], dq[1]), jnp.where(low, dk[0], dk[1]), dv)
            ):
                base = kind * half + pair * 128
                out_ref[:, base : base + 128] = value.astype(BF16)


def attend_back_on_kernel(*refs):
    inputs, (wo_ref, wp_ref, first_ref), (go_ref, gp_ref, up_ref, dstate) = (
        refs[:12], refs[12:15], refs[15:],
    )
    attend_back_kernel(*inputs, go_ref, gp_ref, dstate)
    input_back_kernel(go_ref, gp_ref, wo_ref, wp_ref, first_ref, up_ref)


def attend_back(here, own, peer, gx, states, dkv, cos, sin, after=(), onward=None):
    rows = cos.shape[0]
    half = own[2].shape[1]
    heads = half // HEAD
    steps = rows // CHUNK
    back = lambda i: steps - 1 - i
    cat, narrow, trig = (row_spec(CHUNK, n, back) for n in (heads * 128, half, 128))
    args = (here, own[0], peer[0], own[1], peer[1], own[2], peer[2], gx, states, dkv, cos, sin)
    specs = [
        IN_SMEM,
        cat, cat, cat, cat, narrow, narrow,
        row_spec(CHUNK, heads * 256, back),
        pl.BlockSpec((1, heads, 128, 256), lambda i: (back(i), 0, 0, 0)),
        whole(dkv.shape), trig, trig,
    ]
    outs = [row_spec(CHUNK, 3 * half, back)] * 2
    shapes = [shape((rows, 3 * half), BF16)] * 2
    kernel = attend_back_kernel
    if onward is not None:
        w_own, w_peer, layer, gfb = onward
        kernel = attend_back_on_kernel
        width = gfb.shape[2]
        args += (w_own, w_peer, gfb)
        specs += [layer_spec(w_own, layer), layer_spec(w_peer, layer)]
        specs += [pl.BlockSpec((None, CHUNK, width), lambda i: (1, back(i), 0))]
        outs, shapes = outs + [row_spec(CHUNK, width, back)], shapes + [shape((rows, width), BF16)]
    return run(
        kernel, args, specs, outs, shapes, (steps,), "attend_back",
        [pltpu.VMEM((heads, 128, 256), F32)],
        after,
    )


def input_back_kernel(go_ref, gp_ref, wo_ref, wp_ref, first_ref, out_ref):
    half = wo_ref.shape[2]
    total = first_ref[...].astype(F32)
    for g_ref, w_ref in ((go_ref, wo_ref), (gp_ref, wp_ref)):
        for kind in range(3):
            total = total + dot_nt(g_ref[:, kind * half : kind * half + half], w_ref[kind])
    out_ref[...] = total.astype(out_ref.dtype)


def input_back(g_own, g_peer, w_own, w_peer, layer, gfb, after=()):
    _, rows, width = gfb.shape
    block = rows // 2
    third, full = row_spec(block, g_own.shape[1]), row_spec(block, width)
    return run(
        input_back_kernel,
        (g_own, g_peer, w_own, w_peer, gfb),
        [
            third, third, layer_spec(w_own, layer), layer_spec(w_peer, layer),
            pl.BlockSpec((None, block, width), lambda i: (1, i, 0)),
        ],
        full,
        shape((rows, width), F32),
        (rows // block,),
        "input_back",
        (),
        after,
    )


def weight_kernel(a_ref, b_ref, c_ref, d_ref, out_ref):
    out_ref[...] = (dot_tn(a_ref[...], b_ref[...]) + dot_tn(c_ref[...], d_ref[...])).astype(
        out_ref.dtype
    )


def weight_grad(a, b, c, d, block_m, block_n, name):
    rows, m = a.shape
    n = b.shape[1]
    left = pl.BlockSpec((rows, block_m), lambda i, j: (0, i))
    right = pl.BlockSpec((rows, block_n), lambda i, j: (0, j))
    return run(
        weight_kernel,
        (a, b, c, d),
        [left, right, left, right],
        pl.BlockSpec((block_m, block_n), lambda i, j: (i, j)),
        shape((m, n), BF16),
        (m // block_m, n // block_n),
        name,
    )


FF_ROWS = 448
Q_ROWS = 144
NORM_ROW = 408


def fold_lanes(values, width):
    pieces = [values[:, at : at + width] for at in range(0, values.shape[1], width)]
    return jnp.concatenate(pieces, axis=0) if len(pieces) > 1 else values


def blocks_of(index_ref, scr, rows, z_local, x_first, other, kept):
    x, y = index_ref[0, 0], index_ref[0, 1]
    if x_first:
        spot = other * 2 + (x if kept else 1 - x)
    else:
        spot = (y if kept else 1 - y) * 2 + other
    start = pl.multiple_of((z_local * 4 + spot) * rows, 8)
    return scr[pl.ds(start, rows), :]


def back_pack_kernel(index_ref, a_ref, b_ref, c_ref, d_ref, ka, sa, kb, sb, scr):
    rows = scr.shape[0] // 4
    scr[...] = dot_tn(a_ref[...], b_ref[...]) + dot_tn(c_ref[...], d_ref[...])
    z = pl.program_id(0)
    for x_first, (keep, send) in ((True, (ka, sa)), (False, (kb, sb))):

        @pl.when((z < 2) == x_first)
        def _():
            for other in range(2):
                for kept, out in ((True, keep), (False, send)):
                    value = blocks_of(index_ref, scr, rows, 0, x_first, other, kept)
                    out[0, other] = fold_lanes(value, out.shape[3]).astype(BF16)


def half_spec(array, at):
    return pl.BlockSpec((None,) + array.shape[1:], lambda *_: (at, 0, 0))


def back_pack(index, a, b, c, d, after=()):
    rows, m = a.shape
    n = b.shape[2]
    block = m // 4
    left = pl.BlockSpec((rows, block), lambda z: (0, z))
    buffer = shape((2, 2, FF_ROWS, n // 2), BF16)
    low = pl.BlockSpec((1, 2, block // 2, n // 2), lambda z: (jnp.minimum(z, 1), 0, 0, 0))
    high = pl.BlockSpec((1, 2, block // 2, n // 2), lambda z: (jnp.maximum(z - 2, 0), 0, 0, 0))
    return run(
        back_pack_kernel,
        (index, a, b, c, d),
        [IN_SMEM, left, half_spec(b, 0), left, half_spec(d, 0)],
        [low, low, high, high],
        [buffer] * 4,
        (4,),
        "back_grad",
        [pltpu.VMEM((block, n), F32)],
        after,
    )


def spread(index_ref, scr, rows, outs, tail=None):
    ka, sa, kb, sb = outs
    for x_first, keep, send in ((True, ka, sa), (False, kb, sb)):
        for z in range(2):
            z_local = z if x_first else z + 2
            for other in range(2):
                for kept, out in ((True, keep), (False, send)):
                    value = blocks_of(index_ref, scr, rows, z_local, x_first, other, kept)
                    if tail is not None:
                        x, y = index_ref[0, 0], index_ref[0, 1]
                        if x_first:
                            w = z_local * 4 + other * 2 + (x if kept else 1 - x)
                        else:
                            w = z_local * 4 + (y if kept else 1 - y) * 2 + other
                        value = jnp.concatenate([value, tail(w)], axis=0)
                    out[z, other] = fold_lanes(value, out.shape[3]).astype(BF16)


def in_pack_kernel(index_ref, a_ref, b_ref, c_ref, d_ref, _ka, _sa, _kb, _sb, ka, sa, kb, sb, scr):
    scr[...] = dot_tn(a_ref[...], b_ref[...]) + dot_tn(c_ref[...], d_ref[...])
    spread(index_ref, scr, scr.shape[0] // 16, (ka, sa, kb, sb))


def column_pack(index, a, b, c, d, buffers, block_n, lanes, block_rows, first_block, name, after=()):
    rows, m = a.shape
    n = b.shape[1]
    right = pl.BlockSpec((rows, block_n), lambda j: (0, j))
    out_rows = m // 16 * (block_n // lanes)
    out = pl.BlockSpec((2, 2, out_rows, lanes), lambda j: (0, 0, first_block + j, 0))
    specs = [IN_SMEM, whole(a.shape), right, whole(c.shape), right]
    scratch = [pltpu.VMEM((m, block_n), F32)]
    if buffers is None:

        def fresh(index_ref, a_ref, b_ref, c_ref, d_ref, *outs):
            in_pack_kernel(index_ref, a_ref, b_ref, c_ref, d_ref, *([None] * 4), *outs)

        return run(
            fresh, (index, a, b, c, d), specs, [out] * 4,
            [shape((2, 2, block_rows, lanes), BF16)] * 4, (n // block_n,), name, scratch, after,
        )
    return run(
        in_pack_kernel,
        (index, a, b, c, d, *buffers),
        specs + [pl.BlockSpec(memory_space=pl.ANY)] * 4,
        [out] * 4,
        [shape(buffer.shape, BF16) for buffer in buffers],
        (n // block_n,),
        name,
        scratch,
        after,
        {5 + i: i for i in range(4)},
    )


def out_pack_kernel(
    index_ref, a_ref, b_ref, c_ref, d_ref, norm_ref, norm_got_ref, _ka, _sa, _kb, _sb,
    ka, sa, kb, sb, scr,
):
    scr[...] = dot_tn(a_ref[...], b_ref[...]) + dot_tn(c_ref[...], d_ref[...])
    blank = jnp.zeros((8, scr.shape[1] - 128), F32)
    spread(
        index_ref, scr, scr.shape[0] // 16, (ka, sa, kb, sb),
        lambda w: jnp.concatenate([norm_ref[w] + norm_got_ref[w], blank], axis=1),
    )


def out_pack(index, a, b, c, d, norms, norms_got, buffers, after=()):
    m, n = a.shape[1], b.shape[2]
    block = 2 * (m // 16 + 8)
    out = pl.BlockSpec((2, 2, block, n // 2), lambda j: (0, 0, (FF_ROWS - block) // block, 0))
    return run(
        out_pack_kernel,
        (index, a, b, c, d, norms, norms_got, *buffers),
        [IN_SMEM, whole(a.shape), half_spec(b, 1), whole(c.shape), half_spec(d, 1)]
        + [whole(norms.shape)] * 2
        + [pl.BlockSpec(memory_space=pl.ANY)] * 4,
        [out] * 4,
        [shape(buffer.shape, BF16) for buffer in buffers],
        (1,),
        "out_grad",
        [pltpu.VMEM((m, n), F32)],
        after,
        {7 + i: i for i in range(4)},
    )


def swap(values, axis="narrow"):
    return lax.ppermute(values, axis, [(0, 1), (1, 0)])


def sum_of(a_ref, b_ref, *at):
    return (a_ref[at].astype(F32) + b_ref[at].astype(F32)).astype(BF16)


def fold_split_kernel(index_ref, ka, ga, kb, gb, ka_out, sa_out, kb_out, sb_out):
    x, y = index_ref[0, 0], index_ref[0, 1]
    ka_out[0] = sum_of(ka, ga, 0, y)
    sa_out[0] = sum_of(ka, ga, 0, 1 - y)
    kb_out[0] = sum_of(kb, gb, 0, x)
    sb_out[0] = sum_of(kb, gb, 0, 1 - x)


def fold_split(index, ka, ga, kb, gb, after=()):
    _, _, r, c = ka.shape
    return run(
        fold_split_kernel,
        (index, ka, ga, kb, gb),
        [IN_SMEM]
        + [pl.BlockSpec((1, 2, r, c), lambda z: (z, 0, 0, 0))] * 4,
        [pl.BlockSpec((1, r, c), lambda z: (z, 0, 0))] * 4,
        [shape((2, r, c), BF16)] * 4,
        (2,),
        "fold_split",
        (),
        after,
        weight=FOLD_WEIGHT,
    )


def fold_near_kernel(index_ref, *refs):
    z = index_ref[0, 2]
    keep, send = refs[-2:]
    for half in range(2):
        done = 0
        for at in range(0, len(refs) - 2, 4):
            k, g = refs[at + 2 * half], refs[at + 2 * half + 1]
            rows = slice(done, done + k.shape[1])
            done += k.shape[1]
            keep[half, rows] = sum_of(k, g, z)
            send[half, rows] = sum_of(k, g, 1 - z)


def fold_near(index, groups, after=()):
    arrays = [array for group in groups for array in group]
    rows, lanes = sum(group[0].shape[1] for group in groups), arrays[0].shape[2]
    return run(
        fold_near_kernel,
        (index, *arrays),
        [IN_SMEM] + [whole(array.shape) for array in arrays],
        [whole((2, rows, lanes))] * 2,
        [shape((2, rows, lanes), BF16)] * 2,
        (1,),
        "fold_near",
        (),
        after,
        weight=FOLD_WEIGHT,
    )


def fold_far_kernel(index_ref, k, g, keep, send):
    z = index_ref[0, 3]
    keep[...] = sum_of(k, g, z)
    send[...] = sum_of(k, g, 1 - z)


def fold_far(index, keep, got, after=()):
    return run(
        fold_far_kernel,
        (index, keep, got),
        [IN_SMEM] + [whole(keep.shape)] * 2,
        [whole(keep.shape[1:])] * 2,
        [shape(keep.shape[1:], BF16)] * 2,
        (1,),
        "fold_far",
        (),
        after,
        weight=FOLD_WEIGHT,
    )


def settle_kernel(norms, index_ref, k, g, out, squares):
    total = k[...].astype(F32) + g[...].astype(F32)
    out[...] = total
    if norms:
        row, lane = (lax.broadcasted_iota(jnp.int32, total.shape, n) for n in (0, 1))
        here = jnp.logical_and(row >= NORM_ROW, row < NORM_ROW + 8)
        other = jnp.logical_or(lane < index_ref[0, 4] * norms, lane >= (index_ref[0, 4] + 1) * norms)
        total = jnp.where(jnp.logical_and(here, other), 0.0, total)
    total = total * total
    part = total[:, :128] + total[:, 128:256] + total[:, 256:]
    squares[...] = jnp.sum(part.reshape(-1, 8, 128), axis=0)


def settle(index, keep, got, norms=0, after=()):
    return run(
        functools.partial(settle_kernel, norms),
        (index, keep, got),
        [IN_SMEM, whole(keep.shape), whole(keep.shape)],
        [whole(keep.shape), whole((8, 128))],
        [shape(keep.shape, F32), shape((8, 128), F32)],
        (1,),
        "settle",
        (),
        after,
    )


def shuffle(values, axis, bit):
    return lax.ppermute(values, axis, [(i, i ^ bit) for i in range(lax.axis_size(axis))])


def adamw(master, first, second, gradient, factor, step_rate, decay_rate):
    fix_one = 1.0 - BETA_ONE**STEP_NUMBER
    fix_two = 1.0 - BETA_TWO**STEP_NUMBER
    clipped = gradient * factor
    first = BETA_ONE * first + (1.0 - BETA_ONE) * clipped
    second = BETA_TWO * second + (1.0 - BETA_TWO) * clipped * clipped
    update = first / fix_one / (jnp.sqrt(second / fix_two) + ADAM_EPS)
    master = master - step_rate * (update + decay_rate * master)
    return (master, first, second)


def update_kernel(wide, sums_ref, index_ref, one_ref, ff_ref, q_ref, *refs):
    states, news, clip_ref = refs[:15], refs[15:30], refs[30]
    layer = pl.program_id(0)
    total = jnp.sum(jnp.sum(sums_ref[...], axis=0, keepdims=True), axis=1, keepdims=True)
    clip_norm = jnp.sqrt(total)
    factor = jnp.minimum(1.0, CLIP / clip_norm)
    clip_ref[...] = jnp.broadcast_to(clip_norm, clip_ref.shape)

    def kind(at, gradient, rate, decay):
        old = [ref[...] for ref in states[3 * at : 3 * at + 3]]
        for ref, value in zip(news[3 * at : 3 * at + 3], adamw(*old, gradient, factor, rate, decay)):
            ref[...] = value

    def all_kinds(ff, q):
        three, rows, half = news[0].shape
        kind(0, q.reshape(three, rows, half), LR_MATRIX, DECAY_MATRIX)
        kind(1, jnp.concatenate([ff[384:408], ff[416:440]], axis=1), LR_MATRIX, DECAY_MATRIX)
        kind(2, jnp.concatenate([ff[n : n + 48] for n in range(192, 384, 48)], axis=1), LR_MATRIX, DECAY_MATRIX)
        kind(3, jnp.concatenate([ff[:96], ff[96:192]], axis=1), LR_MATRIX, DECAY_MATRIX)

    @pl.when(layer == 0)
    def _():
        all_kinds(ff_ref[...], q_ref[...])
        part = states[12].shape[1]
        columns = ff_ref[NORM_ROW : NORM_ROW + 8, :128]
        mine = jnp.where(index_ref[0, 4] == 0, columns[:, :part], columns[:, part : 2 * part])
        kind(4, mine, LR_NORMS, 0.0)

    @pl.when(layer == 1)
    def _():
        all_kinds(one_ref[:FF_ROWS], one_ref[FF_ROWS:])


def update(sums, index, one, ff, q, states, wide):
    specs = [layer_at(state) for state in states[:12]] + [whole(state.shape) for state in states[12:]]
    *news, clip_norm = run(
        functools.partial(update_kernel, wide),
        (sums, index, one, ff, q, *states),
        [whole(sums.shape), IN_SMEM, whole(one.shape), whole(ff.shape), whole(q.shape)] + specs,
        specs + [whole((8, 128))],
        [shape(state.shape, F32) for state in states] + [shape((8, 128), F32)],
        (LAYERS,),
        "update",
    )
    return news, clip_norm[0, :1]


def layer_at(array):
    rest = array.shape[1:]
    return pl.BlockSpec((None,) + rest, lambda l: (l,) + (0,) * len(rest))


def shards(
    stream, seq_lengths, cotangent, w_qkv, w_out, w_in, w_back, norm_params,
    qkv_master, qkv_first, qkv_second, out_master, out_first, out_second,
    in_master, in_first, in_second, back_master, back_first, back_second,
    norm_master, norm_first, norm_second,
    wide_axes,
):
    rows, width = stream.shape
    half = w_qkv.shape[3]
    every = wide_axes + ("narrow",)
    wide = math.prod(lax.axis_size(axis) for axis in wide_axes)
    by_axes = len(wide_axes) == 3
    lengths = seq_lengths[0]
    core = lax.axis_index("narrow")
    z, y, x = (lax.axis_index(axis) for axis in wide_axes) if by_axes else (0, 0, 0)
    goes_on = (lengths[0] > rows).astype(jnp.int32)
    lane = lax.broadcasted_iota(jnp.int32, (1, 8), 1)
    here = jnp.zeros((1, 8), jnp.int32)
    for n, value in enumerate((x, y, z % 2, z // 2, core, lengths[0], lengths[1], goes_on)):
        here = jnp.where(lane == n, value, here)
    cos, sin, live = tables(here, rows)

    qkv = jnp.transpose(w_qkv, (0, 2, 1, 3))
    qkv_peer, out_peer = swap(qkv), swap(w_out)
    in_peer = swap(lax.optimization_barrier((w_in, cos, out_peer))[0])
    back_peer = None

    low = stream
    kept = []
    got = [None] * LAYERS
    for layer in range(LAYERS):
        last = layer == LAYERS - 1
        if layer == 0:
            *own, kv_own = project(low, (qkv,), layer, cos, sin)
            *peer, kv_peer = project(low, (qkv_peer,), layer, cos, sin)
            kv, kv_at = (swap(kv_peer), swap(kv_own)), (0, 0)
            back_peer = swap(lax.optimization_barrier((w_back, *kv))[0])
        else:
            *parts, kv = project(low, (qkv, qkv_peer), layer, cos, sin)
            own, peer = parts[:3], parts[3:]
            kv, kv_at = (swap(kv),) * 2, (0, 1)
        low_got = swap(low)
        m_own, m_peer, rden, ffn_in, xh1, rs1, states = attend(
            here, own, peer, kv, kv_at, w_out, out_peer, layer, low, norm_params
        )
        h_own, h_peer, slope, out, xh2, rs2 = feed(
            ffn_in, w_in, in_peer, w_back, back_peer, layer, norm_params, F32 if last else BF16,
            got[layer - 1] + (low_got,) if last else (),
        )
        got[layer] = (low_got, swap(m_peer), swap(ffn_in), swap(h_peer))
        kept.append((low, own, peer, m_own, m_peer, rden, ffn_in, xh1, rs1, states, h_own, slope, xh2, rs2))
        low = out

    up = cotangent
    norm_grads = [None] * LAYERS
    shares = [None] * LAYERS
    by_x, by_y = (lambda v: swap(v, "x")), (lambda v: swap(v, "y"))
    near, far = (lambda v: shuffle(v, "z", 1)), (lambda v: shuffle(v, "z", 2))
    after = got[LAYERS - 1][1:3]
    for layer in reversed(range(LAYERS)):
        (low, own, peer, m_own, m_peer, rden, ffn_in, xh1, rs1, states, h_own, slope, xh2, rs2) = (
            kept[layer]
        )
        low_got, m_got, ffn_got, h_got = got[layer]
        last = layer == 0
        gfb, gh_own, gh_peer, norm_grads[layer] = feed_back(
            up, None if last else live, xh2, rs2, xh1, rs1, slope, w_in, in_peer, w_back, back_peer,
            layer, norm_params, after,
        )
        gfb_got, gh_got = swap(gfb), swap(gh_peer)
        mix = (gfb, w_out, out_peer, layer, rden, m_own, m_peer, own[0], peer[0])
        back = (here, own, peer)
        norm_sum = jnp.stack(norm_grads) if last else None
        if not by_axes:
            back_grad = weight_grad(h_own, gfb[0], h_got, gfb_got[0], 512, width, "back_grad")
            in_grad = weight_grad(ffn_in, gh_own, ffn_got, gh_got, width, 512, "in_grad")
            out_grad = weight_grad(m_own, gfb[1], m_got, gfb_got[1], half, width, "out_grad")
            gx, dkv = mix_back(*mix)
            g_own, g_peer = attend_back(*back, gx, states, swap(dkv), cos, sin)
            up = input_back(g_own, g_peer, qkv, qkv_peer, layer, gfb)
            qkv_grad = weight_grad(low, g_own, low_got, swap(g_peer), width, half, "qkv_grad")
            shares[layer] = [
                lax.psum_scatter(g, wide_axes, scatter_dimension=0, tiled=True).astype(F32)
                for g in (qkv_grad, out_grad, in_grad, back_grad)
            ]
            shares[layer][0] = shares[layer][0].reshape(-1, 3, half)
            after = ()
            continue
        after = ()
        if last:
            norms = jnp.transpose(norm_sum.reshape(8, wide, width // wide), (1, 0, 2))
            norms = jnp.pad(norms, ((0, 0), (0, 0), (0, 128 - width // wide)))
            norms_got = swap(norms)
            ka, sa, kb, sb = fold_split(here, *q_first, (gfb,))
            q_second = (ka, by_y(sa), kb, by_x(sb))
            gx = None
            after = (ka,)
        else:
            norms = norms_got = jnp.zeros((wide, 8, 128), F32)
            gx, dkv = mix_back(*mix)
            after = (gx,)
        buffers = back_pack(here, h_own, gfb, h_got, gfb_got, after)
        after = ()
        if last:
            keep, send = fold_near(here, (ff_second, q_second), (buffers[0],))
            one_near = (keep, near(send))
            after = (keep,)
        buffers = column_pack(
            here, ffn_in, gh_own, ffn_got, gh_got, buffers, width, half, FF_ROWS, 2, "in_grad", after
        )
        ka, sa, kb, sb = out_pack(here, m_own, gfb, m_got, gfb_got, norms, norms_got, buffers)
        ff_first = (ka, by_x(sa), kb, by_y(sb))
        if last:
            keep, send = fold_far(here, *one_near, (ka,))
            one_far = (keep, far(send))
            gx, dkv = mix_back(*mix, (keep,))
            g_own, g_peer = attend_back(*back, gx, states, swap(dkv), cos, sin)
        else:
            g_own, g_peer, up = attend_back(
                *back, gx, states, swap(dkv), cos, sin, (ka,), (qkv, qkv_peer, layer, gfb)
            )
        g_got = swap(g_peer)
        ka, sa, kb, sb = fold_split(here, *ff_first, (g_own,))
        ff_second = (ka, by_y(sa), kb, by_x(sb))
        q_ka, q_sa, q_kb, q_sb = column_pack(
            here, low, g_own, low_got, g_got, None, half, half, Q_ROWS, 0, "qkv_grad", (ka,)
        )
        q_first = (q_ka, by_x(q_sa), q_kb, by_y(q_sb))
        after = (q_ka,)
        if not last:
            continue
        keep, send = fold_near(here, (ff_second,), (q_ka,))
        ff_near = (keep, near(send))
        up = input_back(g_own, g_peer, qkv, qkv_peer, layer, gfb, (keep,))
        ka, sa, kb, sb = fold_split(here, *q_first, (up,))
        q_second = (ka, by_y(sa), kb, by_x(sb))
        keep, send = fold_far(here, *ff_near, (ka,))
        ff_far = (keep, far(send))
        keep, send = fold_near(here, (q_second,), (keep,))
        q_near = (keep, near(send))
        one, one_squares = settle(here, *one_far, 0, (keep,))
        keep, send = fold_far(here, *q_near, (one,))
        q_far = (keep, far(send))
        ff, ff_squares = settle(here, *ff_far, width // wide // 2, (keep,))
        q, q_squares = settle(here, *q_far, 0, (ff,))

    count = wide * lax.axis_size("narrow")
    states = (
        qkv_master, qkv_first, qkv_second, out_master, out_first, out_second,
        in_master, in_first, in_second, back_master, back_first, back_second,
        norm_master, norm_first, norm_second,
    )
    exchange = lambda rows_in: lax.all_to_all(rows_in, every, 0, 0, tiled=True)
    if by_axes:
        squares = (one_squares + ff_squares + q_squares).sum(0, keepdims=True)
        sums = exchange(jnp.broadcast_to(squares, (count, 128)))
        flip = lambda array: jnp.transpose(array, (0, 2, 1, 3))
        states = tuple(flip(v) for v in states[:3]) + states[3:12] + tuple(
            v.reshape(8, -1) for v in states[12:]
        )
        new, clip_norm = update(sums, here, one, ff, q, states, wide)
        new = [flip(v) for v in new[:3]] + new[3:12] + [v.reshape(LAYERS, 4, -1) for v in new[12:]]
        return (out, up, *new, clip_norm)
    gradients = [jnp.stack([shares[l][kind] for l in range(LAYERS)]) for kind in range(4)]
    gradients.append(lax.psum_scatter(norm_sum, every, scatter_dimension=2, tiled=True))
    squares = sum(jnp.sum(g * g) for g in gradients)
    clip_norm = jnp.sqrt(exchange(jnp.broadcast_to(squares, (count, 128))).sum(0)[:1])
    factor = jnp.minimum(1.0, CLIP / clip_norm[0])
    new = []
    for kind, gradient in enumerate(gradients):
        rates = (LR_MATRIX, DECAY_MATRIX) if kind < 4 else (LR_NORMS, 0.0)
        new += adamw(*states[3 * kind : 3 * kind + 3], gradient, factor, *rates)
    return (out, up, *new, clip_norm)


def solution(mesh):
    wide_axes = ("wide",)
    if mesh.shape["wide"] == 16:
        wide_axes = ("z", "y", "x")
        mesh = Mesh(mesh.devices.reshape(4, 2, 2, 2), wide_axes + ("narrow",))
    rows = P(wide_axes + ("narrow",), None)
    qkv = P(None, wide_axes, None, "narrow")
    deep = P(None, ("narrow",) + wide_axes, None)
    in_part = P(None, wide_axes, "narrow")
    norm = P(None, None, wide_axes + ("narrow",))
    states = (qkv,) * 3 + (deep,) * 3 + (in_part,) * 3 + (deep,) * 3 + (norm,) * 3
    in_specs = (
        rows, P(wide_axes, None), rows,
        P(None, None, None, "narrow"), P(None, "narrow", None), P(None, None, "narrow"),
        P(None, "narrow", None), P(),
    ) + states
    out_specs = (rows, rows) + states + (P(),)
    return jax.shard_map(
        functools.partial(shards, wide_axes=wide_axes),
        mesh=mesh, in_specs=in_specs, out_specs=out_specs, check_vma=False,
    )
```

time: 483 us -> 420 us (0.87)
  waiting for transfers between devices: 56.2 us -> 34 us
  between operations: 20.9 us -> 1.8 us
  other arithmetic: 19.5 us -> 2.55 us
  local copies, waits for them, and re-layouts: 11.1 us -> 3.3 us
    ppermute x40, waiting for transfers between devices: 33.4 us -> 16.4 us  [swap(): return lax.ppermute(values, axis, [(0, 1), (1, 0)])]
    sub x5 -> x0, other arithmetic: 6.75 us -> none  [adamw(): master = master - step_rate * (update + decay_rate * master)]
    ppermute x2 -> x6, starting transfers between devices: 3.49 us -> 9.84 us  [shuffle(): lax.ppermute(values, axis, [(i, i ^ bit) for i in range(lax.axis_size(axi...]
    ppermute x2 -> x6, waiting for transfers between devices: 22 us -> 17.7 us  [shuffle(): lax.ppermute(values, axis, [(i, i ^ bit) for i in range(lax.axis_size(axi...]
    pallas_call x32 -> x37, Pallas kernels: 330 us -> 327 us  [run(): pl.pallas_call(body, grid=grid, in_specs=list(in_specs) + [pl.BlockSpec(m...]
  transfers between devices with their start and end apart: 45 -> 46, of which waited for: 13 -> 16; matrix products, arithmetic and copies ran while one was open for 4% -> 1% of each run, Pallas kernels for 67% -> 61%
where the time goes in v3:
time: 420 us; the launch traced here: 414 us
  Pallas kernels  327 us (78%)
  waiting for transfers between devices  34 us (8%)
  starting transfers between devices  32.8 us (8%)
  blocking collectives  11.9 us (3%)
    pallas_call x37, Pallas kernels, run(): pl.pallas_call(body, grid=grid, in_specs=list(in_specs) + [pl.BlockSpec(m...  327 us
    ppermute x40, starting transfers between devices, swap(): return lax.ppermute(values, axis, [(0, 1), (1, 0)])  22.9 us
    ppermute x6, waiting for transfers between devices, shuffle(): lax.ppermute(values, axis, [(i, i ^ bit) for i in range(lax.axis_size(axi...  17.7 us
    ppermute x40, waiting for transfers between devices, swap(): return lax.ppermute(values, axis, [(0, 1), (1, 0)])  16.4 us
    all_to_all x1, blocking collectives, shards(): exchange = lambda rows_in: lax.all_to_all(rows_in, every, 0, 0, tiled=True)  11.9 us
    ppermute x6, starting transfers between devices, shuffle(): lax.ppermute(values, axis, [(i, i ^ bit) for i in range(lax.axis_size(axi...  9.84 us
  transfers between devices with their start and end apart: 46, of which 16 were waited for; matrix products, arithmetic and copies ran while one was open for 1% of the time, Pallas kernels for 61%

profile of v3, /device:TPU:0, one launch (start us, length us, event | category | flops | bytes accessed | tf_op | source)
XLA Modules:
  0.0 413.6 jit_solution(7548537678416364919)
XLA Ops:
  1.3 1.3 fusion
  3.2 1.8 compare_select_fusion.7.refs_0_.refs_1_
  5.1 2.4 tables.1
  7.5 6.4 %project.3 = (bf16[1024,768]{1,0:T(8,128)(2,1)}, bf16[1024,768]{1,0:T(8,128)(2,1)}, bf16[1024,384]{1,0:T(8,128)(2,1)}, f32[1,3,128,256]{3,2,1,0:T(8,128)}) custom-call(bf16[1024,768]{1,0:T(8,128)(2,1)} %refs_1_.9, bf16[2,3,768,384]{3,2,1,0:T(8,128)(2,1)} %bitcast.23, f32[1024,128]{1,0:T(8,128)} %get-tuple-element.163.refs_2_.refs_3_.refs_10_, ...), custom_call_target="tpu_custom_call" | custom-call | tf_op jit(solution)/shard_map/project/pallas_call | solution.py:42
  14.4 6.4 %project.4 = (bf16[1024,768]{1,0:T(8,128)(2,1)}, bf16[1024,768]{1,0:T(8,128)(2,1)}, bf16[1024,384]{1,0:T(8,128)(2,1)}, f32[1,3,128,256]{3,2,1,0:T(8,128)}) custom-call(bf16[1024,768]{1,0:T(8,128)(2,1)} %refs_1_.9, bf16[2,3,768,384]{3,2,1,0:T(8,128)(2,1)} %collective-permute-done.refs_1_.refs_2_.refs_13_.refs_3_, ...), custom_call_target="tpu_custom_call" | custom-call | tf_op jit(solution)/shard_map/project/pallas_call | solution.py:42
  21.4 1.5 collective-permute-done.1.refs_7_
  23.1 14.3 %attend.2 = (bf16[1024,384]{1,0:T(8,128)(2,1)}, bf16[1024,384]{1,0:T(8,128)(2,1)}, bf16[1024,768]{1,0:T(8,128)(2,1)}, bf16[1024,768]{1,0:T(8,128)(2,1)}, bf16[10...) custom-call(s32[1,8]{1,0:T(1,128)} %compare_select_fusion.7.refs_0_.refs_1_, ...), custom_call_target="tpu_custom_call" | custom-call | tf_op jit(solution)/shard_map/attend/pallas_call | solution.py:42
  37.4 21.0 %feed.2 = (bf16[1024,1536]{1,0:T(8,128)(2,1)}, bf16[1024,1536]{1,0:T(8,128)(2,1)}, bf16[1024,3072]{1,0:T(8,128)(2,1)}, bf16[1024,768]{1,0:T(8,128)(2,1)}, bf16[1...) custom-call(bf16[1024,768]{1,0:T(8,128)(2,1)} %get-tuple-element.173.refs_0_.refs_1_, bf16[2,768,1536]{2,1,0:T(8,128)(2,1)} %refs_6_.1, ...), custom_call_target="tpu_custom_call" | custom-call | tf_op jit(solution)/shard_map/feed/pallas_call | solution.py:42
  59.0 10.8 %project.5 = (bf16[1024,768]{1,0:T(8,128)(2,1)}, bf16[1024,768]{1,0:T(8,128)(2,1)}, bf16[1024,384]{1,0:T(8,128)(2,1)}, bf16[1024,768]{1,0:T(8,128)(2,1)}, bf16[1...) custom-call(bf16[1024,768]{1,0:T(8,128)(2,1)} %get-tuple-element.176.refs_0_.refs_11_.refs_1_, ...), custom_call_target="tpu_custom_call" | custom-call | tf_op jit(solution)/shard_map/project/pallas_call | solution.py:42
  70.8 1.7 collective-permute-done.6.refs_7_.refs_8_
  72.9 14.3 %attend.3 = (bf16[1024,384]{1,0:T(8,128)(2,1)}, bf16[1024,384]{1,0:T(8,128)(2,1)}, bf16[1024,768]{1,0:T(8,128)(2,1)}, bf16[1024,768]{1,0:T(8,128)(2,1)}, bf16[10...) custom-call(s32[1,8]{1,0:T(1,128)} %compare_select_fusion.7.refs_0_.refs_1_, ...), custom_call_target="tpu_custom_call" | custom-call | tf_op jit(solution)/shard_map/attend/pallas_call | solution.py:42
  87.8 21.8 %feed.3 = (bf16[1024,1536]{1,0:T(8,128)(2,1)}, bf16[1024,1536]{1,0:T(8,128)(2,1)}, bf16[1024,3072]{1,0:T(8,128)(2,1)}, f32[1024,768]{1,0:T(8,128)}, bf16[1024,768]{1,0:T(8,128)(2,1)}, /*index=5*/f32[1024,128]{1,0:T(8,128)}) custom-call(bf16[1024,768]{1,0:T(8,128)(2,1)} %get-tuple-element.184.refs_0_.refs_1_, bf16[2,768,1536]{2,1,0:T(8,128)(2,1)} %refs_6_.1, ...), custom_call_target="tpu_custom_call" | custom-call | tf_op jit(solution)/shard_map/feed/pallas_call | solution.py:42
  109.6 23.5 %feed_back.2 = (bf16[2,1024,768]{2,1,0:T(8,128)(2,1)}, bf16[1024,1536]{1,0:T(8,128)(2,1)}, bf16[1024,1536]{1,0:T(8,128)(2,1)}, f32[4,768]{1,0:T(4,128)}) custom-call(f32[1024,768]{1,0:T(8,128)} %refs_0_.5, f32[1024,128]{1,0:T(8,128)} %get-tuple-element.188.refs_1_, bf16[1024,768]{1,0:T(8,128)(2,1)} %get-tuple-element.189.refs_2_, ...), custom_call_target="tpu_custom_call" | custom-call | tf_op jit(solution)/shard_map/feed_back/pallas_call | solution.py:42
  133.8 9.7 %mix_back.2 = (bf16[1024,1536]{1,0:T(8,128)(2,1)}, bf16[6,128,256]{2,1,0:T(8,128)(2,1)}) custom-call(bf16[2,1024,768]{2,1,0:T(8,128)(2,1)} %get-tuple-element.195.refs_0_.refs_2_.refs_14_, bf16[2,384,768]{2,1,0:T(8,128)(2,1)} %refs_1_.8, bf16[2,384,768]{2,1,0:T(8,128)(2,1)} %collective-permute-done.3.refs_10_.refs_2_, ...), custom_call_target="tpu_custom_call" | custom-call | tf_op jit(solution)/shard_map/mix_back/pallas_call | solution.py:42
  143.6 9.6 %back_grad.2 = (bf16[2,2,448,384]{3,2,1,0:T(8,128)(2,1)}, bf16[2,2,448,384]{3,2,1,0:T(8,128)(2,1)}, bf16[2,2,448,384]{3,2,1,0:T(8,128)(2,1)}, bf16[2,2,448,384]{3,2,1,0:T(8,128)(2,1)}) custom-call(s32[1,8]{1,0:T(1,128)} %compare_select_fusion.7.refs_0_.refs_1_, bf16[1024,1536]{1,0:T(8,128)(2,1)} %get-tuple-element.203.refs_1_, ...), custom_call_target="tpu_custom_call" | custom-call | tf_op jit(solution)/shard_map/back_grad/pallas_call | solution.py:42
  153.3 9.6 %in_grad.2 = (bf16[2,2,448,384]{3,2,1,0:T(8,128)(2,1)}, bf16[2,2,448,384]{3,2,1,0:T(8,128)(2,1)}, bf16[2,2,448,384]{3,2,1,0:T(8,128)(2,1)}, bf16[2,2,448,384]{3,2,1,0:T(8,128)(2,1)}) custom-call(s32[1,8]{1,0:T(1,128)} %compare_select_fusion.7.refs_0_.refs_1_, ...), custom_call_target="tpu_custom_call", output_to_operand_aliasing={{0}: (5, {}), {1}: (6, {}), {2}: (7, {}), {3}: (8, {})} | custom-call | tf_op jit(solution)/shard_map/in_grad/pallas_call | solution.py:42
  163.4 4.7 %out_grad.2 = (bf16[2,2,448,384]{3,2,1,0:T(8,128)(2,1)}, bf16[2,2,448,384]{3,2,1,0:T(8,128)(2,1)}, bf16[2,2,448,384]{3,2,1,0:T(8,128)(2,1)}, bf16[2,2,448,384]{3,2,1,0:T(8,128)(2,1)}) custom-call(s32[1,8]{1,0:T(1,128)} %compare_select_fusion.7.refs_0_.refs_1_, ...), custom_call_target="tpu_custom_call", output_to_operand_aliasing={{0}: (7, {}), {1}: (8, {}), {2}: (9, {}), {3}: (10, {})} | custom-call | tf_op jit(solution)/shard_map/out_grad/pallas_call | solution.py:42
  168.1 2.7 collective-permute-start.19
  170.9 1.5 collective-permute-start.20
  172.4 2.1 collective-permute-done.14.refs_9_
  174.5 28.4 %attend_back.2 = (bf16[1024,1152]{1,0:T(8,128)(2,1)}, bf16[1024,1152]{1,0:T(8,128)(2,1)}, bf16[1024,768]{1,0:T(8,128)(2,1)}) custom-call(s32[1,8]{1,0:T(1,128)} %compare_select_fusion.7.refs_0_.refs_1_, bf16[1024,768]{1,0:T(8,128)(2,1)} %get-tuple-element.177.refs_1_.refs_6_, bf16[1024,768]{1,0:T(8,128)(2,1)} %get-tuple-element.178.refs_2_.refs_7_, ...), custom_call_target="tpu_custom_call" | custom-call | tf_op jit(solution)/shard_map/attend_back/pallas_call | solution.py:42
  203.2 4.0 fold_split.4
  207.8 9.0 %qkv_grad.2 = (bf16[2,2,144,384]{3,2,1,0:T(8,128)(2,1)}, bf16[2,2,144,384]{3,2,1,0:T(8,128)(2,1)}, bf16[2,2,144,384]{3,2,1,0:T(8,128)(2,1)}, bf16[2,2,144,384]{3,2,1,0:T(8,128)(2,1)}) custom-call(s32[1,8]{1,0:T(1,128)} %compare_select_fusion.7.refs_0_.refs_1_, bf16[1024,768]{1,0:T(8,128)(2,1)} %get-tuple-element.176.refs_0_.refs_11_.refs_1_, ...), custom_call_target="tpu_custom_call" | custom-call | tf_op jit(solution)/shard_map/qkv_grad/pallas_call | solution.py:42
  219.3 1.5 collective-permute-start.22
  220.8 22.9 %feed_back.3 = (bf16[2,1024,768]{2,1,0:T(8,128)(2,1)}, bf16[1024,1536]{1,0:T(8,128)(2,1)}, bf16[1024,1536]{1,0:T(8,128)(2,1)}, f32[4,768]{1,0:T(4,128)}) custom-call(bf16[1024,768]{1,0:T(8,128)(2,1)} %get-tuple-element.214.refs_0_, bf16[1024,768]{1,0:T(8,128)(2,1)} %get-tuple-element.215.refs_1_, f32[1024,128]{1,0:T(8,128)} %get-tuple-element.216.refs_2_, ...), custom_call_target="tpu_custom_call" | custom-call | tf_op jit(solution)/shard_map/feed_back/pallas_call | solution.py:42
  243.9 2.4 fold_split.5
  246.2 1.1 collective-permute-start.25
  247.8 2.0 collective-permute-done.27.refs_4_
  250.0 9.6 %back_grad.3 = (bf16[2,2,448,384]{3,2,1,0:T(8,128)(2,1)}, bf16[2,2,448,384]{3,2,1,0:T(8,128)(2,1)}, bf16[2,2,448,384]{3,2,1,0:T(8,128)(2,1)}, bf16[2,2,448,384]{3,2,1,0:T(8,128)(2,1)}) custom-call(s32[1,8]{1,0:T(1,128)} %compare_select_fusion.7.refs_0_.refs_1_, bf16[1024,1536]{1,0:T(8,128)(2,1)} %get-tuple-element.240.refs_1_, ...), custom_call_target="tpu_custom_call" | custom-call | tf_op jit(solution)/shard_map/back_grad/pallas_call | solution.py:42
  259.6 3.6 fold_near.3
  263.2 1.6 collective-permute-start.28
  265.2 9.5 %in_grad.3 = (bf16[2,2,448,384]{3,2,1,0:T(8,128)(2,1)}, bf16[2,2,448,384]{3,2,1,0:T(8,128)(2,1)}, bf16[2,2,448,384]{3,2,1,0:T(8,128)(2,1)}, bf16[2,2,448,384]{3,2,1,0:T(8,128)(2,1)}) custom-call(s32[1,8]{1,0:T(1,128)} %compare_select_fusion.7.refs_0_.refs_1_, ...), custom_call_target="tpu_custom_call", output_to_operand_aliasing={{0}: (5, {}), {1}: (6, {}), {2}: (7, {}), {3}: (8, {})} | custom-call | tf_op jit(solution)/shard_map/in_grad/pallas_call | solution.py:42
  274.7 4.7 %out_grad.3 = (bf16[2,2,448,384]{3,2,1,0:T(8,128)(2,1)}, bf16[2,2,448,384]{3,2,1,0:T(8,128)(2,1)}, bf16[2,2,448,384]{3,2,1,0:T(8,128)(2,1)}, bf16[2,2,448,384]{3,2,1,0:T(8,128)(2,1)}) custom-call(s32[1,8]{1,0:T(1,128)} %compare_select_fusion.7.refs_0_.refs_1_, ...), custom_call_target="tpu_custom_call", output_to_operand_aliasing={{0}: (7, {}), {1}: (8, {}), {2}: (9, {}), {3}: (10, {})} | custom-call | tf_op jit(solution)/shard_map/out_grad/pallas_call | solution.py:42
  280.9 5.1 %collective-permute-done.28.refs_2_ = bf16[2,592,384]{2,1,0:T(8,128)(2,1)} collective-permute-done((bf16[2,592,384]{2,1,0:T(8,128)(2,1)}, bf16[2,592,384]{2,1,0:T(8,128)(2,1)}, u32[]{:S(2)}, u32[]{:S(2)}) %collective-permute-start.28) | collective-permute-done | bytes 909344 | tf_op jit(solution)/shard_map/ppermute | solution.py:991
  286.0 2.5 fold_far.3
  288.5 10.0 %mix_back.3 = (bf16[1024,1536]{1,0:T(8,128)(2,1)}, bf16[6,128,256]{2,1,0:T(8,128)(2,1)}) custom-call(bf16[2,1024,768]{2,1,0:T(8,128)(2,1)} %get-tuple-element.227.refs_5_.refs_2_.refs_0_.refs_4_, bf16[2,384,768]{2,1,0:T(8,128)(2,1)} %refs_1_.8, bf16[2,384,768]{2,1,0:T(8,128)(2,1)} %collective-permute-done.3.refs_10_.refs_2_, ...), custom_call_target="tpu_custom_call" | custom-call | tf_op jit(solution)/shard_map/mix_back/pallas_call | solution.py:42
  298.6 2.0 collective-permute-done.31.refs_9_
  300.6 19.5 %attend_back.3 = (bf16[1024,1152]{1,0:T(8,128)(2,1)}, bf16[1024,1152]{1,0:T(8,128)(2,1)}) custom-call(s32[1,8]{1,0:T(1,128)} %compare_select_fusion.7.refs_0_.refs_1_, bf16[1024,768]{1,0:T(8,128)(2,1)} %get-tuple-element.165.refs_1_.refs_6_, bf16[1024,768]{1,0:T(8,128)(2,1)} %get-tuple-element.166.refs_2_.refs_7_, ...), custom_call_target="tpu_custom_call" | custom-call | tf_op jit(solution)/shard_map/attend_back/pallas_call | solution.py:42
  320.3 3.9 fold_split.6
  324.2 1.0 collective-permute-start.34
  325.8 2.6 collective-permute-start.37
  328.4 9.0 %qkv_grad.3 = (bf16[2,2,144,384]{3,2,1,0:T(8,128)(2,1)}, bf16[2,2,144,384]{3,2,1,0:T(8,128)(2,1)}, bf16[2,2,144,384]{3,2,1,0:T(8,128)(2,1)}, bf16[2,2,144,384]{3,2,1,0:T(8,128)(2,1)}) custom-call(s32[1,8]{1,0:T(1,128)} %compare_select_fusion.7.refs_0_.refs_1_, bf16[1024,768]{1,0:T(8,128)(2,1)} %refs_1_.9, ...), custom_call_target="tpu_custom_call" | custom-call | tf_op jit(solution)/shard_map/qkv_grad/pallas_call | solution.py:42
  337.4 1.5 collective-permute-start.38
  339.9 2.9 collective-permute-done.34.refs_2_
  342.8 1.1 collective-permute-done.35.refs_4_
  343.8 3.1 fold_near.4
  346.9 1.6 collective-permute-start.42
  348.5 9.7 %input_back.1.refs_5_ = f32[1024,768]{1,0:T(8,128)} custom-call(bf16[1024,1152]{1,0:T(8,128)(2,1)} %get-tuple-element.260.refs_5_.refs_2_.refs_0_, bf16[1024,1152]{1,0:T(8,128)(2,1)} %get-tuple-element.261.refs_1_, bf16[2,3,768,384]{3,2,1,0:T(8,128)(2,1)} %bitcast.26, bf16[2,3,768,384]{3,2,1,0:T(8,128)(2,1)} %collective-permute-done.refs_1_.refs_2_.refs_13_.refs_3_, ...), custom_call_target="tpu_custom_call" | custom-call | tf_op jit(solution)/shard_map/input_back/pallas_call | solution.py:42
  358.2 2.4 fold_split.7
  360.6 1.0 collective-permute-start.40
  362.2 1.4 collective-permute-done.42.refs_2_
  363.6 2.3 fold_far.4
  367.9 2.1 fold_near.5
  370.5 2.6 collective-permute-start.43
  373.1 2.2 settle.3
  375.3 4.6 %collective-permute-done.44.refs_2_ = bf16[2,144,384]{2,1,0:T(8,128)(2,1)} collective-permute-done((bf16[2,144,384]{2,1,0:T(8,128)(2,1)}, bf16[2,144,384]{2,1,0:T(8,128)(2,1)}, u32[]{:S(2)}, u32[]{:S(2)}) %collective-permute-start.44) | collective-permute-done | bytes 221216 | tf_op jit(solution)/shard_map/ppermute | solution.py:991
  379.9 1.8 fold_far.5
  381.7 1.0 collective-permute-start.45
  382.7 6.6 %collective-permute-done.43.refs_2_ = bf16[448,384]{1,0:T(8,128)(2,1)} collective-permute-done((bf16[448,384]{1,0:T(8,128)(2,1)}, bf16[448,384]{1,0:T(8,128)(2,1)}, u32[]{:S(2)}, u32[]{:S(2)}) %collective-permute-start.43) | collective-permute-done | bytes 344096 | tf_op jit(solution)/shard_map/ppermute | solution.py:991
  389.3 2.1 settle.4
  391.3 1.7 settle.5
  393.8 11.9 %all_to_all.8 = f32[32,1,128]{2,1,0:T(1,128)} all-to-all(f32[32,1,128]{2,1,0:T(1,128)S(1)} %broadcast_in_dim.43), channel_id=1, replica_groups=mesh['z'=4,'y'=2,'x'=2,'narrow'=2] {'z','y','x','narrow'}, dimensions={0} | all-to-all | bytes 32768 | tf_op jit(solution)/shard_map/all_to_all | solution.py:1209
  405.7 6.5 %update.1 = (f32[2,3,48,384]{3,2,1,0:T(8,128)}, f32[2,3,48,384]{3,2,1,0:T(8,128)}, f32[2,3,48,384]{3,2,1,0:T(8,128)}, f32[2,24,768]{2,1,0:T(8,128)}, f32[2,24,76...) custom-call(f32[32,128]{1,0:T(8,128)} %bitcast.31, ...), custom_call_target="tpu_custom_call" | custom-call | tf_op jit(solution)/shard_map/update/pallas_call | solution.py:42
  412.2 1.2 slice.14
  (84 shorter events, 17.5 us)
Async XLA Ops:
  0.7 13.7 %collective-permute-start = (bf16[2,3,768,384]{3,2,1,0:T(8,128)(2,1)}, bf16[2,3,768,384]{3,2,1,0:T(8,128)(2,1)}, u32[]{:S(2)}, u32[]{:S(2)}) collective-permute-start(bf16[2,3,768,384]{3,2,1,0:T(8,128)(2,1)} %bitcast.22), channel_id=1, source_target_pairs={{0,1},{1,0},{2,3},{3,2},{4,5},{5,4},{6,7},{7,6},{8,9},{9,8},{10,11... | collective-permute-start | bytes 10616840 | tf_op jit(solution)/shard_map/ppermute | solution.py:880
  1.2 19.8 %collective-permute-start.3 = (bf16[2,384,768]{2,1,0:T(8,128)(2,1)}, bf16[2,384,768]{2,1,0:T(8,128)(2,1)}, u32[]{:S(2)}, u32[]{:S(2)}) collective-permute-start(bf16[2,384,768]{2,1,0:T(8,128)(2,1)} %refs_1_.8), channel_id=1, source_target_pairs={{0,1},{1,0},{2,3},{3,2},{4,5},{5,4},{6,7},{7,6},{8,9},{9,8},{10,11... | collective-permute-start | bytes 3538952 | tf_op jit(solution)/shard_map/ppermute | solution.py:880
  13.9 7.5 %collective-permute-start.2 = (f32[1,3,128,256]{3,2,1,0:T(8,128)}, f32[1,3,128,256]{3,2,1,0:T(8,128)}, u32[]{:S(2)}, u32[]{:S(2)}) collective-permute-start(f32[1,3,128,256]{3,2,1,0:T(8,128)} %get-tuple-element.172), channel_id=1, source_target_pairs={{0,1},{1,0},{2,3},{3,2},{4,5},{5,4},{6,7},{7,6},{8,9},{9,8},{10,11... | collective-permute-start | bytes 1179656 | tf_op jit(solution)/shard_map/ppermute | solution.py:880
  20.8 2.1 collective-permute-start.1
  21.0 16.4 %collective-permute-start.4 = (bf16[2,768,1536]{2,1,0:T(8,128)(2,1)}, bf16[2,768,1536]{2,1,0:T(8,128)(2,1)}, u32[]{:S(2)}, u32[]{:S(2)}) collective-permute-start(bf16[2,768,1536]{2,1,0:T(8,128)(2,1)} %refs_6_.1), channel_id=1, source_target_pairs={{0,1},{1,0},{2,3},{3,2},{4,5},{5,4},{6,7},{7,6},{8,9},{9,8},{10,11... | collective-permute-start | bytes 14155784 | tf_op jit(solution)/shard_map/ppermute | solution.py:880
  22.9 14.4 %collective-permute-start.5 = (bf16[2,1536,768]{2,1,0:T(8,128)(2,1)}, bf16[2,1536,768]{2,1,0:T(8,128)(2,1)}, u32[]{:S(2)}, u32[]{:S(2)}) collective-permute-start(bf16[2,1536,768]{2,1,0:T(8,128)(2,1)} %refs_8_.2), channel_id=1, source_target_pairs={{0,1},{1,0},{2,3},{3,2},{4,5},{5,4},{6,7},{7,6},{8,9},{9,8},{10,11... | collective-permute-start | bytes 14155784 | tf_op jit(solution)/shard_map/ppermute | solution.py:880
  58.4 29.4 %collective-permute-start.10 = (bf16[1024,1536]{1,0:T(8,128)(2,1)}, bf16[1024,1536]{1,0:T(8,128)(2,1)}, u32[]{:S(2)}, u32[]{:S(2)}) collective-permute-start(bf16[1024,1536]{1,0:T(8,128)(2,1)} %get-tuple-element.186), channel_id=1, source_target_pairs={{0,1},{1,0},{2,3},{3,2},{4,5},{5,4},{6,7},{7,6},{8,9},{9,8},{10,11... | collective-permute-start | bytes 9437192 | tf_op jit(solution)/shard_map/ppermute | solution.py:880
  58.8 28.4 %collective-permute-start.7 = (bf16[1024,768]{1,0:T(8,128)(2,1)}, bf16[1024,768]{1,0:T(8,128)(2,1)}, u32[]{:S(2)}, u32[]{:S(2)}) collective-permute-start(bf16[1024,768]{1,0:T(8,128)(2,1)} %refs_1_.9), channel_id=1, source_target_pairs={{0,1},{1,0},{2,3},{3,2},{4,5},{5,4},{6,7},{7,6},{8,9},{9,8},{10,11... | collective-permute-start | bytes 4718600 | tf_op jit(solution)/shard_map/ppermute | solution.py:880
  69.8 2.7 collective-permute-start.6
  70.2 17.5 %collective-permute-start.9 = (bf16[1024,768]{1,0:T(8,128)(2,1)}, bf16[1024,768]{1,0:T(8,128)(2,1)}, u32[]{:S(2)}, u32[]{:S(2)}) collective-permute-start(bf16[1024,768]{1,0:T(8,128)(2,1)} %get-tuple-element.173.refs_0_.refs_1_), channel_id=1, source_target_pairs={{0,1},{1,0},{2,3},{3,2},{4,5},{5,4},{6,7},{7,6},{8,9},{9,8},{10,11... | collective-permute-start | bytes 4718600 | tf_op jit(solution)/shard_map/ppermute | solution.py:880
  70.4 17.0 %collective-permute-start.8 = (bf16[1024,384]{1,0:T(8,128)(2,1)}, bf16[1024,384]{1,0:T(8,128)(2,1)}, u32[]{:S(2)}, u32[]{:S(2)}) collective-permute-start(bf16[1024,384]{1,0:T(8,128)(2,1)} %get-tuple-element.185.refs_5_), channel_id=1, source_target_pairs={{0,1},{1,0},{2,3},{3,2},{4,5},{5,4},{6,7},{7,6},{8,9},{9,8},{10,11... | collective-permute-start | bytes 2359304 | tf_op jit(solution)/shard_map/ppermute | solution.py:880
  72.5 15.3 %collective-permute-start.11 = (bf16[1024,768]{1,0:T(8,128)(2,1)}, bf16[1024,768]{1,0:T(8,128)(2,1)}, u32[]{:S(2)}, u32[]{:S(2)}) collective-permute-start(bf16[1024,768]{1,0:T(8,128)(2,1)} %get-tuple-element.176.refs_0_.refs_11_.refs_1_), channel_id=1, source_target_pairs={{0,1},{1,0},{2,3},{3,2},{4,5},{5,4},{6,7},{7,6},{8,9},{9,8},{10,11... | collective-permute-start | bytes 4718600 | tf_op jit(solution)/shard_map/ppermute | solution.py:880
  87.2 22.4 %collective-permute-start.13 = (bf16[1024,768]{1,0:T(8,128)(2,1)}, bf16[1024,768]{1,0:T(8,128)(2,1)}, u32[]{:S(2)}, u32[]{:S(2)}) collective-permute-start(bf16[1024,768]{1,0:T(8,128)(2,1)} %get-tuple-element.184.refs_0_.refs_1_), channel_id=1, source_target_pairs={{0,1},{1,0},{2,3},{3,2},{4,5},{5,4},{6,7},{7,6},{8,9},{9,8},{10,11... | collective-permute-start | bytes 4718600 | tf_op jit(solution)/shard_map/ppermute | solution.py:880
  87.4 22.1 %collective-permute-start.12 = (bf16[1024,384]{1,0:T(8,128)(2,1)}, bf16[1024,384]{1,0:T(8,128)(2,1)}, u32[]{:S(2)}, u32[]{:S(2)}) collective-permute-start(bf16[1024,384]{1,0:T(8,128)(2,1)} %get-tuple-element.194.refs_5_), channel_id=1, source_target_pairs={{0,1},{1,0},{2,3},{3,2},{4,5},{5,4},{6,7},{7,6},{8,9},{9,8},{10,11... | collective-permute-start | bytes 2359304 | tf_op jit(solution)/shard_map/ppermute | solution.py:880
  133.0 10.4 %collective-permute-start.15 = (bf16[2,1024,768]{2,1,0:T(8,128)(2,1)}, bf16[2,1024,768]{2,1,0:T(8,128)(2,1)}, u32[]{:S(2)}, u32[]{:S(2)}) collective-permute-start(bf16[2,1024,768]{2,1,0:T(8,128)(2,1)} %get-tuple-element.195.refs_0_.refs_2_.refs_14_), channel_id=1, source_target_pairs={{0,1},{1,0},{2,3},{3,2},{4,5},{5,4},{6,7},{7,6},{8,9},{9,8},{10,11... | collective-permute-start | bytes 9437192 | tf_op jit(solution)/shard_map/ppermute | solution.py:880
  133.2 10.4 %collective-permute-start.17 = (bf16[1024,1536]{1,0:T(8,128)(2,1)}, bf16[1024,1536]{1,0:T(8,128)(2,1)}, u32[]{:S(2)}, u32[]{:S(2)}) collective-permute-start(bf16[1024,1536]{1,0:T(8,128)(2,1)} %get-tuple-element.204), channel_id=1, source_target_pairs={{0,1},{1,0},{2,3},{3,2},{4,5},{5,4},{6,7},{7,6},{8,9},{9,8},{10,11... | collective-permute-start | bytes 9437192 | tf_op jit(solution)/shard_map/ppermute | solution.py:880
  133.6 19.6 %collective-permute-start.16 = (bf16[1024,1536]{1,0:T(8,128)(2,1)}, bf16[1024,1536]{1,0:T(8,128)(2,1)}, u32[]{:S(2)}, u32[]{:S(2)}) collective-permute-start(bf16[1024,1536]{1,0:T(8,128)(2,1)} %get-tuple-element.202), channel_id=1, source_target_pairs={{0,1},{1,0},{2,3},{3,2},{4,5},{5,4},{6,7},{7,6},{8,9},{9,8},{10,11... | collective-permute-start | bytes 9437192 | tf_op jit(solution)/shard_map/ppermute | solution.py:880
  168.1 34.9 %collective-permute-start.19 = (bf16[2,2,448,384]{3,2,1,0:T(8,128)(2,1)}, bf16[2,2,448,384]{3,2,1,0:T(8,128)(2,1)}, u32[]{:S(2)}, u32[]{:S(2)}) collective-permute-start(bf16[2,2,448,384]{3,2,1,0:T(8,128)(2,1)} %get-tuple-element.222), channel_id=1, source_target_pairs={{0,2},{2,0},{1,3},{3,1},{4,6},{6,4},{5,7},{7,5},{8,10},{10,8},{9,1... | collective-permute-start | bytes 4128776 | tf_op jit(solution)/shard_map/ppermute | solution.py:880
  170.9 32.4 %collective-permute-start.20 = (bf16[2,2,448,384]{3,2,1,0:T(8,128)(2,1)}, bf16[2,2,448,384]{3,2,1,0:T(8,128)(2,1)}, u32[]{:S(2)}, u32[]{:S(2)}) collective-permute-start(bf16[2,2,448,384]{3,2,1,0:T(8,128)(2,1)} %get-tuple-element.224), channel_id=1, source_target_pairs={{0,4},{4,0},{1,5},{5,1},{2,6},{6,2},{3,7},{7,3},{8,12},{12,8},{9,1... | collective-permute-start | bytes 4128776 | tf_op jit(solution)/shard_map/ppermute | solution.py:880
  172.4 2.1 collective-permute-start.14
  202.8 4.9 %collective-permute-start.18 = (bf16[1024,1152]{1,0:T(8,128)(2,1)}, bf16[1024,1152]{1,0:T(8,128)(2,1)}, u32[]{:S(2)}, u32[]{:S(2)}) collective-permute-start(bf16[1024,1152]{1,0:T(8,128)(2,1)} %get-tuple-element.221), channel_id=1, source_target_pairs={{0,1},{1,0},{2,3},{3,2},{4,5},{5,4},{6,7},{7,6},{8,9},{9,8},{10,11... | collective-permute-start | bytes 7077896 | tf_op jit(solution)/shard_map/ppermute | solution.py:880
  216.8 27.1 %collective-permute-start.23 = (bf16[2,2,144,384]{3,2,1,0:T(8,128)(2,1)}, bf16[2,2,144,384]{3,2,1,0:T(8,128)(2,1)}, u32[]{:S(2)}, u32[]{:S(2)}) collective-permute-start(bf16[2,2,144,384]{3,2,1,0:T(8,128)(2,1)} %get-tuple-element.233), channel_id=1, source_target_pairs={{0,2},{2,0},{1,3},{3,1},{4,6},{6,4},{5,7},{7,5},{8,10},{10,8},{9,1... | collective-permute-start | bytes 1327112 | tf_op jit(solution)/shard_map/ppermute | solution.py:880
  217.3 26.5 %collective-permute-start.24 = (bf16[2,2,144,384]{3,2,1,0:T(8,128)(2,1)}, bf16[2,2,144,384]{3,2,1,0:T(8,128)(2,1)}, u32[]{:S(2)}, u32[]{:S(2)}) collective-permute-start(bf16[2,2,144,384]{3,2,1,0:T(8,128)(2,1)} %get-tuple-element.235), channel_id=1, source_target_pairs={{0,4},{4,0},{1,5},{5,1},{2,6},{6,2},{3,7},{7,3},{8,12},{12,8},{9,1... | collective-permute-start | bytes 1327112 | tf_op jit(solution)/shard_map/ppermute | solution.py:880
  218.3 41.2 %collective-permute-start.21 = (bf16[2,448,384]{2,1,0:T(8,128)(2,1)}, bf16[2,448,384]{2,1,0:T(8,128)(2,1)}, u32[]{:S(2)}, u32[]{:S(2)}) collective-permute-start(bf16[2,448,384]{2,1,0:T(8,128)(2,1)} %get-tuple-element.230), channel_id=1, source_target_pairs={{0,4},{4,0},{1,5},{5,1},{2,6},{6,2},{3,7},{7,3},{8,12},{12,8},{9,1... | collective-permute-start | bytes 2064392 | tf_op jit(solution)/shard_map/ppermute | solution.py:880
  219.3 40.2 %collective-permute-start.22 = (bf16[2,448,384]{2,1,0:T(8,128)(2,1)}, bf16[2,448,384]{2,1,0:T(8,128)(2,1)}, u32[]{:S(2)}, u32[]{:S(2)}) collective-permute-start(bf16[2,448,384]{2,1,0:T(8,128)(2,1)} %get-tuple-element.232), channel_id=1, source_target_pairs={{0,2},{2,0},{1,3},{3,1},{4,6},{6,4},{5,7},{7,5},{8,10},{10,8},{9,1... | collective-permute-start | bytes 2064392 | tf_op jit(solution)/shard_map/ppermute | solution.py:880
  243.8 6.1 %collective-permute-start.27 = (bf16[2,1024,768]{2,1,0:T(8,128)(2,1)}, bf16[2,1024,768]{2,1,0:T(8,128)(2,1)}, u32[]{:S(2)}, u32[]{:S(2)}) collective-permute-start(bf16[2,1024,768]{2,1,0:T(8,128)(2,1)} %get-tuple-element.227.refs_5_.refs_2_.refs_0_.refs_4_), channel_id=1, source_target_pairs={{0,1},{1,0},{2,3},{3,2},{4,5},{5,4},{6,7},{7,6},{8,9},{9,8},{10,11... | collective-permute-start | bytes 9437192 | tf_op jit(solution)/shard_map/ppermute | solution.py:880
  246.2 13.4 %collective-permute-start.25 = (bf16[2,144,384]{2,1,0:T(8,128)(2,1)}, bf16[2,144,384]{2,1,0:T(8,128)(2,1)}, u32[]{:S(2)}, u32[]{:S(2)}) collective-permute-start(bf16[2,144,384]{2,1,0:T(8,128)(2,1)} %get-tuple-element.237), channel_id=1, source_target_pairs={{0,4},{4,0},{1,5},{5,1},{2,6},{6,2},{3,7},{7,3},{8,12},{12,8},{9,1... | collective-permute-start | bytes 663560 | tf_op jit(solution)/shard_map/ppermute | solution.py:880
  247.3 12.3 %collective-permute-start.26 = (bf16[2,144,384]{2,1,0:T(8,128)(2,1)}, bf16[2,144,384]{2,1,0:T(8,128)(2,1)}, u32[]{:S(2)}, u32[]{:S(2)}) collective-permute-start(bf16[2,144,384]{2,1,0:T(8,128)(2,1)} %get-tuple-element.239), channel_id=1, source_target_pairs={{0,2},{2,0},{1,3},{3,1},{4,6},{6,4},{5,7},{7,5},{8,10},{10,8},{9,1... | collective-permute-start | bytes 663560 | tf_op jit(solution)/shard_map/ppermute | solution.py:880
  249.8 15.3 %collective-permute-start.30 = (bf16[1024,1536]{1,0:T(8,128)(2,1)}, bf16[1024,1536]{1,0:T(8,128)(2,1)}, u32[]{:S(2)}, u32[]{:S(2)}) collective-permute-start(bf16[1024,1536]{1,0:T(8,128)(2,1)} %get-tuple-element.247), channel_id=1, source_target_pairs={{0,1},{1,0},{2,3},{3,2},{4,5},{5,4},{6,7},{7,6},{8,9},{9,8},{10,11... | collective-permute-start | bytes 9437192 | tf_op jit(solution)/shard_map/ppermute | solution.py:880
  259.6 5.2 %copy-start.1 = (f32[4,768]{1,0:T(4,128)S(1)}, f32[4,768]{1,0:T(4,128)}, u32[]{:S(2)}) copy-start(f32[4,768]{1,0:T(4,128)} %get-tuple-element.245) | copy-start | bytes 36868
  259.6 5.2 %copy-start.2 = (f32[4,768]{1,0:T(4,128)S(1)}, f32[4,768]{1,0:T(4,128)}, u32[]{:S(2)}) copy-start(f32[4,768]{1,0:T(4,128)} %get-tuple-element.244) | copy-start | bytes 36868
  263.2 22.8 %collective-permute-start.28 = (bf16[2,592,384]{2,1,0:T(8,128)(2,1)}, bf16[2,592,384]{2,1,0:T(8,128)(2,1)}, u32[]{:S(2)}, u32[]{:S(2)}) collective-permute-start(bf16[2,592,384]{2,1,0:T(8,128)(2,1)} %get-tuple-element.243), channel_id=1, source_target_pairs={{0,8},{8,0},{16,24},{24,16},{1,9},{9,1},{17,25},{25,17},{2,10},{10... | collective-permute-start | bytes 2727944 | tf_op jit(solution)/shard_map/ppermute | solution.py:991
  265.0 9.7 %copy-start = (f32[16,8,128]{2,1,0:T(8,128)}, f32[16,8,128]{2,1,0:T(8,128)S(1)}, u32[]{:S(2)}) copy-start(f32[16,8,128]{2,1,0:T(8,128)S(1)} %pad.4.refs_5_) | copy-start | bytes 196612
  265.0 9.7 %collective-permute-start.29 = (f32[16,8,128]{2,1,0:T(8,128)S(1)}, f32[16,8,128]{2,1,0:T(8,128)}, u32[]{:S(2)}, u32[]{:S(2)}) collective-permute-start(f32[16,8,128]{2,1,0:T(8,128)S(1)} %pad.4.refs_5_), channel_id=1, source_target_pairs={{0,1},{1,0},{2,3},{3,2},{4,5},{5,4},{6,7},{7,6},{8,9},{9,8},{10,11... | collective-permute-start | bytes 196616 | tf_op jit(solution)/shard_map/ppermute | solution.py:880
  279.4 40.9 %collective-permute-start.32 = (bf16[2,2,448,384]{3,2,1,0:T(8,128)(2,1)}, bf16[2,2,448,384]{3,2,1,0:T(8,128)(2,1)}, u32[]{:S(2)}, u32[]{:S(2)}) collective-permute-start(bf16[2,2,448,384]{3,2,1,0:T(8,128)(2,1)} %get-tuple-element.262), channel_id=1, source_target_pairs={{0,2},{2,0},{1,3},{3,1},{4,6},{6,4},{5,7},{7,5},{8,10},{10,8},{9,1... | collective-permute-start | bytes 4128776 | tf_op jit(solution)/shard_map/ppermute | solution.py:880
  279.9 40.4 %collective-permute-start.33 = (bf16[2,2,448,384]{3,2,1,0:T(8,128)(2,1)}, bf16[2,2,448,384]{3,2,1,0:T(8,128)(2,1)}, u32[]{:S(2)}, u32[]{:S(2)}) collective-permute-start(bf16[2,2,448,384]{3,2,1,0:T(8,128)(2,1)} %get-tuple-element.264), channel_id=1, source_target_pairs={{0,4},{4,0},{1,5},{5,1},{2,6},{6,2},{3,7},{7,3},{8,12},{12,8},{9,1... | collective-permute-start | bytes 4128776 | tf_op jit(solution)/shard_map/ppermute | solution.py:880
  298.5 2.1 collective-permute-start.31
  320.1 8.3 %collective-permute-start.36 = (bf16[1024,1152]{1,0:T(8,128)(2,1)}, bf16[1024,1152]{1,0:T(8,128)(2,1)}, u32[]{:S(2)}, u32[]{:S(2)}) collective-permute-start(bf16[1024,1152]{1,0:T(8,128)(2,1)} %get-tuple-element.261.refs_1_), channel_id=1, source_target_pairs={{0,1},{1,0},{2,3},{3,2},{4,5},{5,4},{6,7},{7,6},{8,9},{9,8},{10,11... | collective-permute-start | bytes 7077896 | tf_op jit(solution)/shard_map/ppermute | solution.py:880
  324.2 18.6 %collective-permute-start.34 = (bf16[2,448,384]{2,1,0:T(8,128)(2,1)}, bf16[2,448,384]{2,1,0:T(8,128)(2,1)}, u32[]{:S(2)}, u32[]{:S(2)}) collective-permute-start(bf16[2,448,384]{2,1,0:T(8,128)(2,1)} %get-tuple-element.266), channel_id=1, source_target_pairs={{0,4},{4,0},{1,5},{5,1},{2,6},{6,2},{3,7},{7,3},{8,12},{12,8},{9,1... | collective-permute-start | bytes 2064392 | tf_op jit(solution)/shard_map/ppermute | solution.py:880
  325.2 18.6 %collective-permute-start.35 = (bf16[2,448,384]{2,1,0:T(8,128)(2,1)}, bf16[2,448,384]{2,1,0:T(8,128)(2,1)}, u32[]{:S(2)}, u32[]{:S(2)}) collective-permute-start(bf16[2,448,384]{2,1,0:T(8,128)(2,1)} %get-tuple-element.268), channel_id=1, source_target_pairs={{0,2},{2,0},{1,3},{3,1},{4,6},{6,4},{5,7},{7,5},{8,10},{10,8},{9,1... | collective-permute-start | bytes 2064392 | tf_op jit(solution)/shard_map/ppermute | solution.py:880
  325.8 47.3 %collective-permute-start.37 = (bf16[592,384]{1,0:T(8,128)(2,1)}, bf16[592,384]{1,0:T(8,128)(2,1)}, u32[]{:S(2)}, u32[]{:S(2)}) collective-permute-start(bf16[592,384]{1,0:T(8,128)(2,1)} %get-tuple-element.271), channel_id=1, source_target_pairs={{0,16},{8,24},{16,0},{24,8},{1,17},{9,25},{17,1},{25,9},{2,18},{10... | collective-permute-start | bytes 1363976 | tf_op jit(solution)/shard_map/ppermute | solution.py:991
  337.4 20.9 %collective-permute-start.38 = (bf16[2,2,144,384]{3,2,1,0:T(8,128)(2,1)}, bf16[2,2,144,384]{3,2,1,0:T(8,128)(2,1)}, u32[]{:S(2)}, u32[]{:S(2)}) collective-permute-start(bf16[2,2,144,384]{3,2,1,0:T(8,128)(2,1)} %get-tuple-element.272), channel_id=1, source_target_pairs={{0,2},{2,0},{1,3},{3,1},{4,6},{6,4},{5,7},{7,5},{8,10},{10,8},{9,1... | collective-permute-start | bytes 1327112 | tf_op jit(solution)/shard_map/ppermute | solution.py:880
  338.9 19.4 %collective-permute-start.39 = (bf16[2,2,144,384]{3,2,1,0:T(8,128)(2,1)}, bf16[2,2,144,384]{3,2,1,0:T(8,128)(2,1)}, u32[]{:S(2)}, u32[]{:S(2)}) collective-permute-start(bf16[2,2,144,384]{3,2,1,0:T(8,128)(2,1)} %get-tuple-element.274), channel_id=1, source_target_pairs={{0,4},{4,0},{1,5},{5,1},{2,6},{6,2},{3,7},{7,3},{8,12},{12,8},{9,1... | collective-permute-start | bytes 1327112 | tf_op jit(solution)/shard_map/ppermute | solution.py:880
  346.9 16.7 %collective-permute-start.42 = (bf16[2,448,384]{2,1,0:T(8,128)(2,1)}, bf16[2,448,384]{2,1,0:T(8,128)(2,1)}, u32[]{:S(2)}, u32[]{:S(2)}) collective-permute-start(bf16[2,448,384]{2,1,0:T(8,128)(2,1)} %get-tuple-element.279), channel_id=1, source_target_pairs={{0,8},{8,0},{16,24},{24,16},{1,9},{9,1},{17,25},{25,17},{2,10},{10... | collective-permute-start | bytes 2064392 | tf_op jit(solution)/shard_map/ppermute | solution.py:991
  360.6 6.3 %collective-permute-start.40 = (bf16[2,144,384]{2,1,0:T(8,128)(2,1)}, bf16[2,144,384]{2,1,0:T(8,128)(2,1)}, u32[]{:S(2)}, u32[]{:S(2)}) collective-permute-start(bf16[2,144,384]{2,1,0:T(8,128)(2,1)} %get-tuple-element.276), channel_id=1, source_target_pairs={{0,4},{4,0},{1,5},{5,1},{2,6},{6,2},{3,7},{7,3},{8,12},{12,8},{9,1... | collective-permute-start | bytes 663560 | tf_op jit(solution)/shard_map/ppermute | solution.py:880
  361.6 6.2 %collective-permute-start.41 = (bf16[2,144,384]{2,1,0:T(8,128)(2,1)}, bf16[2,144,384]{2,1,0:T(8,128)(2,1)}, u32[]{:S(2)}, u32[]{:S(2)}) collective-permute-start(bf16[2,144,384]{2,1,0:T(8,128)(2,1)} %get-tuple-element.278), channel_id=1, source_target_pairs={{0,2},{2,0},{1,3},{3,1},{4,6},{6,4},{5,7},{7,5},{8,10},{10,8},{9,1... | collective-permute-start | bytes 663560 | tf_op jit(solution)/shard_map/ppermute | solution.py:880
  370.0 9.9 %collective-permute-start.44 = (bf16[2,144,384]{2,1,0:T(8,128)(2,1)}, bf16[2,144,384]{2,1,0:T(8,128)(2,1)}, u32[]{:S(2)}, u32[]{:S(2)}) collective-permute-start(bf16[2,144,384]{2,1,0:T(8,128)(2,1)} %get-tuple-element.284), channel_id=1, source_target_pairs={{0,8},{8,0},{16,24},{24,16},{1,9},{9,1},{17,25},{25,17},{2,10},{10... | collective-permute-start | bytes 663560 | tf_op jit(solution)/shard_map/ppermute | solution.py:991
  370.5 18.8 %collective-permute-start.43 = (bf16[448,384]{1,0:T(8,128)(2,1)}, bf16[448,384]{1,0:T(8,128)(2,1)}, u32[]{:S(2)}, u32[]{:S(2)}) collective-permute-start(bf16[448,384]{1,0:T(8,128)(2,1)} %get-tuple-element.283), channel_id=1, source_target_pairs={{0,16},{8,24},{16,0},{24,8},{1,17},{9,25},{17,1},{25,9},{2,18},{10... | collective-permute-start | bytes 1032200 | tf_op jit(solution)/shard_map/ppermute | solution.py:991
  381.7 11.4 %copy-start.3 = (f32[8,128]{1,0:T(8,128)S(1)}, f32[8,128]{1,0:T(8,128)}, u32[]{:S(2)}) copy-start(f32[8,128]{1,0:T(8,128)} %get-tuple-element.282) | copy-start | bytes 12292
  381.7 9.7 %collective-permute-start.45 = (bf16[144,384]{1,0:T(8,128)(2,1)}, bf16[144,384]{1,0:T(8,128)(2,1)}, u32[]{:S(2)}, u32[]{:S(2)}) collective-permute-start(bf16[144,384]{1,0:T(8,128)(2,1)} %get-tuple-element.288), channel_id=1, source_target_pairs={{0,16},{8,24},{16,0},{24,8},{1,17},{9,25},{17,1},{25,9},{2,18},{10... | collective-permute-start | bytes 331784 | tf_op jit(solution)/shard_map/ppermute | solution.py:991

commit v4 on v3

--- a/solution.py
+++ b/solution.py
@@ -13,6 +13,8 @@
 LAYERS = 2
 CHUNK = 256
 FF_BLOCK = 768
+FF_CHUNK = 256
+MIX_CHUNK = 512
 VMEM = 64 * 1024 * 1024 - 128 * 1024
 FOLD_WEIGHT = 1e12
 
@@ -80,6 +82,21 @@
 IN_SMEM = pl.BlockSpec(memory_space=pltpu.SMEM)
 
 
+ANY = pl.BlockSpec(memory_space=pl.ANY)
+
+
+class Copies:
+    def __init__(self, semaphores):
+        self.semaphores = semaphores
+        self.count = 0
+
+    def start(self, source, target):
+        copy = pltpu.make_async_copy(source, target, self.semaphores.at[self.count])
+        self.count += 1
+        copy.start()
+        return copy
+
+
 def whole(array_shape):
     return pl.BlockSpec(array_shape, lambda *_: (0,) * len(array_shape))
 
@@ -113,7 +130,7 @@
 
 def tables_kernel(here_ref, cos_ref, sin_ref, live_ref):
     rows = cos_ref.shape[0]
-    core, first_len, second_len = (here_ref[0, n] for n in (4, 5, 6))
+    core, first_len, second_len = lax.axis_index("narrow"), here_ref[0, 0], here_ref[0, 1]
     index = core * rows + lax.broadcasted_iota(jnp.int32, (rows, 128), 0)
     in_first = index < first_len
     in_second = jnp.logical_and(index >= first_len, index < first_len + second_len)
@@ -131,6 +148,11 @@
     live_ref[...] = live
 
 
+def hands_on(lengths_ref, rows, core):
+    goes_on = jnp.logical_and(lengths_ref[0, 0] > rows, lax.axis_index("narrow") == core)
+    return jnp.where(goes_on, 1.0, 0.0)
+
+
 def tables(here, rows):
     return run(
         tables_kernel, (here,), [IN_SMEM], [whole((rows, 128))] * 3,
@@ -222,7 +244,7 @@
 
     @pl.when(pl.program_id(0) == 0)
     def _():
-        carry = here_ref[0, 7].astype(F32) * here_ref[0, 4].astype(F32)
+        carry = hands_on(here_ref, rows * pl.num_programs(0), 1)
         state[:pairs] = kvo_ref[...] * carry
         state[pairs:] = kvp_ref[...] * carry
 
@@ -311,6 +333,89 @@
 
 
 def feed_kernel(
+    layer,
+    x_ref, wio_ref, wip_ref, wbo_ref, wbp_ref, norm_ref,
+    ho_ref, hp_ref, slope_ref, out_ref, xhat_ref, rstd_ref,
+    x, w_in, w_back, h, slope, acc, out, xhat, rstd, semaphores,
+):
+    rows = x.shape[0]
+    blocks = w_in.shape[0] // 2
+    width = FF_BLOCK
+    copies = Copies(semaphores)
+    waits = [copies.start(x_ref, x)]
+    for n in range(2 * blocks):
+        wi, wb = (wio_ref, wbo_ref) if n < blocks else (wip_ref, wbp_ref)
+        at = pl.ds(n % blocks * width, width)
+        waits.append(copies.start(wi.at[layer, :, at], w_in.at[n]))
+        waits.append(copies.start(wb.at[layer, at, :], w_back.at[n]))
+    waits.pop(0).wait()
+    outgoing = []
+    for n in range(2 * blocks):
+        waits.pop(0).wait()
+        waits.pop(0).wait()
+        for i in range(rows // FF_CHUNK):
+            at = slice(i * FF_CHUNK, i * FF_CHUNK + FF_CHUNK)
+            act, deriv = gelu_both(dot(x[at, :], w_in[n]))
+            act = act.astype(BF16)
+            h[n, at, :] = act
+            slope[n, at, :] = deriv.astype(BF16)
+            base = x[at, :].astype(F32) if n == 0 else acc[at, :]
+            total = base + dot(act, w_back[n])
+            if n < 2 * blocks - 1:
+                acc[at, :] = total
+                continue
+            y, x_hat, inverse = norm_rows(total, norm_ref[2:3], norm_ref[3:4])
+            out[at, :] = y.astype(out.dtype)
+            xhat[at, :] = x_hat.astype(BF16)
+            rstd[at, :] = jnp.broadcast_to(inverse, (FF_CHUNK, 128))
+            here = pl.ds(i * FF_CHUNK, FF_CHUNK)
+            for source, target in ((out, out_ref), (xhat, xhat_ref), (rstd, rstd_ref)):
+                outgoing.append(copies.start(source.at[here, :], target.at[here, :]))
+        part = pl.ds(n % blocks * width, width)
+        target = ho_ref if n < blocks else hp_ref
+        outgoing.append(copies.start(h.at[n], target.at[:, part]))
+        outgoing.append(copies.start(slope.at[n], slope_ref.at[:, pl.ds(n * width, width)]))
+    for copy in outgoing:
+        copy.wait()
+
+
+def feed(x, wi_own, wi_peer, wb_own, wb_peer, layer, norms, dtype, after=()):
+    rows, width = x.shape
+    half = wi_own.shape[2]
+    blocks = half // FF_BLOCK
+    copies = 1 + 8 * blocks + 3 * (rows // FF_CHUNK)
+    return run(
+        functools.partial(feed_kernel, layer),
+        (x, wi_own, wi_peer, wb_own, wb_peer, norms),
+        [ANY] * 5 + [layer_spec(norms, layer)],
+        [ANY] * 6,
+        [
+            shape((rows, half), BF16),
+            shape((rows, half), BF16),
+            shape((rows, 2 * half), BF16),
+            shape((rows, width), dtype),
+            shape((rows, width), BF16),
+            shape((rows, 128), F32),
+        ],
+        (1,),
+        "feed",
+        [
+            pltpu.VMEM((rows, width), BF16),
+            pltpu.VMEM((2 * blocks, width, FF_BLOCK), BF16),
+            pltpu.VMEM((2 * blocks, FF_BLOCK, width), BF16),
+            pltpu.VMEM((2 * blocks, rows, FF_BLOCK), BF16),
+            pltpu.VMEM((2 * blocks, rows, FF_BLOCK), BF16),
+            pltpu.VMEM((rows, width), F32),
+            pltpu.VMEM((rows, width), dtype),
+            pltpu.VMEM((rows, width), BF16),
+            pltpu.VMEM((rows, 128), F32),
+            pltpu.SemaphoreType.DMA((copies,)),
+        ],
+        after,
+    )
+
+
+def feed_grid_kernel(
     x_ref, wio_ref, wip_ref, wbo_ref, wbp_ref, norm_ref,
     ho_ref, hp_ref, slope_ref, out_ref, xhat_ref, rstd_ref,
     acc,
@@ -364,14 +469,14 @@
     return own, peer, w_in, w_back
 
 
-def feed(x, wi_own, wi_peer, wb_own, wb_peer, layer, norms, dtype, after=()):
+def feed_grid(x, wi_own, wi_peer, wb_own, wb_peer, layer, norms, dtype, after=()):
     rows, width = x.shape
     half = wi_own.shape[2]
     blocks = half // FF_BLOCK
     own, peer, w_in, w_back = ff_specs(layer, width, blocks)
     full = whole((rows, width))
     return run(
-        feed_kernel,
+        feed_grid_kernel,
         (x, wi_own, wi_peer, wb_own, wb_peer, norms),
         [full, *w_in, *w_back, layer_spec(norms, layer)],
         [
@@ -405,70 +510,83 @@
 
 
 def feed_back_kernel(
-    up_ref, live_ref, xh2_ref, rs2_ref, xh1_ref, rs1_ref, slope_ref,
-    wio_ref, wip_ref, wbo_ref, wbp_ref, norm_ref,
-    gfb_ref, gho_ref, ghp_ref, ng_ref,
-    acc,
+    layer, masked, *refs,
 ):
-    step, steps = pl.program_id(0), pl.num_programs(0)
-    rows, width = up_ref.shape
-    tiles = width // 128
-
-    def chunk(i):
-        return pl.ds(pl.multiple_of(i * CHUNK, CHUNK), CHUNK)
-
-    def wide(ref, at):
-        return jnp.concatenate([ref[at, :]] * tiles, axis=1)
-
-    @pl.when(step == 0)
-    def _():
-        ng_ref[...] = jnp.zeros_like(ng_ref)
-
-        def part(i, _):
-            at = chunk(i)
-            y = up_ref[at, :].astype(F32)
-            if live_ref is not None:
-                y = y * wide(live_ref, at)
+    count = 12 if masked else 11
+    up_ref, *refs_in = refs[:count]
+    live_ref = refs_in.pop(0) if masked else None
+    xh2_ref, rs2_ref, xh1_ref, rs1_ref, slope_ref, wio_ref, wip_ref, wbo_ref, wbp_ref, norm_ref = refs_in
+    gfb_ref, gho_ref, ghp_ref, ng_ref = refs[count : count + 4]
+    up, live, xh2, rs2, xh1, rs1, slope, w_in, w_back, gfb, gh, acc, semaphores = refs[count + 4 :]
+    rows, width = up.shape
+    blocks = w_in.shape[0] // 2
+    copies = Copies(semaphores)
+    chunks = [pl.ds(i * FF_CHUNK, FF_CHUNK) for i in range(rows // FF_CHUNK)]
+
+    def wide(value):
+        return jnp.concatenate([value] * (width // 128), axis=1)
+
+    first = []
+    for at in chunks:
+        pairs = [(up_ref, up), (xh2_ref, xh2), (rs2_ref, rs2)]
+        if masked:
+            pairs.append((live_ref, live))
+        first.append([copies.start(source.at[at, :], target.at[at, :]) for source, target in pairs])
+    waits = []
+    for n in range(2 * blocks):
+        wi, wb = (wio_ref, wbo_ref) if n < blocks else (wip_ref, wbp_ref)
+        at = pl.ds(n % blocks * FF_BLOCK, FF_BLOCK)
+        waits.append(copies.start(wb.at[layer, at, :], w_back.at[n]))
+        waits.append(copies.start(slope_ref.at[:, pl.ds(n * FF_BLOCK, FF_BLOCK)], slope.at[n]))
+        waits.append(copies.start(wi.at[layer, :, at], w_in.at[n]))
+    late = [copies.start(xh1_ref, xh1), copies.start(rs1_ref, rs1)]
+    sums = [None] * 4
+
+    def add(kind, value):
+        sums[kind] = value if sums[kind] is None else sums[kind] + value
+
+    outgoing = []
+    for at, arrivals in zip(chunks, first):
+        for copy in arrivals:
+            copy.wait()
+        y = up[at, :].astype(F32)
+        if masked:
+            y = y * wide(live[at, :])
+        grad, gain_grad, shift_grad = norm_back(
+            y, xh2[at, :].astype(F32), wide(rs2[at, :]), norm_ref[2:3]
+        )
+        acc[at, :] = grad
+        gfb[0, at, :] = grad.astype(BF16)
+        add(2, gain_grad)
+        add(3, shift_grad)
+    outgoing.append(copies.start(gfb.at[0], gfb_ref.at[0]))
+    for n in range(2 * blocks):
+        for _ in range(3):
+            waits.pop(0).wait()
+        if n == 2 * blocks - 1:
+            for copy in late:
+                copy.wait()
+        for at in chunks:
+            act = dot_nt(gfb[0, at, :], w_back[n])
+            gh_part = (act * slope[n, at, :].astype(F32)).astype(BF16)
+            gh[n, at, :] = gh_part
+            total = acc[at, :] + dot_nt(gh_part, w_in[n])
+            if n < 2 * blocks - 1:
+                acc[at, :] = total
+                continue
             grad, gain_grad, shift_grad = norm_back(
-                y, xh2_ref[at, :].astype(F32), wide(rs2_ref, at), norm_ref[2:3]
+                total, xh1[at, :].astype(F32), wide(rs1[at, :]), norm_ref[0:1]
             )
-            acc[at, :] = grad
-            gfb_ref[0, at, :] = grad.astype(BF16)
-            ng_ref[2:3] += gain_grad
-            ng_ref[3:4] += shift_grad
-            return 0
-
-        lax.fori_loop(0, rows // CHUNK, part, 0)
-
-    def side(w_in, w_back, gh_ref):
-        for i in range(rows // CHUNK):
-            at = slice(i * CHUNK, i * CHUNK + CHUNK)
-            act = dot_nt(gfb_ref[0, at, :], w_back[...])
-            gh = (act * slope_ref[at, :].astype(F32)).astype(BF16)
-            gh_ref[at, :] = gh
-            acc[at, :] += dot_nt(gh, w_in[...])
-
-    @pl.when(step < steps // 2)
-    def _():
-        side(wio_ref, wbo_ref, gho_ref)
-
-    @pl.when(step >= steps // 2)
-    def _():
-        side(wip_ref, wbp_ref, ghp_ref)
-
-    @pl.when(step == steps - 1)
-    def _():
-        def part(i, _):
-            at = chunk(i)
-            grad, gain_grad, shift_grad = norm_back(
-                acc[at, :], xh1_ref[at, :].astype(F32), wide(rs1_ref, at), norm_ref[0:1]
-            )
-            gfb_ref[1, at, :] = grad.astype(BF16)
-            ng_ref[0:1] += gain_grad
-            ng_ref[1:2] += shift_grad
-            return 0
-
-        lax.fori_loop(0, rows // CHUNK, part, 0)
+            gfb[1, at, :] = grad.astype(BF16)
+            outgoing.append(copies.start(gfb.at[1, at, :], gfb_ref.at[1, at, :]))
+            add(0, gain_grad)
+            add(1, shift_grad)
+        target = gho_ref if n < blocks else ghp_ref
+        part = pl.ds(n % blocks * FF_BLOCK, FF_BLOCK)
+        outgoing.append(copies.start(gh.at[n], target.at[:, part]))
+    ng_ref[...] = jnp.concatenate(sums, axis=0)
+    for copy in outgoing:
+        copy.wait()
 
 
 def feed_back(
@@ -477,100 +595,120 @@
     rows, width = up.shape
     half = wi_own.shape[2]
     blocks = half // FF_BLOCK
-    own, peer, w_in, w_back = ff_specs(layer, width, blocks)
-    full, thin = whole((rows, width)), whole((rows, 128))
-    if live is None:
-
-        def kernel(up_ref, *refs):
-            feed_back_kernel(up_ref, None, *refs)
-
-        args, specs = (up,), [full]
-    else:
-        kernel, args, specs = feed_back_kernel, (up, live), [full, thin]
-    return run(
-        kernel,
-        args + (xh2, rs2, xh1, rs1, slope, wi_own, wi_peer, wb_own, wb_peer, norms),
-        specs
-        + [
-            full, thin, full, thin,
-            pl.BlockSpec((rows, FF_BLOCK), lambda j: (0, j)),
-            *w_in, *w_back, layer_spec(norms, layer),
-        ],
-        [
-            whole((2, rows, width)),
-            pl.BlockSpec((rows, FF_BLOCK), lambda j: (0, own(j))),
-            pl.BlockSpec((rows, FF_BLOCK), lambda j: (0, peer(j))),
-            whole((4, width)),
-        ],
+    chunks = rows // FF_CHUNK
+    masked = live is not None
+    args = (up,) + ((live,) if masked else ())
+    args += (xh2, rs2, xh1, rs1, slope, wi_own, wi_peer, wb_own, wb_peer, norms)
+    thin = pltpu.VMEM((rows, 128), F32)
+    full = pltpu.VMEM((rows, width), BF16)
+    return run(
+        functools.partial(feed_back_kernel, layer, masked),
+        args,
+        [ANY] * (len(args) - 1) + [layer_spec(norms, layer)],
+        [ANY] * 3 + [whole((4, width))],
         [
             shape((2, rows, width), BF16),
             shape((rows, half), BF16),
             shape((rows, half), BF16),
             shape((4, width), F32),
         ],
-        (2 * blocks,),
+        (1,),
         "feed_back",
-        [pltpu.VMEM((rows, width), F32)],
+        [
+            pltpu.VMEM((rows, width), up.dtype), thin if masked else pltpu.VMEM((8, 128), F32),
+            full, thin, full, thin,
+            pltpu.VMEM((2 * blocks, rows, FF_BLOCK), BF16),
+            pltpu.VMEM((2 * blocks, width, FF_BLOCK), BF16),
+            pltpu.VMEM((2 * blocks, FF_BLOCK, width), BF16),
+            pltpu.VMEM((2, rows, width), BF16),
+            pltpu.VMEM((2 * blocks, rows, FF_BLOCK), BF16),
+            pltpu.VMEM((rows, width), F32),
+            pltpu.SemaphoreType.DMA((5 * chunks + 8 * blocks + 3,)),
+        ],
         after,
     )
 
 
 def mix_back_kernel(
-    gfb_ref, wo_ref, wp_ref, rden_ref, mo_ref, mp_ref, qo_ref, qp_ref, gx_ref, dkv_ref, total
+    layer,
+    gfb_ref, wo_ref, wp_ref, rden_ref, mo_ref, mp_ref, qo_ref, qp_ref,
+    gx_ref, dkv_ref,
+    gb, w, rden, m, q, gx_out, semaphores,
 ):
-    rows = gfb_ref.shape[0]
-    half = mo_ref.shape[1]
+    rows = MIX_CHUNK
+    total_rows, half = m.shape[1:]
     pairs = half // 128
-    first = pl.program_id(0) == 0
+    copies = Copies(semaphores)
+    arrivals, leaving = [], []
+    for n in range(total_rows // rows):
+        at = pl.ds(n * rows, rows)
+        part = [copies.start(gfb_ref.at[1, at, :], gb.at[at, :])]
+        if n == 0:
+            part += [copies.start(ref.at[layer], w.at[n]) for n, ref in enumerate((wo_ref, wp_ref))]
+        part.append(copies.start(rden_ref.at[at, :], rden.at[at, :]))
+        for side, (m_in, q_in) in enumerate(((mo_ref, qo_ref), (mp_ref, qp_ref))):
+            part.append(copies.start(m_in.at[at, :], m.at[side, at, :]))
+            part.append(copies.start(q_in.at[at, :], q.at[side, at, :]))
+        arrivals.append(part)
     r = lax.broadcasted_iota(jnp.int32, (256, 128), 0) % 128
     c = lax.broadcasted_iota(jnp.int32, (256, 128), 1)
     spread_c = jnp.where((r < HEAD) == (c < HEAD), -1.0 / HEAD, 0.0).astype(BF16)
-    gb = gfb_ref[...]
-    for side, (w_ref, m_ref, q_ref) in enumerate(
-        ((wo_ref, mo_ref, qo_ref), (wp_ref, mp_ref, qp_ref))
-    ):
-        gm = dot_nt(gb, w_ref[...])
+    totals = [None] * (2 * pairs)
+    for n in range(total_rows // rows):
+        at = slice(n * rows, n * rows + rows)
+        for copy in arrivals[n]:
+            copy.wait()
+        for side in range(2):
+            gm = dot_nt(gb[at, :], w[side])
+            for pair in range(pairs):
+                base = side * half + pair * 128
+                inverse = rden[at, base : base + 128].astype(F32)
+                g = gm[:, pair * 128 : pair * 128 + 128] * inverse
+                mixed = m[side, at, pair * 128 : pair * 128 + 128].astype(F32)
+                prod = jnp.where(inverse < 1.0, g * mixed, 0.0)
+                high = prod.astype(BF16)
+                rest = (prod - high.astype(F32)).astype(BF16)
+                minus_c = dot(jnp.concatenate([high, rest], axis=1), spread_c).astype(BF16)
+                gx = jnp.concatenate([g.astype(BF16), minus_c], axis=1)
+                gx_out[at, 2 * base : 2 * base + 256] = gx
+        here = pl.ds(n * rows, rows)
+        leaving.append(copies.start(gx_out.at[here, :], gx_ref.at[here, :]))
+    for side in range(2):
         for pair in range(pairs):
-            base = side * half + pair * 128
-            rden = rden_ref[:, base : base + 128].astype(F32)
-            g = gm[:, pair * 128 : pair * 128 + 128] * rden
-            m = m_ref[:, pair * 128 : pair * 128 + 128].astype(F32)
-            prod = jnp.where(rden < 1.0, g * m, 0.0)
-            high = prod.astype(BF16)
-            rest = (prod - high.astype(F32)).astype(BF16)
-            minus_c = dot(jnp.concatenate([high, rest], axis=1), spread_c).astype(BF16)
-            gx = jnp.concatenate([g.astype(BF16), minus_c], axis=1)
-            gx_ref[:, 2 * base : 2 * base + 256] = gx
-            part = pair_state(q_ref[:, pair * 256 : pair * 256 + 256], gx)
-            at = side * pairs + pair
-            total[at] = jnp.where(first, part, total[at] + part)
-
-    @pl.when(pl.program_id(0) == pl.num_programs(0) - 1)
-    def _():
-        dkv_ref[...] = total[...].astype(BF16)
+            wide = 2 * (side * half + pair * 128)
+            state = pair_state(
+                q[side, :, pair * 256 : pair * 256 + 256], gx_out[:, wide : wide + 256]
+            )
+            dkv_ref[side * pairs + pair] = state.astype(BF16)
+    for copy in leaving:
+        copy.wait()
 
 
 def mix_back(gfb, w_own, w_peer, layer, rden, m_own, m_peer, q_own, q_peer, after=()):
     _, rows, width = gfb.shape
     half = m_own.shape[1]
     heads = half // HEAD
-    full, narrow, cat = (row_spec(CHUNK, n) for n in (width, half, heads * 128))
-    return run(
-        mix_back_kernel,
+    steps = rows // MIX_CHUNK
+    return run(
+        functools.partial(mix_back_kernel, layer),
         (gfb, w_own, w_peer, rden, m_own, m_peer, q_own, q_peer),
-        [
-            pl.BlockSpec((None, CHUNK, width), lambda i: (1, i, 0)),
-            layer_spec(w_own, layer), layer_spec(w_peer, layer),
-            full, narrow, narrow, cat, cat,
-        ],
-        [row_spec(CHUNK, 2 * width), whole((heads, 128, 256))],
+        [ANY] * 8,
+        [ANY, whole((heads, 128, 256))],
         [
             shape((rows, 2 * width), BF16),
             shape((heads, 128, 256), BF16),
         ],
-        (rows // CHUNK,),
+        (1,),
         "mix_back",
-        [pltpu.VMEM((heads, 128, 256), F32)],
+        [
+            pltpu.VMEM((rows, width), BF16),
+            pltpu.VMEM((2, half, width), BF16),
+            pltpu.VMEM((rows, width), BF16),
+            pltpu.VMEM((2, rows, half), BF16),
+            pltpu.VMEM((2, rows, heads * 128), BF16),
+            pltpu.VMEM((rows, 2 * width), BF16),
+            pltpu.SemaphoreType.DMA((7 * steps + 2,)),
+        ],
         after,
     )
 
@@ -587,7 +725,7 @@
 
     @pl.when(pl.program_id(0) == 0)
     def _():
-        carry = here_ref[0, 7].astype(F32) * (1 - here_ref[0, 4]).astype(F32)
+        carry = hands_on(here_ref, rows * pl.num_programs(0), 0)
         for at in range(2 * pairs):
             dstate[at] = dkv_ref[(at + pairs) % (2 * pairs)].astype(F32) * carry
 
@@ -644,7 +782,12 @@
         refs[:12], refs[12:15], refs[15:],
     )
     attend_back_kernel(*inputs, go_ref, gp_ref, dstate)
-    input_back_kernel(go_ref, gp_ref, wo_ref, wp_ref, first_ref, up_ref)
+    half = wo_ref.shape[2]
+    total = first_ref[...].astype(F32)
+    for g_ref, w_ref in ((go_ref, wo_ref), (gp_ref, wp_ref)):
+        for kind in range(3):
+            total = total + dot_nt(g_ref[:, kind * half : kind * half + half], w_ref[kind])
+    up_ref[...] = total.astype(up_ref.dtype)
 
 
 def attend_back(here, own, peer, gx, states, dkv, cos, sin, after=(), onward=None):
@@ -732,7 +875,6 @@
 
 
 FF_ROWS = 448
-Q_ROWS = 144
 NORM_ROW = 408
 
 
@@ -741,8 +883,8 @@
     return jnp.concatenate(pieces, axis=0) if len(pieces) > 1 else values
 
 
-def blocks_of(index_ref, scr, rows, z_local, x_first, other, kept):
-    x, y = index_ref[0, 0], index_ref[0, 1]
+def blocks_of(scr, rows, z_local, x_first, other, kept):
+    x, y = lax.axis_index("x"), lax.axis_index("y")
     if x_first:
         spot = other * 2 + (x if kept else 1 - x)
     else:
@@ -751,128 +893,184 @@
     return scr[pl.ds(start, rows), :]
 
 
-def back_pack_kernel(index_ref, a_ref, b_ref, c_ref, d_ref, ka, sa, kb, sb, scr):
-    rows = scr.shape[0] // 4
-    scr[...] = dot_tn(a_ref[...], b_ref[...]) + dot_tn(c_ref[...], d_ref[...])
-    z = pl.program_id(0)
-    for x_first, (keep, send) in ((True, (ka, sa)), (False, (kb, sb))):
-
-        @pl.when((z < 2) == x_first)
-        def _():
-            for other in range(2):
-                for kept, out in ((True, keep), (False, send)):
-                    value = blocks_of(index_ref, scr, rows, 0, x_first, other, kept)
-                    out[0, other] = fold_lanes(value, out.shape[3]).astype(BF16)
-
-
-def half_spec(array, at):
-    return pl.BlockSpec((None,) + array.shape[1:], lambda *_: (at, 0, 0))
-
-
-def back_pack(index, a, b, c, d, after=()):
-    rows, m = a.shape
-    n = b.shape[2]
-    block = m // 4
-    left = pl.BlockSpec((rows, block), lambda z: (0, z))
-    buffer = shape((2, 2, FF_ROWS, n // 2), BF16)
-    low = pl.BlockSpec((1, 2, block // 2, n // 2), lambda z: (jnp.minimum(z, 1), 0, 0, 0))
-    high = pl.BlockSpec((1, 2, block // 2, n // 2), lambda z: (jnp.maximum(z - 2, 0), 0, 0, 0))
-    return run(
-        back_pack_kernel,
-        (index, a, b, c, d),
-        [IN_SMEM, left, half_spec(b, 0), left, half_spec(d, 0)],
-        [low, low, high, high],
-        [buffer] * 4,
-        (4,),
-        "back_grad",
-        [pltpu.VMEM((block, n), F32)],
-        after,
-    )
-
-
-def spread(index_ref, scr, rows, outs, tail=None):
+def spread(scr, rows, outs):
     ka, sa, kb, sb = outs
     for x_first, keep, send in ((True, ka, sa), (False, kb, sb)):
         for z in range(2):
             z_local = z if x_first else z + 2
             for other in range(2):
                 for kept, out in ((True, keep), (False, send)):
-                    value = blocks_of(index_ref, scr, rows, z_local, x_first, other, kept)
-                    if tail is not None:
-                        x, y = index_ref[0, 0], index_ref[0, 1]
-                        if x_first:
-                            w = z_local * 4 + other * 2 + (x if kept else 1 - x)
-                        else:
-                            w = z_local * 4 + (y if kept else 1 - y) * 2 + other
-                        value = jnp.concatenate([value, tail(w)], axis=0)
-                    out[z, other] = fold_lanes(value, out.shape[3]).astype(BF16)
-
-
-def in_pack_kernel(index_ref, a_ref, b_ref, c_ref, d_ref, _ka, _sa, _kb, _sb, ka, sa, kb, sb, scr):
-    scr[...] = dot_tn(a_ref[...], b_ref[...]) + dot_tn(c_ref[...], d_ref[...])
-    spread(index_ref, scr, scr.shape[0] // 16, (ka, sa, kb, sb))
-
-
-def column_pack(index, a, b, c, d, buffers, block_n, lanes, block_rows, first_block, name, after=()):
+                    value = blocks_of(scr, rows, z_local, x_first, other, kept)
+                    out[z, other] = value.astype(BF16)
+
+
+def q_pack_kernel(
+    a_ref, b_ref, c_ref, d_ref, ka_ref, sa_ref, kb_ref, sb_ref, left, right, out, scr, semaphores
+):
+    parts, _, lanes = right.shape
+    rows, m = a_ref.shape
+    block = m // 16
+    outs = (ka_ref, sa_ref, kb_ref, sb_ref)
+    copies = Copies(semaphores)
+    first = [
+        copies.start(ref, left.at[pl.ds(side * rows, rows), :])
+        for side, ref in enumerate((a_ref, c_ref))
+    ]
+    arrivals = [
+        [
+            copies.start(ref.at[:, pl.ds(n * lanes, lanes)], right.at[n, pl.ds(side * rows, rows), :])
+            for side, ref in enumerate((b_ref, d_ref))
+        ]
+        for n in range(parts)
+    ]
+    leaving = []
+    for n in range(parts):
+        for copy in (first if n == 0 else []) + arrivals[n]:
+            copy.wait()
+        scr[n % 2] = dot_tn(left[...], right[n])
+        here = slice(n * block, n * block + block)
+        spread(scr.at[n % 2], block, [out.at[which, :, :, here, :] for which in range(4)])
+        for which in range(4):
+            at = pl.ds(n * block, block)
+            leaving.append(copies.start(out.at[which, :, :, at, :], outs[which].at[:, :, at, :]))
+    for copy in leaving:
+        copy.wait()
+
+
+def q_pack(a, b, c, d, lanes, after=()):
     rows, m = a.shape
-    n = b.shape[1]
-    right = pl.BlockSpec((rows, block_n), lambda j: (0, j))
-    out_rows = m // 16 * (block_n // lanes)
-    out = pl.BlockSpec((2, 2, out_rows, lanes), lambda j: (0, 0, first_block + j, 0))
-    specs = [IN_SMEM, whole(a.shape), right, whole(c.shape), right]
-    scratch = [pltpu.VMEM((m, block_n), F32)]
-    if buffers is None:
-
-        def fresh(index_ref, a_ref, b_ref, c_ref, d_ref, *outs):
-            in_pack_kernel(index_ref, a_ref, b_ref, c_ref, d_ref, *([None] * 4), *outs)
-
-        return run(
-            fresh, (index, a, b, c, d), specs, [out] * 4,
-            [shape((2, 2, block_rows, lanes), BF16)] * 4, (n // block_n,), name, scratch, after,
-        )
-    return run(
-        in_pack_kernel,
-        (index, a, b, c, d, *buffers),
-        specs + [pl.BlockSpec(memory_space=pl.ANY)] * 4,
-        [out] * 4,
-        [shape(buffer.shape, BF16) for buffer in buffers],
-        (n // block_n,),
-        name,
-        scratch,
+    parts = b.shape[1] // lanes
+    buffer = (2, 2, m // 16 * parts, lanes)
+    return run(
+        q_pack_kernel,
+        (a, b, c, d),
+        [ANY] * 4,
+        [ANY] * 4,
+        [shape(buffer, BF16)] * 4,
+        (1,),
+        "qkv_grad",
+        [
+            pltpu.VMEM((2 * rows, m), BF16),
+            pltpu.VMEM((parts, 2 * rows, lanes), BF16),
+            pltpu.VMEM((4,) + buffer, BF16),
+            pltpu.VMEM((2, m, lanes), F32),
+            pltpu.SemaphoreType.DMA((2 + 6 * parts,)),
+        ],
         after,
-        {5 + i: i for i in range(4)},
-    )
-
-
-def out_pack_kernel(
-    index_ref, a_ref, b_ref, c_ref, d_ref, norm_ref, norm_got_ref, _ka, _sa, _kb, _sb,
-    ka, sa, kb, sb, scr,
+    )
+
+
+def pack_kernel(
+    index_ref, ho_ref, gfb_ref, hg_ref, gfbg_ref, fi_ref, gho_ref, fg_ref, ghg_ref, mo_ref, mg_ref,
+    norm_ref, norm_got_ref,
+    ka_ref, sa_ref, kb_ref, sb_ref,
+    h, gfb, f, gh, m, out, scr, semaphores,
 ):
-    scr[...] = dot_tn(a_ref[...], b_ref[...]) + dot_tn(c_ref[...], d_ref[...])
-    blank = jnp.zeros((8, scr.shape[1] - 128), F32)
-    spread(
-        index_ref, scr, scr.shape[0] // 16, (ka, sa, kb, sb),
-        lambda w: jnp.concatenate([norm_ref[w] + norm_got_ref[w], blank], axis=1),
-    )
-
-
-def out_pack(index, a, b, c, d, norms, norms_got, buffers, after=()):
-    m, n = a.shape[1], b.shape[2]
-    block = 2 * (m // 16 + 8)
-    out = pl.BlockSpec((2, 2, block, n // 2), lambda j: (0, 0, (FF_ROWS - block) // block, 0))
-    return run(
-        out_pack_kernel,
-        (index, a, b, c, d, norms, norms_got, *buffers),
-        [IN_SMEM, whole(a.shape), half_spec(b, 1), whole(c.shape), half_spec(d, 1)]
-        + [whole(norms.shape)] * 2
-        + [pl.BlockSpec(memory_space=pl.ANY)] * 4,
-        [out] * 4,
-        [shape(buffer.shape, BF16) for buffer in buffers],
+    x, y = lax.axis_index("x"), lax.axis_index("y")
+    outs = (ka_ref, sa_ref, kb_ref, sb_ref)
+    lanes = out.shape[4]
+    block = h.shape[2]
+    columns = gh.shape[2]
+    copies = Copies(semaphores)
+    start = copies.start
+
+    def both(sources, target, *at):
+        rows = sources[0].shape[0]
+        return [
+            start(source, target.at[(*at, pl.ds(side * rows, rows))])
+            for side, source in enumerate(sources)
+        ]
+
+    back_first = both((gfb_ref.at[0], gfbg_ref.at[0]), gfb, 0)
+    back_parts = [
+        both((ho_ref.at[:, pl.ds(n * block, block)], hg_ref.at[:, pl.ds(n * block, block)]), h, n)
+        for n in range(4)
+    ]
+    in_first = both((fi_ref, fg_ref), f)
+    in_parts = [
+        both((gho_ref.at[:, pl.ds(n * columns, columns)], ghg_ref.at[:, pl.ds(n * columns, columns)]), gh, n)
+        for n in range(2)
+    ]
+    out_parts = both((mo_ref, mg_ref), m) + both((gfb_ref.at[1], gfbg_ref.at[1]), gfb, 1)
+    outgoing = []
+
+    def wait(parts):
+        for copy in parts:
+            copy.wait()
+
+    def place(slot, base, z, rows, at, tail=None):
+        x_first = z < 2
+        for other in range(2):
+            for kept in (True, False):
+                if x_first:
+                    spot = other * 2 + (x if kept else 1 - x)
+                else:
+                    spot = (y if kept else 1 - y) * 2 + other
+                value = scr[slot, pl.ds(pl.multiple_of(base + spot * rows, 8), rows), :]
+                if tail is not None:
+                    value = jnp.concatenate([value, tail(z * 4 + spot)], axis=0)
+                value = fold_lanes(value, lanes).astype(BF16)
+                which = (0 if x_first else 2) + (0 if kept else 1)
+                out[which, z % 2, other, at : at + value.shape[0], :] = value
+
+    wait(back_first)
+    for z in range(4):
+        wait(back_parts[z])
+        scr[z % 2, :block, :] = dot_tn(h[z], gfb[0])
+        place(z % 2, 0, z, block // 4, 0)
+        for which in (0, 1) if z < 2 else (2, 3):
+            rows = pl.ds(0, block // 2)
+            outgoing.append(
+                start(out.at[which, z % 2, :, rows, :], outs[which].at[z % 2, :, rows, :])
+            )
+    wait(in_first)
+    at = block // 2
+    for n in range(2):
+        wait(in_parts[n])
+        scr[n] = dot_tn(f[...], gh[n])
+        rows = scr.shape[1] // 16
+        for z in range(4):
+            place(n, z * 4 * rows, z, rows, at)
+        here = pl.ds(at, 2 * rows)
+        at += 2 * rows
+        for which in range(4):
+            outgoing.append(start(out.at[which, :, :, here, :], outs[which].at[:, :, here, :]))
+    wait(out_parts)
+    scr[0, :block, :] = dot_tn(m[...], gfb[1])
+    blank = jnp.zeros((8, scr.shape[2] - 128), F32)
+    tail = lambda w: jnp.concatenate([norm_ref[w] + norm_got_ref[w], blank], axis=1)
+    for z in range(4):
+        place(0, z * (block // 4), z, block // 16, at, tail)
+    here = pl.ds(at, 2 * (block // 16 + 8))
+    for which in range(4):
+        outgoing.append(start(out.at[which, :, :, here, :], outs[which].at[:, :, here, :]))
+    for copy in outgoing:
+        copy.wait()
+
+
+def pack(index, h_own, gfb, h_got, gfb_got, ffn_in, gh_own, ffn_got, gh_got, m_own, m_got, norms, norms_got, after=()):
+    rows, hidden = h_own.shape
+    width = ffn_in.shape[1]
+    half = m_own.shape[1]
+    return run(
+        pack_kernel,
+        (index, h_own, gfb, h_got, gfb_got, ffn_in, gh_own, ffn_got, gh_got, m_own, m_got, norms, norms_got),
+        [IN_SMEM] + [ANY] * 10 + [whole(norms.shape)] * 2,
+        [ANY] * 4,
+        [shape((2, 2, FF_ROWS, half), BF16)] * 4,
         (1,),
-        "out_grad",
-        [pltpu.VMEM((m, n), F32)],
+        "pack",
+        [
+            pltpu.VMEM((4, 2 * rows, hidden // 4), BF16),
+            pltpu.VMEM((2, 2 * rows, width), BF16),
+            pltpu.VMEM((2 * rows, width), BF16),
+            pltpu.VMEM((2, 2 * rows, hidden // 2), BF16),
+            pltpu.VMEM((2 * rows, half), BF16),
+            pltpu.VMEM((4, 2, 2, FF_ROWS, half), BF16),
+            pltpu.VMEM((2, width, width), F32),
+            pltpu.SemaphoreType.DMA((40,)),
+        ],
         after,
-        {7 + i: i for i in range(4)},
     )
 
 
@@ -885,7 +1083,7 @@
 
 
 def fold_split_kernel(index_ref, ka, ga, kb, gb, ka_out, sa_out, kb_out, sb_out):
-    x, y = index_ref[0, 0], index_ref[0, 1]
+    x, y = lax.axis_index("x"), lax.axis_index("y")
     ka_out[0] = sum_of(ka, ga, 0, y)
     sa_out[0] = sum_of(ka, ga, 0, 1 - y)
     kb_out[0] = sum_of(kb, gb, 0, x)
@@ -910,7 +1108,7 @@
 
 
 def fold_near_kernel(index_ref, *refs):
-    z = index_ref[0, 2]
+    z = lax.axis_index("z") % 2
     keep, send = refs[-2:]
     for half in range(2):
         done = 0
@@ -940,7 +1138,7 @@
 
 
 def fold_far_kernel(index_ref, k, g, keep, send):
-    z = index_ref[0, 3]
+    z = lax.axis_index("z") // 2
     keep[...] = sum_of(k, g, z)
     send[...] = sum_of(k, g, 1 - z)
 
@@ -966,7 +1164,7 @@
     if norms:
         row, lane = (lax.broadcasted_iota(jnp.int32, total.shape, n) for n in (0, 1))
         here = jnp.logical_and(row >= NORM_ROW, row < NORM_ROW + 8)
-        other = jnp.logical_or(lane < index_ref[0, 4] * norms, lane >= (index_ref[0, 4] + 1) * norms)
+        other = jnp.logical_or(lane < lax.axis_index("narrow") * norms, lane >= (lax.axis_index("narrow") + 1) * norms)
         total = jnp.where(jnp.logical_and(here, other), 0.0, total)
     total = total * total
     part = total[:, :128] + total[:, 128:256] + total[:, 256:]
@@ -1008,7 +1206,7 @@
     total = jnp.sum(jnp.sum(sums_ref[...], axis=0, keepdims=True), axis=1, keepdims=True)
     clip_norm = jnp.sqrt(total)
     factor = jnp.minimum(1.0, CLIP / clip_norm)
-    clip_ref[...] = jnp.broadcast_to(clip_norm, clip_ref.shape)
+    clip_ref[0] = clip_norm[0, 0]
 
     def kind(at, gradient, rate, decay):
         old = [ref[...] for ref in states[3 * at : 3 * at + 3]]
@@ -1027,7 +1225,7 @@
         all_kinds(ff_ref[...], q_ref[...])
         part = states[12].shape[1]
         columns = ff_ref[NORM_ROW : NORM_ROW + 8, :128]
-        mine = jnp.where(index_ref[0, 4] == 0, columns[:, :part], columns[:, part : 2 * part])
+        mine = jnp.where(lax.axis_index("narrow") == 0, columns[:, :part], columns[:, part : 2 * part])
         kind(4, mine, LR_NORMS, 0.0)
 
     @pl.when(layer == 1)
@@ -1041,12 +1239,12 @@
         functools.partial(update_kernel, wide),
         (sums, index, one, ff, q, *states),
         [whole(sums.shape), IN_SMEM, whole(one.shape), whole(ff.shape), whole(q.shape)] + specs,
-        specs + [whole((8, 128))],
-        [shape(state.shape, F32) for state in states] + [shape((8, 128), F32)],
+        specs + [IN_SMEM],
+        [shape(state.shape, F32) for state in states] + [shape((1,), F32)],
         (LAYERS,),
         "update",
     )
-    return news, clip_norm[0, :1]
+    return news, clip_norm
 
 
 def layer_at(array):
@@ -1066,14 +1264,7 @@
     every = wide_axes + ("narrow",)
     wide = math.prod(lax.axis_size(axis) for axis in wide_axes)
     by_axes = len(wide_axes) == 3
-    lengths = seq_lengths[0]
-    core = lax.axis_index("narrow")
-    z, y, x = (lax.axis_index(axis) for axis in wide_axes) if by_axes else (0, 0, 0)
-    goes_on = (lengths[0] > rows).astype(jnp.int32)
-    lane = lax.broadcasted_iota(jnp.int32, (1, 8), 1)
-    here = jnp.zeros((1, 8), jnp.int32)
-    for n, value in enumerate((x, y, z % 2, z // 2, core, lengths[0], lengths[1], goes_on)):
-        here = jnp.where(lane == n, value, here)
+    here = seq_lengths
     cos, sin, live = tables(here, rows)
 
     qkv = jnp.transpose(w_qkv, (0, 2, 1, 3))
@@ -1099,7 +1290,7 @@
         m_own, m_peer, rden, ffn_in, xh1, rs1, states = attend(
             here, own, peer, kv, kv_at, w_out, out_peer, layer, low, norm_params
         )
-        h_own, h_peer, slope, out, xh2, rs2 = feed(
+        h_own, h_peer, slope, out, xh2, rs2 = (feed if last else feed_grid)(
             ffn_in, w_in, in_peer, w_back, back_peer, layer, norm_params, F32 if last else BF16,
             got[layer - 1] + (low_got,) if last else (),
         )
@@ -1142,29 +1333,22 @@
             shares[layer][0] = shares[layer][0].reshape(-1, 3, half)
             after = ()
             continue
-        after = ()
         if last:
             norms = jnp.transpose(norm_sum.reshape(8, wide, width // wide), (1, 0, 2))
             norms = jnp.pad(norms, ((0, 0), (0, 0), (0, 128 - width // wide)))
             norms_got = swap(norms)
             ka, sa, kb, sb = fold_split(here, *q_first, (gfb,))
-            q_second = (ka, by_y(sa), kb, by_x(sb))
-            gx = None
-            after = (ka,)
+            keep, send = fold_near(here, (ff_second, (ka, by_y(sa), kb, by_x(sb))))
+            one_near = (keep, near(send))
+            after = (keep,)
         else:
             norms = norms_got = jnp.zeros((wide, 8, 128), F32)
-            gx, dkv = mix_back(*mix)
+            gx, dkv = mix_back(*mix, (h_got,))
             after = (gx,)
-        buffers = back_pack(here, h_own, gfb, h_got, gfb_got, after)
-        after = ()
-        if last:
-            keep, send = fold_near(here, (ff_second, q_second), (buffers[0],))
-            one_near = (keep, near(send))
-            after = (keep,)
-        buffers = column_pack(
-            here, ffn_in, gh_own, ffn_got, gh_got, buffers, width, half, FF_ROWS, 2, "in_grad", after
+        ka, sa, kb, sb = pack(
+            here, h_own, gfb, h_got, gfb_got, ffn_in, gh_own, ffn_got, gh_got, m_own, m_got,
+            norms, norms_got, after,
         )
-        ka, sa, kb, sb = out_pack(here, m_own, gfb, m_got, gfb_got, norms, norms_got, buffers)
         ff_first = (ka, by_x(sa), kb, by_y(sb))
         if last:
             keep, send = fold_far(here, *one_near, (ka,))
@@ -1178,9 +1362,7 @@
         g_got = swap(g_peer)
         ka, sa, kb, sb = fold_split(here, *ff_first, (g_own,))
         ff_second = (ka, by_y(sa), kb, by_x(sb))
-        q_ka, q_sa, q_kb, q_sb = column_pack(
-            here, low, g_own, low_got, g_got, None, half, half, Q_ROWS, 0, "qkv_grad", (ka,)
-        )
+        q_ka, q_sa, q_kb, q_sb = q_pack(low, g_own, low_got, g_got, half, (ka,))
         q_first = (q_ka, by_x(q_sa), q_kb, by_y(q_sb))
         after = (q_ka,)
         if not last:

time: 420 us -> 399 us (0.950)
  Pallas kernels: 327 us -> 307 us
    pallas_call x37 -> x33, Pallas kernels: 327 us -> 307 us  [run(): pl.pallas_call(body, grid=grid, in_specs=list(in_specs) + [pl.BlockSpec(m...]
    ppermute x40, waiting for transfers between devices: 16.4 us -> 22.6 us  [swap(): return lax.ppermute(values, axis, [(0, 1), (1, 0)])]
    ppermute x6, waiting for transfers between devices: 17.7 us -> 11.7 us  [shuffle(): lax.ppermute(values, axis, [(i, i ^ bit) for i in range(lax.axis_size(axi...]
  transfers between devices with their start and end apart: 46 -> 46, of which waited for: 16 -> 18; matrix products, arithmetic and copies ran while one was open for 1% -> 0% of each run, Pallas kernels for 61% -> 63%
where the time goes in v4:
time: 399 us; the launch traced here: 392 us
  Pallas kernels  307 us (77%)
  starting transfers between devices  35.4 us (9%)
  waiting for transfers between devices  34.3 us (9%)
  blocking collectives  11.5 us (3%)
    pallas_call x33, Pallas kernels, run(): pl.pallas_call(body, grid=grid, in_specs=list(in_specs) + [pl.BlockSpec(m...  307 us
    ppermute x40, starting transfers between devices, swap(): return lax.ppermute(values, axis, [(0, 1), (1, 0)])  23.9 us
    ppermute x40, waiting for transfers between devices, swap(): return lax.ppermute(values, axis, [(0, 1), (1, 0)])  22.6 us
    ppermute x6, waiting for transfers between devices, shuffle(): lax.ppermute(values, axis, [(i, i ^ bit) for i in range(lax.axis_size(axi...  11.7 us
    all_to_all x1, blocking collectives, shards(): exchange = lambda rows_in: lax.all_to_all(rows_in, every, 0, 0, tiled=True)  11.5 us
    ppermute x6, starting transfers between devices, shuffle(): lax.ppermute(values, axis, [(i, i ^ bit) for i in range(lax.axis_size(axi...  11.5 us
  transfers between devices with their start and end apart: 46, of which 18 were waited for; matrix products, arithmetic and copies ran while one was open for 0% of the time, Pallas kernels for 63%

profile of v4, /device:TPU:0, one launch (start us, length us, event | category | flops | bytes accessed | tf_op | source)
XLA Modules:
  0.0 392.5 jit_solution(16758936183782961405)
XLA Ops:
  1.3 2.4 tables.1
  3.7 6.4 %project.3 = (bf16[1024,768]{1,0:T(8,128)(2,1)}, bf16[1024,768]{1,0:T(8,128)(2,1)}, bf16[1024,384]{1,0:T(8,128)(2,1)}, f32[1,3,128,256]{3,2,1,0:T(8,128)}) custom-call(bf16[1024,768]{1,0:T(8,128)(2,1)} %refs_0_.39, bf16[2,3,768,384]{3,2,1,0:T(8,128)(2,1)} %bitcast.20, f32[1024,128]{1,0:T(8,128)} %get-tuple-element.147.refs_2_.refs_3_.refs_10_, ...), custom_call_target="tpu_custom_call" | custom-call | tf_op jit(solution)/shard_map/project/pallas_call | solution.py:44
  10.6 6.4 %project.4 = (bf16[1024,768]{1,0:T(8,128)(2,1)}, bf16[1024,768]{1,0:T(8,128)(2,1)}, bf16[1024,384]{1,0:T(8,128)(2,1)}, f32[1,3,128,256]{3,2,1,0:T(8,128)}) custom-call(bf16[1024,768]{1,0:T(8,128)(2,1)} %refs_0_.39, bf16[2,3,768,384]{3,2,1,0:T(8,128)(2,1)} %collective-permute-done.refs_1_.refs_2_.refs_13_.refs_3_, ...), custom_call_target="tpu_custom_call" | custom-call | tf_op jit(solution)/shard_map/project/pallas_call | solution.py:44
  17.6 1.5 collective-permute-done.1.refs_7_
  19.3 14.3 %attend.2 = (bf16[1024,384]{1,0:T(8,128)(2,1)}, bf16[1024,384]{1,0:T(8,128)(2,1)}, bf16[1024,768]{1,0:T(8,128)(2,1)}, bf16[1024,768]{1,0:T(8,128)(2,1)}, bf16[10...) custom-call(s32[1,2]{1,0:T(1,128)} %refs_1_.9, ...), custom_call_target="tpu_custom_call" | custom-call | tf_op jit(solution)/shard_map/attend/pallas_call | solution.py:44
  33.6 21.0 %feed.2 = (bf16[1024,1536]{1,0:T(8,128)(2,1)}, bf16[1024,1536]{1,0:T(8,128)(2,1)}, bf16[1024,3072]{1,0:T(8,128)(2,1)}, bf16[1024,768]{1,0:T(8,128)(2,1)}, bf16[1...) custom-call(bf16[1024,768]{1,0:T(8,128)(2,1)} %get-tuple-element.157.refs_0_.refs_5_, bf16[2,768,1536]{2,1,0:T(8,128)(2,1)} %refs_6_.1, ...), custom_call_target="tpu_custom_call" | custom-call | tf_op jit(solution)/shard_map/feed/pallas_call | solution.py:44
  55.2 11.0 %project.5 = (bf16[1024,768]{1,0:T(8,128)(2,1)}, bf16[1024,768]{1,0:T(8,128)(2,1)}, bf16[1024,384]{1,0:T(8,128)(2,1)}, bf16[1024,768]{1,0:T(8,128)(2,1)}, bf16[1...) custom-call(bf16[1024,768]{1,0:T(8,128)(2,1)} %get-tuple-element.160.refs_0_.refs_11_, ...), custom_call_target="tpu_custom_call" | custom-call | tf_op jit(solution)/shard_map/project/pallas_call | solution.py:44
  67.2 1.7 collective-permute-done.6.refs_7_.refs_8_
  69.3 14.3 %attend.3 = (bf16[1024,384]{1,0:T(8,128)(2,1)}, bf16[1024,384]{1,0:T(8,128)(2,1)}, bf16[1024,768]{1,0:T(8,128)(2,1)}, bf16[1024,768]{1,0:T(8,128)(2,1)}, bf16[10...) custom-call(s32[1,2]{1,0:T(1,128)} %refs_1_.9, ...), custom_call_target="tpu_custom_call" | custom-call | tf_op jit(solution)/shard_map/attend/pallas_call | solution.py:44
  84.2 19.9 %feed.3 = (bf16[1024,1536]{1,0:T(8,128)(2,1)}, bf16[1024,1536]{1,0:T(8,128)(2,1)}, bf16[1024,3072]{1,0:T(8,128)(2,1)}, f32[1024,768]{1,0:T(8,128)}, bf16[1024,768]{1,0:T(8,128)(2,1)}, /*index=5*/f32[1024,128]{1,0:T(8,128)}) custom-call(bf16[1024,768]{1,0:T(8,128)(2,1)} %get-tuple-element.168.refs_0_.refs_5_, bf16[2,768,1536]{2,1,0:T(8,128)(2,1)} %refs_6_.1, ...), custom_call_target="tpu_custom_call" | custom-call | tf_op jit(solution)/shard_map/feed/pallas_call | solution.py:44
  104.3 18.6 %feed_back.2 = (bf16[2,1024,768]{2,1,0:T(8,128)(2,1)}, bf16[1024,1536]{1,0:T(8,128)(2,1)}, bf16[1024,1536]{1,0:T(8,128)(2,1)}, f32[4,768]{1,0:T(4,128)}) custom-call(f32[1024,768]{1,0:T(8,128)} %refs_0_.29, f32[1024,128]{1,0:T(8,128)} %get-tuple-element.172.refs_1_, bf16[1024,768]{1,0:T(8,128)(2,1)} %get-tuple-element.173.refs_2_, ...), custom_call_target="tpu_custom_call" | custom-call | tf_op jit(solution)/shard_map/feed_back/pallas_call | solution.py:44
  123.5 7.4 %mix_back.2 = (bf16[1024,1536]{1,0:T(8,128)(2,1)}, bf16[6,128,256]{2,1,0:T(8,128)(2,1)}) custom-call(bf16[2,1024,768]{2,1,0:T(8,128)(2,1)} %get-tuple-element.179.refs_0_.refs_2_.refs_14_, bf16[2,384,768]{2,1,0:T(8,128)(2,1)} %refs_1_.8, bf16[2,384,768]{2,1,0:T(8,128)(2,1)} %collective-permute-done.3.refs_10_.refs_2_, ...), custom_call_target="tpu_custom_call" | custom-call | tf_op jit(solution)/shard_map/mix_back/pallas_call | solution.py:44
  130.9 2.6 collective-permute-done.17.refs_8_
  134.1 21.8 %pack.2 = (bf16[2,2,448,384]{3,2,1,0:T(8,128)(2,1)}, bf16[2,2,448,384]{3,2,1,0:T(8,128)(2,1)}, bf16[2,2,448,384]{3,2,1,0:T(8,128)(2,1)}, bf16[2,2,448,384]{3,2,1,0:T(8,128)(2,1)}) custom-call(s32[1,2]{1,0:T(1,128)} %refs_1_.9, bf16[1024,1536]{1,0:T(8,128)(2,1)} %get-tuple-element.186.refs_1_, ...), custom_call_target="tpu_custom_call" | custom-call | tf_op jit(solution)/shard_map/pack/pallas_call | solution.py:44
  155.9 3.0 collective-permute-start.19
  158.9 1.6 collective-permute-start.20
  160.5 2.1 collective-permute-done.15.refs_9_
  162.6 28.2 %attend_back.2 = (bf16[1024,1152]{1,0:T(8,128)(2,1)}, bf16[1024,1152]{1,0:T(8,128)(2,1)}, bf16[1024,768]{1,0:T(8,128)(2,1)}) custom-call(s32[1,2]{1,0:T(1,128)} %refs_1_.9, bf16[1024,768]{1,0:T(8,128)(2,1)} %get-tuple-element.161.refs_1_.refs_6_, bf16[1024,768]{1,0:T(8,128)(2,1)} %get-tuple-element.162.refs_2_.refs_7_, ...), custom_call_target="tpu_custom_call" | custom-call | tf_op jit(solution)/shard_map/attend_back/pallas_call | solution.py:44
  191.2 4.0 %fold_split.4 = (bf16[2,448,384]{2,1,0:T(8,128)(2,1)}, bf16[2,448,384]{2,1,0:T(8,128)(2,1)}, bf16[2,448,384]{2,1,0:T(8,128)(2,1)}, bf16[2,448,384]{2,1,0:T(8,128)(2,1)}) custom-call(s32[1,2]{1,0:T(1,128)} %refs_1_.9, bf16[2,2,448,384]{3,2,1,0:T(8,128)(2,1)} %get-tuple-element.189.refs_15_.refs_1_, bf16[2,2,448,384]{3,2,1,0:T(8,128)(2,1)} %collective-permute-done.19.refs_2_, ...), custom_call_target="tpu_custom_call" | custom-call | flops 999999995904 | bytes 999999995904 | tf_op jit(solution)/shard_map/fold_split/pallas_call | solution.py:44
  195.7 9.1 %qkv_grad.2 = (bf16[2,2,144,384]{3,2,1,0:T(8,128)(2,1)}, bf16[2,2,144,384]{3,2,1,0:T(8,128)(2,1)}, bf16[2,2,144,384]{3,2,1,0:T(8,128)(2,1)}, bf16[2,2,144,384]{3,2,1,0:T(8,128)(2,1)}) custom-call(bf16[1024,768]{1,0:T(8,128)(2,1)} %get-tuple-element.160.refs_0_.refs_11_, bf16[1024,1152]{1,0:T(8,128)(2,1)} %get-tuple-element.196.refs_5_.refs_1_, ...), custom_call_target="tpu_custom_call" | custom-call | tf_op jit(solution)/shard_map/qkv_grad/pallas_call | solution.py:44
  205.4 1.2 collective-permute-start.24
  206.6 0.8 collective-permute-start.21
  207.4 1.5 collective-permute-start.22
  208.9 18.2 %feed_back.3 = (bf16[2,1024,768]{2,1,0:T(8,128)(2,1)}, bf16[1024,1536]{1,0:T(8,128)(2,1)}, bf16[1024,1536]{1,0:T(8,128)(2,1)}, f32[4,768]{1,0:T(4,128)}) custom-call(bf16[1024,768]{1,0:T(8,128)(2,1)} %get-tuple-element.190.refs_0_, bf16[1024,768]{1,0:T(8,128)(2,1)} %get-tuple-element.191.refs_1_, f32[1024,128]{1,0:T(8,128)} %get-tuple-element.192.refs_2_, ...), custom_call_target="tpu_custom_call" | custom-call | tf_op jit(solution)/shard_map/feed_back/pallas_call | solution.py:44
  227.2 2.4 fold_split.5
  229.6 1.2 collective-permute-start.25
  231.3 1.8 collective-permute-done.21.refs_2_
  233.1 3.9 collective-permute-done.25.refs_6_
  237.0 0.7 copy-done.5
  237.7 3.7 fold_near.3
  241.4 1.6 collective-permute-start.27
  243.2 1.2 collective-permute-done.30.refs_12_
  245.1 21.6 %pack.3 = (bf16[2,2,448,384]{3,2,1,0:T(8,128)(2,1)}, bf16[2,2,448,384]{3,2,1,0:T(8,128)(2,1)}, bf16[2,2,448,384]{3,2,1,0:T(8,128)(2,1)}, bf16[2,2,448,384]{3,2,1,0:T(8,128)(2,1)}) custom-call(s32[1,2]{1,0:T(1,128)} %refs_1_.9, bf16[1024,1536]{1,0:T(8,128)(2,1)} %get-tuple-element.218.refs_1_, ...), custom_call_target="tpu_custom_call" | custom-call | tf_op jit(solution)/shard_map/pack/pallas_call | solution.py:44
  266.7 1.7 collective-permute-start.32
  269.0 2.5 fold_far.3
  271.5 7.4 %mix_back.3 = (bf16[1024,1536]{1,0:T(8,128)(2,1)}, bf16[6,128,256]{2,1,0:T(8,128)(2,1)}) custom-call(bf16[2,1024,768]{2,1,0:T(8,128)(2,1)} %get-tuple-element.203.refs_5_.refs_2_.refs_0_.refs_4_, bf16[2,384,768]{2,1,0:T(8,128)(2,1)} %refs_1_.8, bf16[2,384,768]{2,1,0:T(8,128)(2,1)} %collective-permute-done.3.refs_10_.refs_2_, ...), custom_call_target="tpu_custom_call" | custom-call | tf_op jit(solution)/shard_map/mix_back/pallas_call | solution.py:44
  278.9 2.0 collective-permute-done.31.refs_9_
  281.0 19.5 %attend_back.3 = (bf16[1024,1152]{1,0:T(8,128)(2,1)}, bf16[1024,1152]{1,0:T(8,128)(2,1)}) custom-call(s32[1,2]{1,0:T(1,128)} %refs_1_.9, bf16[1024,768]{1,0:T(8,128)(2,1)} %get-tuple-element.149.refs_1_.refs_6_, bf16[1024,768]{1,0:T(8,128)(2,1)} %get-tuple-element.150.refs_2_.refs_7_, bf16[1024,768]{1,0:T(8,128)(2,1)} %get-tuple-element.151.refs_3_, ...), custom_call_target="tpu_custom_call" | custom-call | tf_op jit(solution)/shard_map/attend_back/pallas_call | solution.py:44
  300.7 4.1 %fold_split.6 = (bf16[2,448,384]{2,1,0:T(8,128)(2,1)}, bf16[2,448,384]{2,1,0:T(8,128)(2,1)}, bf16[2,448,384]{2,1,0:T(8,128)(2,1)}, bf16[2,448,384]{2,1,0:T(8,128)(2,1)}) custom-call(s32[1,2]{1,0:T(1,128)} %refs_1_.9, bf16[2,2,448,384]{3,2,1,0:T(8,128)(2,1)} %get-tuple-element.223.refs_3_.refs_1_, bf16[2,2,448,384]{3,2,1,0:T(8,128)(2,1)} %collective-permute-done.32.refs_2_, ...), custom_call_target="tpu_custom_call" | custom-call | flops 999999995904 | bytes 999999995904 | tf_op jit(solution)/shard_map/fold_split/pallas_call | solution.py:44
  304.8 1.5 collective-permute-start.34
  306.7 2.6 collective-permute-start.37
  309.3 9.1 %qkv_grad.3 = (bf16[2,2,144,384]{3,2,1,0:T(8,128)(2,1)}, bf16[2,2,144,384]{3,2,1,0:T(8,128)(2,1)}, bf16[2,2,144,384]{3,2,1,0:T(8,128)(2,1)}, bf16[2,2,144,384]{3,2,1,0:T(8,128)(2,1)}) custom-call(bf16[1024,768]{1,0:T(8,128)(2,1)} %refs_0_.39, bf16[1024,1152]{1,0:T(8,128)(2,1)} %get-tuple-element.228.refs_5_.refs_1_.refs_0_, ...), custom_call_target="tpu_custom_call" | custom-call | tf_op jit(solution)/shard_map/qkv_grad/pallas_call | solution.py:44
  318.4 1.7 collective-permute-start.38
  320.7 2.6 collective-permute-done.34.refs_2_
  323.3 1.6 collective-permute-done.35.refs_4_
  324.9 3.1 fold_near.4
  328.5 9.7 %input_back.1.refs_5_ = f32[1024,768]{1,0:T(8,128)} custom-call(bf16[1024,1152]{1,0:T(8,128)(2,1)} %get-tuple-element.228.refs_5_.refs_1_.refs_0_, bf16[1024,1152]{1,0:T(8,128)(2,1)} %get-tuple-element.229.refs_1_, bf16[2,3,768,384]{3,2,1,0:T(8,128)(2,1)} %bitcast.23, bf16[2,3,768,384]{3,2,1,0:T(8,128)(2,1)} %collective-permute-done.refs_1_.refs_2_.refs_13_.refs_3_, ...), custom_call_target="tpu_custom_call" | custom-call | tf_op jit(solution)/shard_map/input_back/pallas_call | solution.py:44
  338.2 2.4 fold_split.7
  341.2 0.8 collective-permute-start.41
  341.9 2.5 collective-permute-done.42.refs_2_
  344.4 2.3 fold_far.4
  347.4 2.1 fold_near.5
  349.5 1.6 collective-permute-start.44
  351.1 2.6 collective-permute-start.43
  353.7 2.3 settle.3
  356.0 1.7 collective-permute-done.44.refs_2_
  357.7 1.8 fold_far.5
  359.5 2.7 collective-permute-start.45
  362.2 7.5 %collective-permute-done.43.refs_2_ = bf16[448,384]{1,0:T(8,128)(2,1)} collective-permute-done((bf16[448,384]{1,0:T(8,128)(2,1)}, bf16[448,384]{1,0:T(8,128)(2,1)}, u32[]{:S(2)}, u32[]{:S(2)}) %collective-permute-start.43) | collective-permute-done | bytes 344096 | tf_op jit(solution)/shard_map/ppermute | solution.py:1189
  369.7 2.1 settle.4
  371.7 1.7 settle.5
  373.4 0.7 add_reduce_fusion
  374.2 11.5 %all_to_all.8 = f32[32,1,128]{2,1,0:T(1,128)} all-to-all(f32[32,1,128]{2,1,0:T(1,128)S(1)} %broadcast_in_dim.10), channel_id=1, replica_groups=mesh['z'=4,'y'=2,'x'=2,'narrow'=2] {'z','y','x','narrow'}, dimensions={0} | all-to-all | bytes 32768 | tf_op jit(solution)/shard_map/all_to_all | solution.py:1391
  385.7 6.5 %update.1 = (f32[2,3,48,384]{3,2,1,0:T(8,128)}, f32[2,3,48,384]{3,2,1,0:T(8,128)}, f32[2,3,48,384]{3,2,1,0:T(8,128)}, f32[2,24,768]{2,1,0:T(8,128)}, f32[2,24,76...) custom-call(f32[32,128]{1,0:T(8,128)} %bitcast.28, ...), custom_call_target="tpu_custom_call" | custom-call | tf_op jit(solution)/shard_map/update/pallas_call | solution.py:44
  (83 shorter events, 12.3 us)
Async XLA Ops:
  0.7 9.9 %collective-permute-start = (bf16[2,3,768,384]{3,2,1,0:T(8,128)(2,1)}, bf16[2,3,768,384]{3,2,1,0:T(8,128)(2,1)}, u32[]{:S(2)}, u32[]{:S(2)}) collective-permute-start(bf16[2,3,768,384]{3,2,1,0:T(8,128)(2,1)} %bitcast.19), channel_id=1, source_target_pairs={{0,1},{1,0},{2,3},{3,2},{4,5},{5,4},{6,7},{7,6},{8,9},{9,8},{10,11... | collective-permute-start | bytes 10616840 | tf_op jit(solution)/shard_map/ppermute | solution.py:1078
  1.2 16.0 %collective-permute-start.3 = (bf16[2,384,768]{2,1,0:T(8,128)(2,1)}, bf16[2,384,768]{2,1,0:T(8,128)(2,1)}, u32[]{:S(2)}, u32[]{:S(2)}) collective-permute-start(bf16[2,384,768]{2,1,0:T(8,128)(2,1)} %refs_1_.8), channel_id=1, source_target_pairs={{0,1},{1,0},{2,3},{3,2},{4,5},{5,4},{6,7},{7,6},{8,9},{9,8},{10,11... | collective-permute-start | bytes 3538952 | tf_op jit(solution)/shard_map/ppermute | solution.py:1078
  10.1 7.5 %collective-permute-start.2 = (f32[1,3,128,256]{3,2,1,0:T(8,128)}, f32[1,3,128,256]{3,2,1,0:T(8,128)}, u32[]{:S(2)}, u32[]{:S(2)}) collective-permute-start(f32[1,3,128,256]{3,2,1,0:T(8,128)} %get-tuple-element.156), channel_id=1, source_target_pairs={{0,1},{1,0},{2,3},{3,2},{4,5},{5,4},{6,7},{7,6},{8,9},{9,8},{10,11... | collective-permute-start | bytes 1179656 | tf_op jit(solution)/shard_map/ppermute | solution.py:1078
  17.0 2.1 collective-permute-start.1
  17.2 16.4 %collective-permute-start.4 = (bf16[2,768,1536]{2,1,0:T(8,128)(2,1)}, bf16[2,768,1536]{2,1,0:T(8,128)(2,1)}, u32[]{:S(2)}, u32[]{:S(2)}) collective-permute-start(bf16[2,768,1536]{2,1,0:T(8,128)(2,1)} %refs_6_.1), channel_id=1, source_target_pairs={{0,1},{1,0},{2,3},{3,2},{4,5},{5,4},{6,7},{7,6},{8,9},{9,8},{10,11... | collective-permute-start | bytes 14155784 | tf_op jit(solution)/shard_map/ppermute | solution.py:1078
  19.1 14.4 %collective-permute-start.5 = (bf16[2,1536,768]{2,1,0:T(8,128)(2,1)}, bf16[2,1536,768]{2,1,0:T(8,128)(2,1)}, u32[]{:S(2)}, u32[]{:S(2)}) collective-permute-start(bf16[2,1536,768]{2,1,0:T(8,128)(2,1)} %refs_8_.2), channel_id=1, source_target_pairs={{0,1},{1,0},{2,3},{3,2},{4,5},{5,4},{6,7},{7,6},{8,9},{9,8},{10,11... | collective-permute-start | bytes 14155784 | tf_op jit(solution)/shard_map/ppermute | solution.py:1078
  54.6 29.6 %collective-permute-start.10 = (bf16[1024,1536]{1,0:T(8,128)(2,1)}, bf16[1024,1536]{1,0:T(8,128)(2,1)}, u32[]{:S(2)}, u32[]{:S(2)}) collective-permute-start(bf16[1024,1536]{1,0:T(8,128)(2,1)} %get-tuple-element.170), channel_id=1, source_target_pairs={{0,1},{1,0},{2,3},{3,2},{4,5},{5,4},{6,7},{7,6},{8,9},{9,8},{10,11... | collective-permute-start | bytes 9437192 | tf_op jit(solution)/shard_map/ppermute | solution.py:1078
  55.1 28.6 %collective-permute-start.7 = (bf16[1024,768]{1,0:T(8,128)(2,1)}, bf16[1024,768]{1,0:T(8,128)(2,1)}, u32[]{:S(2)}, u32[]{:S(2)}) collective-permute-start(bf16[1024,768]{1,0:T(8,128)(2,1)} %refs_0_.39), channel_id=1, source_target_pairs={{0,1},{1,0},{2,3},{3,2},{4,5},{5,4},{6,7},{7,6},{8,9},{9,8},{10,11... | collective-permute-start | bytes 4718600 | tf_op jit(solution)/shard_map/ppermute | solution.py:1078
  66.3 2.7 collective-permute-start.6
  66.7 17.5 %collective-permute-start.9 = (bf16[1024,768]{1,0:T(8,128)(2,1)}, bf16[1024,768]{1,0:T(8,128)(2,1)}, u32[]{:S(2)}, u32[]{:S(2)}) collective-permute-start(bf16[1024,768]{1,0:T(8,128)(2,1)} %get-tuple-element.157.refs_0_.refs_5_), channel_id=1, source_target_pairs={{0,1},{1,0},{2,3},{3,2},{4,5},{5,4},{6,7},{7,6},{8,9},{9,8},{10,11... | collective-permute-start | bytes 4718600 | tf_op jit(solution)/shard_map/ppermute | solution.py:1078
  66.8 17.0 %collective-permute-start.8 = (bf16[1024,384]{1,0:T(8,128)(2,1)}, bf16[1024,384]{1,0:T(8,128)(2,1)}, u32[]{:S(2)}, u32[]{:S(2)}) collective-permute-start(bf16[1024,384]{1,0:T(8,128)(2,1)} %get-tuple-element.169.refs_5_), channel_id=1, source_target_pairs={{0,1},{1,0},{2,3},{3,2},{4,5},{5,4},{6,7},{7,6},{8,9},{9,8},{10,11... | collective-permute-start | bytes 2359304 | tf_op jit(solution)/shard_map/ppermute | solution.py:1078
  69.0 15.3 %collective-permute-start.11 = (bf16[1024,768]{1,0:T(8,128)(2,1)}, bf16[1024,768]{1,0:T(8,128)(2,1)}, u32[]{:S(2)}, u32[]{:S(2)}) collective-permute-start(bf16[1024,768]{1,0:T(8,128)(2,1)} %get-tuple-element.160.refs_0_.refs_11_), channel_id=1, source_target_pairs={{0,1},{1,0},{2,3},{3,2},{4,5},{5,4},{6,7},{7,6},{8,9},{9,8},{10,11... | collective-permute-start | bytes 4718600 | tf_op jit(solution)/shard_map/ppermute | solution.py:1078
  83.6 20.7 %collective-permute-start.13 = (bf16[1024,768]{1,0:T(8,128)(2,1)}, bf16[1024,768]{1,0:T(8,128)(2,1)}, u32[]{:S(2)}, u32[]{:S(2)}) collective-permute-start(bf16[1024,768]{1,0:T(8,128)(2,1)} %get-tuple-element.168.refs_0_.refs_5_), channel_id=1, source_target_pairs={{0,1},{1,0},{2,3},{3,2},{4,5},{5,4},{6,7},{7,6},{8,9},{9,8},{10,11... | collective-permute-start | bytes 4718600 | tf_op jit(solution)/shard_map/ppermute | solution.py:1078
  83.8 20.5 %collective-permute-start.12 = (bf16[1024,384]{1,0:T(8,128)(2,1)}, bf16[1024,384]{1,0:T(8,128)(2,1)}, u32[]{:S(2)}, u32[]{:S(2)}) collective-permute-start(bf16[1024,384]{1,0:T(8,128)(2,1)} %get-tuple-element.178.refs_5_), channel_id=1, source_target_pairs={{0,1},{1,0},{2,3},{3,2},{4,5},{5,4},{6,7},{7,6},{8,9},{9,8},{10,11... | collective-permute-start | bytes 2359304 | tf_op jit(solution)/shard_map/ppermute | solution.py:1078
  104.1 19.4 %collective-permute-start.14 = (bf16[1024,1536]{1,0:T(8,128)(2,1)}, bf16[1024,1536]{1,0:T(8,128)(2,1)}, u32[]{:S(2)}, u32[]{:S(2)}) collective-permute-start(bf16[1024,1536]{1,0:T(8,128)(2,1)} %get-tuple-element.182), channel_id=1, source_target_pairs={{0,1},{1,0},{2,3},{3,2},{4,5},{5,4},{6,7},{7,6},{8,9},{9,8},{10,11... | collective-permute-start | bytes 9437192 | tf_op jit(solution)/shard_map/ppermute | solution.py:1078
  122.9 8.0 %collective-permute-start.16 = (bf16[2,1024,768]{2,1,0:T(8,128)(2,1)}, bf16[2,1024,768]{2,1,0:T(8,128)(2,1)}, u32[]{:S(2)}, u32[]{:S(2)}) collective-permute-start(bf16[2,1024,768]{2,1,0:T(8,128)(2,1)} %get-tuple-element.179.refs_0_.refs_2_.refs_14_), channel_id=1, source_target_pairs={{0,1},{1,0},{2,3},{3,2},{4,5},{5,4},{6,7},{7,6},{8,9},{9,8},{10,11... | collective-permute-start | bytes 9437192 | tf_op jit(solution)/shard_map/ppermute | solution.py:1078
  123.4 10.1 %collective-permute-start.17 = (bf16[1024,1536]{1,0:T(8,128)(2,1)}, bf16[1024,1536]{1,0:T(8,128)(2,1)}, u32[]{:S(2)}, u32[]{:S(2)}) collective-permute-start(bf16[1024,1536]{1,0:T(8,128)(2,1)} %get-tuple-element.188), channel_id=1, source_target_pairs={{0,1},{1,0},{2,3},{3,2},{4,5},{5,4},{6,7},{7,6},{8,9},{9,8},{10,11... | collective-permute-start | bytes 9437192 | tf_op jit(solution)/shard_map/ppermute | solution.py:1078
  155.9 35.0 %collective-permute-start.19 = (bf16[2,2,448,384]{3,2,1,0:T(8,128)(2,1)}, bf16[2,2,448,384]{3,2,1,0:T(8,128)(2,1)}, u32[]{:S(2)}, u32[]{:S(2)}) collective-permute-start(bf16[2,2,448,384]{3,2,1,0:T(8,128)(2,1)} %get-tuple-element.198), channel_id=1, source_target_pairs={{0,2},{2,0},{1,3},{3,1},{4,6},{6,4},{5,7},{7,5},{8,10},{10,8},{9,1... | collective-permute-start | bytes 4128776 | tf_op jit(solution)/shard_map/ppermute | solution.py:1078
  158.9 32.3 %collective-permute-start.20 = (bf16[2,2,448,384]{3,2,1,0:T(8,128)(2,1)}, bf16[2,2,448,384]{3,2,1,0:T(8,128)(2,1)}, u32[]{:S(2)}, u32[]{:S(2)}) collective-permute-start(bf16[2,2,448,384]{3,2,1,0:T(8,128)(2,1)} %get-tuple-element.200), channel_id=1, source_target_pairs={{0,4},{4,0},{1,5},{5,1},{2,6},{6,2},{3,7},{7,3},{8,12},{12,8},{9,1... | collective-permute-start | bytes 4128776 | tf_op jit(solution)/shard_map/ppermute | solution.py:1078
  160.5 2.1 collective-permute-start.15
  190.7 4.9 %collective-permute-start.18 = (bf16[1024,1152]{1,0:T(8,128)(2,1)}, bf16[1024,1152]{1,0:T(8,128)(2,1)}, u32[]{:S(2)}, u32[]{:S(2)}) collective-permute-start(bf16[1024,1152]{1,0:T(8,128)(2,1)} %get-tuple-element.197), channel_id=1, source_target_pairs={{0,1},{1,0},{2,3},{3,2},{4,5},{5,4},{6,7},{7,6},{8,9},{9,8},{10,11... | collective-permute-start | bytes 7077896 | tf_op jit(solution)/shard_map/ppermute | solution.py:1078
  204.8 22.4 %collective-permute-start.23 = (bf16[2,2,144,384]{3,2,1,0:T(8,128)(2,1)}, bf16[2,2,144,384]{3,2,1,0:T(8,128)(2,1)}, u32[]{:S(2)}, u32[]{:S(2)}) collective-permute-start(bf16[2,2,144,384]{3,2,1,0:T(8,128)(2,1)} %get-tuple-element.209), channel_id=1, source_target_pairs={{0,2},{2,0},{1,3},{3,1},{4,6},{6,4},{5,7},{7,5},{8,10},{10,8},{9,1... | collective-permute-start | bytes 1327112 | tf_op jit(solution)/shard_map/ppermute | solution.py:1078
  205.4 21.8 %collective-permute-start.24 = (bf16[2,2,144,384]{3,2,1,0:T(8,128)(2,1)}, bf16[2,2,144,384]{3,2,1,0:T(8,128)(2,1)}, u32[]{:S(2)}, u32[]{:S(2)}) collective-permute-start(bf16[2,2,144,384]{3,2,1,0:T(8,128)(2,1)} %get-tuple-element.211), channel_id=1, source_target_pairs={{0,4},{4,0},{1,5},{5,1},{2,6},{6,2},{3,7},{7,3},{8,12},{12,8},{9,1... | collective-permute-start | bytes 1327112 | tf_op jit(solution)/shard_map/ppermute | solution.py:1078
  206.6 26.5 %collective-permute-start.21 = (bf16[2,448,384]{2,1,0:T(8,128)(2,1)}, bf16[2,448,384]{2,1,0:T(8,128)(2,1)}, u32[]{:S(2)}, u32[]{:S(2)}) collective-permute-start(bf16[2,448,384]{2,1,0:T(8,128)(2,1)} %get-tuple-element.206), channel_id=1, source_target_pairs={{0,4},{4,0},{1,5},{5,1},{2,6},{6,2},{3,7},{7,3},{8,12},{12,8},{9,1... | collective-permute-start | bytes 2064392 | tf_op jit(solution)/shard_map/ppermute | solution.py:1078
  207.4 25.7 %collective-permute-start.22 = (bf16[2,448,384]{2,1,0:T(8,128)(2,1)}, bf16[2,448,384]{2,1,0:T(8,128)(2,1)}, u32[]{:S(2)}, u32[]{:S(2)}) collective-permute-start(bf16[2,448,384]{2,1,0:T(8,128)(2,1)} %get-tuple-element.208), channel_id=1, source_target_pairs={{0,2},{2,0},{1,3},{3,1},{4,6},{6,4},{5,7},{7,5},{8,10},{10,8},{9,1... | collective-permute-start | bytes 2064392 | tf_op jit(solution)/shard_map/ppermute | solution.py:1078
  229.6 7.4 %collective-permute-start.25 = (bf16[2,144,384]{2,1,0:T(8,128)(2,1)}, bf16[2,144,384]{2,1,0:T(8,128)(2,1)S(1)}, u32[]{:S(2)}, u32[]{:S(2)}) collective-permute-start(bf16[2,144,384]{2,1,0:T(8,128)(2,1)} %get-tuple-element.213), channel_id=1, source_target_pairs={{0,4},{4,0},{1,5},{5,1},{2,6},{6,2},{3,7},{7,3},{8,12},{12,8},{9,1... | collective-permute-start | bytes 663560 | tf_op jit(solution)/shard_map/ppermute | solution.py:1078
  230.8 6.2 %collective-permute-start.26 = (bf16[2,144,384]{2,1,0:T(8,128)(2,1)}, bf16[2,144,384]{2,1,0:T(8,128)(2,1)S(1)}, u32[]{:S(2)}, u32[]{:S(2)}) collective-permute-start(bf16[2,144,384]{2,1,0:T(8,128)(2,1)} %get-tuple-element.215), channel_id=1, source_target_pairs={{0,2},{2,0},{1,3},{3,1},{4,6},{6,4},{5,7},{7,5},{8,10},{10,8},{9,1... | collective-permute-start | bytes 663560 | tf_op jit(solution)/shard_map/ppermute | solution.py:1078
  231.3 13.8 %collective-permute-start.28 = (bf16[2,1024,768]{2,1,0:T(8,128)(2,1)}, bf16[2,1024,768]{2,1,0:T(8,128)(2,1)}, u32[]{:S(2)}, u32[]{:S(2)}) collective-permute-start(bf16[2,1024,768]{2,1,0:T(8,128)(2,1)} %get-tuple-element.203.refs_5_.refs_2_.refs_0_.refs_4_), channel_id=1, source_target_pairs={{0,1},{1,0},{2,3},{3,2},{4,5},{5,4},{6,7},{7,6},{8,9},{9,8},{10,11... | collective-permute-start | bytes 9437192 | tf_op jit(solution)/shard_map/ppermute | solution.py:1078
  233.1 12.0 %collective-permute-start.29 = (bf16[1024,1536]{1,0:T(8,128)(2,1)}, bf16[1024,1536]{1,0:T(8,128)(2,1)}, u32[]{:S(2)}, u32[]{:S(2)}) collective-permute-start(bf16[1024,1536]{1,0:T(8,128)(2,1)} %get-tuple-element.220), channel_id=1, source_target_pairs={{0,1},{1,0},{2,3},{3,2},{4,5},{5,4},{6,7},{7,6},{8,9},{9,8},{10,11... | collective-permute-start | bytes 9437192 | tf_op jit(solution)/shard_map/ppermute | solution.py:1078
  237.0 0.7 copy-start.5
  237.0 0.8 copy-start.6
  237.7 5.3 %copy-start.2 = (f32[4,768]{1,0:T(4,128)S(1)}, f32[4,768]{1,0:T(4,128)}, u32[]{:S(2)}) copy-start(f32[4,768]{1,0:T(4,128)} %get-tuple-element.222) | copy-start | bytes 36868
  237.7 5.3 %copy-start.3 = (f32[4,768]{1,0:T(4,128)S(1)}, f32[4,768]{1,0:T(4,128)}, u32[]{:S(2)}) copy-start(f32[4,768]{1,0:T(4,128)} %get-tuple-element.221) | copy-start | bytes 36868
  241.4 27.5 %collective-permute-start.27 = (bf16[2,592,384]{2,1,0:T(8,128)(2,1)}, bf16[2,592,384]{2,1,0:T(8,128)(2,1)}, u32[]{:S(2)}, u32[]{:S(2)}) collective-permute-start(bf16[2,592,384]{2,1,0:T(8,128)(2,1)} %get-tuple-element.217), channel_id=1, source_target_pairs={{0,8},{8,0},{16,24},{24,16},{1,9},{9,1},{17,25},{25,17},{2,10},{10... | collective-permute-start | bytes 2727944 | tf_op jit(solution)/shard_map/ppermute | solution.py:1189
  243.2 2.0 copy-start
  243.2 1.3 collective-permute-start.30
  244.5 0.6 copy-start.1
  266.7 33.9 %collective-permute-start.32 = (bf16[2,2,448,384]{3,2,1,0:T(8,128)(2,1)}, bf16[2,2,448,384]{3,2,1,0:T(8,128)(2,1)}, u32[]{:S(2)}, u32[]{:S(2)}) collective-permute-start(bf16[2,2,448,384]{3,2,1,0:T(8,128)(2,1)} %get-tuple-element.230), channel_id=1, source_target_pairs={{0,2},{2,0},{1,3},{3,1},{4,6},{6,4},{5,7},{7,5},{8,10},{10,8},{9,1... | collective-permute-start | bytes 4128776 | tf_op jit(solution)/shard_map/ppermute | solution.py:1078
  268.4 32.3 %collective-permute-start.33 = (bf16[2,2,448,384]{3,2,1,0:T(8,128)(2,1)}, bf16[2,2,448,384]{3,2,1,0:T(8,128)(2,1)}, u32[]{:S(2)}, u32[]{:S(2)}) collective-permute-start(bf16[2,2,448,384]{3,2,1,0:T(8,128)(2,1)} %get-tuple-element.232), channel_id=1, source_target_pairs={{0,4},{4,0},{1,5},{5,1},{2,6},{6,2},{3,7},{7,3},{8,12},{12,8},{9,1... | collective-permute-start | bytes 4128776 | tf_op jit(solution)/shard_map/ppermute | solution.py:1078
  278.8 2.1 collective-permute-start.31
  300.4 8.9 %collective-permute-start.36 = (bf16[1024,1152]{1,0:T(8,128)(2,1)}, bf16[1024,1152]{1,0:T(8,128)(2,1)}, u32[]{:S(2)}, u32[]{:S(2)}) collective-permute-start(bf16[1024,1152]{1,0:T(8,128)(2,1)} %get-tuple-element.229.refs_1_), channel_id=1, source_target_pairs={{0,1},{1,0},{2,3},{3,2},{4,5},{5,4},{6,7},{7,6},{8,9},{9,8},{10,11... | collective-permute-start | bytes 7077896 | tf_op jit(solution)/shard_map/ppermute | solution.py:1078
  304.8 18.6 %collective-permute-start.34 = (bf16[2,448,384]{2,1,0:T(8,128)(2,1)}, bf16[2,448,384]{2,1,0:T(8,128)(2,1)}, u32[]{:S(2)}, u32[]{:S(2)}) collective-permute-start(bf16[2,448,384]{2,1,0:T(8,128)(2,1)} %get-tuple-element.234), channel_id=1, source_target_pairs={{0,4},{4,0},{1,5},{5,1},{2,6},{6,2},{3,7},{7,3},{8,12},{12,8},{9,1... | collective-permute-start | bytes 2064392 | tf_op jit(solution)/shard_map/ppermute | solution.py:1078
  306.3 18.6 %collective-permute-start.35 = (bf16[2,448,384]{2,1,0:T(8,128)(2,1)}, bf16[2,448,384]{2,1,0:T(8,128)(2,1)}, u32[]{:S(2)}, u32[]{:S(2)}) collective-permute-start(bf16[2,448,384]{2,1,0:T(8,128)(2,1)} %get-tuple-element.236), channel_id=1, source_target_pairs={{0,2},{2,0},{1,3},{3,1},{4,6},{6,4},{5,7},{7,5},{8,10},{10,8},{9,1... | collective-permute-start | bytes 2064392 | tf_op jit(solution)/shard_map/ppermute | solution.py:1078
  306.7 47.0 %collective-permute-start.37 = (bf16[592,384]{1,0:T(8,128)(2,1)}, bf16[592,384]{1,0:T(8,128)(2,1)}, u32[]{:S(2)}, u32[]{:S(2)}) collective-permute-start(bf16[592,384]{1,0:T(8,128)(2,1)} %get-tuple-element.239), channel_id=1, source_target_pairs={{0,16},{8,24},{16,0},{24,8},{1,17},{9,25},{17,1},{25,9},{2,18},{10... | collective-permute-start | bytes 1363976 | tf_op jit(solution)/shard_map/ppermute | solution.py:1189
  318.4 19.7 %collective-permute-start.38 = (bf16[2,2,144,384]{3,2,1,0:T(8,128)(2,1)}, bf16[2,2,144,384]{3,2,1,0:T(8,128)(2,1)}, u32[]{:S(2)}, u32[]{:S(2)}) collective-permute-start(bf16[2,2,144,384]{3,2,1,0:T(8,128)(2,1)} %get-tuple-element.240), channel_id=1, source_target_pairs={{0,2},{2,0},{1,3},{3,1},{4,6},{6,4},{5,7},{7,5},{8,10},{10,8},{9,1... | collective-permute-start | bytes 1327112 | tf_op jit(solution)/shard_map/ppermute | solution.py:1078
  320.1 18.1 %collective-permute-start.39 = (bf16[2,2,144,384]{3,2,1,0:T(8,128)(2,1)}, bf16[2,2,144,384]{3,2,1,0:T(8,128)(2,1)}, u32[]{:S(2)}, u32[]{:S(2)}) collective-permute-start(bf16[2,2,144,384]{3,2,1,0:T(8,128)(2,1)} %get-tuple-element.242), channel_id=1, source_target_pairs={{0,4},{4,0},{1,5},{5,1},{2,6},{6,2},{3,7},{7,3},{8,12},{12,8},{9,1... | collective-permute-start | bytes 1327112 | tf_op jit(solution)/shard_map/ppermute | solution.py:1078
  328.0 16.4 %collective-permute-start.42 = (bf16[2,448,384]{2,1,0:T(8,128)(2,1)}, bf16[2,448,384]{2,1,0:T(8,128)(2,1)}, u32[]{:S(2)}, u32[]{:S(2)}) collective-permute-start(bf16[2,448,384]{2,1,0:T(8,128)(2,1)} %get-tuple-element.247), channel_id=1, source_target_pairs={{0,8},{8,0},{16,24},{24,16},{1,9},{9,1},{17,25},{25,17},{2,10},{10... | collective-permute-start | bytes 2064392 | tf_op jit(solution)/shard_map/ppermute | solution.py:1189
  340.6 6.3 %collective-permute-start.40 = (bf16[2,144,384]{2,1,0:T(8,128)(2,1)}, bf16[2,144,384]{2,1,0:T(8,128)(2,1)}, u32[]{:S(2)}, u32[]{:S(2)}) collective-permute-start(bf16[2,144,384]{2,1,0:T(8,128)(2,1)} %get-tuple-element.244), channel_id=1, source_target_pairs={{0,4},{4,0},{1,5},{5,1},{2,6},{6,2},{3,7},{7,3},{8,12},{12,8},{9,1... | collective-permute-start | bytes 663560 | tf_op jit(solution)/shard_map/ppermute | solution.py:1078
  341.2 6.2 %collective-permute-start.41 = (bf16[2,144,384]{2,1,0:T(8,128)(2,1)}, bf16[2,144,384]{2,1,0:T(8,128)(2,1)}, u32[]{:S(2)}, u32[]{:S(2)}) collective-permute-start(bf16[2,144,384]{2,1,0:T(8,128)(2,1)} %get-tuple-element.246), channel_id=1, source_target_pairs={{0,2},{2,0},{1,3},{3,1},{4,6},{6,4},{5,7},{7,5},{8,10},{10,8},{9,1... | collective-permute-start | bytes 663560 | tf_op jit(solution)/shard_map/ppermute | solution.py:1078
  349.5 8.1 %collective-permute-start.44 = (bf16[2,144,384]{2,1,0:T(8,128)(2,1)}, bf16[2,144,384]{2,1,0:T(8,128)(2,1)}, u32[]{:S(2)}, u32[]{:S(2)}) collective-permute-start(bf16[2,144,384]{2,1,0:T(8,128)(2,1)} %get-tuple-element.252), channel_id=1, source_target_pairs={{0,8},{8,0},{16,24},{24,16},{1,9},{9,1},{17,25},{25,17},{2,10},{10... | collective-permute-start | bytes 663560 | tf_op jit(solution)/shard_map/ppermute | solution.py:1189
  351.1 18.6 %collective-permute-start.43 = (bf16[448,384]{1,0:T(8,128)(2,1)}, bf16[448,384]{1,0:T(8,128)(2,1)}, u32[]{:S(2)}, u32[]{:S(2)}) collective-permute-start(bf16[448,384]{1,0:T(8,128)(2,1)} %get-tuple-element.251), channel_id=1, source_target_pairs={{0,16},{8,24},{16,0},{24,8},{1,17},{9,25},{17,1},{25,9},{2,18},{10... | collective-permute-start | bytes 1032200 | tf_op jit(solution)/shard_map/ppermute | solution.py:1189
  359.5 14.0 %copy-start.4 = (f32[8,128]{1,0:T(8,128)S(1)}, f32[8,128]{1,0:T(8,128)}, u32[]{:S(2)}) copy-start(f32[8,128]{1,0:T(8,128)} %get-tuple-element.250) | copy-start | bytes 12292
  359.5 12.3 %collective-permute-start.45 = (bf16[144,384]{1,0:T(8,128)(2,1)}, bf16[144,384]{1,0:T(8,128)(2,1)}, u32[]{:S(2)}, u32[]{:S(2)}) collective-permute-start(bf16[144,384]{1,0:T(8,128)(2,1)} %get-tuple-element.256), channel_id=1, source_target_pairs={{0,16},{8,24},{16,0},{24,8},{1,17},{9,25},{17,1},{25,9},{2,18},{10... | collective-permute-start | bytes 331784 | tf_op jit(solution)/shard_map/ppermute | solution.py:1189

commit v5 on v4

--- a/solution.py
+++ b/solution.py
@@ -716,7 +716,7 @@
 def attend_back_kernel(
     here_ref, qo_ref, qp_ref, ko_ref, kp_ref, vo_ref, vp_ref, gx_ref, state_ref, dkv_ref,
     cos_ref, sin_ref,
-    go_ref, gp_ref,
+    go_ref, gpq_ref, gpk_ref, gpv_ref,
     dstate,
 ):
     rows = qo_ref.shape[0]
@@ -736,8 +736,8 @@
     causal, anti = col <= row, row <= col
     cos, sin = cos_ref[...], sin_ref[...]
     trig = jnp.where(low, cos, sin), jnp.where(low, sin, cos)
-    for side, (q_ref, k_ref, v_ref, out_ref) in enumerate(
-        ((qo_ref, ko_ref, vo_ref, go_ref), (qp_ref, kp_ref, vp_ref, gp_ref))
+    for side, (q_ref, k_ref, v_ref) in enumerate(
+        ((qo_ref, ko_ref, vo_ref), (qp_ref, kp_ref, vp_ref))
     ):
         for pair in range(pairs):
             at = side * pairs + pair
@@ -773,21 +773,56 @@
             for kind, value in enumerate(
                 (jnp.where(low, dq[0], dq[1]), jnp.where(low, dk[0], dk[1]), dv)
             ):
-                base = kind * half + pair * 128
-                out_ref[:, base : base + 128] = value.astype(BF16)
-
-
-def attend_back_on_kernel(*refs):
-    inputs, (wo_ref, wp_ref, first_ref), (go_ref, gp_ref, up_ref, dstate) = (
-        refs[:12], refs[12:15], refs[15:],
-    )
-    attend_back_kernel(*inputs, go_ref, gp_ref, dstate)
-    half = wo_ref.shape[2]
-    total = first_ref[...].astype(F32)
-    for g_ref, w_ref in ((go_ref, wo_ref), (gp_ref, wp_ref)):
-        for kind in range(3):
-            total = total + dot_nt(g_ref[:, kind * half : kind * half + half], w_ref[kind])
-    up_ref[...] = total.astype(up_ref.dtype)
+                if side == 0:
+                    base = kind * half + pair * 128
+                    go_ref[:, base : base + 128] = value.astype(BF16)
+                else:
+                    out_ref = (gpq_ref, gpk_ref, gpv_ref)[kind]
+                    out_ref[:, pair * 128 : pair * 128 + 128] = value.astype(BF16)
+
+
+def attend_back_on_kernel(layer, *refs):
+    inputs, (wo_ref, wp_ref, gfb_ref), (go_ref, *gp_refs, up_ref), scratch = (
+        refs[:12], refs[12:15], refs[15:20], refs[20:],
+    )
+    dstate, g, w, gb, up, semaphores = scratch
+    step, steps = pl.program_id(0), pl.num_programs(0)
+    rows, third = go_ref.shape[0], wo_ref.shape[3]
+    total = gb.shape[0]
+    pieces = [
+        (ref.at[layer, kind], w.at[side, :, pl.ds(kind * third, third)])
+        for side, ref in enumerate((wo_ref, wp_ref))
+        for kind in range(3)
+    ] + [(gfb_ref.at[1], gb)]
+    copies = [pltpu.make_async_copy(*piece, semaphores.at[n]) for n, piece in enumerate(pieces)]
+
+    @pl.when(step == 0)
+    def _():
+        for copy in copies:
+            copy.start()
+
+    attend_back_kernel(*inputs, go_ref, *gp_refs, dstate)
+    at = pl.ds(pl.multiple_of((steps - 1 - step) * rows, rows), rows)
+    g[0, at, :] = go_ref[...]
+    for kind, gp_ref in enumerate(gp_refs):
+        g[1, at, kind * third : kind * third + third] = gp_ref[...]
+
+    @pl.when(step == steps - 1)
+    def _():
+        for copy in copies:
+            copy.wait()
+        leaving = []
+        for n in range(2):
+            part = slice(n * total // 2, (n + 1) * total // 2)
+            value = gb[part, :].astype(F32)
+            value = value + dot_nt(g[0, part, :], w[0]) + dot_nt(g[1, part, :], w[1])
+            up[part, :] = value.astype(BF16)
+            here = pl.ds(n * total // 2, total // 2)
+            copy = pltpu.make_async_copy(up.at[here, :], up_ref.at[here, :], semaphores.at[7 + n])
+            copy.start()
+            leaving.append(copy)
+        for copy in leaving:
+            copy.wait()
 
 
 def attend_back(here, own, peer, gx, states, dkv, cos, sin, after=(), onward=None):
@@ -805,42 +840,47 @@
         pl.BlockSpec((1, heads, 128, 256), lambda i: (back(i), 0, 0, 0)),
         whole(dkv.shape), trig, trig,
     ]
-    outs = [row_spec(CHUNK, 3 * half, back)] * 2
-    shapes = [shape((rows, 3 * half), BF16)] * 2
+    outs = [row_spec(CHUNK, 3 * half, back)] + [row_spec(CHUNK, half, back)] * 3
+    shapes = [shape((rows, 3 * half), BF16)] + [shape((rows, half), BF16)] * 3
     kernel = attend_back_kernel
+    scratch = [pltpu.VMEM((heads, 128, 256), F32)]
     if onward is not None:
         w_own, w_peer, layer, gfb = onward
-        kernel = attend_back_on_kernel
+        kernel = functools.partial(attend_back_on_kernel, layer)
         width = gfb.shape[2]
         args += (w_own, w_peer, gfb)
-        specs += [layer_spec(w_own, layer), layer_spec(w_peer, layer)]
-        specs += [pl.BlockSpec((None, CHUNK, width), lambda i: (1, back(i), 0))]
-        outs, shapes = outs + [row_spec(CHUNK, width, back)], shapes + [shape((rows, width), BF16)]
+        specs += [ANY] * 3
+        outs, shapes = outs + [ANY], shapes + [shape((rows, width), BF16)]
+        scratch += [
+            pltpu.VMEM((2, rows, 3 * half), BF16),
+            pltpu.VMEM((2, width, 3 * half), BF16),
+            pltpu.VMEM((rows, width), BF16),
+            pltpu.VMEM((rows, width), BF16),
+            pltpu.SemaphoreType.DMA((9,)),
+        ]
     return run(
-        kernel, args, specs, outs, shapes, (steps,), "attend_back",
-        [pltpu.VMEM((heads, 128, 256), F32)],
-        after,
-    )
-
-
-def input_back_kernel(go_ref, gp_ref, wo_ref, wp_ref, first_ref, out_ref):
+        kernel, args, specs, outs, shapes, (steps,), "attend_back", scratch, after,
+    )
+
+
+def input_back_kernel(go_ref, gpq_ref, gpk_ref, gpv_ref, wo_ref, wp_ref, first_ref, out_ref):
     half = wo_ref.shape[2]
     total = first_ref[...].astype(F32)
-    for g_ref, w_ref in ((go_ref, wo_ref), (gp_ref, wp_ref)):
-        for kind in range(3):
-            total = total + dot_nt(g_ref[:, kind * half : kind * half + half], w_ref[kind])
+    for kind, gp_ref in enumerate((gpq_ref, gpk_ref, gpv_ref)):
+        total = total + dot_nt(go_ref[:, kind * half : kind * half + half], wo_ref[kind])
+        total = total + dot_nt(gp_ref[...], wp_ref[kind])
     out_ref[...] = total.astype(out_ref.dtype)
 
 
 def input_back(g_own, g_peer, w_own, w_peer, layer, gfb, after=()):
     _, rows, width = gfb.shape
     block = rows // 2
-    third, full = row_spec(block, g_own.shape[1]), row_spec(block, width)
+    third, full = row_spec(block, g_own.shape[1] // 3), row_spec(block, width)
     return run(
         input_back_kernel,
-        (g_own, g_peer, w_own, w_peer, gfb),
-        [
-            third, third, layer_spec(w_own, layer), layer_spec(w_peer, layer),
+        (g_own, *g_peer, w_own, w_peer, gfb),
+        [
+            row_spec(block, g_own.shape[1]), third, third, third, layer_spec(w_own, layer), layer_spec(w_peer, layer),
             pl.BlockSpec((None, block, width), lambda i: (1, i, 0)),
         ],
         full,
@@ -905,7 +945,9 @@
 
 
 def q_pack_kernel(
-    a_ref, b_ref, c_ref, d_ref, ka_ref, sa_ref, kb_ref, sb_ref, left, right, out, scr, semaphores
+    a_ref, b_ref, c_ref, d0_ref, d1_ref, d2_ref,
+    ka_ref, sa_ref, kb_ref, sb_ref,
+    left, right, out, scr, semaphores,
 ):
     parts, _, lanes = right.shape
     rows, m = a_ref.shape
@@ -918,10 +960,10 @@
     ]
     arrivals = [
         [
-            copies.start(ref.at[:, pl.ds(n * lanes, lanes)], right.at[n, pl.ds(side * rows, rows), :])
-            for side, ref in enumerate((b_ref, d_ref))
+            copies.start(b_ref.at[:, pl.ds(n * lanes, lanes)], right.at[n, pl.ds(0, rows), :]),
+            copies.start(d_ref, right.at[n, pl.ds(rows, rows), :]),
         ]
-        for n in range(parts)
+        for n, d_ref in enumerate((d0_ref, d1_ref, d2_ref))
     ]
     leaving = []
     for n in range(parts):
@@ -943,8 +985,8 @@
     buffer = (2, 2, m // 16 * parts, lanes)
     return run(
         q_pack_kernel,
-        (a, b, c, d),
-        [ANY] * 4,
+        (a, b, c, *d),
+        [ANY] * 6,
         [ANY] * 4,
         [shape(buffer, BF16)] * 4,
         (1,),
@@ -1082,56 +1124,91 @@
     return (a_ref[at].astype(F32) + b_ref[at].astype(F32)).astype(BF16)
 
 
-def fold_split_kernel(index_ref, ka, ga, kb, gb, ka_out, sa_out, kb_out, sb_out):
-    x, y = lax.axis_index("x"), lax.axis_index("y")
-    ka_out[0] = sum_of(ka, ga, 0, y)
-    sa_out[0] = sum_of(ka, ga, 0, 1 - y)
-    kb_out[0] = sum_of(kb, gb, 0, x)
-    sb_out[0] = sum_of(kb, gb, 0, 1 - x)
-
-
-def fold_split(index, ka, ga, kb, gb, after=()):
+def fold_split_kernel(ka, ga, kb, gb, sa_ref, sb_ref, held, out, semaphores):
+    other = 1 - lax.axis_index("y"), 1 - lax.axis_index("x")
+    copies = Copies(semaphores)
+    arrivals = {}
+    for z in range(2):
+        for which, (k, g) in enumerate(((ka, ga), (kb, gb))):
+            arrivals[which, z] = [
+                copies.start(ref.at[z, other[which]], held.at[which, n, z])
+                for n, ref in enumerate((k, g))
+            ]
+    leaving = []
+    for (which, z), pair in arrivals.items():
+        for copy in pair:
+            copy.wait()
+        out[which, z] = sum_of(held.at[which, 0], held.at[which, 1], z)
+        leaving.append(copies.start(out.at[which, z], (sa_ref, sb_ref)[which].at[z]))
+    for copy in leaving:
+        copy.wait()
+
+
+def fold_split(ka, ga, kb, gb, after=()):
     _, _, r, c = ka.shape
     return run(
         fold_split_kernel,
-        (index, ka, ga, kb, gb),
-        [IN_SMEM]
-        + [pl.BlockSpec((1, 2, r, c), lambda z: (z, 0, 0, 0))] * 4,
-        [pl.BlockSpec((1, r, c), lambda z: (z, 0, 0))] * 4,
-        [shape((2, r, c), BF16)] * 4,
-        (2,),
+        (ka, ga, kb, gb),
+        [ANY] * 4,
+        [ANY] * 2,
+        [shape((2, r, c), BF16)] * 2,
+        (1,),
         "fold_split",
-        (),
+        [
+            pltpu.VMEM((2, 2, 2, r, c), BF16),
+            pltpu.VMEM((2, 2, r, c), BF16),
+            pltpu.SemaphoreType.DMA((12,)),
+        ],
         after,
         weight=FOLD_WEIGHT,
     )
 
 
-def fold_near_kernel(index_ref, *refs):
-    z = lax.axis_index("z") % 2
-    keep, send = refs[-2:]
-    for half in range(2):
-        done = 0
-        for at in range(0, len(refs) - 2, 4):
-            k, g = refs[at + 2 * half], refs[at + 2 * half + 1]
-            rows = slice(done, done + k.shape[1])
-            done += k.shape[1]
-            keep[half, rows] = sum_of(k, g, z)
-            send[half, rows] = sum_of(k, g, 1 - z)
-
-
-def fold_near(index, groups, after=()):
+def fold_near_kernel(groups, *refs):
+    inputs, (keep_ref, send_ref, *held, out, semaphores) = refs[: 6 * groups], refs[6 * groups :]
+    mine = lax.axis_index("y"), lax.axis_index("x")
+    z_mine = lax.axis_index("z") % 2
+    copies = Copies(semaphores)
+    arrivals = []
+    for group in range(groups):
+        arrays = inputs[6 * group : 6 * group + 6]
+        for which in range(2):
+            k, g, got = arrays[3 * which : 3 * which + 3]
+            place = held[group]
+            arrivals.append(
+                [copies.start(ref.at[z, mine[which]], place.at[which, n, z]) for z in range(2) for n, ref in enumerate((k, g))]
+                + [copies.start(got, place.at[which, 2])]
+            )
+    leaving = []
+    done = 0
+    for group in range(groups):
+        rows = held[group].shape[3]
+        here = pl.ds(done, rows)
+        for which in range(2):
+            for copy in arrivals[2 * group + which]:
+                copy.wait()
+            for n, (target, z) in enumerate(((send_ref, 1 - z_mine), (keep_ref, z_mine))):
+                total = sum(held[group][which, m, z].astype(F32) for m in range(3))
+                out[n, which, done : done + rows, :] = total.astype(BF16)
+                leaving.append(copies.start(out.at[n, which, here, :], target.at[which, here, :]))
+        done += rows
+    for copy in leaving:
+        copy.wait()
+
+
+def fold_near(groups, after=()):
     arrays = [array for group in groups for array in group]
-    rows, lanes = sum(group[0].shape[1] for group in groups), arrays[0].shape[2]
+    rows, lanes = sum(group[0].shape[2] for group in groups), arrays[0].shape[3]
     return run(
-        fold_near_kernel,
-        (index, *arrays),
-        [IN_SMEM] + [whole(array.shape) for array in arrays],
-        [whole((2, rows, lanes))] * 2,
+        functools.partial(fold_near_kernel, len(groups)),
+        arrays,
+        [ANY] * len(arrays),
+        [ANY] * 2,
         [shape((2, rows, lanes), BF16)] * 2,
         (1,),
         "fold_near",
-        (),
+        [pltpu.VMEM((2, 3, 2) + group[0].shape[2:], BF16) for group in groups]
+        + [pltpu.VMEM((2, 2, rows, lanes), BF16), pltpu.SemaphoreType.DMA((14 * len(groups),))],
         after,
         weight=FOLD_WEIGHT,
     )
@@ -1143,7 +1220,7 @@
     send[...] = sum_of(k, g, 1 - z)
 
 
-def fold_far(index, keep, got, after=()):
+def fold_far(index, keep, got, after=(), weight=FOLD_WEIGHT):
     return run(
         fold_far_kernel,
         (index, keep, got),
@@ -1154,30 +1231,39 @@
         "fold_far",
         (),
         after,
-        weight=FOLD_WEIGHT,
-    )
-
-
-def settle_kernel(norms, index_ref, k, g, out, squares):
-    total = k[...].astype(F32) + g[...].astype(F32)
-    out[...] = total
-    if norms:
-        row, lane = (lax.broadcasted_iota(jnp.int32, total.shape, n) for n in (0, 1))
-        here = jnp.logical_and(row >= NORM_ROW, row < NORM_ROW + 8)
-        other = jnp.logical_or(lane < lax.axis_index("narrow") * norms, lane >= (lax.axis_index("narrow") + 1) * norms)
-        total = jnp.where(jnp.logical_and(here, other), 0.0, total)
-    total = total * total
-    part = total[:, :128] + total[:, 128:256] + total[:, 256:]
-    squares[...] = jnp.sum(part.reshape(-1, 8, 128), axis=0)
-
-
-def settle(index, keep, got, norms=0, after=()):
+        weight=weight,
+    )
+
+
+def settle_kernel(norms, *refs):
+    out, squares = refs[-2:]
+    done = 0
+    parts = 0.0
+    for at in range(0, len(refs) - 2, 2):
+        total = refs[at][...].astype(F32) + refs[at + 1][...].astype(F32)
+        out[done : done + total.shape[0], :] = total
+        if norms and done == 0:
+            core = lax.axis_index("narrow")
+            row, lane = (lax.broadcasted_iota(jnp.int32, total.shape, n) for n in (0, 1))
+            shared = jnp.logical_and(row >= NORM_ROW, row < NORM_ROW + 8)
+            other = jnp.logical_or(lane < core * norms, lane >= (core + 1) * norms)
+            total = jnp.where(jnp.logical_and(shared, other), 0.0, total)
+        done += total.shape[0]
+        total = total * total
+        part = total[:, :128] + total[:, 128:256] + total[:, 256:]
+        parts = parts + jnp.sum(part.reshape(-1, 8, 128), axis=0)
+    squares[...] = parts
+
+
+def settle(pairs, norms=0, after=()):
+    arrays = [array for pair in pairs for array in pair]
+    rows, lanes = sum(pair[0].shape[0] for pair in pairs), arrays[0].shape[1]
     return run(
         functools.partial(settle_kernel, norms),
-        (index, keep, got),
-        [IN_SMEM, whole(keep.shape), whole(keep.shape)],
-        [whole(keep.shape), whole((8, 128))],
-        [shape(keep.shape, F32), shape((8, 128), F32)],
+        arrays,
+        [whole(array.shape) for array in arrays],
+        [whole((rows, lanes)), whole((8, 128))],
+        [shape((rows, lanes), F32), shape((8, 128), F32)],
         (1,),
         "settle",
         (),
@@ -1200,7 +1286,7 @@
     return (master, first, second)
 
 
-def update_kernel(wide, sums_ref, index_ref, one_ref, ff_ref, q_ref, *refs):
+def update_kernel(sums_ref, zero_ref, one_ref, *refs):
     states, news, clip_ref = refs[:15], refs[15:30], refs[30]
     layer = pl.program_id(0)
     total = jnp.sum(jnp.sum(sums_ref[...], axis=0, keepdims=True), axis=1, keepdims=True)
@@ -1213,32 +1299,32 @@
         for ref, value in zip(news[3 * at : 3 * at + 3], adamw(*old, gradient, factor, rate, decay)):
             ref[...] = value
 
-    def all_kinds(ff, q):
-        three, rows, half = news[0].shape
-        kind(0, q.reshape(three, rows, half), LR_MATRIX, DECAY_MATRIX)
-        kind(1, jnp.concatenate([ff[384:408], ff[416:440]], axis=1), LR_MATRIX, DECAY_MATRIX)
-        kind(2, jnp.concatenate([ff[n : n + 48] for n in range(192, 384, 48)], axis=1), LR_MATRIX, DECAY_MATRIX)
-        kind(3, jnp.concatenate([ff[:96], ff[96:192]], axis=1), LR_MATRIX, DECAY_MATRIX)
+    def all_kinds(grads):
+        kind(0, grads[FF_ROWS:].reshape(news[0].shape), LR_MATRIX, DECAY_MATRIX)
+        kind(1, jnp.concatenate([grads[384:408], grads[416:440]], axis=1), LR_MATRIX, DECAY_MATRIX)
+        parts = [grads[at : at + 48] for at in range(192, 384, 48)]
+        kind(2, jnp.concatenate(parts, axis=1), LR_MATRIX, DECAY_MATRIX)
+        kind(3, jnp.concatenate([grads[:96], grads[96:192]], axis=1), LR_MATRIX, DECAY_MATRIX)
 
     @pl.when(layer == 0)
     def _():
-        all_kinds(ff_ref[...], q_ref[...])
+        all_kinds(zero_ref[...])
         part = states[12].shape[1]
-        columns = ff_ref[NORM_ROW : NORM_ROW + 8, :128]
+        columns = zero_ref[NORM_ROW : NORM_ROW + 8, :128]
         mine = jnp.where(lax.axis_index("narrow") == 0, columns[:, :part], columns[:, part : 2 * part])
         kind(4, mine, LR_NORMS, 0.0)
 
     @pl.when(layer == 1)
     def _():
-        all_kinds(one_ref[:FF_ROWS], one_ref[FF_ROWS:])
-
-
-def update(sums, index, one, ff, q, states, wide):
+        all_kinds(one_ref[...])
+
+
+def update(sums, zero, one, states):
     specs = [layer_at(state) for state in states[:12]] + [whole(state.shape) for state in states[12:]]
     *news, clip_norm = run(
-        functools.partial(update_kernel, wide),
-        (sums, index, one, ff, q, *states),
-        [whole(sums.shape), IN_SMEM, whole(one.shape), whole(ff.shape), whole(q.shape)] + specs,
+        update_kernel,
+        (sums, zero, one, *states),
+        [whole(sums.shape), whole(zero.shape), whole(one.shape)] + specs,
         specs + [IN_SMEM],
         [shape(state.shape, F32) for state in states] + [shape((1,), F32)],
         (LAYERS,),
@@ -1323,9 +1409,10 @@
             in_grad = weight_grad(ffn_in, gh_own, ffn_got, gh_got, width, 512, "in_grad")
             out_grad = weight_grad(m_own, gfb[1], m_got, gfb_got[1], half, width, "out_grad")
             gx, dkv = mix_back(*mix)
-            g_own, g_peer = attend_back(*back, gx, states, swap(dkv), cos, sin)
+            g_own, *g_peer = attend_back(*back, gx, states, swap(dkv), cos, sin)
             up = input_back(g_own, g_peer, qkv, qkv_peer, layer, gfb)
-            qkv_grad = weight_grad(low, g_own, low_got, swap(g_peer), width, half, "qkv_grad")
+            g_got = jnp.concatenate([swap(g) for g in g_peer], axis=1)
+            qkv_grad = weight_grad(low, g_own, low_got, g_got, width, half, "qkv_grad")
             shares[layer] = [
                 lax.psum_scatter(g, wide_axes, scatter_dimension=0, tiled=True).astype(F32)
                 for g in (qkv_grad, out_grad, in_grad, back_grad)
@@ -1337,50 +1424,55 @@
             norms = jnp.transpose(norm_sum.reshape(8, wide, width // wide), (1, 0, 2))
             norms = jnp.pad(norms, ((0, 0), (0, 0), (0, 128 - width // wide)))
             norms_got = swap(norms)
-            ka, sa, kb, sb = fold_split(here, *q_first, (gfb,))
-            keep, send = fold_near(here, (ff_second, (ka, by_y(sa), kb, by_x(sb))))
-            one_near = (keep, near(send))
-            after = (keep,)
+            sa, sb = fold_split(*q_first, (gfb,))
+            q_second = q_first[:2] + (by_y(sa),) + q_first[2:] + (by_x(sb),)
+            after = (sa,)
         else:
             norms = norms_got = jnp.zeros((wide, 8, 128), F32)
-            gx, dkv = mix_back(*mix, (h_got,))
-            after = (gx,)
+            after = (h_got,)
+        gx, dkv = mix_back(*mix, after)
+        dkv_got = swap(dkv)
         ka, sa, kb, sb = pack(
             here, h_own, gfb, h_got, gfb_got, ffn_in, gh_own, ffn_got, gh_got, m_own, m_got,
-            norms, norms_got, after,
+            norms, norms_got, (dkv_got,),
         )
         ff_first = (ka, by_x(sa), kb, by_y(sb))
         if last:
-            keep, send = fold_far(here, *one_near, (ka,))
+            keep, send = fold_near((ff_second, q_second), (ka,))
+            one_near = (keep, near(send))
+            g_own, *g_peer = attend_back(*back, gx, states, dkv_got, cos, sin, (keep,))
+            keep, send = fold_far(here, *one_near, (g_own,), 0)
             one_far = (keep, far(send))
-            gx, dkv = mix_back(*mix, (keep,))
-            g_own, g_peer = attend_back(*back, gx, states, swap(dkv), cos, sin)
+            after = (keep,)
         else:
-            g_own, g_peer, up = attend_back(
-                *back, gx, states, swap(dkv), cos, sin, (ka,), (qkv, qkv_peer, layer, gfb)
+            g_own, *g_peer, up = attend_back(
+                *back, gx, states, dkv_got, cos, sin, (ka,), (qkv, qkv_peer, layer, gfb)
             )
-        g_got = swap(g_peer)
-        ka, sa, kb, sb = fold_split(here, *ff_first, (g_own,))
-        ff_second = (ka, by_y(sa), kb, by_x(sb))
-        q_ka, q_sa, q_kb, q_sb = q_pack(low, g_own, low_got, g_got, half, (ka,))
+            after = (g_own,)
+        g_got = [swap(g) for g in g_peer]
+        if last:
+            sa, sb = fold_split(*ff_first, after)
+            ff_second = ff_first[:2] + (by_y(sa),) + ff_first[2:] + (by_x(sb),)
+            after = (sa,)
+        q_ka, q_sa, q_kb, q_sb = q_pack(low, g_own, low_got, g_got, half, after)
         q_first = (q_ka, by_x(q_sa), q_kb, by_y(q_sb))
-        after = (q_ka,)
         if not last:
+            sa, sb = fold_split(*ff_first, (q_ka,))
+            ff_second = ff_first[:2] + (by_y(sa),) + ff_first[2:] + (by_x(sb),)
+            after = (sa,)
             continue
-        keep, send = fold_near(here, (ff_second,), (q_ka,))
+        keep, send = fold_near((ff_second,), (q_ka,))
         ff_near = (keep, near(send))
         up = input_back(g_own, g_peer, qkv, qkv_peer, layer, gfb, (keep,))
-        ka, sa, kb, sb = fold_split(here, *q_first, (up,))
-        q_second = (ka, by_y(sa), kb, by_x(sb))
-        keep, send = fold_far(here, *ff_near, (ka,))
-        ff_far = (keep, far(send))
-        keep, send = fold_near(here, (q_second,), (keep,))
+        sa, sb = fold_split(*q_first, (up,))
+        q_second = q_first[:2] + (by_y(sa),) + q_first[2:] + (by_x(sb),)
+        ff_keep, ff_send = fold_far(here, *ff_near, (sa,))
+        one, one_squares = settle((one_far,), 0, (ff_keep,))
+        keep, send = fold_near((q_second,), (one,))
         q_near = (keep, near(send))
-        one, one_squares = settle(here, *one_far, 0, (keep,))
-        keep, send = fold_far(here, *q_near, (one,))
-        q_far = (keep, far(send))
-        ff, ff_squares = settle(here, *ff_far, width // wide // 2, (keep,))
-        q, q_squares = settle(here, *q_far, 0, (ff,))
+        ff_far = (ff_keep, far(ff_send))
+        keep, send = fold_far(here, *q_near, (), 0)
+        zero, zero_squares = settle((ff_far, (keep, far(send))), width // wide // 2)
 
     count = wide * lax.axis_size("narrow")
     states = (
@@ -1390,13 +1482,13 @@
     )
     exchange = lambda rows_in: lax.all_to_all(rows_in, every, 0, 0, tiled=True)
     if by_axes:
-        squares = (one_squares + ff_squares + q_squares).sum(0, keepdims=True)
+        squares = (one_squares + zero_squares).sum(0, keepdims=True)
         sums = exchange(jnp.broadcast_to(squares, (count, 128)))
         flip = lambda array: jnp.transpose(array, (0, 2, 1, 3))
         states = tuple(flip(v) for v in states[:3]) + states[3:12] + tuple(
             v.reshape(8, -1) for v in states[12:]
         )
-        new, clip_norm = update(sums, here, one, ff, q, states, wide)
+        new, clip_norm = update(sums, zero, one, states)
         new = [flip(v) for v in new[:3]] + new[3:12] + [v.reshape(LAYERS, 4, -1) for v in new[12:]]
         return (out, up, *new, clip_norm)
     gradients = [jnp.stack([shares[l][kind] for l in range(LAYERS)]) for kind in range(4)]

time: 399 us -> 398 us (level); the launches traced: 392 us -> 398 us
  Pallas kernels: 307 us -> 312 us
    pallas_call x33 -> x32, Pallas kernels: 307 us -> 312 us  [run(): pl.pallas_call(body, grid=grid, in_specs=list(in_specs) + [pl.BlockSpec(m...]
    ppermute x40 -> x44, waiting for transfers between devices: 22.6 us -> 18.8 us  [swap(): return lax.ppermute(values, axis, [(0, 1), (1, 0)])]
    ppermute x40 -> x44, starting transfers between devices: 23.9 us -> 25.3 us  [swap(): return lax.ppermute(values, axis, [(0, 1), (1, 0)])]
  transfers between devices with their start and end apart: 46 -> 50, of which waited for: 18 -> 15; matrix products, arithmetic and copies ran while one was open for 0% -> 0% of each run, Pallas kernels for 63% -> 65%
where the time goes in v5:
time: 398 us
  Pallas kernels  312 us (78%)
  starting transfers between devices  35.3 us (9%)
  waiting for transfers between devices  34.4 us (9%)
  blocking collectives  11.9 us (3%)
    pallas_call x32, Pallas kernels, run(): pl.pallas_call(body, grid=grid, in_specs=list(in_specs) + [pl.BlockSpec(m...  312 us
    ppermute x44, starting transfers between devices, swap(): return lax.ppermute(values, axis, [(0, 1), (1, 0)])  25.3 us
    ppermute x44, waiting for transfers between devices, swap(): return lax.ppermute(values, axis, [(0, 1), (1, 0)])  18.8 us
    ppermute x6, waiting for transfers between devices, shuffle(): lax.ppermute(values, axis, [(i, i ^ bit) for i in range(lax.axis_size(axi...  15.6 us
    all_to_all x1, blocking collectives, shards(): exchange = lambda rows_in: lax.all_to_all(rows_in, every, 0, 0, tiled=True)  11.9 us
    ppermute x6, starting transfers between devices, shuffle(): lax.ppermute(values, axis, [(i, i ^ bit) for i in range(lax.axis_size(axi...  10 us
  transfers between devices with their start and end apart: 50, of which 15 were waited for; matrix products, arithmetic and copies ran while one was open for 0% of the time, Pallas kernels for 65%

profile of v5, /device:TPU:0, one launch (start us, length us, event | category | flops | bytes accessed | tf_op | source)
XLA Modules:
  0.0 397.8 jit_solution(12727000160249964946)
XLA Ops:
  1.3 2.4 tables.1
  3.7 6.4 %project.3 = (bf16[1024,768]{1,0:T(8,128)(2,1)}, bf16[1024,768]{1,0:T(8,128)(2,1)}, bf16[1024,384]{1,0:T(8,128)(2,1)}, f32[1,3,128,256]{3,2,1,0:T(8,128)}) custom-call(bf16[1024,768]{1,0:T(8,128)(2,1)} %refs_0_.25, bf16[2,3,768,384]{3,2,1,0:T(8,128)(2,1)} %bitcast.20, f32[1024,128]{1,0:T(8,128)} %get-tuple-element.141.refs_2_.refs_3_.refs_10_, ...), custom_call_target="tpu_custom_call" | custom-call | tf_op jit(solution)/shard_map/project/pallas_call | solution.py:44
  10.6 6.4 %project.4 = (bf16[1024,768]{1,0:T(8,128)(2,1)}, bf16[1024,768]{1,0:T(8,128)(2,1)}, bf16[1024,384]{1,0:T(8,128)(2,1)}, f32[1,3,128,256]{3,2,1,0:T(8,128)}) custom-call(bf16[1024,768]{1,0:T(8,128)(2,1)} %refs_0_.25, bf16[2,3,768,384]{3,2,1,0:T(8,128)(2,1)} %collective-permute-done.refs_1_.refs_2_.refs_13_.refs_5_, ...), custom_call_target="tpu_custom_call" | custom-call | tf_op jit(solution)/shard_map/project/pallas_call | solution.py:44
  17.6 1.5 collective-permute-done.1.refs_7_
  19.3 14.3 %attend.2 = (bf16[1024,384]{1,0:T(8,128)(2,1)}, bf16[1024,384]{1,0:T(8,128)(2,1)}, bf16[1024,768]{1,0:T(8,128)(2,1)}, bf16[1024,768]{1,0:T(8,128)(2,1)}, bf16[10...) custom-call(s32[1,2]{1,0:T(1,128)} %refs_0_.27, ...), custom_call_target="tpu_custom_call" | custom-call | tf_op jit(solution)/shard_map/attend/pallas_call | solution.py:44
  33.6 21.2 %feed.2 = (bf16[1024,1536]{1,0:T(8,128)(2,1)}, bf16[1024,1536]{1,0:T(8,128)(2,1)}, bf16[1024,3072]{1,0:T(8,128)(2,1)}, bf16[1024,768]{1,0:T(8,128)(2,1)}, bf16[1...) custom-call(bf16[1024,768]{1,0:T(8,128)(2,1)} %get-tuple-element.151.refs_0_.refs_5_, bf16[2,768,1536]{2,1,0:T(8,128)(2,1)} %refs_6_.2, ...), custom_call_target="tpu_custom_call" | custom-call | tf_op jit(solution)/shard_map/feed/pallas_call | solution.py:44
  55.4 22.9 %project.5 = (bf16[1024,768]{1,0:T(8,128)(2,1)}, bf16[1024,768]{1,0:T(8,128)(2,1)}, bf16[1024,384]{1,0:T(8,128)(2,1)}, bf16[1024,768]{1,0:T(8,128)(2,1)}, bf16[1...) custom-call(bf16[1024,768]{1,0:T(8,128)(2,1)} %get-tuple-element.154.refs_0_.refs_11_, ...), custom_call_target="tpu_custom_call" | custom-call | tf_op jit(solution)/shard_map/project/pallas_call | solution.py:44
  79.2 1.7 collective-permute-done.6.refs_7_.refs_8_
  81.4 14.3 %attend.3 = (bf16[1024,384]{1,0:T(8,128)(2,1)}, bf16[1024,384]{1,0:T(8,128)(2,1)}, bf16[1024,768]{1,0:T(8,128)(2,1)}, bf16[1024,768]{1,0:T(8,128)(2,1)}, bf16[10...) custom-call(s32[1,2]{1,0:T(1,128)} %refs_0_.27, ...), custom_call_target="tpu_custom_call" | custom-call | tf_op jit(solution)/shard_map/attend/pallas_call | solution.py:44
  96.3 20.0 %feed.3 = (bf16[1024,1536]{1,0:T(8,128)(2,1)}, bf16[1024,1536]{1,0:T(8,128)(2,1)}, bf16[1024,3072]{1,0:T(8,128)(2,1)}, f32[1024,768]{1,0:T(8,128)}, bf16[1024,768]{1,0:T(8,128)(2,1)}, /*index=5*/f32[1024,128]{1,0:T(8,128)}) custom-call(bf16[1024,768]{1,0:T(8,128)(2,1)} %get-tuple-element.162.refs_0_.refs_5_, bf16[2,768,1536]{2,1,0:T(8,128)(2,1)} %refs_6_.2, ...), custom_call_target="tpu_custom_call" | custom-call | tf_op jit(solution)/shard_map/feed/pallas_call | solution.py:44
  116.5 18.7 %feed_back.2 = (bf16[2,1024,768]{2,1,0:T(8,128)(2,1)}, bf16[1024,1536]{1,0:T(8,128)(2,1)}, bf16[1024,1536]{1,0:T(8,128)(2,1)}, f32[4,768]{1,0:T(4,128)}) custom-call(f32[1024,768]{1,0:T(8,128)} %refs_0_.19, f32[1024,128]{1,0:T(8,128)} %get-tuple-element.166.refs_1_, bf16[1024,768]{1,0:T(8,128)(2,1)} %get-tuple-element.167.refs_2_, ...), custom_call_target="tpu_custom_call" | custom-call | tf_op jit(solution)/shard_map/feed_back/pallas_call | solution.py:44
  135.8 7.4 %mix_back.2 = (bf16[1024,1536]{1,0:T(8,128)(2,1)}, bf16[6,128,256]{2,1,0:T(8,128)(2,1)}) custom-call(bf16[2,1024,768]{2,1,0:T(8,128)(2,1)} %get-tuple-element.173.refs_0_.refs_2_.refs_14_, bf16[2,384,768]{2,1,0:T(8,128)(2,1)} %refs_1_.7, bf16[2,384,768]{2,1,0:T(8,128)(2,1)} %collective-permute-done.3.refs_10_.refs_2_, ...), custom_call_target="tpu_custom_call" | custom-call | tf_op jit(solution)/shard_map/mix_back/pallas_call | solution.py:44
  143.6 2.2 collective-permute-done.17.refs_8_
  146.3 0.6 broadcast_in_dim.4.refs_11_.refs_12_
  147.0 21.6 %pack.2 = (bf16[2,2,448,384]{3,2,1,0:T(8,128)(2,1)}, bf16[2,2,448,384]{3,2,1,0:T(8,128)(2,1)}, bf16[2,2,448,384]{3,2,1,0:T(8,128)(2,1)}, bf16[2,2,448,384]{3,2,1,0:T(8,128)(2,1)}) custom-call(s32[1,2]{1,0:T(1,128)} %refs_0_.27, bf16[1024,1536]{1,0:T(8,128)(2,1)} %get-tuple-element.180.refs_1_, ...), custom_call_target="tpu_custom_call" | custom-call | tf_op jit(solution)/shard_map/pack/pallas_call | solution.py:44
  168.6 3.0 collective-permute-start.18
  171.6 1.6 collective-permute-start.19
  173.2 26.0 %attend_back.2 = (bf16[1024,1152]{1,0:T(8,128)(2,1)}, bf16[1024,384]{1,0:T(8,128)(2,1)}, bf16[1024,384]{1,0:T(8,128)(2,1)}, bf16[1024,384]{1,0:T(8,128)(2,1)}, bf16[1024,768]{1,0:T(8,128)(2,1)}) custom-call(s32[1,2]{1,0:T(1,128)} %refs_0_.27, bf16[1024,768]{1,0:T(8,128)(2,1)} %get-tuple-element.155.refs_1_.refs_6_, ...), custom_call_target="tpu_custom_call" | custom-call | tf_op jit(solution)/shard_map/attend_back/pallas_call | solution.py:44
  199.9 2.0 collective-permute-done.20.refs_3_
  201.9 1.1 collective-permute-done.21.refs_4_
  203.1 1.1 collective-permute-done.22.refs_5_
  204.2 9.1 %qkv_grad.2 = (bf16[2,2,144,384]{3,2,1,0:T(8,128)(2,1)}, bf16[2,2,144,384]{3,2,1,0:T(8,128)(2,1)}, bf16[2,2,144,384]{3,2,1,0:T(8,128)(2,1)}, bf16[2,2,144,384]{3,2,1,0:T(8,128)(2,1)}) custom-call(bf16[1024,768]{1,0:T(8,128)(2,1)} %get-tuple-element.154.refs_0_.refs_11_, bf16[1024,1152]{1,0:T(8,128)(2,1)} %get-tuple-element.193.refs_1_.refs_6_, ...), custom_call_target="tpu_custom_call" | custom-call | tf_op jit(solution)/shard_map/qkv_grad/pallas_call | solution.py:44
  214.0 2.6 fold_split.4
  216.6 2.0 collective-permute-start.26
  218.6 18.0 %feed_back.3 = (bf16[2,1024,768]{2,1,0:T(8,128)(2,1)}, bf16[1024,1536]{1,0:T(8,128)(2,1)}, bf16[1024,1536]{1,0:T(8,128)(2,1)}, f32[4,768]{1,0:T(4,128)}) custom-call(bf16[1024,768]{1,0:T(8,128)(2,1)} %get-tuple-element.184.refs_0_, bf16[1024,768]{1,0:T(8,128)(2,1)} %get-tuple-element.185.refs_1_, f32[1024,128]{1,0:T(8,128)} %get-tuple-element.186.refs_2_, ...), custom_call_target="tpu_custom_call" | custom-call | tf_op jit(solution)/shard_map/feed_back/pallas_call | solution.py:44
  236.6 0.7 pad_maximum_fusion
  237.4 0.6 pad.4.refs_11_
  238.6 1.6 collective-permute-start.27
  240.2 2.0 fold_split.5
  242.2 7.4 %mix_back.3 = (bf16[1024,1536]{1,0:T(8,128)(2,1)}, bf16[6,128,256]{2,1,0:T(8,128)(2,1)}) custom-call(bf16[2,1024,768]{2,1,0:T(8,128)(2,1)} %get-tuple-element.199.refs_4_.refs_0_.refs_2_.refs_6_, bf16[2,384,768]{2,1,0:T(8,128)(2,1)} %refs_1_.7, bf16[2,384,768]{2,1,0:T(8,128)(2,1)} %collective-permute-done.3.refs_10_.refs_2_, ...), custom_call_target="tpu_custom_call" | custom-call | tf_op jit(solution)/shard_map/mix_back/pallas_call | solution.py:44
  249.8 1.9 collective-permute-done.25.refs_13_.refs_9_
  252.3 21.5 %pack.3 = (bf16[2,2,448,384]{3,2,1,0:T(8,128)(2,1)}, bf16[2,2,448,384]{3,2,1,0:T(8,128)(2,1)}, bf16[2,2,448,384]{3,2,1,0:T(8,128)(2,1)}, bf16[2,2,448,384]{3,2,1,0:T(8,128)(2,1)}) custom-call(s32[1,2]{1,0:T(1,128)} %refs_0_.27, bf16[1024,1536]{1,0:T(8,128)(2,1)} %get-tuple-element.211.refs_1_, ...), custom_call_target="tpu_custom_call" | custom-call | tf_op jit(solution)/shard_map/pack/pallas_call | solution.py:44
  273.9 2.0 collective-permute-start.33
  275.9 1.6 collective-permute-start.34
  277.6 3.5 fold_near.3
  281.1 1.6 collective-permute-start.35
  282.8 19.6 %attend_back.3 = (bf16[1024,1152]{1,0:T(8,128)(2,1)}, bf16[1024,384]{1,0:T(8,128)(2,1)}, bf16[1024,384]{1,0:T(8,128)(2,1)}, bf16[1024,384]{1,0:T(8,128)(2,1)}) custom-call(s32[1,2]{1,0:T(1,128)} %refs_0_.27, bf16[1024,768]{1,0:T(8,128)(2,1)} %get-tuple-element.143.refs_1_.refs_6_, bf16[1024,768]{1,0:T(8,128)(2,1)} %get-tuple-element.144.refs_2_.refs_7_, ...), custom_call_target="tpu_custom_call" | custom-call | tf_op jit(solution)/shard_map/attend_back/pallas_call | solution.py:44
  303.0 2.5 fold_far.3
  305.5 0.6 collective-permute-done.33.refs_1_
  306.2 1.5 collective-permute-done.34.refs_3_.refs_4_
  307.7 2.6 fold_split.6
  310.3 1.7 collective-permute-start.36
  312.4 2.6 collective-permute-start.41
  315.0 9.1 %qkv_grad.3 = (bf16[2,2,144,384]{3,2,1,0:T(8,128)(2,1)}, bf16[2,2,144,384]{3,2,1,0:T(8,128)(2,1)}, bf16[2,2,144,384]{3,2,1,0:T(8,128)(2,1)}, bf16[2,2,144,384]{3,2,1,0:T(8,128)(2,1)}) custom-call(bf16[1024,768]{1,0:T(8,128)(2,1)} %refs_0_.25, bf16[1024,1152]{1,0:T(8,128)(2,1)} %get-tuple-element.218.refs_3_.refs_1_.refs_0_, ...), custom_call_target="tpu_custom_call" | custom-call | tf_op jit(solution)/shard_map/qkv_grad/pallas_call | solution.py:44
  324.1 1.7 collective-permute-start.43
  326.3 0.8 collective-permute-done.36.refs_2_
  327.1 3.6 collective-permute-done.37.refs_5_
  330.7 3.3 fold_near.4
  334.0 1.6 collective-permute-start.42
  335.6 9.8 %input_back.1.refs_4_ = f32[1024,768]{1,0:T(8,128)} custom-call(bf16[1024,1152]{1,0:T(8,128)(2,1)} %get-tuple-element.218.refs_3_.refs_1_.refs_0_, bf16[1024,384]{1,0:T(8,128)(2,1)} %get-tuple-element.219.refs_1_, bf16[1024,384]{1,0:T(8,128)(2,1)} %get-tuple-element.220.refs_2_, bf16[1024,384]{1,0:T(8,128)(2,1)} %get-tuple-element.221.refs_3_, ...), custom_call_target="tpu_custom_call" | custom-call | tf_op jit(solution)/shard_map/input_back/pallas_call | solution.py:44
  345.4 2.0 fold_split.7
  347.8 0.6 collective-permute-done.42.refs_2_
  348.4 2.3 fold_far.4
  350.7 2.5 collective-permute-start.45
  353.2 2.3 settle.2
  355.5 2.3 fold_near.5
  357.7 1.7 collective-permute-start.48
  359.4 8.8 %collective-permute-done.48.refs_2_ = bf16[2,144,384]{2,1,0:T(8,128)(2,1)} collective-permute-done((bf16[2,144,384]{2,1,0:T(8,128)(2,1)}, bf16[2,144,384]{2,1,0:T(8,128)(2,1)}, u32[]{:S(2)}, u32[]{:S(2)}) %collective-permute-start.48) | collective-permute-done | bytes 221216 | tf_op jit(solution)/shard_map/ppermute | solution.py:1275
  368.2 1.8 fold_far.5
  370.0 6.2 %collective-permute-done.49.refs_3_ = bf16[144,384]{1,0:T(8,128)(2,1)} collective-permute-done((bf16[144,384]{1,0:T(8,128)(2,1)}, bf16[144,384]{1,0:T(8,128)(2,1)}, u32[]{:S(2)}, u32[]{:S(2)}) %collective-permute-start.49) | collective-permute-done | bytes 110624 | tf_op jit(solution)/shard_map/ppermute | solution.py:1275
  376.2 2.2 settle.3
  378.4 0.7 add_reduce_fusion
  379.1 11.9 %all_to_all.8 = f32[32,1,128]{2,1,0:T(1,128)} all-to-all(f32[32,1,128]{2,1,0:T(1,128)S(1)} %broadcast_in_dim.10), channel_id=1, replica_groups=mesh['z'=4,'y'=2,'x'=2,'narrow'=2] {'z','y','x','narrow'}, dimensions={0} | all-to-all | bytes 32768 | tf_op jit(solution)/shard_map/all_to_all | solution.py:1483
  391.0 6.5 %update.1 = (f32[2,3,48,384]{3,2,1,0:T(8,128)}, f32[2,3,48,384]{3,2,1,0:T(8,128)}, f32[2,3,48,384]{3,2,1,0:T(8,128)}, f32[2,24,768]{2,1,0:T(8,128)}, f32[2,24,76...) custom-call(f32[32,128]{1,0:T(8,128)} %bitcast.28, ...), custom_call_target="tpu_custom_call" | custom-call | tf_op jit(solution)/shard_map/update/pallas_call | solution.py:44
  (80 shorter events, 10.8 us)
Async XLA Ops:
  0.7 9.9 %collective-permute-start = (bf16[2,3,768,384]{3,2,1,0:T(8,128)(2,1)}, bf16[2,3,768,384]{3,2,1,0:T(8,128)(2,1)}, u32[]{:S(2)}, u32[]{:S(2)}) collective-permute-start(bf16[2,3,768,384]{3,2,1,0:T(8,128)(2,1)} %bitcast.19), channel_id=1, source_target_pairs={{0,1},{1,0},{2,3},{3,2},{4,5},{5,4},{6,7},{7,6},{8,9},{9,8},{10,11... | collective-permute-start | bytes 10616840 | tf_op jit(solution)/shard_map/ppermute | solution.py:1120
  1.2 16.0 %collective-permute-start.3 = (bf16[2,384,768]{2,1,0:T(8,128)(2,1)}, bf16[2,384,768]{2,1,0:T(8,128)(2,1)}, u32[]{:S(2)}, u32[]{:S(2)}) collective-permute-start(bf16[2,384,768]{2,1,0:T(8,128)(2,1)} %refs_1_.7), channel_id=1, source_target_pairs={{0,1},{1,0},{2,3},{3,2},{4,5},{5,4},{6,7},{7,6},{8,9},{9,8},{10,11... | collective-permute-start | bytes 3538952 | tf_op jit(solution)/shard_map/ppermute | solution.py:1120
  10.1 7.5 %collective-permute-start.2 = (f32[1,3,128,256]{3,2,1,0:T(8,128)}, f32[1,3,128,256]{3,2,1,0:T(8,128)}, u32[]{:S(2)}, u32[]{:S(2)}) collective-permute-start(f32[1,3,128,256]{3,2,1,0:T(8,128)} %get-tuple-element.150), channel_id=1, source_target_pairs={{0,1},{1,0},{2,3},{3,2},{4,5},{5,4},{6,7},{7,6},{8,9},{9,8},{10,11... | collective-permute-start | bytes 1179656 | tf_op jit(solution)/shard_map/ppermute | solution.py:1120
  17.0 2.1 collective-permute-start.1
  17.2 16.4 %collective-permute-start.4 = (bf16[2,768,1536]{2,1,0:T(8,128)(2,1)}, bf16[2,768,1536]{2,1,0:T(8,128)(2,1)}, u32[]{:S(2)}, u32[]{:S(2)}) collective-permute-start(bf16[2,768,1536]{2,1,0:T(8,128)(2,1)} %refs_6_.2), channel_id=1, source_target_pairs={{0,1},{1,0},{2,3},{3,2},{4,5},{5,4},{6,7},{7,6},{8,9},{9,8},{10,11... | collective-permute-start | bytes 14155784 | tf_op jit(solution)/shard_map/ppermute | solution.py:1120
  19.1 14.4 %collective-permute-start.5 = (bf16[2,1536,768]{2,1,0:T(8,128)(2,1)}, bf16[2,1536,768]{2,1,0:T(8,128)(2,1)}, u32[]{:S(2)}, u32[]{:S(2)}) collective-permute-start(bf16[2,1536,768]{2,1,0:T(8,128)(2,1)} %refs_8_.2), channel_id=1, source_target_pairs={{0,1},{1,0},{2,3},{3,2},{4,5},{5,4},{6,7},{7,6},{8,9},{9,8},{10,11... | collective-permute-start | bytes 14155784 | tf_op jit(solution)/shard_map/ppermute | solution.py:1120
  54.8 41.5 %collective-permute-start.10 = (bf16[1024,1536]{1,0:T(8,128)(2,1)}, bf16[1024,1536]{1,0:T(8,128)(2,1)}, u32[]{:S(2)}, u32[]{:S(2)}) collective-permute-start(bf16[1024,1536]{1,0:T(8,128)(2,1)} %get-tuple-element.164), channel_id=1, source_target_pairs={{0,1},{1,0},{2,3},{3,2},{4,5},{5,4},{6,7},{7,6},{8,9},{9,8},{10,11... | collective-permute-start | bytes 9437192 | tf_op jit(solution)/shard_map/ppermute | solution.py:1120
  55.2 40.5 %collective-permute-start.7 = (bf16[1024,768]{1,0:T(8,128)(2,1)}, bf16[1024,768]{1,0:T(8,128)(2,1)}, u32[]{:S(2)}, u32[]{:S(2)}) collective-permute-start(bf16[1024,768]{1,0:T(8,128)(2,1)} %refs_0_.25), channel_id=1, source_target_pairs={{0,1},{1,0},{2,3},{3,2},{4,5},{5,4},{6,7},{7,6},{8,9},{9,8},{10,11... | collective-permute-start | bytes 4718600 | tf_op jit(solution)/shard_map/ppermute | solution.py:1120
  78.3 2.7 collective-permute-start.6
  78.7 17.5 %collective-permute-start.9 = (bf16[1024,768]{1,0:T(8,128)(2,1)}, bf16[1024,768]{1,0:T(8,128)(2,1)}, u32[]{:S(2)}, u32[]{:S(2)}) collective-permute-start(bf16[1024,768]{1,0:T(8,128)(2,1)} %get-tuple-element.151.refs_0_.refs_5_), channel_id=1, source_target_pairs={{0,1},{1,0},{2,3},{3,2},{4,5},{5,4},{6,7},{7,6},{8,9},{9,8},{10,11... | collective-permute-start | bytes 4718600 | tf_op jit(solution)/shard_map/ppermute | solution.py:1120
  78.9 17.4 %collective-permute-start.11 = (bf16[1024,768]{1,0:T(8,128)(2,1)}, bf16[1024,768]{1,0:T(8,128)(2,1)}, u32[]{:S(2)}, u32[]{:S(2)}) collective-permute-start(bf16[1024,768]{1,0:T(8,128)(2,1)} %get-tuple-element.154.refs_0_.refs_11_), channel_id=1, source_target_pairs={{0,1},{1,0},{2,3},{3,2},{4,5},{5,4},{6,7},{7,6},{8,9},{9,8},{10,11... | collective-permute-start | bytes 4718600 | tf_op jit(solution)/shard_map/ppermute | solution.py:1120
  81.0 14.9 %collective-permute-start.8 = (bf16[1024,384]{1,0:T(8,128)(2,1)}, bf16[1024,384]{1,0:T(8,128)(2,1)}, u32[]{:S(2)}, u32[]{:S(2)}) collective-permute-start(bf16[1024,384]{1,0:T(8,128)(2,1)} %get-tuple-element.163.refs_5_), channel_id=1, source_target_pairs={{0,1},{1,0},{2,3},{3,2},{4,5},{5,4},{6,7},{7,6},{8,9},{9,8},{10,11... | collective-permute-start | bytes 2359304 | tf_op jit(solution)/shard_map/ppermute | solution.py:1120
  95.7 20.8 %collective-permute-start.13 = (bf16[1024,768]{1,0:T(8,128)(2,1)}, bf16[1024,768]{1,0:T(8,128)(2,1)}, u32[]{:S(2)}, u32[]{:S(2)}) collective-permute-start(bf16[1024,768]{1,0:T(8,128)(2,1)} %get-tuple-element.162.refs_0_.refs_5_), channel_id=1, source_target_pairs={{0,1},{1,0},{2,3},{3,2},{4,5},{5,4},{6,7},{7,6},{8,9},{9,8},{10,11... | collective-permute-start | bytes 4718600 | tf_op jit(solution)/shard_map/ppermute | solution.py:1120
  95.9 20.6 %collective-permute-start.12 = (bf16[1024,384]{1,0:T(8,128)(2,1)}, bf16[1024,384]{1,0:T(8,128)(2,1)}, u32[]{:S(2)}, u32[]{:S(2)}) collective-permute-start(bf16[1024,384]{1,0:T(8,128)(2,1)} %get-tuple-element.172.refs_5_), channel_id=1, source_target_pairs={{0,1},{1,0},{2,3},{3,2},{4,5},{5,4},{6,7},{7,6},{8,9},{9,8},{10,11... | collective-permute-start | bytes 2359304 | tf_op jit(solution)/shard_map/ppermute | solution.py:1120
  116.3 19.5 %collective-permute-start.14 = (bf16[1024,1536]{1,0:T(8,128)(2,1)}, bf16[1024,1536]{1,0:T(8,128)(2,1)}, u32[]{:S(2)}, u32[]{:S(2)}) collective-permute-start(bf16[1024,1536]{1,0:T(8,128)(2,1)} %get-tuple-element.176), channel_id=1, source_target_pairs={{0,1},{1,0},{2,3},{3,2},{4,5},{5,4},{6,7},{7,6},{8,9},{9,8},{10,11... | collective-permute-start | bytes 9437192 | tf_op jit(solution)/shard_map/ppermute | solution.py:1120
  135.2 8.4 %collective-permute-start.16 = (bf16[2,1024,768]{2,1,0:T(8,128)(2,1)}, bf16[2,1024,768]{2,1,0:T(8,128)(2,1)}, u32[]{:S(2)}, u32[]{:S(2)}) collective-permute-start(bf16[2,1024,768]{2,1,0:T(8,128)(2,1)} %get-tuple-element.173.refs_0_.refs_2_.refs_14_), channel_id=1, source_target_pairs={{0,1},{1,0},{2,3},{3,2},{4,5},{5,4},{6,7},{7,6},{8,9},{9,8},{10,11... | collective-permute-start | bytes 9437192 | tf_op jit(solution)/shard_map/ppermute | solution.py:1120
  135.6 10.1 %collective-permute-start.17 = (bf16[1024,1536]{1,0:T(8,128)(2,1)}, bf16[1024,1536]{1,0:T(8,128)(2,1)}, u32[]{:S(2)}, u32[]{:S(2)}) collective-permute-start(bf16[1024,1536]{1,0:T(8,128)(2,1)} %get-tuple-element.182), channel_id=1, source_target_pairs={{0,1},{1,0},{2,3},{3,2},{4,5},{5,4},{6,7},{7,6},{8,9},{9,8},{10,11... | collective-permute-start | bytes 9437192 | tf_op jit(solution)/shard_map/ppermute | solution.py:1120
  143.1 3.2 collective-permute-start.15
  168.6 45.4 %collective-permute-start.18 = (bf16[2,2,448,384]{3,2,1,0:T(8,128)(2,1)}, bf16[2,2,448,384]{3,2,1,0:T(8,128)(2,1)}, u32[]{:S(2)}, u32[]{:S(2)}) collective-permute-start(bf16[2,2,448,384]{3,2,1,0:T(8,128)(2,1)} %get-tuple-element.190), channel_id=1, source_target_pairs={{0,2},{2,0},{1,3},{3,1},{4,6},{6,4},{5,7},{7,5},{8,10},{10,8},{9,1... | collective-permute-start | bytes 4128776 | tf_op jit(solution)/shard_map/ppermute | solution.py:1120
  171.6 42.4 %collective-permute-start.19 = (bf16[2,2,448,384]{3,2,1,0:T(8,128)(2,1)}, bf16[2,2,448,384]{3,2,1,0:T(8,128)(2,1)}, u32[]{:S(2)}, u32[]{:S(2)}) collective-permute-start(bf16[2,2,448,384]{3,2,1,0:T(8,128)(2,1)} %get-tuple-element.192), channel_id=1, source_target_pairs={{0,4},{4,0},{1,5},{5,1},{2,6},{6,2},{3,7},{7,3},{8,12},{12,8},{9,1... | collective-permute-start | bytes 4128776 | tf_op jit(solution)/shard_map/ppermute | solution.py:1120
  199.2 2.7 collective-permute-start.20
  199.3 3.7 collective-permute-start.21
  199.8 4.4 %collective-permute-start.22 = (bf16[1024,384]{1,0:T(8,128)(2,1)}, bf16[1024,384]{1,0:T(8,128)(2,1)}, u32[]{:S(2)}, u32[]{:S(2)}) collective-permute-start(bf16[1024,384]{1,0:T(8,128)(2,1)} %get-tuple-element.196), channel_id=1, source_target_pairs={{0,1},{1,0},{2,3},{3,2},{4,5},{5,4},{6,7},{7,6},{8,9},{9,8},{10,11... | collective-permute-start | bytes 2359304 | tf_op jit(solution)/shard_map/ppermute | solution.py:1120
  213.3 25.3 %collective-permute-start.23 = (bf16[2,2,144,384]{3,2,1,0:T(8,128)(2,1)}, bf16[2,2,144,384]{3,2,1,0:T(8,128)(2,1)}, u32[]{:S(2)}, u32[]{:S(2)}) collective-permute-start(bf16[2,2,144,384]{3,2,1,0:T(8,128)(2,1)} %get-tuple-element.202), channel_id=1, source_target_pairs={{0,2},{2,0},{1,3},{3,1},{4,6},{6,4},{5,7},{7,5},{8,10},{10,8},{9,1... | collective-permute-start | bytes 1327112 | tf_op jit(solution)/shard_map/ppermute | solution.py:1120
  213.9 24.7 %collective-permute-start.24 = (bf16[2,2,144,384]{3,2,1,0:T(8,128)(2,1)}, bf16[2,2,144,384]{3,2,1,0:T(8,128)(2,1)}, u32[]{:S(2)}, u32[]{:S(2)}) collective-permute-start(bf16[2,2,144,384]{3,2,1,0:T(8,128)(2,1)} %get-tuple-element.204), channel_id=1, source_target_pairs={{0,4},{4,0},{1,5},{5,1},{2,6},{6,2},{3,7},{7,3},{8,12},{12,8},{9,1... | collective-permute-start | bytes 1327112 | tf_op jit(solution)/shard_map/ppermute | solution.py:1120
  216.6 61.0 %collective-permute-start.26 = (bf16[2,448,384]{2,1,0:T(8,128)(2,1)}, bf16[2,448,384]{2,1,0:T(8,128)(2,1)}, u32[]{:S(2)}, u32[]{:S(2)}) collective-permute-start(bf16[2,448,384]{2,1,0:T(8,128)(2,1)} %get-tuple-element.198.refs_11_), channel_id=1, source_target_pairs={{0,4},{4,0},{1,5},{5,1},{2,6},{6,2},{3,7},{7,3},{8,12},{12,8},{9,1... | collective-permute-start | bytes 2064392 | tf_op jit(solution)/shard_map/ppermute | solution.py:1120
  218.6 18.0 %copy-start = (f32[4,768]{1,0:T(4,128)S(1)}, f32[4,768]{1,0:T(4,128)}, u32[]{:S(2)}) copy-start(f32[4,768]{1,0:T(4,128)} %get-tuple-element.215) | copy-start | bytes 36868
  238.1 11.5 %collective-permute-start.32 = (f32[16,8,128]{2,1,0:T(8,128)}, f32[16,8,128]{2,1,0:T(8,128)}, u32[]{:S(2)}, u32[]{:S(2)}) collective-permute-start(f32[16,8,128]{2,1,0:T(8,128)} %pad.4.refs_11_), channel_id=1, source_target_pairs={{0,1},{1,0},{2,3},{3,2},{4,5},{5,4},{6,7},{7,6},{8,9},{9,8},{10,11... | collective-permute-start | bytes 196616 | tf_op jit(solution)/shard_map/ppermute | solution.py:1120
  238.1 14.1 %collective-permute-start.30 = (bf16[2,1024,768]{2,1,0:T(8,128)(2,1)}, bf16[2,1024,768]{2,1,0:T(8,128)(2,1)}, u32[]{:S(2)}, u32[]{:S(2)}) collective-permute-start(bf16[2,1024,768]{2,1,0:T(8,128)(2,1)} %get-tuple-element.199.refs_4_.refs_0_.refs_2_.refs_6_), channel_id=1, source_target_pairs={{0,1},{1,0},{2,3},{3,2},{4,5},{5,4},{6,7},{7,6},{8,9},{9,8},{10,11... | collective-permute-start | bytes 9437192 | tf_op jit(solution)/shard_map/ppermute | solution.py:1120
  238.6 13.8 %collective-permute-start.31 = (bf16[1024,1536]{1,0:T(8,128)(2,1)}, bf16[1024,1536]{1,0:T(8,128)(2,1)}, u32[]{:S(2)}, u32[]{:S(2)}) collective-permute-start(bf16[1024,1536]{1,0:T(8,128)(2,1)} %get-tuple-element.213), channel_id=1, source_target_pairs={{0,1},{1,0},{2,3},{3,2},{4,5},{5,4},{6,7},{7,6},{8,9},{9,8},{10,11... | collective-permute-start | bytes 9437192 | tf_op jit(solution)/shard_map/ppermute | solution.py:1120
  238.6 39.0 %collective-permute-start.27 = (bf16[2,448,384]{2,1,0:T(8,128)(2,1)}, bf16[2,448,384]{2,1,0:T(8,128)(2,1)}, u32[]{:S(2)}, u32[]{:S(2)}) collective-permute-start(bf16[2,448,384]{2,1,0:T(8,128)(2,1)} %get-tuple-element.209), channel_id=1, source_target_pairs={{0,2},{2,0},{1,3},{3,1},{4,6},{6,4},{5,7},{7,5},{8,10},{10,8},{9,1... | collective-permute-start | bytes 2064392 | tf_op jit(solution)/shard_map/ppermute | solution.py:1120
  249.6 2.1 collective-permute-start.25
  251.8 24.2 %collective-permute-start.28 = (bf16[2,144,384]{2,1,0:T(8,128)(2,1)}, bf16[2,144,384]{2,1,0:T(8,128)(2,1)}, u32[]{:S(2)}, u32[]{:S(2)}) collective-permute-start(bf16[2,144,384]{2,1,0:T(8,128)(2,1)} %get-tuple-element.205.refs_8_), channel_id=1, source_target_pairs={{0,4},{4,0},{1,5},{5,1},{2,6},{6,2},{3,7},{7,3},{8,12},{12,8},{9,1... | collective-permute-start | bytes 663560 | tf_op jit(solution)/shard_map/ppermute | solution.py:1120
  252.2 25.4 %collective-permute-start.29 = (bf16[2,144,384]{2,1,0:T(8,128)(2,1)}, bf16[2,144,384]{2,1,0:T(8,128)(2,1)}, u32[]{:S(2)}, u32[]{:S(2)}) collective-permute-start(bf16[2,144,384]{2,1,0:T(8,128)(2,1)} %get-tuple-element.210), channel_id=1, source_target_pairs={{0,2},{2,0},{1,3},{3,1},{4,6},{6,4},{5,7},{7,5},{8,10},{10,8},{9,1... | collective-permute-start | bytes 663560 | tf_op jit(solution)/shard_map/ppermute | solution.py:1120
  273.9 32.3 %collective-permute-start.33 = (bf16[2,2,448,384]{3,2,1,0:T(8,128)(2,1)}, bf16[2,2,448,384]{3,2,1,0:T(8,128)(2,1)}, u32[]{:S(2)}, u32[]{:S(2)}) collective-permute-start(bf16[2,2,448,384]{3,2,1,0:T(8,128)(2,1)} %get-tuple-element.222), channel_id=1, source_target_pairs={{0,2},{2,0},{1,3},{3,1},{4,6},{6,4},{5,7},{7,5},{8,10},{10,8},{9,1... | collective-permute-start | bytes 4128776 | tf_op jit(solution)/shard_map/ppermute | solution.py:1120
  275.9 31.7 %collective-permute-start.34 = (bf16[2,2,448,384]{3,2,1,0:T(8,128)(2,1)}, bf16[2,2,448,384]{3,2,1,0:T(8,128)(2,1)}, u32[]{:S(2)}, u32[]{:S(2)}) collective-permute-start(bf16[2,2,448,384]{3,2,1,0:T(8,128)(2,1)} %get-tuple-element.224), channel_id=1, source_target_pairs={{0,4},{4,0},{1,5},{5,1},{2,6},{6,2},{3,7},{7,3},{8,12},{12,8},{9,1... | collective-permute-start | bytes 4128776 | tf_op jit(solution)/shard_map/ppermute | solution.py:1120
  281.1 21.8 %collective-permute-start.35 = (bf16[2,592,384]{2,1,0:T(8,128)(2,1)}, bf16[2,592,384]{2,1,0:T(8,128)(2,1)}, u32[]{:S(2)}, u32[]{:S(2)}) collective-permute-start(bf16[2,592,384]{2,1,0:T(8,128)(2,1)} %get-tuple-element.225), channel_id=1, source_target_pairs={{0,8},{8,0},{16,24},{24,16},{1,9},{9,1},{17,25},{25,17},{2,10},{10... | collective-permute-start | bytes 2727944 | tf_op jit(solution)/shard_map/ppermute | solution.py:1275
  302.4 10.0 %collective-permute-start.38 = (bf16[1024,384]{1,0:T(8,128)(2,1)}, bf16[1024,384]{1,0:T(8,128)(2,1)}, u32[]{:S(2)}, u32[]{:S(2)}) collective-permute-start(bf16[1024,384]{1,0:T(8,128)(2,1)} %get-tuple-element.219.refs_1_), channel_id=1, source_target_pairs={{0,1},{1,0},{2,3},{3,2},{4,5},{5,4},{6,7},{7,6},{8,9},{9,8},{10,11... | collective-permute-start | bytes 2359304 | tf_op jit(solution)/shard_map/ppermute | solution.py:1120
  302.5 12.6 %collective-permute-start.39 = (bf16[1024,384]{1,0:T(8,128)(2,1)}, bf16[1024,384]{1,0:T(8,128)(2,1)}, u32[]{:S(2)}, u32[]{:S(2)}) collective-permute-start(bf16[1024,384]{1,0:T(8,128)(2,1)} %get-tuple-element.220.refs_2_), channel_id=1, source_target_pairs={{0,1},{1,0},{2,3},{3,2},{4,5},{5,4},{6,7},{7,6},{8,9},{9,8},{10,11... | collective-permute-start | bytes 2359304 | tf_op jit(solution)/shard_map/ppermute | solution.py:1120
  303.0 12.1 %collective-permute-start.40 = (bf16[1024,384]{1,0:T(8,128)(2,1)}, bf16[1024,384]{1,0:T(8,128)(2,1)}, u32[]{:S(2)}, u32[]{:S(2)}) collective-permute-start(bf16[1024,384]{1,0:T(8,128)(2,1)} %get-tuple-element.221.refs_3_), channel_id=1, source_target_pairs={{0,1},{1,0},{2,3},{3,2},{4,5},{5,4},{6,7},{7,6},{8,9},{9,8},{10,11... | collective-permute-start | bytes 2359304 | tf_op jit(solution)/shard_map/ppermute | solution.py:1120
  310.3 16.8 %collective-permute-start.36 = (bf16[2,448,384]{2,1,0:T(8,128)(2,1)}, bf16[2,448,384]{2,1,0:T(8,128)(2,1)}, u32[]{:S(2)}, u32[]{:S(2)}) collective-permute-start(bf16[2,448,384]{2,1,0:T(8,128)(2,1)} %get-tuple-element.227.refs_6_), channel_id=1, source_target_pairs={{0,4},{4,0},{1,5},{5,1},{2,6},{6,2},{3,7},{7,3},{8,12},{12,8},{9,1... | collective-permute-start | bytes 2064392 | tf_op jit(solution)/shard_map/ppermute | solution.py:1120
  312.0 18.7 %collective-permute-start.37 = (bf16[2,448,384]{2,1,0:T(8,128)(2,1)}, bf16[2,448,384]{2,1,0:T(8,128)(2,1)}, u32[]{:S(2)}, u32[]{:S(2)}) collective-permute-start(bf16[2,448,384]{2,1,0:T(8,128)(2,1)} %get-tuple-element.228), channel_id=1, source_target_pairs={{0,2},{2,0},{1,3},{3,1},{4,6},{6,4},{5,7},{7,5},{8,10},{10,8},{9,1... | collective-permute-start | bytes 2064392 | tf_op jit(solution)/shard_map/ppermute | solution.py:1120
  312.4 40.8 %collective-permute-start.41 = (bf16[592,384]{1,0:T(8,128)(2,1)}, bf16[592,384]{1,0:T(8,128)(2,1)}, u32[]{:S(2)}, u32[]{:S(2)}) collective-permute-start(bf16[592,384]{1,0:T(8,128)(2,1)} %get-tuple-element.231), channel_id=1, source_target_pairs={{0,16},{8,24},{16,0},{24,8},{1,17},{9,25},{17,1},{25,9},{2,18},{10... | collective-permute-start | bytes 1363976 | tf_op jit(solution)/shard_map/ppermute | solution.py:1275
  324.1 21.2 %collective-permute-start.43 = (bf16[2,2,144,384]{3,2,1,0:T(8,128)(2,1)}, bf16[2,2,144,384]{3,2,1,0:T(8,128)(2,1)}, u32[]{:S(2)}, u32[]{:S(2)}) collective-permute-start(bf16[2,2,144,384]{3,2,1,0:T(8,128)(2,1)} %get-tuple-element.233), channel_id=1, source_target_pairs={{0,2},{2,0},{1,3},{3,1},{4,6},{6,4},{5,7},{7,5},{8,10},{10,8},{9,1... | collective-permute-start | bytes 1327112 | tf_op jit(solution)/shard_map/ppermute | solution.py:1120
  325.8 19.5 %collective-permute-start.44 = (bf16[2,2,144,384]{3,2,1,0:T(8,128)(2,1)}, bf16[2,2,144,384]{3,2,1,0:T(8,128)(2,1)}, u32[]{:S(2)}, u32[]{:S(2)}) collective-permute-start(bf16[2,2,144,384]{3,2,1,0:T(8,128)(2,1)} %get-tuple-element.235), channel_id=1, source_target_pairs={{0,4},{4,0},{1,5},{5,1},{2,6},{6,2},{3,7},{7,3},{8,12},{12,8},{9,1... | collective-permute-start | bytes 1327112 | tf_op jit(solution)/shard_map/ppermute | solution.py:1120
  334.0 14.5 %collective-permute-start.42 = (bf16[2,448,384]{2,1,0:T(8,128)(2,1)}, bf16[2,448,384]{2,1,0:T(8,128)(2,1)}, u32[]{:S(2)}, u32[]{:S(2)}) collective-permute-start(bf16[2,448,384]{2,1,0:T(8,128)(2,1)} %get-tuple-element.232), channel_id=1, source_target_pairs={{0,8},{8,0},{16,24},{24,16},{1,9},{9,1},{17,25},{25,17},{2,10},{10... | collective-permute-start | bytes 2064392 | tf_op jit(solution)/shard_map/ppermute | solution.py:1275
  347.4 8.0 %collective-permute-start.46 = (bf16[2,144,384]{2,1,0:T(8,128)(2,1)}, bf16[2,144,384]{2,1,0:T(8,128)(2,1)}, u32[]{:S(2)}, u32[]{:S(2)}) collective-permute-start(bf16[2,144,384]{2,1,0:T(8,128)(2,1)} %get-tuple-element.236.refs_3_), channel_id=1, source_target_pairs={{0,4},{4,0},{1,5},{5,1},{2,6},{6,2},{3,7},{7,3},{8,12},{12,8},{9,1... | collective-permute-start | bytes 663560 | tf_op jit(solution)/shard_map/ppermute | solution.py:1120
  347.8 7.7 %collective-permute-start.47 = (bf16[2,144,384]{2,1,0:T(8,128)(2,1)}, bf16[2,144,384]{2,1,0:T(8,128)(2,1)}, u32[]{:S(2)}, u32[]{:S(2)}) collective-permute-start(bf16[2,144,384]{2,1,0:T(8,128)(2,1)} %get-tuple-element.240), channel_id=1, source_target_pairs={{0,2},{2,0},{1,3},{3,1},{4,6},{6,4},{5,7},{7,5},{8,10},{10,8},{9,1... | collective-permute-start | bytes 663560 | tf_op jit(solution)/shard_map/ppermute | solution.py:1120
  350.7 25.5 %collective-permute-start.45 = (bf16[448,384]{1,0:T(8,128)(2,1)}, bf16[448,384]{1,0:T(8,128)(2,1)}, u32[]{:S(2)}, u32[]{:S(2)}) collective-permute-start(bf16[448,384]{1,0:T(8,128)(2,1)} %get-tuple-element.239), channel_id=1, source_target_pairs={{0,16},{8,24},{16,0},{24,8},{1,17},{9,25},{17,1},{25,9},{2,18},{10... | collective-permute-start | bytes 1032200 | tf_op jit(solution)/shard_map/ppermute | solution.py:1275
  355.5 22.9 %copy-start.1 = (f32[8,128]{1,0:T(8,128)S(1)}, f32[8,128]{1,0:T(8,128)}, u32[]{:S(2)}) copy-start(f32[8,128]{1,0:T(8,128)} %get-tuple-element.238) | copy-start | bytes 12292
  357.7 10.5 %collective-permute-start.48 = (bf16[2,144,384]{2,1,0:T(8,128)(2,1)}, bf16[2,144,384]{2,1,0:T(8,128)(2,1)}, u32[]{:S(2)}, u32[]{:S(2)}) collective-permute-start(bf16[2,144,384]{2,1,0:T(8,128)(2,1)} %get-tuple-element.243), channel_id=1, source_target_pairs={{0,8},{8,0},{16,24},{24,16},{1,9},{9,1},{17,25},{25,17},{2,10},{10... | collective-permute-start | bytes 663560 | tf_op jit(solution)/shard_map/ppermute | solution.py:1275
  370.0 6.2 %collective-permute-start.49 = (bf16[144,384]{1,0:T(8,128)(2,1)}, bf16[144,384]{1,0:T(8,128)(2,1)}, u32[]{:S(2)}, u32[]{:S(2)}) collective-permute-start(bf16[144,384]{1,0:T(8,128)(2,1)} %get-tuple-element.245), channel_id=1, source_target_pairs={{0,16},{8,24},{16,0},{24,8},{1,17},{9,25},{17,1},{25,9},{2,18},{10... | collective-permute-start | bytes 331784 | tf_op jit(solution)/shard_map/ppermute | solution.py:1275

commit v6 on v5

--- a/solution.py
+++ b/solution.py
@@ -1165,33 +1165,32 @@
 
 
 def fold_near_kernel(groups, *refs):
-    inputs, (keep_ref, send_ref, *held, out, semaphores) = refs[: 6 * groups], refs[6 * groups :]
+    inputs, targets = refs[: 6 * groups], refs[6 * groups : 6 * groups + 4]
+    *held, out, semaphores = refs[6 * groups + 4 :]
     mine = lax.axis_index("y"), lax.axis_index("x")
-    z_mine = lax.axis_index("z") % 2
+    low, high = lax.axis_index("z") % 2, lax.axis_index("z") // 2
     copies = Copies(semaphores)
     arrivals = []
     for group in range(groups):
         arrays = inputs[6 * group : 6 * group + 6]
         for which in range(2):
-            k, g, got = arrays[3 * which : 3 * which + 3]
+            *kept, got = arrays[3 * which : 3 * which + 3]
             place = held[group]
-            arrivals.append(
-                [copies.start(ref.at[z, mine[which]], place.at[which, n, z]) for z in range(2) for n, ref in enumerate((k, g))]
-                + [copies.start(got, place.at[which, 2])]
-            )
+            arrivals.append(copies.start(got, place.at[which, 2]))
+            for z in range(2):
+                for n, ref in enumerate(kept):
+                    arrivals.append(copies.start(ref.at[z, mine[which]], place.at[which, n, z]))
+    for copy in arrivals:
+        copy.wait()
     leaving = []
-    done = 0
-    for group in range(groups):
-        rows = held[group].shape[3]
-        here = pl.ds(done, rows)
-        for which in range(2):
-            for copy in arrivals[2 * group + which]:
-                copy.wait()
-            for n, (target, z) in enumerate(((send_ref, 1 - z_mine), (keep_ref, z_mine))):
-                total = sum(held[group][which, m, z].astype(F32) for m in range(3))
-                out[n, which, done : done + rows, :] = total.astype(BF16)
-                leaving.append(copies.start(out.at[n, which, here, :], target.at[which, here, :]))
-        done += rows
+    for n, (half, z) in enumerate(((1 - high, 1 - low), (high, 1 - low), (1 - high, low), (high, low))):
+        done = 0
+        for place in held:
+            rows = place.shape[3]
+            total = sum(place[half, m, z].astype(F32) for m in range(3))
+            out[n, done : done + rows, :] = total.astype(BF16)
+            done += rows
+        leaving.append(copies.start(out.at[n], targets[n]))
     for copy in leaving:
         copy.wait()
 
@@ -1203,44 +1202,57 @@
         functools.partial(fold_near_kernel, len(groups)),
         arrays,
         [ANY] * len(arrays),
-        [ANY] * 2,
-        [shape((2, rows, lanes), BF16)] * 2,
+        [ANY] * 4,
+        [shape((rows, lanes), BF16)] * 4,
         (1,),
         "fold_near",
         [pltpu.VMEM((2, 3, 2) + group[0].shape[2:], BF16) for group in groups]
-        + [pltpu.VMEM((2, 2, rows, lanes), BF16), pltpu.SemaphoreType.DMA((14 * len(groups),))],
+        + [pltpu.VMEM((4, rows, lanes), BF16), pltpu.SemaphoreType.DMA((10 * len(groups) + 4,))],
         after,
         weight=FOLD_WEIGHT,
     )
 
 
-def fold_far_kernel(index_ref, k, g, keep, send):
-    z = lax.axis_index("z") // 2
-    keep[...] = sum_of(k, g, z)
-    send[...] = sum_of(k, g, 1 - z)
-
-
-def fold_far(index, keep, got, after=(), weight=FOLD_WEIGHT):
+def fold_far_kernel(k, g, send_ref, held, out, semaphores):
+    copies = Copies(semaphores)
+    for copy in [copies.start(ref, held.at[n]) for n, ref in enumerate((k, g))]:
+        copy.wait()
+    out[...] = sum_of(held.at[0], held.at[1], slice(None))
+    copies.start(out, send_ref).wait()
+
+
+def fold_far(keep, got, after=(), weight=FOLD_WEIGHT):
     return run(
         fold_far_kernel,
-        (index, keep, got),
-        [IN_SMEM] + [whole(keep.shape)] * 2,
-        [whole(keep.shape[1:])] * 2,
-        [shape(keep.shape[1:], BF16)] * 2,
+        (keep, got),
+        [ANY] * 2,
+        ANY,
+        shape(keep.shape, BF16),
         (1,),
         "fold_far",
-        (),
+        [
+            pltpu.VMEM((2,) + keep.shape, BF16),
+            pltpu.VMEM(keep.shape, BF16),
+            pltpu.SemaphoreType.DMA((3,)),
+        ],
         after,
         weight=weight,
     )
 
 
-def settle_kernel(norms, *refs):
-    out, squares = refs[-2:]
+def settle_kernel(norms, groups, *refs):
+    inputs, (before, out, squares, *held, semaphores) = refs[: 3 * groups], refs[3 * groups :]
+    copies = Copies(semaphores)
+    arrivals = []
+    for group in range(groups):
+        sources = inputs[3 * group : 3 * group + 3]
+        arrivals.append([copies.start(ref, held[group].at[n]) for n, ref in enumerate(sources)])
     done = 0
-    parts = 0.0
-    for at in range(0, len(refs) - 2, 2):
-        total = refs[at][...].astype(F32) + refs[at + 1][...].astype(F32)
+    parts = before[...]
+    for group in range(groups):
+        for copy in arrivals[group]:
+            copy.wait()
+        total = sum(held[group][n].astype(F32) for n in range(3))
         out[done : done + total.shape[0], :] = total
         if norms and done == 0:
             core = lax.axis_index("narrow")
@@ -1252,21 +1264,24 @@
         total = total * total
         part = total[:, :128] + total[:, 128:256] + total[:, 256:]
         parts = parts + jnp.sum(part.reshape(-1, 8, 128), axis=0)
+    if squares.shape != parts.shape:
+        parts = jnp.broadcast_to(jnp.sum(parts, axis=0, keepdims=True), squares.shape)
     squares[...] = parts
 
 
-def settle(pairs, norms=0, after=()):
-    arrays = [array for pair in pairs for array in pair]
-    rows, lanes = sum(pair[0].shape[0] for pair in pairs), arrays[0].shape[1]
+def settle(groups, before, norms=0, count=8, after=()):
+    arrays = [array for group in groups for array in group]
+    rows, lanes = sum(group[0].shape[0] for group in groups), arrays[0].shape[1]
     return run(
-        functools.partial(settle_kernel, norms),
-        arrays,
-        [whole(array.shape) for array in arrays],
-        [whole((rows, lanes)), whole((8, 128))],
-        [shape((rows, lanes), F32), shape((8, 128), F32)],
+        functools.partial(settle_kernel, norms, len(groups)),
+        (*arrays, before),
+        [ANY] * len(arrays) + [whole((8, 128))],
+        [whole((rows, lanes)), whole((count, 128))],
+        [shape((rows, lanes), F32), shape((count, 128), F32)],
         (1,),
         "settle",
-        (),
+        [pltpu.VMEM((3,) + group[2].shape, BF16) for group in groups]
+        + [pltpu.SemaphoreType.DMA((3 * len(groups),))],
         after,
     )
 
@@ -1384,6 +1399,7 @@
         kept.append((low, own, peer, m_own, m_peer, rden, ffn_in, xh1, rs1, states, h_own, slope, xh2, rs2))
         low = out
 
+    count = wide * lax.axis_size("narrow")
     up = cotangent
     norm_grads = [None] * LAYERS
     shares = [None] * LAYERS
@@ -1438,12 +1454,12 @@
         )
         ff_first = (ka, by_x(sa), kb, by_y(sb))
         if last:
-            keep, send = fold_near((ff_second, q_second), (ka,))
-            one_near = (keep, near(send))
+            send, side, keep, own_part = fold_near((ff_second, q_second), (ka,))
+            one_cross, one_own = (keep, near(send)), (own_part, near(side))
             g_own, *g_peer = attend_back(*back, gx, states, dkv_got, cos, sin, (keep,))
-            keep, send = fold_far(here, *one_near, (g_own,), 0)
-            one_far = (keep, far(send))
-            after = (keep,)
+            send = fold_far(*one_cross, (g_own,), 0)
+            one_parts = one_own + (far(send),)
+            after = (send,)
         else:
             g_own, *g_peer, up = attend_back(
                 *back, gx, states, dkv_got, cos, sin, (ka,), (qkv, qkv_peer, layer, gfb)
@@ -1461,20 +1477,20 @@
             ff_second = ff_first[:2] + (by_y(sa),) + ff_first[2:] + (by_x(sb),)
             after = (sa,)
             continue
-        keep, send = fold_near((ff_second,), (q_ka,))
-        ff_near = (keep, near(send))
+        send, side, keep, own_part = fold_near((ff_second,), (q_ka,))
+        ff_cross, ff_own = (keep, near(send)), (own_part, near(side))
         up = input_back(g_own, g_peer, qkv, qkv_peer, layer, gfb, (keep,))
         sa, sb = fold_split(*q_first, (up,))
         q_second = q_first[:2] + (by_y(sa),) + q_first[2:] + (by_x(sb),)
-        ff_keep, ff_send = fold_far(here, *ff_near, (sa,))
-        one, one_squares = settle((one_far,), 0, (ff_keep,))
-        keep, send = fold_near((q_second,), (one,))
-        q_near = (keep, near(send))
-        ff_far = (ff_keep, far(ff_send))
-        keep, send = fold_far(here, *q_near, (), 0)
-        zero, zero_squares = settle((ff_far, (keep, far(send))), width // wide // 2)
-
-    count = wide * lax.axis_size("narrow")
+        ff_send = fold_far(*ff_cross, (sa,))
+        ff_parts = ff_own + (far(ff_send),)
+        one, squares = settle((one_parts,), jnp.zeros((8, 128), F32), after=(ff_send,))
+        send, side, keep, own_part = fold_near((q_second,), (one,))
+        q_cross, q_own = (keep, near(send)), (own_part, near(side))
+        send = fold_far(*q_cross, (), 0)
+        part = width // wide // 2
+        zero, squares = settle((ff_parts, q_own + (far(send),)), squares, part, count)
+
     states = (
         qkv_master, qkv_first, qkv_second, out_master, out_first, out_second,
         in_master, in_first, in_second, back_master, back_first, back_second,
@@ -1482,8 +1498,7 @@
     )
     exchange = lambda rows_in: lax.all_to_all(rows_in, every, 0, 0, tiled=True)
     if by_axes:
-        squares = (one_squares + zero_squares).sum(0, keepdims=True)
-        sums = exchange(jnp.broadcast_to(squares, (count, 128)))
+        sums = exchange(squares)
         flip = lambda array: jnp.transpose(array, (0, 2, 1, 3))
         states = tuple(flip(v) for v in states[:3]) + states[3:12] + tuple(
             v.reshape(8, -1) for v in states[12:]

time: 398 us -> 397 us (level)
  waiting for transfers between devices: 34.4 us -> 22.5 us
  starting transfers between devices: 35.3 us -> 42.1 us
    ppermute x6 -> x9, waiting for transfers between devices: 15.6 us -> 6.91 us  [shuffle(): lax.ppermute(values, axis, [(i, i ^ bit) for i in range(lax.axis_size(axi...]
    ppermute x6 -> x9, starting transfers between devices: 10 us -> 16.7 us  [shuffle(): lax.ppermute(values, axis, [(i, i ^ bit) for i in range(lax.axis_size(axi...]
  transfers between devices with their start and end apart: 50 -> 53, of which waited for: 15 -> 13; matrix products, arithmetic and copies ran while one was open for 0% -> 1% of each run, Pallas kernels for 65% -> 66%
where the time goes in v6:
time: 397 us; the launch traced here: 396 us
  Pallas kernels  314 us (79%)
  starting transfers between devices  42.1 us (11%)
  waiting for transfers between devices  22.5 us (6%)
  blocking collectives  14 us (4%)
    pallas_call x32, Pallas kernels, run(): pl.pallas_call(body, grid=grid, in_specs=list(in_specs) + [pl.BlockSpec(m...  314 us
    ppermute x44, starting transfers between devices, swap(): return lax.ppermute(values, axis, [(0, 1), (1, 0)])  25.4 us
    ppermute x9, starting transfers between devices, shuffle(): lax.ppermute(values, axis, [(i, i ^ bit) for i in range(lax.axis_size(axi...  16.7 us
    ppermute x44, waiting for transfers between devices, swap(): return lax.ppermute(values, axis, [(0, 1), (1, 0)])  15.5 us
    all_to_all x1, blocking collectives, shards(): exchange = lambda rows_in: lax.all_to_all(rows_in, every, 0, 0, tiled=True)  14 us
  transfers between devices with their start and end apart: 53, of which 13 were waited for; matrix products, arithmetic and copies ran while one was open for 1% of the time, Pallas kernels for 66%

profile of v6, /device:TPU:0, one launch (start us, length us, event | category | flops | bytes accessed | tf_op | source)
XLA Modules:
  0.0 396.5 jit_solution(5039062588950403957)
XLA Ops:
  1.3 2.4 tables.1
  3.7 6.4 %project.3 = (bf16[1024,768]{1,0:T(8,128)(2,1)}, bf16[1024,768]{1,0:T(8,128)(2,1)}, bf16[1024,384]{1,0:T(8,128)(2,1)}, f32[1,3,128,256]{3,2,1,0:T(8,128)}) custom-call(bf16[1024,768]{1,0:T(8,128)(2,1)} %refs_0_.21, bf16[2,3,768,384]{3,2,1,0:T(8,128)(2,1)} %bitcast.23, f32[1024,128]{1,0:T(8,128)} %get-tuple-element.141.refs_2_.refs_3_.refs_10_, ...), custom_call_target="tpu_custom_call" | custom-call | tf_op jit(solution)/shard_map/project/pallas_call | solution.py:44
  10.6 6.4 %project.4 = (bf16[1024,768]{1,0:T(8,128)(2,1)}, bf16[1024,768]{1,0:T(8,128)(2,1)}, bf16[1024,384]{1,0:T(8,128)(2,1)}, f32[1,3,128,256]{3,2,1,0:T(8,128)}) custom-call(bf16[1024,768]{1,0:T(8,128)(2,1)} %refs_0_.21, bf16[2,3,768,384]{3,2,1,0:T(8,128)(2,1)} %collective-permute-done.refs_1_.refs_2_.refs_13_.refs_5_, ...), custom_call_target="tpu_custom_call" | custom-call | tf_op jit(solution)/shard_map/project/pallas_call | solution.py:44
  17.6 1.5 collective-permute-done.1.refs_7_
  19.3 14.3 %attend.2 = (bf16[1024,384]{1,0:T(8,128)(2,1)}, bf16[1024,384]{1,0:T(8,128)(2,1)}, bf16[1024,768]{1,0:T(8,128)(2,1)}, bf16[1024,768]{1,0:T(8,128)(2,1)}, bf16[10...) custom-call(s32[1,2]{1,0:T(1,128)} %refs_0_.20, ...), custom_call_target="tpu_custom_call" | custom-call | tf_op jit(solution)/shard_map/attend/pallas_call | solution.py:44
  33.6 21.2 %feed.2 = (bf16[1024,1536]{1,0:T(8,128)(2,1)}, bf16[1024,1536]{1,0:T(8,128)(2,1)}, bf16[1024,3072]{1,0:T(8,128)(2,1)}, bf16[1024,768]{1,0:T(8,128)(2,1)}, bf16[1...) custom-call(bf16[1024,768]{1,0:T(8,128)(2,1)} %get-tuple-element.151.refs_0_.refs_5_, bf16[2,768,1536]{2,1,0:T(8,128)(2,1)} %refs_6_.2, ...), custom_call_target="tpu_custom_call" | custom-call | tf_op jit(solution)/shard_map/feed/pallas_call | solution.py:44
  55.4 22.9 %project.5 = (bf16[1024,768]{1,0:T(8,128)(2,1)}, bf16[1024,768]{1,0:T(8,128)(2,1)}, bf16[1024,384]{1,0:T(8,128)(2,1)}, bf16[1024,768]{1,0:T(8,128)(2,1)}, bf16[1...) custom-call(bf16[1024,768]{1,0:T(8,128)(2,1)} %get-tuple-element.154.refs_0_.refs_11_, ...), custom_call_target="tpu_custom_call" | custom-call | tf_op jit(solution)/shard_map/project/pallas_call | solution.py:44
  79.2 1.7 collective-permute-done.6.refs_7_.refs_8_
  81.4 14.3 %attend.3 = (bf16[1024,384]{1,0:T(8,128)(2,1)}, bf16[1024,384]{1,0:T(8,128)(2,1)}, bf16[1024,768]{1,0:T(8,128)(2,1)}, bf16[1024,768]{1,0:T(8,128)(2,1)}, bf16[10...) custom-call(s32[1,2]{1,0:T(1,128)} %refs_0_.20, ...), custom_call_target="tpu_custom_call" | custom-call | tf_op jit(solution)/shard_map/attend/pallas_call | solution.py:44
  96.3 20.0 %feed.3 = (bf16[1024,1536]{1,0:T(8,128)(2,1)}, bf16[1024,1536]{1,0:T(8,128)(2,1)}, bf16[1024,3072]{1,0:T(8,128)(2,1)}, f32[1024,768]{1,0:T(8,128)}, bf16[1024,768]{1,0:T(8,128)(2,1)}, /*index=5*/f32[1024,128]{1,0:T(8,128)}) custom-call(bf16[1024,768]{1,0:T(8,128)(2,1)} %get-tuple-element.162.refs_0_.refs_5_, bf16[2,768,1536]{2,1,0:T(8,128)(2,1)} %refs_6_.2, ...), custom_call_target="tpu_custom_call" | custom-call | tf_op jit(solution)/shard_map/feed/pallas_call | solution.py:44
  116.5 18.6 %feed_back.2 = (bf16[2,1024,768]{2,1,0:T(8,128)(2,1)}, bf16[1024,1536]{1,0:T(8,128)(2,1)}, bf16[1024,1536]{1,0:T(8,128)(2,1)}, f32[4,768]{1,0:T(4,128)}) custom-call(f32[1024,768]{1,0:T(8,128)} %refs_0_.16, f32[1024,128]{1,0:T(8,128)} %get-tuple-element.166.refs_1_, bf16[1024,768]{1,0:T(8,128)(2,1)} %get-tuple-element.167.refs_2_, ...), custom_call_target="tpu_custom_call" | custom-call | tf_op jit(solution)/shard_map/feed_back/pallas_call | solution.py:44
  135.7 7.4 %mix_back.2 = (bf16[1024,1536]{1,0:T(8,128)(2,1)}, bf16[6,128,256]{2,1,0:T(8,128)(2,1)}) custom-call(bf16[2,1024,768]{2,1,0:T(8,128)(2,1)} %get-tuple-element.173.refs_0_.refs_2_.refs_14_, bf16[2,384,768]{2,1,0:T(8,128)(2,1)} %refs_1_.7, bf16[2,384,768]{2,1,0:T(8,128)(2,1)} %collective-permute-done.3.refs_10_.refs_2_, ...), custom_call_target="tpu_custom_call" | custom-call | tf_op jit(solution)/shard_map/mix_back/pallas_call | solution.py:44
  143.5 2.2 collective-permute-done.17.refs_8_
  146.3 0.6 broadcast_in_dim.6.refs_11_.refs_12_
  146.9 21.6 %pack.2 = (bf16[2,2,448,384]{3,2,1,0:T(8,128)(2,1)}, bf16[2,2,448,384]{3,2,1,0:T(8,128)(2,1)}, bf16[2,2,448,384]{3,2,1,0:T(8,128)(2,1)}, bf16[2,2,448,384]{3,2,1,0:T(8,128)(2,1)}) custom-call(s32[1,2]{1,0:T(1,128)} %refs_0_.20, bf16[1024,1536]{1,0:T(8,128)(2,1)} %get-tuple-element.180.refs_1_, ...), custom_call_target="tpu_custom_call" | custom-call | tf_op jit(solution)/shard_map/pack/pallas_call | solution.py:44
  168.5 3.0 collective-permute-start.18
  171.5 1.6 collective-permute-start.19
  173.1 26.0 %attend_back.2 = (bf16[1024,1152]{1,0:T(8,128)(2,1)}, bf16[1024,384]{1,0:T(8,128)(2,1)}, bf16[1024,384]{1,0:T(8,128)(2,1)}, bf16[1024,384]{1,0:T(8,128)(2,1)}, bf16[1024,768]{1,0:T(8,128)(2,1)}) custom-call(s32[1,2]{1,0:T(1,128)} %refs_0_.20, bf16[1024,768]{1,0:T(8,128)(2,1)} %get-tuple-element.155.refs_1_.refs_6_, ...), custom_call_target="tpu_custom_call" | custom-call | tf_op jit(solution)/shard_map/attend_back/pallas_call | solution.py:44
  199.8 2.0 collective-permute-done.20.refs_3_
  201.8 1.1 collective-permute-done.21.refs_4_
  203.0 1.1 collective-permute-done.22.refs_5_
  204.1 9.1 %qkv_grad.2 = (bf16[2,2,144,384]{3,2,1,0:T(8,128)(2,1)}, bf16[2,2,144,384]{3,2,1,0:T(8,128)(2,1)}, bf16[2,2,144,384]{3,2,1,0:T(8,128)(2,1)}, bf16[2,2,144,384]{3,2,1,0:T(8,128)(2,1)}) custom-call(bf16[1024,768]{1,0:T(8,128)(2,1)} %get-tuple-element.154.refs_0_.refs_11_, bf16[1024,1152]{1,0:T(8,128)(2,1)} %get-tuple-element.193.refs_1_.refs_6_, ...), custom_call_target="tpu_custom_call" | custom-call | tf_op jit(solution)/shard_map/qkv_grad/pallas_call | solution.py:44
  213.9 2.6 fold_split.4
  216.5 2.0 collective-permute-start.26
  218.5 18.1 %feed_back.3 = (bf16[2,1024,768]{2,1,0:T(8,128)(2,1)}, bf16[1024,1536]{1,0:T(8,128)(2,1)}, bf16[1024,1536]{1,0:T(8,128)(2,1)}, f32[4,768]{1,0:T(4,128)}) custom-call(bf16[1024,768]{1,0:T(8,128)(2,1)} %get-tuple-element.184.refs_0_, bf16[1024,768]{1,0:T(8,128)(2,1)} %get-tuple-element.185.refs_1_, f32[1024,128]{1,0:T(8,128)} %get-tuple-element.186.refs_2_, ...), custom_call_target="tpu_custom_call" | custom-call | tf_op jit(solution)/shard_map/feed_back/pallas_call | solution.py:44
  236.6 0.7 pad_maximum_fusion
  237.4 0.6 pad.4.refs_11_
  238.6 1.6 collective-permute-start.27
  240.2 2.0 fold_split.5
  242.2 7.4 %mix_back.3 = (bf16[1024,1536]{1,0:T(8,128)(2,1)}, bf16[6,128,256]{2,1,0:T(8,128)(2,1)}) custom-call(bf16[2,1024,768]{2,1,0:T(8,128)(2,1)} %get-tuple-element.199.refs_4_.refs_0_.refs_2_.refs_6_, bf16[2,384,768]{2,1,0:T(8,128)(2,1)} %refs_1_.7, bf16[2,384,768]{2,1,0:T(8,128)(2,1)} %collective-permute-done.3.refs_10_.refs_2_, ...), custom_call_target="tpu_custom_call" | custom-call | tf_op jit(solution)/shard_map/mix_back/pallas_call | solution.py:44
  249.8 1.9 collective-permute-done.25.refs_13_.refs_9_
  252.3 21.6 %pack.3 = (bf16[2,2,448,384]{3,2,1,0:T(8,128)(2,1)}, bf16[2,2,448,384]{3,2,1,0:T(8,128)(2,1)}, bf16[2,2,448,384]{3,2,1,0:T(8,128)(2,1)}, bf16[2,2,448,384]{3,2,1,0:T(8,128)(2,1)}) custom-call(s32[1,2]{1,0:T(1,128)} %refs_0_.20, bf16[1024,1536]{1,0:T(8,128)(2,1)} %get-tuple-element.211.refs_1_, ...), custom_call_target="tpu_custom_call" | custom-call | tf_op jit(solution)/shard_map/pack/pallas_call | solution.py:44
  273.9 2.1 collective-permute-start.33
  276.0 1.6 collective-permute-start.34
  277.6 4.2 %fold_near.3 = (bf16[592,384]{1,0:T(8,128)(2,1)}, bf16[592,384]{1,0:T(8,128)(2,1)}, bf16[592,384]{1,0:T(8,128)(2,1)}, bf16[592,384]{1,0:T(8,128)(2,1)}) custom-call(bf16[2,2,448,384]{3,2,1,0:T(8,128)(2,1)} %get-tuple-element.183.refs_15_.refs_0_, bf16[2,2,448,384]{3,2,1,0:T(8,128)(2,1)} %collective-permute-done.18.refs_1_, ...), custom_call_target="tpu_custom_call" | custom-call | flops 999999995904 | bytes 999999995904 | tf_op jit(solution)/shard_map/fold_near/pallas_call | solution.py:44
  281.8 1.6 collective-permute-start.35
  283.4 19.6 %attend_back.3 = (bf16[1024,1152]{1,0:T(8,128)(2,1)}, bf16[1024,384]{1,0:T(8,128)(2,1)}, bf16[1024,384]{1,0:T(8,128)(2,1)}, bf16[1024,384]{1,0:T(8,128)(2,1)}) custom-call(s32[1,2]{1,0:T(1,128)} %refs_0_.20, bf16[1024,768]{1,0:T(8,128)(2,1)} %get-tuple-element.143.refs_1_.refs_6_, bf16[1024,768]{1,0:T(8,128)(2,1)} %get-tuple-element.144.refs_2_.refs_7_, ...), custom_call_target="tpu_custom_call" | custom-call | tf_op jit(solution)/shard_map/attend_back/pallas_call | solution.py:44
  303.7 2.1 fold_far.3.refs_4_
  306.2 1.5 collective-permute-done.34.refs_3_.refs_4_
  307.7 2.6 fold_split.6
  310.4 1.7 collective-permute-start.36
  312.5 1.6 collective-permute-start.48
  314.1 2.6 collective-permute-start.49
  316.7 9.1 %qkv_grad.3 = (bf16[2,2,144,384]{3,2,1,0:T(8,128)(2,1)}, bf16[2,2,144,384]{3,2,1,0:T(8,128)(2,1)}, bf16[2,2,144,384]{3,2,1,0:T(8,128)(2,1)}, bf16[2,2,144,384]{3,2,1,0:T(8,128)(2,1)}) custom-call(bf16[1024,768]{1,0:T(8,128)(2,1)} %refs_0_.21, bf16[1024,1152]{1,0:T(8,128)(2,1)} %get-tuple-element.218.refs_2_.refs_1_.refs_0_, ...), custom_call_target="tpu_custom_call" | custom-call | tf_op jit(solution)/shard_map/qkv_grad/pallas_call | solution.py:44
  325.8 1.7 collective-permute-start.43
  327.5 0.6 collective-permute-start.44
  328.1 1.3 collective-permute-done.37.refs_5_
  329.4 3.5 fold_near.4
  332.9 2.8 collective-permute-start.42
  335.7 9.8 %input_back.1.refs_4_ = f32[1024,768]{1,0:T(8,128)} custom-call(bf16[1024,1152]{1,0:T(8,128)(2,1)} %get-tuple-element.218.refs_2_.refs_1_.refs_0_, bf16[1024,384]{1,0:T(8,128)(2,1)} %get-tuple-element.219.refs_1_, bf16[1024,384]{1,0:T(8,128)(2,1)} %get-tuple-element.220.refs_2_, bf16[1024,384]{1,0:T(8,128)(2,1)} %get-tuple-element.221.refs_3_, ...), custom_call_target="tpu_custom_call" | custom-call | tf_op jit(solution)/shard_map/input_back/pallas_call | solution.py:44
  345.5 2.0 fold_split.7
  347.9 1.9 fold_far.4.refs_4_
  349.9 3.8 collective-permute-start.45
  353.7 0.6 broadcast_in_dim.7.refs_3_
  354.3 3.2 settle.2
  357.5 2.3 fold_near.5
  359.8 1.6 collective-permute-start.51
  361.9 3.0 collective-permute-done.51.refs_1_
  364.9 1.6 fold_far.5
  366.6 2.2 collective-permute-start.52
  368.8 3.9 collective-permute-done.52.refs_5_
  372.6 3.1 settle.3
  375.7 14.0 %all_to_all.11 = f32[32,1,128]{2,1,0:T(1,128)} all-to-all(f32[32,1,128]{2,1,0:T(1,128)} %bitcast.32), channel_id=1, replica_groups=mesh['z'=4,'y'=2,'x'=2,'narrow'=2] {'z','y','x','narrow'}, dimensions={0} | all-to-all | bytes 32768 | tf_op jit(solution)/shard_map/all_to_all | solution.py:1499
  389.8 6.5 %update.1 = (f32[2,3,48,384]{3,2,1,0:T(8,128)}, f32[2,3,48,384]{3,2,1,0:T(8,128)}, f32[2,3,48,384]{3,2,1,0:T(8,128)}, f32[2,24,768]{2,1,0:T(8,128)}, f32[2,24,76...) custom-call(f32[32,128]{1,0:T(8,128)} %bitcast.31, ...), custom_call_target="tpu_custom_call" | custom-call | tf_op jit(solution)/shard_map/update/pallas_call | solution.py:44
  (83 shorter events, 11.4 us)
Async XLA Ops:
  0.7 9.9 %collective-permute-start = (bf16[2,3,768,384]{3,2,1,0:T(8,128)(2,1)}, bf16[2,3,768,384]{3,2,1,0:T(8,128)(2,1)}, u32[]{:S(2)}, u32[]{:S(2)}) collective-permute-start(bf16[2,3,768,384]{3,2,1,0:T(8,128)(2,1)} %bitcast.22), channel_id=1, source_target_pairs={{0,1},{1,0},{2,3},{3,2},{4,5},{5,4},{6,7},{7,6},{8,9},{9,8},{10,11... | collective-permute-start | bytes 10616840 | tf_op jit(solution)/shard_map/ppermute | solution.py:1120
  1.2 16.0 %collective-permute-start.3 = (bf16[2,384,768]{2,1,0:T(8,128)(2,1)}, bf16[2,384,768]{2,1,0:T(8,128)(2,1)}, u32[]{:S(2)}, u32[]{:S(2)}) collective-permute-start(bf16[2,384,768]{2,1,0:T(8,128)(2,1)} %refs_1_.7), channel_id=1, source_target_pairs={{0,1},{1,0},{2,3},{3,2},{4,5},{5,4},{6,7},{7,6},{8,9},{9,8},{10,11... | collective-permute-start | bytes 3538952 | tf_op jit(solution)/shard_map/ppermute | solution.py:1120
  10.1 7.5 %collective-permute-start.2 = (f32[1,3,128,256]{3,2,1,0:T(8,128)}, f32[1,3,128,256]{3,2,1,0:T(8,128)}, u32[]{:S(2)}, u32[]{:S(2)}) collective-permute-start(f32[1,3,128,256]{3,2,1,0:T(8,128)} %get-tuple-element.150), channel_id=1, source_target_pairs={{0,1},{1,0},{2,3},{3,2},{4,5},{5,4},{6,7},{7,6},{8,9},{9,8},{10,11... | collective-permute-start | bytes 1179656 | tf_op jit(solution)/shard_map/ppermute | solution.py:1120
  17.0 2.1 collective-permute-start.1
  17.2 16.4 %collective-permute-start.4 = (bf16[2,768,1536]{2,1,0:T(8,128)(2,1)}, bf16[2,768,1536]{2,1,0:T(8,128)(2,1)}, u32[]{:S(2)}, u32[]{:S(2)}) collective-permute-start(bf16[2,768,1536]{2,1,0:T(8,128)(2,1)} %refs_6_.2), channel_id=1, source_target_pairs={{0,1},{1,0},{2,3},{3,2},{4,5},{5,4},{6,7},{7,6},{8,9},{9,8},{10,11... | collective-permute-start | bytes 14155784 | tf_op jit(solution)/shard_map/ppermute | solution.py:1120
  19.1 14.4 %collective-permute-start.5 = (bf16[2,1536,768]{2,1,0:T(8,128)(2,1)}, bf16[2,1536,768]{2,1,0:T(8,128)(2,1)}, u32[]{:S(2)}, u32[]{:S(2)}) collective-permute-start(bf16[2,1536,768]{2,1,0:T(8,128)(2,1)} %refs_8_.2), channel_id=1, source_target_pairs={{0,1},{1,0},{2,3},{3,2},{4,5},{5,4},{6,7},{7,6},{8,9},{9,8},{10,11... | collective-permute-start | bytes 14155784 | tf_op jit(solution)/shard_map/ppermute | solution.py:1120
  54.8 41.5 %collective-permute-start.10 = (bf16[1024,1536]{1,0:T(8,128)(2,1)}, bf16[1024,1536]{1,0:T(8,128)(2,1)}, u32[]{:S(2)}, u32[]{:S(2)}) collective-permute-start(bf16[1024,1536]{1,0:T(8,128)(2,1)} %get-tuple-element.164), channel_id=1, source_target_pairs={{0,1},{1,0},{2,3},{3,2},{4,5},{5,4},{6,7},{7,6},{8,9},{9,8},{10,11... | collective-permute-start | bytes 9437192 | tf_op jit(solution)/shard_map/ppermute | solution.py:1120
  55.2 40.4 %collective-permute-start.7 = (bf16[1024,768]{1,0:T(8,128)(2,1)}, bf16[1024,768]{1,0:T(8,128)(2,1)}, u32[]{:S(2)}, u32[]{:S(2)}) collective-permute-start(bf16[1024,768]{1,0:T(8,128)(2,1)} %refs_0_.21), channel_id=1, source_target_pairs={{0,1},{1,0},{2,3},{3,2},{4,5},{5,4},{6,7},{7,6},{8,9},{9,8},{10,11... | collective-permute-start | bytes 4718600 | tf_op jit(solution)/shard_map/ppermute | solution.py:1120
  78.3 2.7 collective-permute-start.6
  78.7 17.5 %collective-permute-start.9 = (bf16[1024,768]{1,0:T(8,128)(2,1)}, bf16[1024,768]{1,0:T(8,128)(2,1)}, u32[]{:S(2)}, u32[]{:S(2)}) collective-permute-start(bf16[1024,768]{1,0:T(8,128)(2,1)} %get-tuple-element.151.refs_0_.refs_5_), channel_id=1, source_target_pairs={{0,1},{1,0},{2,3},{3,2},{4,5},{5,4},{6,7},{7,6},{8,9},{9,8},{10,11... | collective-permute-start | bytes 4718600 | tf_op jit(solution)/shard_map/ppermute | solution.py:1120
  78.9 17.4 %collective-permute-start.11 = (bf16[1024,768]{1,0:T(8,128)(2,1)}, bf16[1024,768]{1,0:T(8,128)(2,1)}, u32[]{:S(2)}, u32[]{:S(2)}) collective-permute-start(bf16[1024,768]{1,0:T(8,128)(2,1)} %get-tuple-element.154.refs_0_.refs_11_), channel_id=1, source_target_pairs={{0,1},{1,0},{2,3},{3,2},{4,5},{5,4},{6,7},{7,6},{8,9},{9,8},{10,11... | collective-permute-start | bytes 4718600 | tf_op jit(solution)/shard_map/ppermute | solution.py:1120
  81.0 14.9 %collective-permute-start.8 = (bf16[1024,384]{1,0:T(8,128)(2,1)}, bf16[1024,384]{1,0:T(8,128)(2,1)}, u32[]{:S(2)}, u32[]{:S(2)}) collective-permute-start(bf16[1024,384]{1,0:T(8,128)(2,1)} %get-tuple-element.163.refs_5_), channel_id=1, source_target_pairs={{0,1},{1,0},{2,3},{3,2},{4,5},{5,4},{6,7},{7,6},{8,9},{9,8},{10,11... | collective-permute-start | bytes 2359304 | tf_op jit(solution)/shard_map/ppermute | solution.py:1120
  95.7 20.8 %collective-permute-start.13 = (bf16[1024,768]{1,0:T(8,128)(2,1)}, bf16[1024,768]{1,0:T(8,128)(2,1)}, u32[]{:S(2)}, u32[]{:S(2)}) collective-permute-start(bf16[1024,768]{1,0:T(8,128)(2,1)} %get-tuple-element.162.refs_0_.refs_5_), channel_id=1, source_target_pairs={{0,1},{1,0},{2,3},{3,2},{4,5},{5,4},{6,7},{7,6},{8,9},{9,8},{10,11... | collective-permute-start | bytes 4718600 | tf_op jit(solution)/shard_map/ppermute | solution.py:1120
  95.9 20.6 %collective-permute-start.12 = (bf16[1024,384]{1,0:T(8,128)(2,1)}, bf16[1024,384]{1,0:T(8,128)(2,1)}, u32[]{:S(2)}, u32[]{:S(2)}) collective-permute-start(bf16[1024,384]{1,0:T(8,128)(2,1)} %get-tuple-element.172.refs_5_), channel_id=1, source_target_pairs={{0,1},{1,0},{2,3},{3,2},{4,5},{5,4},{6,7},{7,6},{8,9},{9,8},{10,11... | collective-permute-start | bytes 2359304 | tf_op jit(solution)/shard_map/ppermute | solution.py:1120
  116.3 19.4 %collective-permute-start.14 = (bf16[1024,1536]{1,0:T(8,128)(2,1)}, bf16[1024,1536]{1,0:T(8,128)(2,1)}, u32[]{:S(2)}, u32[]{:S(2)}) collective-permute-start(bf16[1024,1536]{1,0:T(8,128)(2,1)} %get-tuple-element.176), channel_id=1, source_target_pairs={{0,1},{1,0},{2,3},{3,2},{4,5},{5,4},{6,7},{7,6},{8,9},{9,8},{10,11... | collective-permute-start | bytes 9437192 | tf_op jit(solution)/shard_map/ppermute | solution.py:1120
  135.1 8.4 %collective-permute-start.16 = (bf16[2,1024,768]{2,1,0:T(8,128)(2,1)}, bf16[2,1024,768]{2,1,0:T(8,128)(2,1)}, u32[]{:S(2)}, u32[]{:S(2)}) collective-permute-start(bf16[2,1024,768]{2,1,0:T(8,128)(2,1)} %get-tuple-element.173.refs_0_.refs_2_.refs_14_), channel_id=1, source_target_pairs={{0,1},{1,0},{2,3},{3,2},{4,5},{5,4},{6,7},{7,6},{8,9},{9,8},{10,11... | collective-permute-start | bytes 9437192 | tf_op jit(solution)/shard_map/ppermute | solution.py:1120
  135.6 10.1 %collective-permute-start.17 = (bf16[1024,1536]{1,0:T(8,128)(2,1)}, bf16[1024,1536]{1,0:T(8,128)(2,1)}, u32[]{:S(2)}, u32[]{:S(2)}) collective-permute-start(bf16[1024,1536]{1,0:T(8,128)(2,1)} %get-tuple-element.182), channel_id=1, source_target_pairs={{0,1},{1,0},{2,3},{3,2},{4,5},{5,4},{6,7},{7,6},{8,9},{9,8},{10,11... | collective-permute-start | bytes 9437192 | tf_op jit(solution)/shard_map/ppermute | solution.py:1120
  143.1 3.2 collective-permute-start.15
  168.5 45.3 %collective-permute-start.18 = (bf16[2,2,448,384]{3,2,1,0:T(8,128)(2,1)}, bf16[2,2,448,384]{3,2,1,0:T(8,128)(2,1)}, u32[]{:S(2)}, u32[]{:S(2)}) collective-permute-start(bf16[2,2,448,384]{3,2,1,0:T(8,128)(2,1)} %get-tuple-element.190), channel_id=1, source_target_pairs={{0,2},{2,0},{1,3},{3,1},{4,6},{6,4},{5,7},{7,5},{8,10},{10,8},{9,1... | collective-permute-start | bytes 4128776 | tf_op jit(solution)/shard_map/ppermute | solution.py:1120
  171.5 42.3 %collective-permute-start.19 = (bf16[2,2,448,384]{3,2,1,0:T(8,128)(2,1)}, bf16[2,2,448,384]{3,2,1,0:T(8,128)(2,1)}, u32[]{:S(2)}, u32[]{:S(2)}) collective-permute-start(bf16[2,2,448,384]{3,2,1,0:T(8,128)(2,1)} %get-tuple-element.192), channel_id=1, source_target_pairs={{0,4},{4,0},{1,5},{5,1},{2,6},{6,2},{3,7},{7,3},{8,12},{12,8},{9,1... | collective-permute-start | bytes 4128776 | tf_op jit(solution)/shard_map/ppermute | solution.py:1120
  199.1 2.7 collective-permute-start.20
  199.2 3.7 collective-permute-start.21
  199.7 4.4 %collective-permute-start.22 = (bf16[1024,384]{1,0:T(8,128)(2,1)}, bf16[1024,384]{1,0:T(8,128)(2,1)}, u32[]{:S(2)}, u32[]{:S(2)}) collective-permute-start(bf16[1024,384]{1,0:T(8,128)(2,1)} %get-tuple-element.196), channel_id=1, source_target_pairs={{0,1},{1,0},{2,3},{3,2},{4,5},{5,4},{6,7},{7,6},{8,9},{9,8},{10,11... | collective-permute-start | bytes 2359304 | tf_op jit(solution)/shard_map/ppermute | solution.py:1120
  213.2 25.4 %collective-permute-start.23 = (bf16[2,2,144,384]{3,2,1,0:T(8,128)(2,1)}, bf16[2,2,144,384]{3,2,1,0:T(8,128)(2,1)}, u32[]{:S(2)}, u32[]{:S(2)}) collective-permute-start(bf16[2,2,144,384]{3,2,1,0:T(8,128)(2,1)} %get-tuple-element.202), channel_id=1, source_target_pairs={{0,2},{2,0},{1,3},{3,1},{4,6},{6,4},{5,7},{7,5},{8,10},{10,8},{9,1... | collective-permute-start | bytes 1327112 | tf_op jit(solution)/shard_map/ppermute | solution.py:1120
  213.8 24.8 %collective-permute-start.24 = (bf16[2,2,144,384]{3,2,1,0:T(8,128)(2,1)}, bf16[2,2,144,384]{3,2,1,0:T(8,128)(2,1)}, u32[]{:S(2)}, u32[]{:S(2)}) collective-permute-start(bf16[2,2,144,384]{3,2,1,0:T(8,128)(2,1)} %get-tuple-element.204), channel_id=1, source_target_pairs={{0,4},{4,0},{1,5},{5,1},{2,6},{6,2},{3,7},{7,3},{8,12},{12,8},{9,1... | collective-permute-start | bytes 1327112 | tf_op jit(solution)/shard_map/ppermute | solution.py:1120
  216.5 61.1 %collective-permute-start.26 = (bf16[2,448,384]{2,1,0:T(8,128)(2,1)}, bf16[2,448,384]{2,1,0:T(8,128)(2,1)}, u32[]{:S(2)}, u32[]{:S(2)}) collective-permute-start(bf16[2,448,384]{2,1,0:T(8,128)(2,1)} %get-tuple-element.198.refs_11_), channel_id=1, source_target_pairs={{0,4},{4,0},{1,5},{5,1},{2,6},{6,2},{3,7},{7,3},{8,12},{12,8},{9,1... | collective-permute-start | bytes 2064392 | tf_op jit(solution)/shard_map/ppermute | solution.py:1120
  218.5 18.1 %copy-start = (f32[4,768]{1,0:T(4,128)S(1)}, f32[4,768]{1,0:T(4,128)}, u32[]{:S(2)}) copy-start(f32[4,768]{1,0:T(4,128)} %get-tuple-element.215) | copy-start | bytes 36868
  238.1 11.5 %collective-permute-start.32 = (f32[16,8,128]{2,1,0:T(8,128)}, f32[16,8,128]{2,1,0:T(8,128)}, u32[]{:S(2)}, u32[]{:S(2)}) collective-permute-start(f32[16,8,128]{2,1,0:T(8,128)} %pad.4.refs_11_), channel_id=1, source_target_pairs={{0,1},{1,0},{2,3},{3,2},{4,5},{5,4},{6,7},{7,6},{8,9},{9,8},{10,11... | collective-permute-start | bytes 196616 | tf_op jit(solution)/shard_map/ppermute | solution.py:1120
  238.1 14.1 %collective-permute-start.30 = (bf16[2,1024,768]{2,1,0:T(8,128)(2,1)}, bf16[2,1024,768]{2,1,0:T(8,128)(2,1)}, u32[]{:S(2)}, u32[]{:S(2)}) collective-permute-start(bf16[2,1024,768]{2,1,0:T(8,128)(2,1)} %get-tuple-element.199.refs_4_.refs_0_.refs_2_.refs_6_), channel_id=1, source_target_pairs={{0,1},{1,0},{2,3},{3,2},{4,5},{5,4},{6,7},{7,6},{8,9},{9,8},{10,11... | collective-permute-start | bytes 9437192 | tf_op jit(solution)/shard_map/ppermute | solution.py:1120
  238.6 13.7 %collective-permute-start.31 = (bf16[1024,1536]{1,0:T(8,128)(2,1)}, bf16[1024,1536]{1,0:T(8,128)(2,1)}, u32[]{:S(2)}, u32[]{:S(2)}) collective-permute-start(bf16[1024,1536]{1,0:T(8,128)(2,1)} %get-tuple-element.213), channel_id=1, source_target_pairs={{0,1},{1,0},{2,3},{3,2},{4,5},{5,4},{6,7},{7,6},{8,9},{9,8},{10,11... | collective-permute-start | bytes 9437192 | tf_op jit(solution)/shard_map/ppermute | solution.py:1120
  238.6 39.0 %collective-permute-start.27 = (bf16[2,448,384]{2,1,0:T(8,128)(2,1)}, bf16[2,448,384]{2,1,0:T(8,128)(2,1)}, u32[]{:S(2)}, u32[]{:S(2)}) collective-permute-start(bf16[2,448,384]{2,1,0:T(8,128)(2,1)} %get-tuple-element.209), channel_id=1, source_target_pairs={{0,2},{2,0},{1,3},{3,1},{4,6},{6,4},{5,7},{7,5},{8,10},{10,8},{9,1... | collective-permute-start | bytes 2064392 | tf_op jit(solution)/shard_map/ppermute | solution.py:1120
  249.6 2.1 collective-permute-start.25
  251.8 24.2 %collective-permute-start.28 = (bf16[2,144,384]{2,1,0:T(8,128)(2,1)}, bf16[2,144,384]{2,1,0:T(8,128)(2,1)}, u32[]{:S(2)}, u32[]{:S(2)}) collective-permute-start(bf16[2,144,384]{2,1,0:T(8,128)(2,1)} %get-tuple-element.205.refs_8_), channel_id=1, source_target_pairs={{0,4},{4,0},{1,5},{5,1},{2,6},{6,2},{3,7},{7,3},{8,12},{12,8},{9,1... | collective-permute-start | bytes 663560 | tf_op jit(solution)/shard_map/ppermute | solution.py:1120
  252.2 25.4 %collective-permute-start.29 = (bf16[2,144,384]{2,1,0:T(8,128)(2,1)}, bf16[2,144,384]{2,1,0:T(8,128)(2,1)}, u32[]{:S(2)}, u32[]{:S(2)}) collective-permute-start(bf16[2,144,384]{2,1,0:T(8,128)(2,1)} %get-tuple-element.210), channel_id=1, source_target_pairs={{0,2},{2,0},{1,3},{3,1},{4,6},{6,4},{5,7},{7,5},{8,10},{10,8},{9,1... | collective-permute-start | bytes 663560 | tf_op jit(solution)/shard_map/ppermute | solution.py:1120
  273.9 32.3 %collective-permute-start.33 = (bf16[2,2,448,384]{3,2,1,0:T(8,128)(2,1)}, bf16[2,2,448,384]{3,2,1,0:T(8,128)(2,1)}, u32[]{:S(2)}, u32[]{:S(2)}) collective-permute-start(bf16[2,2,448,384]{3,2,1,0:T(8,128)(2,1)} %get-tuple-element.222), channel_id=1, source_target_pairs={{0,2},{2,0},{1,3},{3,1},{4,6},{6,4},{5,7},{7,5},{8,10},{10,8},{9,1... | collective-permute-start | bytes 4128776 | tf_op jit(solution)/shard_map/ppermute | solution.py:1120
  276.0 31.7 %collective-permute-start.34 = (bf16[2,2,448,384]{3,2,1,0:T(8,128)(2,1)}, bf16[2,2,448,384]{3,2,1,0:T(8,128)(2,1)}, u32[]{:S(2)}, u32[]{:S(2)}) collective-permute-start(bf16[2,2,448,384]{3,2,1,0:T(8,128)(2,1)} %get-tuple-element.224), channel_id=1, source_target_pairs={{0,4},{4,0},{1,5},{5,1},{2,6},{6,2},{3,7},{7,3},{8,12},{12,8},{9,1... | collective-permute-start | bytes 4128776 | tf_op jit(solution)/shard_map/ppermute | solution.py:1120
  281.8 21.8 %collective-permute-start.35 = (bf16[592,384]{1,0:T(8,128)(2,1)}, bf16[592,384]{1,0:T(8,128)(2,1)}, u32[]{:S(2)}, u32[]{:S(2)}) collective-permute-start(bf16[592,384]{1,0:T(8,128)(2,1)} %get-tuple-element.225), channel_id=1, source_target_pairs={{0,8},{8,0},{16,24},{24,16},{1,9},{9,1},{17,25},{25,17},{2,10},{10... | collective-permute-start | bytes 1363976 | tf_op jit(solution)/shard_map/ppermute | solution.py:1290
  303.1 9.4 %collective-permute-start.38 = (bf16[1024,384]{1,0:T(8,128)(2,1)}, bf16[1024,384]{1,0:T(8,128)(2,1)}, u32[]{:S(2)}, u32[]{:S(2)}) collective-permute-start(bf16[1024,384]{1,0:T(8,128)(2,1)} %get-tuple-element.219.refs_1_), channel_id=1, source_target_pairs={{0,1},{1,0},{2,3},{3,2},{4,5},{5,4},{6,7},{7,6},{8,9},{9,8},{10,11... | collective-permute-start | bytes 2359304 | tf_op jit(solution)/shard_map/ppermute | solution.py:1120
  303.1 10.9 %collective-permute-start.39 = (bf16[1024,384]{1,0:T(8,128)(2,1)}, bf16[1024,384]{1,0:T(8,128)(2,1)}, u32[]{:S(2)}, u32[]{:S(2)}) collective-permute-start(bf16[1024,384]{1,0:T(8,128)(2,1)} %get-tuple-element.220.refs_2_), channel_id=1, source_target_pairs={{0,1},{1,0},{2,3},{3,2},{4,5},{5,4},{6,7},{7,6},{8,9},{9,8},{10,11... | collective-permute-start | bytes 2359304 | tf_op jit(solution)/shard_map/ppermute | solution.py:1120
  303.6 13.1 %collective-permute-start.40 = (bf16[1024,384]{1,0:T(8,128)(2,1)}, bf16[1024,384]{1,0:T(8,128)(2,1)}, u32[]{:S(2)}, u32[]{:S(2)}) collective-permute-start(bf16[1024,384]{1,0:T(8,128)(2,1)} %get-tuple-element.221.refs_3_), channel_id=1, source_target_pairs={{0,1},{1,0},{2,3},{3,2},{4,5},{5,4},{6,7},{7,6},{8,9},{9,8},{10,11... | collective-permute-start | bytes 2359304 | tf_op jit(solution)/shard_map/ppermute | solution.py:1120
  310.4 17.1 %collective-permute-start.36 = (bf16[2,448,384]{2,1,0:T(8,128)(2,1)}, bf16[2,448,384]{2,1,0:T(8,128)(2,1)}, u32[]{:S(2)}, u32[]{:S(2)}) collective-permute-start(bf16[2,448,384]{2,1,0:T(8,128)(2,1)} %get-tuple-element.226.refs_6_), channel_id=1, source_target_pairs={{0,4},{4,0},{1,5},{5,1},{2,6},{6,2},{3,7},{7,3},{8,12},{12,8},{9,1... | collective-permute-start | bytes 2064392 | tf_op jit(solution)/shard_map/ppermute | solution.py:1120
  312.1 17.3 %collective-permute-start.37 = (bf16[2,448,384]{2,1,0:T(8,128)(2,1)}, bf16[2,448,384]{2,1,0:T(8,128)(2,1)}, u32[]{:S(2)}, u32[]{:S(2)}) collective-permute-start(bf16[2,448,384]{2,1,0:T(8,128)(2,1)} %get-tuple-element.227), channel_id=1, source_target_pairs={{0,2},{2,0},{1,3},{3,1},{4,6},{6,4},{5,7},{7,5},{8,10},{10,8},{9,1... | collective-permute-start | bytes 2064392 | tf_op jit(solution)/shard_map/ppermute | solution.py:1120
  312.5 37.4 %collective-permute-start.48 = (bf16[592,384]{1,0:T(8,128)(2,1)}, bf16[592,384]{1,0:T(8,128)(2,1)}, u32[]{:S(2)}, u32[]{:S(2)}) collective-permute-start(bf16[592,384]{1,0:T(8,128)(2,1)} %get-tuple-element.239), channel_id=1, source_target_pairs={{0,8},{8,0},{16,24},{24,16},{1,9},{9,1},{17,25},{25,17},{2,10},{10... | collective-permute-start | bytes 1363976 | tf_op jit(solution)/shard_map/ppermute | solution.py:1290
  314.1 39.6 %collective-permute-start.49 = (bf16[592,384]{1,0:T(8,128)(2,1)}, bf16[592,384]{1,0:T(8,128)(2,1)}, u32[]{:S(2)}, u32[]{:S(2)}) collective-permute-start(bf16[592,384]{1,0:T(8,128)(2,1)} %fold_far.3.refs_4_), channel_id=1, source_target_pairs={{0,16},{8,24},{16,0},{24,8},{1,17},{9,25},{17,1},{25,9},{2,18},{10... | collective-permute-start | bytes 1363976 | tf_op jit(solution)/shard_map/ppermute | solution.py:1290
  325.8 19.7 %collective-permute-start.43 = (bf16[2,2,144,384]{3,2,1,0:T(8,128)(2,1)}, bf16[2,2,144,384]{3,2,1,0:T(8,128)(2,1)}, u32[]{:S(2)}, u32[]{:S(2)}) collective-permute-start(bf16[2,2,144,384]{3,2,1,0:T(8,128)(2,1)} %get-tuple-element.233), channel_id=1, source_target_pairs={{0,2},{2,0},{1,3},{3,1},{4,6},{6,4},{5,7},{7,5},{8,10},{10,8},{9,1... | collective-permute-start | bytes 1327112 | tf_op jit(solution)/shard_map/ppermute | solution.py:1120
  327.5 18.0 %collective-permute-start.44 = (bf16[2,2,144,384]{3,2,1,0:T(8,128)(2,1)}, bf16[2,2,144,384]{3,2,1,0:T(8,128)(2,1)}, u32[]{:S(2)}, u32[]{:S(2)}) collective-permute-start(bf16[2,2,144,384]{3,2,1,0:T(8,128)(2,1)} %get-tuple-element.235), channel_id=1, source_target_pairs={{0,4},{4,0},{1,5},{5,1},{2,6},{6,2},{3,7},{7,3},{8,12},{12,8},{9,1... | collective-permute-start | bytes 1327112 | tf_op jit(solution)/shard_map/ppermute | solution.py:1120
  332.9 15.0 %collective-permute-start.42 = (bf16[448,384]{1,0:T(8,128)(2,1)}, bf16[448,384]{1,0:T(8,128)(2,1)}, u32[]{:S(2)}, u32[]{:S(2)}) collective-permute-start(bf16[448,384]{1,0:T(8,128)(2,1)} %get-tuple-element.232), channel_id=1, source_target_pairs={{0,8},{8,0},{16,24},{24,16},{1,9},{9,1},{17,25},{25,17},{2,10},{10... | collective-permute-start | bytes 1032200 | tf_op jit(solution)/shard_map/ppermute | solution.py:1290
  347.5 9.9 %collective-permute-start.46 = (bf16[2,144,384]{2,1,0:T(8,128)(2,1)}, bf16[2,144,384]{2,1,0:T(8,128)(2,1)}, u32[]{:S(2)}, u32[]{:S(2)}) collective-permute-start(bf16[2,144,384]{2,1,0:T(8,128)(2,1)} %get-tuple-element.236.refs_2_), channel_id=1, source_target_pairs={{0,4},{4,0},{1,5},{5,1},{2,6},{6,2},{3,7},{7,3},{8,12},{12,8},{9,1... | collective-permute-start | bytes 663560 | tf_op jit(solution)/shard_map/ppermute | solution.py:1120
  347.9 9.6 %collective-permute-start.47 = (bf16[2,144,384]{2,1,0:T(8,128)(2,1)}, bf16[2,144,384]{2,1,0:T(8,128)(2,1)}, u32[]{:S(2)}, u32[]{:S(2)}) collective-permute-start(bf16[2,144,384]{2,1,0:T(8,128)(2,1)} %get-tuple-element.237), channel_id=1, source_target_pairs={{0,2},{2,0},{1,3},{3,1},{4,6},{6,4},{5,7},{7,5},{8,10},{10,8},{9,1... | collective-permute-start | bytes 663560 | tf_op jit(solution)/shard_map/ppermute | solution.py:1120
  347.9 20.8 %collective-permute-start.41 = (bf16[448,384]{1,0:T(8,128)(2,1)}, bf16[448,384]{1,0:T(8,128)(2,1)}, u32[]{:S(2)}, u32[]{:S(2)}) collective-permute-start(bf16[448,384]{1,0:T(8,128)(2,1)} %get-tuple-element.231), channel_id=1, source_target_pairs={{0,8},{8,0},{16,24},{24,16},{1,9},{9,1},{17,25},{25,17},{2,10},{10... | collective-permute-start | bytes 1032200 | tf_op jit(solution)/shard_map/ppermute | solution.py:1290
  349.9 22.7 %collective-permute-start.45 = (bf16[448,384]{1,0:T(8,128)(2,1)}, bf16[448,384]{1,0:T(8,128)(2,1)}, u32[]{:S(2)}, u32[]{:S(2)}) collective-permute-start(bf16[448,384]{1,0:T(8,128)(2,1)} %fold_far.4.refs_4_), channel_id=1, source_target_pairs={{0,16},{8,24},{16,0},{24,8},{1,17},{9,25},{17,1},{25,9},{2,18},{10... | collective-permute-start | bytes 1032200 | tf_op jit(solution)/shard_map/ppermute | solution.py:1290
  359.8 5.1 %collective-permute-start.51 = (bf16[144,384]{1,0:T(8,128)(2,1)}, bf16[144,384]{1,0:T(8,128)(2,1)}, u32[]{:S(2)}, u32[]{:S(2)}) collective-permute-start(bf16[144,384]{1,0:T(8,128)(2,1)} %get-tuple-element.244), channel_id=1, source_target_pairs={{0,8},{8,0},{16,24},{24,16},{1,9},{9,1},{17,25},{25,17},{2,10},{10... | collective-permute-start | bytes 331784 | tf_op jit(solution)/shard_map/ppermute | solution.py:1290
  361.4 7.3 %collective-permute-start.50 = (bf16[144,384]{1,0:T(8,128)(2,1)}, bf16[144,384]{1,0:T(8,128)(2,1)}, u32[]{:S(2)}, u32[]{:S(2)}) collective-permute-start(bf16[144,384]{1,0:T(8,128)(2,1)} %get-tuple-element.242), channel_id=1, source_target_pairs={{0,8},{8,0},{16,24},{24,16},{1,9},{9,1},{17,25},{25,17},{2,10},{10... | collective-permute-start | bytes 331784 | tf_op jit(solution)/shard_map/ppermute | solution.py:1290
  366.6 6.0 %collective-permute-start.52 = (bf16[144,384]{1,0:T(8,128)(2,1)}, bf16[144,384]{1,0:T(8,128)(2,1)}, u32[]{:S(2)}, u32[]{:S(2)}) collective-permute-start(bf16[144,384]{1,0:T(8,128)(2,1)} %fold_far.5), channel_id=1, source_target_pairs={{0,16},{8,24},{16,0},{24,8},{1,17},{9,25},{17,1},{25,9},{2,18},{10... | collective-permute-start | bytes 331784 | tf_op jit(solution)/shard_map/ppermute | solution.py:1290
